TPU v7x, 32 devices: a whole 2x2x4 slice. The times are simulated.
32 devices in a mesh: ens: 2 (over y), gx: 4 (over z), gy: 2 (over x), gz: 2 (over core).
Axes of the slice: x: 2, y: 2, z: 4, core: 2. Of those that a mesh axis runs over, the one named last changes fastest.
Arguments:
- velocity: float32 [3, 128, 64, 256], P(None, ('ens', 'gx'), 'gy', 'gz'), parts along dimension 1, may hold values from -6 to 6
- stress: float32 [6, 128, 64, 256], P(None, ('ens', 'gx'), 'gy', 'gz'), parts along dimension 1, may hold values from -6 to 6
- memory: float32 [6, 128, 64, 256], P(None, ('ens', 'gx'), 'gy', 'gz'), parts along dimension 1, may hold values from -3 to 3
- material: int32 [128, 64, 256], P(('ens', 'gx'), 'gy', 'gz'), parts along dimension 0, may hold values from 0 to 7
- material_table: float32 [5, 16], P(None, 'ens'), parts along dimension 1, may hold values from 0.4 to 1.6
- fault_mask: int32 [128, 256], P(('ens', 'gx', 'gy'), 'gz'), parts along dimension 0, may hold values 0 or 1
- zone_label: int32 [128, 256], P(('ens', 'gx', 'gy'), 'gz'), parts along dimension 0, may hold values from 0 to 3
- patch_anchor: int32 [4], P('ens'), parts along dimension 0, may hold values from 0 to 240, as said below
- friction_table: float32 [3, 8], P(None, 'ens'), parts along dimension 1, may hold values from 0.4 to 1.6
- prestress: float32 [128, 2, 256], P(('ens', 'gx', 'gy'), None, 'gz'), parts along dimension 0, may hold values from -8 to 8
- normal_stress: float32 [128, 256], P(('ens', 'gx', 'gy'), 'gz'), parts along dimension 0, may hold values from 2 to 8
- slip_path: float32 [128, 256], P(('ens', 'gx', 'gy'), 'gz'), parts along dimension 0, may hold values from 0 to 0.4
Outputs:
- new_velocity: float32 [3, 128, 64, 256], P(None, ('ens', 'gx'), 'gy', 'gz'), parts along dimension 1
- new_stress: float32 [6, 128, 64, 256], P(None, ('ens', 'gx'), 'gy', 'gz'), parts along dimension 1
- new_memory: float32 [6, 128, 64, 256], P(None, ('ens', 'gx'), 'gy', 'gz'), parts along dimension 1
- new_slip: float32 [128, 256], P(('ens', 'gx', 'gy'), 'gz'), parts along dimension 0
There are 2 independent parts, one for each index of `ens`. A program takes and returns all parts, laid end to end along the dimension named above; each array names one. Nothing has to cross between parts.
Inputs may be any that keep to these rules, and one draw needn't show every extreme that they name: patch_anchor[0] lies in 0 to 48 and patch_anchor[1] in 0 to 240; the index whose range is longer (the first one if both are equal) is at the far end of its range.
All inputs are finite; a program needn't handle non-finite values. No bound on the sum of `fault_mask` on one device may be relied on, other than what follows from the above.
Results may differ from a plain program's by a relative error of at most 0.0001.
Values sent between devices are 32-bit elements; how exact they have to be, the bound alone decides.
No kernel may reach another device: no remote copies, remote signals or barrier semaphores. Data moves between devices by JAX's collectives and lax.ppermute only.
A program may use at most 64 MiB of HBM per device.

v0:
```python
import jax
import jax.numpy as jnp
from jax import lax
from jax.sharding import PartitionSpec as P

STEPS = 2
CLASSES = 8
ZONES = 4
PATCH = 8


coef_near = 9.0 / 8.0
coef_far = -1.0 / 24.0
time_step = 0.15


def with_halo(cells, sides, width):
    for axis, dim in sides:
        count = lax.axis_size(axis)
        ends = count - 1
        head = lax.slice_in_dim(cells, 0, width, axis=dim)
        tail = lax.slice_in_dim(cells, cells.shape[dim] - width, cells.shape[dim], axis=dim)
        cells = jnp.concatenate(
            [
                lax.ppermute(tail, axis, [(i, (i + 1) % count) for i in range(ends)]),
                cells,
                lax.ppermute(head, axis, [((i + 1) % count, i) for i in range(ends)]),
            ],
            axis=dim,
        )
    return cells


def shifted_2(block, axis, distance):
    devices = range(lax.axis_size(axis))
    route = [(i - distance, i) for i in devices if i - distance in devices]
    return lax.ppermute(block, axis, route)


def shifted(field, axis, start, count):
    return lax.slice_in_dim(field, start, start + count, axis=axis)


def forward_diff(field, axis):
    count = field.shape[axis] - 4
    return coef_near * (
        shifted(field, axis, 3, count) - shifted(field, axis, 2, count)
    ) + coef_far * (shifted(field, axis, 4, count) - shifted(field, axis, 1, count))


def backward_diff(field, axis):
    count = field.shape[axis] - 4
    return coef_near * (
        shifted(field, axis, 2, count) - shifted(field, axis, 1, count)
    ) + coef_far * (shifted(field, axis, 3, count) - shifted(field, axis, 0, count))


def accelerate(along_x, along_y, along_z):
    first = (
        forward_diff(along_x[0], 0) + backward_diff(along_y[0], 1) + backward_diff(along_z[0], 2)
    )
    second = (
        backward_diff(along_x[1], 0) + forward_diff(along_y[1], 1) + backward_diff(along_z[1], 2)
    )
    third = (
        backward_diff(along_x[2], 0) + backward_diff(along_y[2], 1) + forward_diff(along_z[2], 2)
    )
    return jnp.stack([first, second, third])


def strain_rates(along_x, along_y, along_z):
    exx = backward_diff(along_x[0], 0)
    eyy = backward_diff(along_y[1], 1)
    ezz = backward_diff(along_z[2], 2)
    exy = forward_diff(along_y[0], 1) + forward_diff(along_x[1], 0)
    exz = forward_diff(along_z[0], 2) + forward_diff(along_x[2], 0)
    eyz = forward_diff(along_z[1], 2) + forward_diff(along_y[2], 1)
    return (exx, eyy, ezz, exy, exz, eyz)


def properties(material, material_table):
    labels = jnp.arange(CLASSES, dtype=jnp.int32)[:, None, None, None]
    onehot = (material[None] == labels).astype(jnp.float32)
    return jnp.einsum("rc,cxyz->rxyz", material_table, onehot, precision=lax.Precision.HIGHEST)


def update_stress(stress, memory, rates, props):
    lame = props[0]
    shear = props[1]
    relax = props[3]
    anelastic = 0.3 * props[4]
    volume = rates[0] + rates[1] + rates[2]
    elastic = jnp.stack(
        [
            lame * volume + 2.0 * shear * rates[0],
            lame * volume + 2.0 * shear * rates[1],
            lame * volume + 2.0 * shear * rates[2],
            shear * rates[3],
            shear * rates[4],
            shear * rates[5],
        ]
    )
    decay = jnp.exp(-time_step / relax)
    new_memory = decay * memory - (1.0 - decay) * anelastic * elastic
    new_stress = stress + time_step * (elastic + new_memory)
    return (new_stress, new_memory)


def friction(
    faces, prestress, normal_stress, slip, zone_label, fault_mask, inpatch, friction_table
):
    labels = jnp.arange(ZONES, dtype=jnp.int32)[:, None, None]
    onehot = (zone_label[None] == labels).astype(jnp.float32)
    params = jnp.einsum("pk,krc->prc", friction_table, onehot, precision=lax.Precision.HIGHEST)
    dynamic = 0.4 * params[0]
    static = jnp.where(inpatch, dynamic, dynamic + 0.5 * params[1])
    distance = 0.2 * params[2]
    minus_x, minus_z, minus_b = (faces[:, 0], faces[:, 1], faces[:, 2])
    plus_x, plus_z, plus_b = (faces[:, 3], faces[:, 4], faces[:, 5])
    bsum = minus_b + plus_b
    trial_x = (plus_x - minus_x) / (time_step * bsum) + prestress[:, 0]
    trial_z = (plus_z - minus_z) / (time_step * bsum) + prestress[:, 1]
    size_trial = jnp.sqrt(trial_x * trial_x + trial_z * trial_z)
    weaken = jnp.minimum(slip / distance, 1.0)
    strength = (static - (static - dynamic) * weaken) * normal_stress
    factor = jnp.where(fault_mask == 1, strength / jnp.maximum(size_trial, strength), 1.0)
    jump_x = trial_x * factor - prestress[:, 0]
    jump_z = trial_z * factor - prestress[:, 1]
    new_slip = slip + time_step * time_step * bsum * (size_trial - size_trial * factor)
    change = jnp.stack(
        [
            jump_x * time_step * minus_b,
            jump_z * time_step * minus_b,
            -jump_x * time_step * plus_b,
            -jump_z * time_step * plus_b,
        ],
        axis=1,
    )
    return (change, new_slip)


def trimmed(padded, keep):
    index = [slice(None)] * 4
    for dim in (1, 2, 3):
        if dim != keep:
            index[dim] = slice(2, -2)
    return padded[tuple(index)]


def fault_cut(padded, dim):
    count = padded.shape[dim]
    shape = [1] * padded.ndim
    shape[dim] = count
    place = jnp.arange(count).reshape(shape)
    band = lax.axis_index("gy")
    middle = lax.axis_size("gy") // 2
    remove = (place < 2) & (band == middle) | (place >= count - 2) & (band == middle - 1)
    return jnp.where(remove, 0.0, padded)


def patch_mask(row_start, rows, depth_start, depths, patch_anchor):
    along = row_start + jnp.arange(rows, dtype=jnp.int32)[:, None]
    depth = depth_start + jnp.arange(depths, dtype=jnp.int32)[None, :]
    return (
        (along >= patch_anchor[0])
        & (along < patch_anchor[0] + 2 * PATCH)
        & (depth >= patch_anchor[1])
        & (depth < patch_anchor[1] + 2 * PATCH)
    )


def shards(
    velocity,
    stress,
    memory,
    material,
    material_table,
    fault_mask,
    zone_label,
    patch_anchor,
    friction_table,
    prestress,
    normal_stress,
    slip_path,
):
    props = properties(material, material_table)
    buoyancy = props[2]
    band = lax.axis_index("gy")
    middle = lax.axis_size("gy") // 2
    minus_flag = (band == middle - 1).astype(jnp.float32)
    plus_flag = (band == middle).astype(jnp.float32)
    plus_side = band == middle
    minus_side = band == middle - 1
    depth_start = lax.axis_index("gz") * velocity.shape[3]
    row_start = lax.axis_index("gx") * velocity.shape[1]
    state_pre, state_normal, state_slip = (
        lax.all_gather(prestress, "gy", axis=0, tiled=True),
        lax.all_gather(normal_stress, "gy", axis=0, tiled=True),
        lax.all_gather(slip_path, "gy", axis=0, tiled=True),
    )
    state_zone, state_mask = (
        lax.all_gather(zone_label, "gy", axis=0, tiled=True),
        lax.all_gather(fault_mask, "gy", axis=0, tiled=True),
    )
    inpatch = patch_mask(row_start, velocity.shape[1], depth_start, velocity.shape[3], patch_anchor)
    for step in range(STEPS):
        padded = fault_cut(with_halo(stress, (("gx", 1), ("gy", 2), ("gz", 3)), 2), 2)
        strip_x = trimmed(padded, 1)
        strip_y = trimmed(padded, 2)
        strip_z = trimmed(padded, 3)
        tuple_x = (strip_x[0], strip_x[3], strip_x[4])
        tuple_y = (strip_y[3], strip_y[1], strip_y[5])
        tuple_z = (strip_z[4], strip_z[5], strip_z[2])
        velocity = velocity + time_step * buoyancy * accelerate(tuple_x, tuple_y, tuple_z)
        last_row = jnp.stack(
            [velocity[0, :, -1, :], velocity[2, :, -1, :], buoyancy[:, -1, :]], axis=1
        )
        first_row = jnp.stack(
            [velocity[0, :, 0, :], velocity[2, :, 0, :], buoyancy[:, 0, :]], axis=1
        )
        own_face = jnp.where(minus_side, last_row, first_row)
        from_above = shifted_2(own_face, "gy", -1)
        from_below = shifted_2(own_face, "gy", 1)
        minus_face = jnp.where(plus_side, from_below, own_face)
        plus_face = jnp.where(plus_side, own_face, from_above)
        change, state_slip = friction(
            jnp.concatenate([minus_face, plus_face], axis=1),
            state_pre,
            state_normal,
            state_slip,
            state_zone,
            state_mask,
            inpatch,
            friction_table,
        )
        velocity = velocity.at[0, :, -1, :].add(change[:, 0] * minus_flag)
        velocity = velocity.at[2, :, -1, :].add(change[:, 1] * minus_flag)
        velocity = velocity.at[0, :, 0, :].add(change[:, 2] * plus_flag)
        velocity = velocity.at[2, :, 0, :].add(change[:, 3] * plus_flag)
        padded_velocity = fault_cut(with_halo(velocity, (("gx", 1), ("gy", 2), ("gz", 3)), 2), 2)
        vel_x = trimmed(padded_velocity, 1)
        vel_y = trimmed(padded_velocity, 2)
        vel_z = trimmed(padded_velocity, 3)
        vel_tuple_x = (vel_x[0], vel_x[1], vel_x[2])
        vel_tuple_y = (vel_y[0], vel_y[1], vel_y[2])
        vel_tuple_z = (vel_z[0], vel_z[1], vel_z[2])
        rates = strain_rates(vel_tuple_x, vel_tuple_y, vel_tuple_z)
        stress, memory = update_stress(stress, memory, rates, props)
    new_slip = lax.psum_scatter(state_slip * plus_flag, "gy", scatter_dimension=0, tiled=True)
    return (velocity, stress, memory, new_slip)


def solution(mesh):
    in_specs = (
        P(None, ("ens", "gx"), "gy", "gz"),
        P(None, ("ens", "gx"), "gy", "gz"),
        P(None, ("ens", "gx"), "gy", "gz"),
        P(("ens", "gx"), "gy", "gz"),
        P(None, "ens"),
        P(("ens", "gx", "gy"), "gz"),
        P(("ens", "gx", "gy"), "gz"),
        P("ens"),
        P(None, "ens"),
        P(("ens", "gx", "gy"), None, "gz"),
        P(("ens", "gx", "gy"), "gz"),
        P(("ens", "gx", "gy"), "gz"),
    )
    out_specs = (
        P(None, ("ens", "gx"), "gy", "gz"),
        P(None, ("ens", "gx"), "gy", "gz"),
        P(None, ("ens", "gx"), "gy", "gz"),
        P(("ens", "gx", "gy"), "gz"),
    )
    return jax.shard_map(shards, mesh=mesh, in_specs=in_specs, out_specs=out_specs, check_vma=False)
```

profile of v0, /device:TPU:0, one launch (start us, length us, event | category | flops | bytes accessed | tf_op | source)
XLA Modules:
  0.0 223.0 jit_solution(9015207075433446364)
XLA Ops:
  1.7 4.9 %collective-permute-start = (f32[6,2,32,128]{3,2,1,0:T(8,128)S(1)}, f32[6,2,32,128]{3,2,1,0:T(8,128)S(1)}, u32[]{:S(2)}, u32[]{:S(2)}) collective-permute-start(f32[6,2,32,128]{3,2,1,0:T(8,128)S(1)} %get-tuple-element.159), channel_id=1, source_target_pairs={{0,4},{4,8},{8,12},{1,5},{5,9},{9,13},{2,6},{6,10},{10,14},{3,7},{... | collective-permute-start | bytes 589832 | tf_op jit(solution)/shard_map/ppermute | solution.py:25
  13.5 4.3 %all_gather.17 = s32[16,128]{1,0:T(8,128)S(1)} all-gather(s32[8,128]{1,0:T(8,128)S(1)} %copy-done.39), channel_id=1, replica_groups=mesh['ens'=2,'gx'=4,'gy'=2,'gz'=2] {'gy'}, dimensions={0}, use_global_device_ids=true | all-gather | bytes 12288 | tf_op jit(solution)/shard_map/all_gather | solution.py:202
  21.0 3.4 %collective-permute-start.2 = (f32[6,20,2,128]{3,2,1,0:T(2,128)S(1)}, f32[6,20,2,128]{3,2,1,0:T(2,128)S(1)}, u32[]{:S(2)}, u32[]{:S(2)}) collective-permute-start(f32[6,20,2,128]{3,2,1,0:T(2,128)S(1)} %get-tuple-element.154), channel_id=1, source_target_pairs={{0,2},{1,3},{4,6},{5,7},{8,10},{9,11},{12,14},{13,15},{16,18},{17,... | collective-permute-start | bytes 368648 | tf_op jit(solution)/shard_map/ppermute | solution.py:25
  33.8 3.3 %copy.45 = f32[6,20,36,2]{2,3,1,0:T(2,128)} copy(f32[6,20,36,2]{3,2,1,0:T(8,128)} %get-tuple-element.147) | data formatting | bytes 69120 | tf_op jit(solution)/shard_map/slice | solution.py:22
  44.5 3.3 %copy.48 = f32[6,20,36,2]{3,2,1,0:T(8,128)} copy(f32[6,20,36,2]{2,3,1,0:T(2,128)} %collective-permute-done.5) | data formatting | bytes 69120 | tf_op jit(solution)/shard_map/ppermute | solution.py:27
  47.8 5.0 %maximum_select_fusion = f32[6,20,36,132]{3,2,1,0:T(8,128)S(1)} fusion(f32[6,20,36,2]{3,2,1,0:T(8,128)} %copy.48, f32[6,20,2,128]{3,2,1,0:T(2,128)S(1)} %collective-permute-done.3, f32[6,20,32,128]{3,2,1,0:T(8,128)} %copy-done.3, f32[6,20,2,128]{3,2,1,0:T(2,128)S(1)} %collective-permute-done.2, f32[6,20,36,2]{3,2,1,0:T(8,128)S(1)} %copy.47, ...), kind=kLoop, calls=%fused_computation | loop fusion | flops 2851200 | bytes 4561956 | tf_op jit(solution)/shard_map/jit(_where)/select_n | solution.py:158
  58.5 4.5 %collective-permute-start.7 = (f32[16,3,128]{2,0,1:T(8,128)S(1)}, f32[16,3,128]{2,0,1:T(8,128)S(1)}, u32[]{:S(2)}, u32[]{:S(2)}) collective-permute-start(f32[16,3,128]{2,0,1:T(8,128)S(1)} %fusion.170), channel_id=1, source_target_pairs={{0,2},{1,3},{4,6},{5,7},{8,10},{9,11},{12,14},{13,15},{16,18},{17,... | collective-permute-start | bytes 73736 | tf_op jit(solution)/shard_map/ppermute | solution.py:37
  63.8 4.3 %all_gather.19 = f32[16,128]{1,0:T(8,128)S(1)} all-gather(f32[8,128]{1,0:T(8,128)S(1)} %copy-done.40), channel_id=1, replica_groups=mesh['ens'=2,'gx'=4,'gy'=2,'gz'=2] {'gy'}, dimensions={0}, use_global_device_ids=true | all-gather | bytes 12288 | tf_op jit(solution)/shard_map/all_gather | solution.py:198
  68.1 4.3 %all_gather.16 = s32[16,128]{1,0:T(8,128)S(1)} all-gather(s32[8,128]{1,0:T(8,128)S(1)} %copy-done.41), channel_id=1, replica_groups=mesh['ens'=2,'gx'=4,'gy'=2,'gz'=2] {'gy'}, dimensions={0}, use_global_device_ids=true | all-gather | bytes 12288 | tf_op jit(solution)/shard_map/all_gather | solution.py:203
  72.4 4.3 %all_gather.18 = f32[16,128]{1,0:T(8,128)S(1)} all-gather(f32[8,128]{1,0:T(8,128)S(1)} %copy-done.42), channel_id=1, replica_groups=mesh['ens'=2,'gx'=4,'gy'=2,'gz'=2] {'gy'}, dimensions={0}, use_global_device_ids=true | all-gather | bytes 12288 | tf_op jit(solution)/shard_map/all_gather | solution.py:199
  76.8 4.4 %all_gather.15 = f32[16,2,128]{2,0,1:T(8,128)S(1)} all-gather(f32[8,2,128]{2,0,1:T(8,128)S(1)} %copy.54), channel_id=1, replica_groups=mesh['ens'=2,'gx'=4,'gy'=2,'gz'=2] {'gy'}, dimensions={0}, use_global_device_ids=true | all-gather | bytes 24576 | tf_op jit(solution)/shard_map/all_gather | solution.py:197
  84.4 4.6 %collective-permute-start.8 = (f32[3,2,32,128]{3,2,1,0:T(8,128)S(1)}, f32[3,2,32,128]{3,2,1,0:T(8,128)S(1)}, u32[]{:S(2)}, u32[]{:S(2)}) collective-permute-start(f32[3,2,32,128]{3,2,1,0:T(8,128)S(1)} %get-tuple-element.175), channel_id=1, source_target_pairs={{0,4},{4,8},{8,12},{1,5},{5,9},{9,13},{2,6},{6,10},{10,14},{3,7},{... | collective-permute-start | bytes 294920 | tf_op jit(solution)/shard_map/ppermute | solution.py:25
  91.1 4.3 %collective-permute-done.9 = f32[3,2,32,128]{3,2,1,0:T(8,128)S(1)} collective-permute-done((f32[3,2,32,128]{3,2,1,0:T(8,128)S(1)}, f32[3,2,32,128]{3,2,1,0:T(8,128)S(1)}, u32[]{:S(2)}, u32[]{:S(2)}) %collective-permute-start.9) | collective-permute-done | bytes 98336 | tf_op jit(solution)/shard_map/ppermute | solution.py:27
  99.2 4.3 %collective-permute-done.11 = f32[3,20,2,128]{3,2,1,0:T(2,128)S(1)} collective-permute-done((f32[3,20,2,128]{3,2,1,0:T(2,128)S(1)}, f32[3,20,2,128]{3,2,1,0:T(2,128)S(1)}, u32[]{:S(2)}, u32[]{:S(2)}) %collective-permute-start.11) | collective-permute-done | bytes 61472 | tf_op jit(solution)/shard_map/ppermute | solution.py:27
  112.3 2.3 %maximum_select_fusion.2 = f32[3,20,36,132]{3,2,1,0:T(8,128)S(1)} fusion(f32[3,20,36,2]{3,2,1,0:T(8,128)S(1)} %copy.65, f32[3,20,2,128]{3,2,1,0:T(2,128)} %copy-done.21, f32[3,2,32,128]{3,2,1,0:T(8,128)} %copy-done.18, f32[3,16,32,128]{3,2,1,0:T(8,128)S(1)} %scatter-add.31, f32[3,2,32,128]{3,2,1,0:T(8,128)} %copy-done.17, f32[3,20,2,128]{3,2,1,0:T(2,128)} %copy-done.20, ...), kind=kLoop, calls=%fused_computation.3 | loop fusion | flops 1995840 | bytes 2280996 | tf_op jit(solution)/shard_map/jit(_where)/select_n | solution.py:158
  120.1 3.5 %collective-permute-start.14 = (f32[6,2,32,128]{3,2,1,0:T(8,128)S(1)}, f32[6,2,32,128]{3,2,1,0:T(8,128)S(1)}, u32[]{:S(2)}, u32[]{:S(2)}) collective-permute-start(f32[6,2,32,128]{3,2,1,0:T(8,128)S(1)} %get-tuple-element.156), channel_id=1, source_target_pairs={{0,4},{4,8},{8,12},{1,5},{5,9},{9,13},{2,6},{6,10},{10,14},{3,7},{... | collective-permute-start | bytes 589832 | tf_op jit(solution)/shard_map/ppermute | solution.py:25
  124.9 3.3 %collective-permute-done.14 = f32[6,2,32,128]{3,2,1,0:T(8,128)S(1)} collective-permute-done((f32[6,2,32,128]{3,2,1,0:T(8,128)S(1)}, f32[6,2,32,128]{3,2,1,0:T(8,128)S(1)}, u32[]{:S(2)}, u32[]{:S(2)}) %collective-permute-start.14) | collective-permute-done | bytes 196640 | tf_op jit(solution)/shard_map/ppermute | solution.py:25
  128.2 4.1 %collective-permute-done.15 = f32[6,2,32,128]{3,2,1,0:T(8,128)S(1)} collective-permute-done((f32[6,2,32,128]{3,2,1,0:T(8,128)S(1)}, f32[6,2,32,128]{3,2,1,0:T(8,128)S(1)}, u32[]{:S(2)}, u32[]{:S(2)}) %collective-permute-start.15) | collective-permute-done | bytes 196640 | tf_op jit(solution)/shard_map/ppermute | solution.py:27
  136.4 4.4 %collective-permute-done.17 = f32[6,20,2,128]{3,2,1,0:T(2,128)S(1)} collective-permute-done((f32[6,20,2,128]{3,2,1,0:T(2,128)S(1)}, f32[6,20,2,128]{3,2,1,0:T(2,128)S(1)}, u32[]{:S(2)}, u32[]{:S(2)}) %collective-permute-start.17) | collective-permute-done | bytes 122912 | tf_op jit(solution)/shard_map/ppermute | solution.py:27
  141.2 3.0 %fusion.213 = (f32[6,20,36,2]{3,2,1,0:T(8,128)}, f32[6,20,36,2]{3,2,1,0:T(8,128)}) fusion(f32[6,20,36,128]{3,2,1,0:T(8,128)S(1)} %pad_maximum_fusion.1), kind=kLoop, calls=%fused_computation.389 | loop fusion | bytes 138240 | tf_op jit(solution)/shard_map/slice | solution.py:22
  144.2 2.6 %copy.66 = f32[6,20,36,2]{2,3,1,0:T(2,128)S(1)} copy(f32[6,20,36,2]{3,2,1,0:T(8,128)} %get-tuple-element.139) | data formatting | bytes 69120 | tf_op jit(solution)/shard_map/slice | solution.py:22
  148.2 3.3 %copy.67 = f32[6,20,36,2]{2,3,1,0:T(2,128)} copy(f32[6,20,36,2]{3,2,1,0:T(8,128)} %get-tuple-element.140) | data formatting | bytes 69120 | tf_op jit(solution)/shard_map/slice | solution.py:21
  153.0 2.4 %copy.68 = f32[6,20,36,2]{3,2,1,0:T(8,128)} copy(f32[6,20,36,2]{2,3,1,0:T(2,128)S(1)} %collective-permute-done.18) | data formatting | bytes 69120 | tf_op jit(solution)/shard_map/ppermute | solution.py:25
  155.4 3.3 %copy.69 = f32[6,20,36,2]{3,2,1,0:T(8,128)} copy(f32[6,20,36,2]{2,3,1,0:T(2,128)} %collective-permute-done.19) | data formatting | bytes 69120 | tf_op jit(solution)/shard_map/ppermute | solution.py:27
  158.7 5.7 %maximum_select_fusion.1 = f32[6,20,36,132]{3,2,1,0:T(8,128)S(1)} fusion(f32[6,20,36,2]{3,2,1,0:T(8,128)} %copy.69, f32[6,20,2,128]{3,2,1,0:T(2,128)S(1)} %collective-permute-done.17, f32[6,2,32,128]{3,2,1,0:T(8,128)S(1)} %collective-permute-done.15, f32[6,16,32,128]{3,2,1,0:T(8,128)S(1)} %multiply_add_fusion.1, ...), kind=kLoop, calls=%fused_computation.1 | loop fusion | flops 3991680 | bytes 4561956 | tf_op jit(solution)/shard_map/jit(_where)/select_n | solution.py:158
  169.9 4.5 %collective-permute-start.21 = (f32[16,3,128]{2,0,1:T(8,128)S(1)}, f32[16,3,128]{2,0,1:T(8,128)S(1)}, u32[]{:S(2)}, u32[]{:S(2)}) collective-permute-start(f32[16,3,128]{2,0,1:T(8,128)S(1)} %fusion.171), channel_id=1, source_target_pairs={{0,2},{1,3},{4,6},{5,7},{8,10},{9,11},{12,14},{13,15},{16,18},{17,... | collective-permute-start | bytes 73736 | tf_op jit(solution)/shard_map/ppermute | solution.py:37
  178.4 3.5 %collective-permute-start.22 = (f32[3,2,32,128]{3,2,1,0:T(8,128)S(1)}, f32[3,2,32,128]{3,2,1,0:T(8,128)S(1)}, u32[]{:S(2)}, u32[]{:S(2)}) collective-permute-start(f32[3,2,32,128]{3,2,1,0:T(8,128)S(1)} %get-tuple-element.168), channel_id=1, source_target_pairs={{0,4},{4,8},{8,12},{1,5},{5,9},{9,13},{2,6},{6,10},{10,14},{3,7},{... | collective-permute-start | bytes 294920 | tf_op jit(solution)/shard_map/ppermute | solution.py:25
  184.5 4.1 %collective-permute-done.23 = f32[3,2,32,128]{3,2,1,0:T(8,128)S(1)} collective-permute-done((f32[3,2,32,128]{3,2,1,0:T(8,128)S(1)}, f32[3,2,32,128]{3,2,1,0:T(8,128)S(1)}, u32[]{:S(2)}, u32[]{:S(2)}) %collective-permute-start.23) | collective-permute-done | bytes 98336 | tf_op jit(solution)/shard_map/ppermute | solution.py:27
  188.7 4.0 %collective-permute-start.24 = (f32[3,20,2,128]{3,2,1,0:T(2,128)S(1)}, f32[3,20,2,128]{3,2,1,0:T(2,128)S(1)}, u32[]{:S(2)}, u32[]{:S(2)}) collective-permute-start(f32[3,20,2,128]{3,2,1,0:T(2,128)S(1)} %get-tuple-element.164), channel_id=1, source_target_pairs={{0,2},{1,3},{4,6},{5,7},{8,10},{9,11},{12,14},{13,15},{16,18},{17,... | collective-permute-start | bytes 184328 | tf_op jit(solution)/shard_map/ppermute | solution.py:25
  195.3 5.6 %all-reduce = f32[16,128]{1,0:T(8,128)S(1)} all-reduce(f32[16,128]{1,0:T(8,128)S(1)} %get-tuple-element.100), channel_id=2, replica_groups=mesh['ens'=2,'gx'=4,'gy'=2,'gz'=2] {'gy'}, use_global_device_ids=true, to_apply=%region_1.2.clone | all-reduce | flops 2048 | bytes 16384
  213.3 3.0 %maximum_select_fusion.3 = f32[3,20,36,132]{3,2,1,0:T(8,128)S(1)} fusion(f32[3,20,36,2]{3,2,1,0:T(8,128)} %copy.85, f32[3,20,2,128]{3,2,1,0:T(2,128)S(1)} %collective-permute-done.25, f32[3,2,32,128]{3,2,1,0:T(8,128)S(1)} %collective-permute-done.23, f32[3,16,32,128]{3,2,1,0:T(8,128)S(1)} %scatter-add.39, f32[3,2,32,128]{3,2,1,0:T(8,128)S(1)} %collective-permute-done.22, ...), kind=kLoop, calls=%fused_computation.5 | loop fusion | flops 1995840 | bytes 2280996 | tf_op jit(solution)/shard_map/jit(_where)/select_n | solution.py:158
  220.5 2.5 %multiply_add_fusion = (f32[6,16,32,128]{3,2,1,0:T(8,128)}, f32[6,16,32,128]{3,2,1,0:T(8,128)}) fusion(f32[6,16,32,128]{3,2,1,0:T(8,128)S(1)} %multiply_add_fusion.1, f32[6,16,32,128]{3,2,1,0:T(8,128)S(1)} %fusion.10, f32[6,16,32,128]{3,2,1,0:T(8,128)S(1)} %copy-done.6, f32[16,32,128]{2,1,0:T(8,128)S(1)} %bitcast.426, f32[6,16,32,128]{3,2,1,0:T(8,128)S(1)} %copy-done.8, ...), kind=kLoop, calls=%fused_computation.9 | loop fusion | flops 3538944 | bytes 9961472 | tf_op jit(solution)/shard_map/add | solution.py:105
  (240 shorter events, 94.7 us)
Async XLA Ops:
  1.7 17.5 %collective-permute-start = (f32[6,2,32,128]{3,2,1,0:T(8,128)S(1)}, f32[6,2,32,128]{3,2,1,0:T(8,128)S(1)}, u32[]{:S(2)}, u32[]{:S(2)}) collective-permute-start(f32[6,2,32,128]{3,2,1,0:T(8,128)S(1)} %get-tuple-element.159), channel_id=1, source_target_pairs={{0,4},{4,8},{8,12},{1,5},{5,9},{9,13},{2,6},{6,10},{10,14},{3,7},{... | collective-permute-start | bytes 589832 | tf_op jit(solution)/shard_map/ppermute | solution.py:25
  6.7 14.2 %collective-permute-start.1 = (f32[6,2,32,128]{3,2,1,0:T(8,128)S(1)}, f32[6,2,32,128]{3,2,1,0:T(8,128)S(1)}, u32[]{:S(2)}, u32[]{:S(2)}) collective-permute-start(f32[6,2,32,128]{3,2,1,0:T(8,128)S(1)} %get-tuple-element.158), channel_id=1, source_target_pairs={{4,0},{8,4},{12,8},{5,1},{9,5},{13,9},{6,2},{10,6},{14,10},{7,3},{... | collective-permute-start | bytes 589832 | tf_op jit(solution)/shard_map/ppermute | solution.py:27
  19.2 61.9 %copy-start.22 = (f32[16,1,128]{2,0,1:T(8,128)}, f32[16,1,128]{2,0,1:T(8,128)S(1)}, u32[]{:S(2)}) copy-start(f32[16,1,128]{2,0,1:T(8,128)S(1)} %get-tuple-element.183) | copy-start | bytes 24580
  21.0 7.9 %collective-permute-start.2 = (f32[6,20,2,128]{3,2,1,0:T(2,128)S(1)}, f32[6,20,2,128]{3,2,1,0:T(2,128)S(1)}, u32[]{:S(2)}, u32[]{:S(2)}) collective-permute-start(f32[6,20,2,128]{3,2,1,0:T(2,128)S(1)} %get-tuple-element.154), channel_id=1, source_target_pairs={{0,2},{1,3},{4,6},{5,7},{8,10},{9,11},{12,14},{13,15},{16,18},{17,... | collective-permute-start | bytes 368648 | tf_op jit(solution)/shard_map/ppermute | solution.py:25
  24.4 6.8 %collective-permute-start.3 = (f32[6,20,2,128]{3,2,1,0:T(2,128)S(1)}, f32[6,20,2,128]{3,2,1,0:T(2,128)S(1)}, u32[]{:S(2)}, u32[]{:S(2)}) collective-permute-start(f32[6,20,2,128]{3,2,1,0:T(2,128)S(1)} %get-tuple-element.155), channel_id=1, source_target_pairs={{2,0},{3,1},{6,4},{7,5},{10,8},{11,9},{14,12},{15,13},{18,16},{19,... | collective-permute-start | bytes 368648 | tf_op jit(solution)/shard_map/ppermute | solution.py:27
  37.0 5.6 %collective-permute-start.4 = (f32[6,20,36,2]{2,3,1,0:T(2,128)}, f32[6,20,36,2]{2,3,1,0:T(2,128)}, u32[]{:S(2)}, u32[]{:S(2)}) collective-permute-start(f32[6,20,36,2]{2,3,1,0:T(2,128)} %copy.45), channel_id=1, source_target_pairs={{0,1},{2,3},{4,5},{6,7},{8,9},{10,11},{12,13},{14,15},{16,17},{18,... | collective-permute-start | bytes 103688 | tf_op jit(solution)/shard_map/ppermute | solution.py:25
  40.5 4.0 %collective-permute-start.5 = (f32[6,20,36,2]{2,3,1,0:T(2,128)}, f32[6,20,36,2]{2,3,1,0:T(2,128)}, u32[]{:S(2)}, u32[]{:S(2)}) collective-permute-start(f32[6,20,36,2]{2,3,1,0:T(2,128)} %copy.46), channel_id=1, source_target_pairs={{1,0},{3,2},{5,4},{7,6},{9,8},{11,10},{13,12},{15,14},{17,16},{19,... | collective-permute-start | bytes 103688 | tf_op jit(solution)/shard_map/ppermute | solution.py:27
  57.2 23.9 %collective-permute-start.6 = (f32[16,3,128]{2,0,1:T(8,128)S(1)}, f32[16,3,128]{2,0,1:T(8,128)S(1)}, u32[]{:S(2)}, u32[]{:S(2)}) collective-permute-start(f32[16,3,128]{2,0,1:T(8,128)S(1)} %fusion.170), channel_id=1, source_target_pairs={{2,0},{3,1},{6,4},{7,5},{10,8},{11,9},{14,12},{15,13},{18,16},{19,... | collective-permute-start | bytes 73736 | tf_op jit(solution)/shard_map/ppermute | solution.py:37
  58.5 22.6 %collective-permute-start.7 = (f32[16,3,128]{2,0,1:T(8,128)S(1)}, f32[16,3,128]{2,0,1:T(8,128)S(1)}, u32[]{:S(2)}, u32[]{:S(2)}) collective-permute-start(f32[16,3,128]{2,0,1:T(8,128)S(1)} %fusion.170), channel_id=1, source_target_pairs={{0,2},{1,3},{4,6},{5,7},{8,10},{9,11},{12,14},{13,15},{16,18},{17,... | collective-permute-start | bytes 73736 | tf_op jit(solution)/shard_map/ppermute | solution.py:37
  63.7 39.8 %copy-start.37 = (pred[16]{0:T(512)(128)(4,1)}, pred[16]{0:T(512)(128)(4,1)S(1)}, u32[]{:S(2)}) copy-start(pred[16]{0:T(512)(128)(4,1)S(1)} %compare_and_fusion) | copy-start | bytes 52
  68.1 35.4 %copy-start.25 = (f32[16,128]{1,0:T(8,128)}, f32[16,128]{1,0:T(8,128)S(1)}, u32[]{:S(2)}) copy-start(f32[16,128]{1,0:T(8,128)S(1)} %all_gather.19) | copy-start | bytes 24580
  84.4 6.8 %collective-permute-start.8 = (f32[3,2,32,128]{3,2,1,0:T(8,128)S(1)}, f32[3,2,32,128]{3,2,1,0:T(8,128)S(1)}, u32[]{:S(2)}, u32[]{:S(2)}) collective-permute-start(f32[3,2,32,128]{3,2,1,0:T(8,128)S(1)} %get-tuple-element.175), channel_id=1, source_target_pairs={{0,4},{4,8},{8,12},{1,5},{5,9},{9,13},{2,6},{6,10},{10,14},{3,7},{... | collective-permute-start | bytes 294920 | tf_op jit(solution)/shard_map/ppermute | solution.py:25
  88.9 6.5 %collective-permute-start.9 = (f32[3,2,32,128]{3,2,1,0:T(8,128)S(1)}, f32[3,2,32,128]{3,2,1,0:T(8,128)S(1)}, u32[]{:S(2)}, u32[]{:S(2)}) collective-permute-start(f32[3,2,32,128]{3,2,1,0:T(8,128)S(1)} %get-tuple-element.176), channel_id=1, source_target_pairs={{4,0},{8,4},{12,8},{5,1},{9,5},{13,9},{6,2},{10,6},{14,10},{7,3},{... | collective-permute-start | bytes 294920 | tf_op jit(solution)/shard_map/ppermute | solution.py:27
  95.5 3.7 %collective-permute-start.10 = (f32[3,20,2,128]{3,2,1,0:T(2,128)S(1)}, f32[3,20,2,128]{3,2,1,0:T(2,128)S(1)}, u32[]{:S(2)}, u32[]{:S(2)}) collective-permute-start(f32[3,20,2,128]{3,2,1,0:T(2,128)S(1)} %get-tuple-element.166), channel_id=1, source_target_pairs={{0,2},{1,3},{4,6},{5,7},{8,10},{9,11},{12,14},{13,15},{16,18},{17,... | collective-permute-start | bytes 184328 | tf_op jit(solution)/shard_map/ppermute | solution.py:25
  97.4 6.1 %collective-permute-start.11 = (f32[3,20,2,128]{3,2,1,0:T(2,128)S(1)}, f32[3,20,2,128]{3,2,1,0:T(2,128)S(1)}, u32[]{:S(2)}, u32[]{:S(2)}) collective-permute-start(f32[3,20,2,128]{3,2,1,0:T(2,128)S(1)} %get-tuple-element.167), channel_id=1, source_target_pairs={{2,0},{3,1},{6,4},{7,5},{10,8},{11,9},{14,12},{15,13},{18,16},{19,... | collective-permute-start | bytes 184328 | tf_op jit(solution)/shard_map/ppermute | solution.py:27
  105.9 3.1 %collective-permute-start.12 = (f32[3,20,36,2]{2,3,1,0:T(2,128)}, f32[3,20,36,2]{2,3,1,0:T(2,128)S(1)}, u32[]{:S(2)}, u32[]{:S(2)}) collective-permute-start(f32[3,20,36,2]{2,3,1,0:T(2,128)} %copy.62), channel_id=1, source_target_pairs={{0,1},{2,3},{4,5},{6,7},{8,9},{10,11},{12,13},{14,15},{16,17},{18,... | collective-permute-start | bytes 51848 | tf_op jit(solution)/shard_map/ppermute | solution.py:25
  107.7 3.3 %collective-permute-start.13 = (f32[3,20,36,2]{2,3,1,0:T(2,128)S(1)}, f32[3,20,36,2]{2,3,1,0:T(2,128)}, u32[]{:S(2)}, u32[]{:S(2)}) collective-permute-start(f32[3,20,36,2]{2,3,1,0:T(2,128)S(1)} %copy.63), channel_id=1, source_target_pairs={{1,0},{3,2},{5,4},{7,6},{9,8},{11,10},{13,12},{15,14},{17,16},{19,... | collective-permute-start | bytes 51848 | tf_op jit(solution)/shard_map/ppermute | solution.py:27
  120.1 8.1 %collective-permute-start.14 = (f32[6,2,32,128]{3,2,1,0:T(8,128)S(1)}, f32[6,2,32,128]{3,2,1,0:T(8,128)S(1)}, u32[]{:S(2)}, u32[]{:S(2)}) collective-permute-start(f32[6,2,32,128]{3,2,1,0:T(8,128)S(1)} %get-tuple-element.156), channel_id=1, source_target_pairs={{0,4},{4,8},{8,12},{1,5},{5,9},{9,13},{2,6},{6,10},{10,14},{3,7},{... | collective-permute-start | bytes 589832 | tf_op jit(solution)/shard_map/ppermute | solution.py:25
  123.6 8.8 %collective-permute-start.15 = (f32[6,2,32,128]{3,2,1,0:T(8,128)S(1)}, f32[6,2,32,128]{3,2,1,0:T(8,128)S(1)}, u32[]{:S(2)}, u32[]{:S(2)}) collective-permute-start(f32[6,2,32,128]{3,2,1,0:T(8,128)S(1)} %get-tuple-element.157), channel_id=1, source_target_pairs={{4,0},{8,4},{12,8},{5,1},{9,5},{13,9},{6,2},{10,6},{14,10},{7,3},{... | collective-permute-start | bytes 589832 | tf_op jit(solution)/shard_map/ppermute | solution.py:27
  132.4 4.0 %collective-permute-start.16 = (f32[6,20,2,128]{3,2,1,0:T(2,128)S(1)}, f32[6,20,2,128]{3,2,1,0:T(2,128)S(1)}, u32[]{:S(2)}, u32[]{:S(2)}) collective-permute-start(f32[6,20,2,128]{3,2,1,0:T(2,128)S(1)} %get-tuple-element.152), channel_id=1, source_target_pairs={{0,2},{1,3},{4,6},{5,7},{8,10},{9,11},{12,14},{13,15},{16,18},{17,... | collective-permute-start | bytes 368648 | tf_op jit(solution)/shard_map/ppermute | solution.py:25
  134.0 6.8 %collective-permute-start.17 = (f32[6,20,2,128]{3,2,1,0:T(2,128)S(1)}, f32[6,20,2,128]{3,2,1,0:T(2,128)S(1)}, u32[]{:S(2)}, u32[]{:S(2)}) collective-permute-start(f32[6,20,2,128]{3,2,1,0:T(2,128)S(1)} %get-tuple-element.153), channel_id=1, source_target_pairs={{2,0},{3,1},{6,4},{7,5},{10,8},{11,9},{14,12},{15,13},{18,16},{19,... | collective-permute-start | bytes 368648 | tf_op jit(solution)/shard_map/ppermute | solution.py:27
  146.9 6.1 %collective-permute-start.18 = (f32[6,20,36,2]{2,3,1,0:T(2,128)S(1)}, f32[6,20,36,2]{2,3,1,0:T(2,128)S(1)}, u32[]{:S(2)}, u32[]{:S(2)}) collective-permute-start(f32[6,20,36,2]{2,3,1,0:T(2,128)S(1)} %copy.66), channel_id=1, source_target_pairs={{0,1},{2,3},{4,5},{6,7},{8,9},{10,11},{12,13},{14,15},{16,17},{18,... | collective-permute-start | bytes 103688 | tf_op jit(solution)/shard_map/ppermute | solution.py:25
  151.4 4.0 %collective-permute-start.19 = (f32[6,20,36,2]{2,3,1,0:T(2,128)}, f32[6,20,36,2]{2,3,1,0:T(2,128)}, u32[]{:S(2)}, u32[]{:S(2)}) collective-permute-start(f32[6,20,36,2]{2,3,1,0:T(2,128)} %copy.67), channel_id=1, source_target_pairs={{1,0},{3,2},{5,4},{7,6},{9,8},{11,10},{13,12},{15,14},{17,16},{19,... | collective-permute-start | bytes 103688 | tf_op jit(solution)/shard_map/ppermute | solution.py:27
  168.6 5.9 %collective-permute-start.20 = (f32[16,3,128]{2,0,1:T(8,128)S(1)}, f32[16,3,128]{2,0,1:T(8,128)S(1)}, u32[]{:S(2)}, u32[]{:S(2)}) collective-permute-start(f32[16,3,128]{2,0,1:T(8,128)S(1)} %fusion.171), channel_id=1, source_target_pairs={{2,0},{3,1},{6,4},{7,5},{10,8},{11,9},{14,12},{15,13},{18,16},{19,... | collective-permute-start | bytes 73736 | tf_op jit(solution)/shard_map/ppermute | solution.py:37
  169.9 6.1 %collective-permute-start.21 = (f32[16,3,128]{2,0,1:T(8,128)S(1)}, f32[16,3,128]{2,0,1:T(8,128)S(1)}, u32[]{:S(2)}, u32[]{:S(2)}) collective-permute-start(f32[16,3,128]{2,0,1:T(8,128)S(1)} %fusion.171), channel_id=1, source_target_pairs={{0,2},{1,3},{4,6},{5,7},{8,10},{9,11},{12,14},{13,15},{16,18},{17,... | collective-permute-start | bytes 73736 | tf_op jit(solution)/shard_map/ppermute | solution.py:37
  178.4 34.9 %copy-start.2 = (f32[3,16,32,128]{3,2,1,0:T(8,128)}, f32[3,16,32,128]{3,2,1,0:T(8,128)S(1)}, u32[]{:S(2)}) copy-start(f32[3,16,32,128]{3,2,1,0:T(8,128)S(1)} %scatter-add.39) | copy-start | bytes 2359300
  178.4 6.1 %collective-permute-start.22 = (f32[3,2,32,128]{3,2,1,0:T(8,128)S(1)}, f32[3,2,32,128]{3,2,1,0:T(8,128)S(1)}, u32[]{:S(2)}, u32[]{:S(2)}) collective-permute-start(f32[3,2,32,128]{3,2,1,0:T(8,128)S(1)} %get-tuple-element.168), channel_id=1, source_target_pairs={{0,4},{4,8},{8,12},{1,5},{5,9},{9,13},{2,6},{6,10},{10,14},{3,7},{... | collective-permute-start | bytes 294920 | tf_op jit(solution)/shard_map/ppermute | solution.py:25
  182.0 6.7 %collective-permute-start.23 = (f32[3,2,32,128]{3,2,1,0:T(8,128)S(1)}, f32[3,2,32,128]{3,2,1,0:T(8,128)S(1)}, u32[]{:S(2)}, u32[]{:S(2)}) collective-permute-start(f32[3,2,32,128]{3,2,1,0:T(8,128)S(1)} %get-tuple-element.169), channel_id=1, source_target_pairs={{4,0},{8,4},{12,8},{5,1},{9,5},{13,9},{6,2},{10,6},{14,10},{7,3},{... | collective-permute-start | bytes 294920 | tf_op jit(solution)/shard_map/ppermute | solution.py:27
  188.7 12.2 %collective-permute-start.24 = (f32[3,20,2,128]{3,2,1,0:T(2,128)S(1)}, f32[3,20,2,128]{3,2,1,0:T(2,128)S(1)}, u32[]{:S(2)}, u32[]{:S(2)}) collective-permute-start(f32[3,20,2,128]{3,2,1,0:T(2,128)S(1)} %get-tuple-element.164), channel_id=1, source_target_pairs={{0,2},{1,3},{4,6},{5,7},{8,10},{9,11},{12,14},{13,15},{16,18},{17,... | collective-permute-start | bytes 184328 | tf_op jit(solution)/shard_map/ppermute | solution.py:25
  192.7 8.2 %collective-permute-start.25 = (f32[3,20,2,128]{3,2,1,0:T(2,128)S(1)}, f32[3,20,2,128]{3,2,1,0:T(2,128)S(1)}, u32[]{:S(2)}, u32[]{:S(2)}) collective-permute-start(f32[3,20,2,128]{3,2,1,0:T(2,128)S(1)} %get-tuple-element.165), channel_id=1, source_target_pairs={{2,0},{3,1},{6,4},{7,5},{10,8},{11,9},{14,12},{15,13},{18,16},{19,... | collective-permute-start | bytes 184328 | tf_op jit(solution)/shard_map/ppermute | solution.py:27
  204.7 5.4 %collective-permute-start.26 = (f32[3,20,36,2]{2,3,1,0:T(2,128)S(1)}, f32[3,20,36,2]{2,3,1,0:T(2,128)S(1)}, u32[]{:S(2)}, u32[]{:S(2)}) collective-permute-start(f32[3,20,36,2]{2,3,1,0:T(2,128)S(1)} %copy.82), channel_id=1, source_target_pairs={{0,1},{2,3},{4,5},{6,7},{8,9},{10,11},{12,13},{14,15},{16,17},{18,... | collective-permute-start | bytes 51848 | tf_op jit(solution)/shard_map/ppermute | solution.py:25
  207.9 3.7 %collective-permute-start.27 = (f32[3,20,36,2]{2,3,1,0:T(2,128)S(1)}, f32[3,20,36,2]{2,3,1,0:T(2,128)S(1)}, u32[]{:S(2)}, u32[]{:S(2)}) collective-permute-start(f32[3,20,36,2]{2,3,1,0:T(2,128)S(1)} %copy.83), channel_id=1, source_target_pairs={{1,0},{3,2},{5,4},{7,6},{9,8},{11,10},{13,12},{15,14},{17,16},{19,... | collective-permute-start | bytes 51848 | tf_op jit(solution)/shard_map/ppermute | solution.py:27
  (43 other events, 308.2 us)
where the time goes:
time: 225 us; the launch traced here: 223 us
  starting transfers between devices  60.9 us (27%)
  local copies, waits for them, and re-layouts  58.2 us (26%)
  other arithmetic  36.5 us (16%)
  waiting for transfers between devices  33.5 us (15%)
  blocking collectives  27.3 us (12%)
  between operations  3.83 us (2%)
  matrix products  2.77 us (1%)
    ppermute x12, starting transfers between devices, with_halo(): lax.ppermute(tail, axis, [(i, (i + 1) % count) for i in range(ends)])  33.3 us
    ppermute x12, waiting for transfers between devices, with_halo(): lax.ppermute(head, axis, [((i + 1) % count, i) for i in range(ends)])  24.8 us
    slice x12, local copies, waits for them, and re-layouts, with_halo(): lax.slice_in_dim(cells, cells.shape[dim] - width, cells.shape[dim], axis=...  16.4 us
    select_n x4, other arithmetic, fault_cut(): return jnp.where(remove, 0.0, padded)  16 us
    ppermute x12, starting transfers between devices, with_halo(): lax.ppermute(head, axis, [((i + 1) % count, i) for i in range(ends)])  15.9 us
    ppermute x4, starting transfers between devices, shifted_2(): return lax.ppermute(block, axis, route)  11.7 us
    ppermute x4, local copies, waits for them, and re-layouts, with_halo(): lax.ppermute(head, axis, [((i + 1) % count, i) for i in range(ends)])  9.47 us
    slice x5, local copies, waits for them, and re-layouts, with_halo(): head = lax.slice_in_dim(cells, 0, width, axis=dim)  8.23 us
  transfers between devices with their start and end apart: 28, of which 13 were waited for; matrix products, arithmetic and copies ran while one was open for 12% of the time, Pallas kernels for 0%

commit v1 on v0

v1 whole, which is shorter than its diff:
```python
import functools

import jax
import jax.numpy as jnp
from jax import lax
from jax.experimental import pallas as pl
from jax.experimental.pallas import tpu as pltpu
from jax.sharding import PartitionSpec as P

STEPS = 2
CLASSES = 8
ZONES = 4
PATCH = 8

NEAR = 9.0 / 8.0
FAR = -1.0 / 24.0
DT = 0.15

XX, YY, ZZ, XY, XZ, YZ = range(6)

STRESS_TAIL = ((XX, -1), (XY, -2), (XY, -1), (XZ, -2), (XZ, -1))
STRESS_HEAD = ((XX, 0), (XX, 1), (XY, 0), (XZ, 0))
VEL_TAIL = ((0, -2), (0, -1), (1, -1), (2, -1))
VEL_HEAD = ((0, 0), (1, 0), (1, 1), (2, 0), (2, 1))
STRESS_TAIL_Y = ((YY, -1), (XY, -2), (XY, -1), (YZ, -2), (YZ, -1))
STRESS_HEAD_Y = ((YY, 0), (YY, 1), (XY, 0), (YZ, 0))
VEL_TAIL_Y = ((1, -2), (1, -1), (0, -1), (2, -1))
VEL_HEAD_Y = ((1, 0), (0, 0), (0, 1), (2, 0), (2, 1))
STRESS_SLOTS = (XZ, YZ, ZZ)
VEL_SLOTS = (0, 1, 2)


def forward(before, here, after, after_2):
    return NEAR * (after - here) + FAR * (after_2 - before)


def backward(before_2, before, here, after):
    return NEAR * (here - before) + FAR * (after - before_2)


class Edges:
    def __init__(self, rows, depths):
        self.rows = rows
        self.depths = depths
        lane = lax.broadcasted_iota(jnp.int32, (rows, depths), 1)
        row = lax.broadcasted_iota(jnp.int32, (rows, depths), 0)
        self.row = row
        self.deep = lax.axis_index("gz")
        self.low = {1: lane < 1, 2: lane < 2}
        self.high = {1: lane >= depths - 1, 2: lane >= depths - 2}
        self.top = {1: row < 1, 2: row < 2}
        self.bottom = {1: row >= rows - 1, 2: row >= rows - 2}
        self.slots = [self.slot(lane, k) for k in range(3)]

    def slot(self, lane, k):
        first = jnp.where(self.deep == 0, self.depths - 2 - 8 * k, 8 * k)
        return (lane == first) | (lane == first + 1)

    def turn(self, k):
        return jnp.where(self.deep == 0, self.depths - 8 * k, 8 * k)

    def packed(self, fields):
        out = jnp.where(self.slots[0], fields[0], 0.0)
        for k in (1, 2):
            if fields[k] is not None:
                out = jnp.where(self.slots[k], pltpu.roll(fields[k], self.turn(k), 1), out)
        return out

    def ends(self, strip, k):
        return strip if k == 0 else pltpu.roll(strip, self.turn(k), 1)

    def shallower(self, field, halo, n):
        return pltpu.roll(jnp.where(self.high[n], halo, field), n, 1)

    def deeper(self, field, halo, n):
        return pltpu.roll(jnp.where(self.low[n], halo, field), self.depths - n, 1)

    def forward_z(self, field, strip, k):
        halo = self.ends(strip, k)
        return forward(
            self.shallower(field, halo, 1),
            field,
            self.deeper(field, halo, 1),
            self.deeper(field, halo, 2),
        )

    def backward_z(self, field, strip, k):
        halo = self.ends(strip, k)
        return backward(
            self.shallower(field, halo, 2),
            self.shallower(field, halo, 1),
            field,
            self.deeper(field, halo, 1),
        )

    def before(self, field, n, halo):
        moved = jnp.where(self.top[n], 0.0, pltpu.roll(field, n, 0))
        if halo:
            for i in range(n):
                moved = jnp.where(self.row == i, halo[n - 1 - i], moved)
        return moved

    def after(self, field, n, halo):
        moved = jnp.where(self.bottom[n], 0.0, pltpu.roll(field, self.rows - n, 0))
        if halo:
            for i in range(n):
                moved = jnp.where(self.row == self.rows - n + i, halo[i], moved)
        return moved

    def forward_y(self, field, halos):
        lower, upper = halos
        return forward(
            self.before(field, 1, lower),
            field,
            self.after(field, 1, upper),
            self.after(field, 2, upper),
        )

    def backward_y(self, field, halos):
        lower, upper = halos
        return backward(
            self.before(field, 2, lower),
            self.before(field, 1, lower),
            field,
            self.after(field, 1, upper),
        )


class Planes:
    def __init__(self, ref, left, right, tail, head):
        self.ref = ref
        self.count = ref.shape[1]
        self.left, self.right = left, right
        self.tail, self.head = tail, head

    def __call__(self, comp, x, offset=0):
        if isinstance(x, int):
            place = x + offset
            if place < 0:
                return self.left[self.tail.index((comp, place))]
            if place >= self.count:
                return self.right[self.head.index((comp, place - self.count))]
        return self.ref[comp, x + offset]

    def forward_x(self, comp, x):
        return forward(self(comp, x, -1), self(comp, x), self(comp, x, 1), self(comp, x, 2))

    def backward_x(self, comp, x):
        return backward(self(comp, x, -2), self(comp, x, -1), self(comp, x), self(comp, x, 1))


class Bands:
    def __init__(self, refs, tail, head):
        self.refs = refs
        self.tail, self.head = tail, head

    def __call__(self, comp, x):
        if not self.refs:
            return (None, None)
        lower, upper = self.refs
        before = [
            lower[i, pl.ds(x, 1), :]
            for i in reversed(range(len(self.tail)))
            if self.tail[i][0] == comp
        ]
        after = [
            upper[i, pl.ds(x, 1), :] for i in range(len(self.head)) if self.head[i][0] == comp
        ]
        return (before, after)


def looked_up(labels, table, row, count):
    out = jnp.full(labels.shape, table[row, 0], jnp.float32)
    for k in range(1, count):
        out = jnp.where(labels == k, table[row, k], out)
    return out


def over_planes(count, body):
    for x in (0, 1):
        body(x)

    def step(x, carry):
        body(x)
        return carry

    lax.fori_loop(2, count - 2, step, 0)
    for x in (count - 2, count - 1):
        body(x)


def edge_planes(ref, planes, out):
    count = ref.shape[1]
    for i, (comp, place) in enumerate(planes):
        out[i] = ref[comp, place % count]


def fault_row(rows):
    return jnp.where(lax.axis_index("gy") == lax.axis_size("gy") // 2, 0, rows - 1)


def pack_kernel(stress, tail_out, head_out, strip_out):
    count, rows, depths = stress.shape[1:]
    edges = Edges(rows, depths)
    edge_planes(stress, STRESS_TAIL, tail_out)
    edge_planes(stress, STRESS_HEAD, head_out)

    def body(x, carry):
        strip_out[x] = edges.packed([stress[c, x] for c in STRESS_SLOTS])
        return carry

    lax.fori_loop(0, count, body, 0)


def velocity_kernel(first, banded, *refs):
    velocity, stress, material, table, left, right, strip = refs[:7]
    refs = refs[7:]
    bands = ()
    if banded:
        bands, refs = refs[:2], refs[2:]
    if first and not banded:
        (prestress, normal, slip, zone, mask), refs = refs[:5], refs[5:]
    out, face, tail_out, head_out, strip_out = refs
    count, rows, depths = velocity.shape[1:]
    edges = Edges(rows, depths)
    planes = Planes(stress, left, right, STRESS_TAIL, STRESS_HEAD)
    band = Bands(bands, STRESS_TAIL_Y, STRESS_HEAD_Y)
    fault = fault_row(rows)

    def body(x):
        sxy, sxz, syz = stress[XY, x], stress[XZ, x], stress[YZ, x]
        push = DT * looked_up(material[x], table, 2, CLASSES)
        ends = strip[x]
        along_x = (
            planes.forward_x(XX, x)
            + edges.backward_y(sxy, band(XY, x))
            + edges.backward_z(sxz, ends, 0)
        )
        along_y = (
            planes.backward_x(XY, x)
            + edges.forward_y(stress[YY, x], band(YY, x))
            + edges.backward_z(syz, ends, 1)
        )
        along_z = (
            planes.backward_x(XZ, x)
            + edges.backward_y(syz, band(YZ, x))
            + edges.forward_z(stress[ZZ, x], ends, 2)
        )
        new = [velocity[c, x] + push * rate for c, rate in enumerate((along_x, along_y, along_z))]
        for c in range(3):
            out[c, x] = new[c]
        strip_out[x] = edges.packed(new)
        face[pl.ds(x, 1), :] = out[0, x, pl.ds(fault, 1), :]
        face[pl.ds(count + x, 1), :] = out[2, x, pl.ds(fault, 1), :]
        if first:
            labels = material[x, pl.ds(fault, 1), :]
            face[pl.ds(2 * count + x, 1), :] = looked_up(labels, table, 2, CLASSES)

    over_planes(count, body)
    edge_planes(out, VEL_TAIL, tail_out)
    edge_planes(out, VEL_HEAD, head_out)
    if first and not banded:
        own = normal.shape[0]
        place = 3 * count
        for i in range(own):
            face[pl.ds(place + i, 1), :] = prestress[i, pl.ds(0, 1), :]
            face[pl.ds(place + own + i, 1), :] = prestress[i, pl.ds(1, 1), :]
        for i, field in enumerate((normal, slip, zone, mask)):
            face[pl.ds(place + (2 + i) * own, own), :] = field[...].astype(jnp.float32)


def fault_kernel(first, banded, *refs):
    (own_face, other_face, tail, head, strip, friction_table, anchor), refs = refs[:7], refs[7:]
    if first:
        if banded:
            still, refs = refs[0], refs[1:]
    else:
        (still, own_first, other_first, slip), refs = refs[:4], refs[4:]
    if first:
        own_first, other_first = own_face, other_face
    change, slip_out, tail_out, head_out, strip_out = refs[:5]
    count, rows, depths = strip.shape
    middle = lax.axis_size("gy") // 2
    side = lax.axis_index("gy")
    plus = side == middle
    minus = side == middle - 1

    def pair(own, other, place):
        mine, theirs = own[pl.ds(place, count), :], other[pl.ds(place, count), :]
        return jnp.where(plus, theirs, mine), jnp.where(plus, mine, theirs)

    if first and not banded:
        still = refs[5]
        share = (own_face.shape[0] - 3 * count) // 6
        for i in range(6):
            mine = own_face[pl.ds(3 * count + i * share, share), :]
            theirs = other_face[pl.ds(3 * count + i * share, share), :]
            still[i, pl.ds(0, share), :] = jnp.where(plus, theirs, mine)
            still[i, pl.ds(share, share), :] = jnp.where(plus, mine, theirs)
    pre_x, pre_z, normal = still[0], still[1], still[2]
    slip = still[3] if first else slip[...]
    zone, mask = still[4], still[5]

    row = lax.broadcasted_iota(jnp.int32, (count, depths), 0) + lax.axis_index("gx") * count
    deep = lax.broadcasted_iota(jnp.int32, (count, depths), 1) + lax.axis_index("gz") * depths
    inside = (row >= anchor[0]) & (row < anchor[0] + 2 * PATCH)
    inside = inside & (deep >= anchor[1]) & (deep < anchor[1] + 2 * PATCH)
    dynamic = 0.4 * looked_up(zone, friction_table, 0, ZONES)
    static = jnp.where(
        inside, dynamic, dynamic + 0.5 * looked_up(zone, friction_table, 1, ZONES)
    )
    distance = 0.2 * looked_up(zone, friction_table, 2, ZONES)
    minus_x, plus_x = pair(own_face, other_face, 0)
    minus_z, plus_z = pair(own_face, other_face, count)
    minus_b, plus_b = pair(own_first, other_first, 2 * count)
    bsum = minus_b + plus_b
    trial_x = (plus_x - minus_x) / (DT * bsum) + pre_x
    trial_z = (plus_z - minus_z) / (DT * bsum) + pre_z
    size = jnp.sqrt(trial_x * trial_x + trial_z * trial_z)
    weaken = jnp.minimum(slip / distance, 1.0)
    strength = (static - (static - dynamic) * weaken) * normal
    factor = jnp.where(mask == 1.0, strength / jnp.maximum(size, strength), 1.0)
    slip_out[...] = slip + DT * DT * bsum * (size - size * factor)
    sign = jnp.where(minus, DT, 0.0) * minus_b - jnp.where(plus, DT, 0.0) * plus_b
    change_x = (trial_x * factor - pre_x) * sign
    change_z = (trial_z * factor - pre_z) * sign
    change[0] = change_x
    change[1] = change_z

    fault = fault_row(rows)
    on_fault = lax.broadcasted_iota(jnp.int32, (rows, depths), 0) == fault
    for planes, source, out in ((VEL_TAIL, tail, tail_out), (VEL_HEAD, head, head_out)):
        for i, (comp, place) in enumerate(planes):
            plane = source[i]
            if comp != 1:
                line = change[comp // 2, pl.ds(place % count, 1), :]
                plane = plane + jnp.where(on_fault, line, 0.0)
            out[i] = plane
    flat = Edges(count, depths)
    ends = flat.packed([change_x, None, change_z])
    for x in range(count):
        strip_out[x] = strip[x] + jnp.where(on_fault, ends[x : x + 1, :], 0.0)


def stress_kernel(last, banded, *refs):
    velocity, stress, memory, material, table, change, left, right, strip = refs[:9]
    refs = refs[9:]
    bands = ()
    if banded:
        bands, refs = refs[:2], refs[2:]
    vel_out, stress_out, memory_out = refs[:3]
    if not last:
        tail_out, head_out, strip_out = refs[3:]
    count, rows, depths = velocity.shape[1:]
    edges = Edges(rows, depths)
    on_fault = edges.row == fault_row(rows)
    for x in range(count):
        for c in (0, 2):
            line = change[c // 2, pl.ds(x, 1), :]
            vel_out[c, x] = velocity[c, x] + jnp.where(on_fault, line, 0.0)
        vel_out[1, x] = velocity[1, x]
    planes = Planes(vel_out, left, right, VEL_TAIL, VEL_HEAD)
    band = Bands(bands, VEL_TAIL_Y, VEL_HEAD_Y)

    def body(x):
        vx, vy, vz = vel_out[0, x], vel_out[1, x], vel_out[2, x]
        ends = strip[x]
        exx = planes.backward_x(0, x)
        eyy = edges.backward_y(vy, band(1, x))
        ezz = edges.backward_z(vz, ends, 2)
        exy = edges.forward_y(vx, band(0, x)) + planes.forward_x(1, x)
        exz = edges.forward_z(vx, ends, 0) + planes.forward_x(2, x)
        eyz = edges.forward_z(vy, ends, 1) + edges.forward_y(vz, band(2, x))
        labels = material[x]
        lame = looked_up(labels, table, 0, CLASSES)
        shear = looked_up(labels, table, 1, CLASSES)
        decay = jnp.exp(-DT / looked_up(labels, table, 3, CLASSES))
        gain = (1.0 - decay) * (0.3 * looked_up(labels, table, 4, CLASSES))
        bulk = lame * (exx + eyy + ezz)
        double = 2.0 * shear
        elastic = (
            bulk + double * exx,
            bulk + double * eyy,
            bulk + double * ezz,
            shear * exy,
            shear * exz,
            shear * eyz,
        )
        new = []
        for c in range(6):
            kept = decay * memory[c, x] - gain * elastic[c]
            memory_out[c, x] = kept
            new.append(stress[c, x] + DT * (elastic[c] + kept))
            stress_out[c, x] = new[c]
        if not last:
            strip_out[x] = edges.packed([new[c] for c in STRESS_SLOTS])

    over_planes(count, body)
    if not last:
        edge_planes(stress_out, STRESS_TAIL, tail_out)
        edge_planes(stress_out, STRESS_HEAD, head_out)


def call(kernel, name, operands, outs, scalars=(), cost=0):
    in_specs = [
        pl.BlockSpec(memory_space=pltpu.SMEM if i in scalars else pltpu.VMEM)
        for i in range(len(operands))
    ]
    outs = [jax.ShapeDtypeStruct(shape, jnp.float32) for shape in outs]
    moved = sum(a.size * 4 for a in operands) + sum(4 * o.size for o in outs)
    return pl.pallas_call(
        kernel,
        out_shape=outs,
        in_specs=in_specs,
        out_specs=[pl.BlockSpec(memory_space=pltpu.VMEM) for _ in outs],
        name=name,
        cost_estimate=pl.CostEstimate(flops=cost, bytes_accessed=moved, transcendentals=0),
        compiler_params=pltpu.CompilerParams(vmem_limit_bytes=24 * 2**20),
    )(*operands)


def along(axis, count, skip=()):
    up = [(i, i + 1) for i in range(count - 1) if i not in skip]
    return (axis, up), (axis, [(b, a) for a, b in up])


def sent(block, route):
    return lax.ppermute(block, *route)


def edge_rows(field, rows):
    count = field.shape[2]
    return jnp.stack([field[c, :, place % count, :] for c, place in rows])


def shards(
    velocity,
    stress,
    memory,
    material,
    material_table,
    fault_mask,
    zone_label,
    patch_anchor,
    friction_table,
    prestress,
    normal_stress,
    slip_path,
):
    _, count, rows, depths = velocity.shape
    sides = lax.axis_size("gy")
    middle = sides // 2
    banded = sides > 2
    cells = count * rows * depths
    up, down = along("gx", lax.axis_size("gx"))
    up_y, down_y = along("gy", sides, (middle - 1,))
    across = ("gy", [(middle - 1, middle), (middle, middle - 1)])
    deep = ("gz", [(0, 1), (1, 0)])

    def strike_shape(planes):
        return (len(planes), rows, depths)

    strip_shape = (count, rows, depths)
    block = (count, rows, depths)

    still = None
    if banded:
        still = jnp.stack(
            [
                prestress[:, 0],
                prestress[:, 1],
                normal_stress,
                slip_path,
                zone_label.astype(jnp.float32),
                fault_mask.astype(jnp.float32),
            ]
        )
        still = lax.all_gather(still, "gy", axis=1, tiled=True)

    tail, head, strip = call(
        pack_kernel,
        "pack",
        [stress],
        [strike_shape(STRESS_TAIL), strike_shape(STRESS_HEAD), strip_shape],
    )
    for step in range(STEPS):
        first, last = step == 0, step == STEPS - 1
        strip = sent(strip, deep)
        left = sent(tail, up)
        right = sent(head, down)
        operands = [velocity, stress, material, material_table, left, right, strip]
        if banded:
            operands += [
                sent(edge_rows(stress, STRESS_TAIL_Y), up_y),
                sent(edge_rows(stress, STRESS_HEAD_Y), down_y),
            ]
        face_rows = 2 * count
        if first:
            face_rows += count
            if not banded:
                operands += [prestress, normal_stress, slip_path, zone_label, fault_mask]
                face_rows += 6 * normal_stress.shape[0]
        free, face, tail, head, strip = call(
            functools.partial(velocity_kernel, first, banded),
            "velocity",
            operands,
            [
                (3, *block),
                (face_rows, depths),
                strike_shape(VEL_TAIL),
                strike_shape(VEL_HEAD),
                strip_shape,
            ],
            scalars=(3,),
            cost=60 * cells,
        )
        other = sent(face, across)
        operands = [face, other, tail, head, strip, friction_table, patch_anchor]
        outs = [
            (2, count, depths),
            (count, depths),
            strike_shape(VEL_TAIL),
            strike_shape(VEL_HEAD),
            strip_shape,
        ]
        if first:
            faces = (face, other)
            if banded:
                operands.append(still)
            else:
                outs.append((6, count, depths))
        else:
            operands += [still, *faces, slip]
        result = call(
            functools.partial(fault_kernel, first, banded),
            "fault",
            operands,
            outs,
            scalars=(5, 6),
        )
        change, slip, tail, head, strip = result[:5]
        if first and not banded:
            still = result[5]
        strip = sent(strip, deep)
        left = sent(tail, up)
        right = sent(head, down)
        operands = [free, stress, memory, material, material_table]
        operands += [change, left, right, strip]
        if banded:
            operands += [
                sent(edge_rows(free, VEL_TAIL_Y), up_y),
                sent(edge_rows(free, VEL_HEAD_Y), down_y),
            ]
        outs = [(3, *block), (6, *block), (6, *block)]
        if not last:
            outs += [strike_shape(STRESS_TAIL), strike_shape(STRESS_HEAD), strip_shape]
        result = call(
            functools.partial(stress_kernel, last, banded),
            "stress",
            operands,
            outs,
            scalars=(4,),
            cost=100 * cells,
        )
        velocity, stress, memory = result[:3]
        if not last:
            tail, head, strip = result[3:]
    side = lax.axis_index("gy")
    if banded:
        held = jnp.where(side == middle, slip, 0.0)
        new_slip = lax.psum_scatter(held, "gy", scatter_dimension=0, tiled=True)
    else:
        share = count // sides
        new_slip = lax.dynamic_slice_in_dim(slip, side * share, share, axis=0)
    return (velocity, stress, memory, new_slip)


def solution(mesh):
    in_specs = (
        P(None, ("ens", "gx"), "gy", "gz"),
        P(None, ("ens", "gx"), "gy", "gz"),
        P(None, ("ens", "gx"), "gy", "gz"),
        P(("ens", "gx"), "gy", "gz"),
        P(None, "ens"),
        P(("ens", "gx", "gy"), "gz"),
        P(("ens", "gx", "gy"), "gz"),
        P("ens"),
        P(None, "ens"),
        P(("ens", "gx", "gy"), None, "gz"),
        P(("ens", "gx", "gy"), "gz"),
        P(("ens", "gx", "gy"), "gz"),
    )
    out_specs = (
        P(None, ("ens", "gx"), "gy", "gz"),
        P(None, ("ens", "gx"), "gy", "gz"),
        P(None, ("ens", "gx"), "gy", "gz"),
        P(("ens", "gx", "gy"), "gz"),
    )
    return jax.shard_map(shards, mesh=mesh, in_specs=in_specs, out_specs=out_specs, check_vma=False)
```

time: 225 us -> 73.7 us (0.33)
  local copies, waits for them, and re-layouts: 58.2 us -> 4.69 us
  other arithmetic: 36.5 us -> 0 us
  starting transfers between devices: 60.9 us -> 25.9 us
  blocking collectives: 27.3 us -> 0 us
  Pallas kernels: 0 us -> 20.8 us
  waiting for transfers between devices: 33.5 us -> 21.1 us
  between operations: 3.83 us -> 0.88 us
  matrix products: 2.77 us -> 0 us
    ppermute x28 -> x14, starting transfers between devices: 60.9 us -> 25.9 us  [sent(): return lax.ppermute(block, *route)]
    slice x21 -> x0, local copies, waits for them, and re-layouts: 27.9 us -> none  [the longest x12 16.4 us: with_halo(): lax.slice_in_dim(cells, cells.shape[dim] - width, cells.shape[dim], axis=...]
    all_gather x5 -> x0, blocking collectives: 21.7 us -> none  [the longest x1 4.35 us: shards(): lax.all_gather(prestress, 'gy', axis=0, tiled=True)]
    pallas_call x0 -> x7, Pallas kernels: none -> 20.8 us  [call(): pl.pallas_call(kernel, out_shape=outs, in_specs=in_specs, out_specs=[pl.B...]
    select_n x8 -> x0, other arithmetic: 16 us -> none  [the longest x4 16 us: fault_cut(): return jnp.where(remove, 0.0, padded)]
    ppermute x8 -> x0, local copies, waits for them, and re-layouts: 15.9 us -> none  [the longest x4 9.47 us: with_halo(): lax.ppermute(head, axis, [((i + 1) % count, i) for i in range(ends)])]
    ppermute x28 -> x14, waiting for transfers between devices: 33.5 us -> 21.1 us  [sent(): return lax.ppermute(block, *route)]
    another operation x12 -> x0, other arithmetic: 7.39 us -> none  [the longest x6 3.43 us: accelerate(): return jnp.stack([first, second, third])]
  transfers between devices with their start and end apart: 28 -> 14, of which waited for: 13 -> 7; matrix products, arithmetic and copies ran while one was open for 12% -> 1% of each run, Pallas kernels for 0% -> 0%
where the time goes in v1:
time: 73.7 us; the launch traced here: 73.4 us
  starting transfers between devices  25.9 us (35%)
  waiting for transfers between devices  21.1 us (29%)
  Pallas kernels  20.8 us (28%)
  local copies, waits for them, and re-layouts  4.69 us (6%)
  between operations  0.88 us (1%)
    ppermute x14, starting transfers between devices, sent(): return lax.ppermute(block, *route)  25.9 us
    ppermute x14, waiting for transfers between devices, sent(): return lax.ppermute(block, *route)  21.1 us
    pallas_call x7, Pallas kernels, call(): pl.pallas_call(kernel, out_shape=outs, in_specs=in_specs, out_specs=[pl.B...  20.8 us
    unnamed x32, local copies, waits for them, and re-layouts  4.09 us
  transfers between devices with their start and end apart: 14, of which 7 were waited for; matrix products, arithmetic and copies ran while one was open for 1% of the time, Pallas kernels for 0%

profile of v1, /device:TPU:0, one launch (start us, length us, event | category | flops | bytes accessed | tf_op | source)
XLA Modules:
  0.0 73.4 jit_solution(17982467323364804449)
XLA Ops:
  0.6 1.4 %copy-done = f32[6,16,32,128]{3,2,1,0:T(8,128)S(1)} copy-done((f32[6,16,32,128]{3,2,1,0:T(8,128)S(1)}, f32[6,16,32,128]{3,2,1,0:T(8,128)}, u32[]{:S(2)}) %copy-start) | copy-done | bytes 1572888
  2.1 1.2 %pack.1 = (f32[5,32,128]{2,1,0:T(8,128)S(1)}, f32[4,32,128]{2,1,0:T(8,128)S(1)}, f32[16,32,128]{2,1,0:T(8,128)S(1)}) custom-call(f32[6,16,32,128]{3,2,1,0:T(8,128)S(1)} %copy-done), custom_call_target="tpu_custom_call" | custom-call | bytes 1982464 | tf_op jit(solution)/shard_map/pack/pallas_call | solution.py:411
  3.3 0.5 collective-permute-start.2
  3.8 4.5 %collective-permute-start = (f32[5,32,128]{2,1,0:T(8,128)S(1)}, f32[5,32,128]{2,1,0:T(8,128)S(1)}, u32[]{:S(2)}, u32[]{:S(2)}) collective-permute-start(f32[5,32,128]{2,1,0:T(8,128)S(1)} %get-tuple-element.37), channel_id=1, source_target_pairs={{0,4},{4,8},{8,12},{1,5},{5,9},{9,13},{2,6},{6,10},{10,14},{3,7},{... | collective-permute-start | bytes 245768 | tf_op jit(solution)/shard_map/ppermute | solution.py:428
  8.4 1.6 %collective-permute-start.1 = (f32[4,32,128]{2,1,0:T(8,128)S(1)}, f32[4,32,128]{2,1,0:T(8,128)S(1)}, u32[]{:S(2)}, u32[]{:S(2)}) collective-permute-start(f32[4,32,128]{2,1,0:T(8,128)S(1)} %get-tuple-element.38), channel_id=1, source_target_pairs={{4,0},{8,4},{12,8},{5,1},{9,5},{13,9},{6,2},{10,6},{14,10},{7,3},{... | collective-permute-start | bytes 196616 | tf_op jit(solution)/shard_map/ppermute | solution.py:428
  9.9 4.9 %collective-permute-done.1.refs_5_ = f32[4,32,128]{2,1,0:T(8,128)S(1)} collective-permute-done((f32[4,32,128]{2,1,0:T(8,128)S(1)}, f32[4,32,128]{2,1,0:T(8,128)S(1)}, u32[]{:S(2)}, u32[]{:S(2)}) %collective-permute-start.1) | collective-permute-done | bytes 65568 | tf_op jit(solution)/shard_map/ppermute | solution.py:428
  14.9 3.9 %velocity.2 = (f32[3,16,32,128]{3,2,1,0:T(8,128)S(1)}, f32[96,128]{1,0:T(8,128)S(1)}, f32[4,32,128]{2,1,0:T(8,128)S(1)}, f32[5,32,128]{2,1,0:T(8,128)S(1)}, f32[16,32,128]{2,1,0:T(8,128)S(1)}) custom-call(f32[3,16,32,128]{3,2,1,0:T(8,128)S(1)} %copy-done.4, f32[6,16,32,128]{3,2,1,0:T(8,128)S(1)} %copy-done, s32[16,32,128]{2,1,0:T(8,128)S(1)} %copy-done.2, ...), custom_call_target="tpu_custom_call" | custom-call | flops 3932160 | bytes 4300960 | tf_op jit(solution)/shard_map/velocity/pallas_call | solution.py:411
  18.8 1.6 %collective-permute-start.3 = (f32[96,128]{1,0:T(8,128)S(1)}, f32[96,128]{1,0:T(8,128)S(1)}, u32[]{:S(2)}, u32[]{:S(2)}) collective-permute-start(f32[96,128]{1,0:T(8,128)S(1)} %get-tuple-element.41.refs_0_.refs_8_), channel_id=1, source_target_pairs={{0,2},{2,0},{1,3},{3,1},{4,6},{6,4},{5,7},{7,5},{8,10},{10,8},{9,1... | collective-permute-start | bytes 147464 | tf_op jit(solution)/shard_map/ppermute | solution.py:428
  20.4 2.6 %collective-permute-done.3.refs_1_.refs_9_ = f32[96,128]{1,0:T(8,128)S(1)} collective-permute-done((f32[96,128]{1,0:T(8,128)S(1)}, f32[96,128]{1,0:T(8,128)S(1)}, u32[]{:S(2)}, u32[]{:S(2)}) %collective-permute-start.3) | collective-permute-done | bytes 49184 | tf_op jit(solution)/shard_map/ppermute | solution.py:428
  23.0 0.7 fault.2
  23.7 0.1 collective-permute-start.6
  23.8 1.3 %collective-permute-start.5 = (f32[5,32,128]{2,1,0:T(8,128)S(1)}, f32[5,32,128]{2,1,0:T(8,128)S(1)}, u32[]{:S(2)}, u32[]{:S(2)}) collective-permute-start(f32[5,32,128]{2,1,0:T(8,128)S(1)} %get-tuple-element.47), channel_id=1, source_target_pairs={{4,0},{8,4},{12,8},{5,1},{9,5},{13,9},{6,2},{10,6},{14,10},{7,3},{... | collective-permute-start | bytes 245768 | tf_op jit(solution)/shard_map/ppermute | solution.py:428
  25.1 4.5 %collective-permute-start.4 = (f32[4,32,128]{2,1,0:T(8,128)S(1)}, f32[4,32,128]{2,1,0:T(8,128)S(1)}, u32[]{:S(2)}, u32[]{:S(2)}) collective-permute-start(f32[4,32,128]{2,1,0:T(8,128)S(1)} %get-tuple-element.46), channel_id=1, source_target_pairs={{0,4},{4,8},{8,12},{1,5},{5,9},{9,13},{2,6},{6,10},{10,14},{3,7},{... | collective-permute-start | bytes 196616 | tf_op jit(solution)/shard_map/ppermute | solution.py:428
  29.6 1.9 %collective-permute-done.4.refs_6_ = f32[4,32,128]{2,1,0:T(8,128)S(1)} collective-permute-done((f32[4,32,128]{2,1,0:T(8,128)S(1)}, f32[4,32,128]{2,1,0:T(8,128)S(1)}, u32[]{:S(2)}, u32[]{:S(2)}) %collective-permute-start.4) | collective-permute-done | bytes 65568 | tf_op jit(solution)/shard_map/ppermute | solution.py:428
  31.5 4.2 %stress.4 = (f32[3,16,32,128]{3,2,1,0:T(8,128)S(1)}, f32[6,16,32,128]{3,2,1,0:T(8,128)S(1)}, f32[6,16,32,128]{3,2,1,0:T(8,128)S(1)}, f32[5,32,128]{2,1,0:T(8,128...) custom-call(f32[3,16,32,128]{3,2,1,0:T(8,128)S(1)} %get-tuple-element.40.refs_0_, ...), custom_call_target="tpu_custom_call" | custom-call | flops 6553600 | bytes 8962208 | tf_op jit(solution)/shard_map/stress/pallas_call | solution.py:411
  35.8 0.1 collective-permute-start.9
  35.8 4.3 %collective-permute-start.7 = (f32[5,32,128]{2,1,0:T(8,128)S(1)}, f32[5,32,128]{2,1,0:T(8,128)S(1)}, u32[]{:S(2)}, u32[]{:S(2)}) collective-permute-start(f32[5,32,128]{2,1,0:T(8,128)S(1)} %get-tuple-element.51), channel_id=1, source_target_pairs={{0,4},{4,8},{8,12},{1,5},{5,9},{9,13},{2,6},{6,10},{10,14},{3,7},{... | collective-permute-start | bytes 245768 | tf_op jit(solution)/shard_map/ppermute | solution.py:428
  40.1 1.3 %collective-permute-start.8 = (f32[4,32,128]{2,1,0:T(8,128)S(1)}, f32[4,32,128]{2,1,0:T(8,128)S(1)}, u32[]{:S(2)}, u32[]{:S(2)}) collective-permute-start(f32[4,32,128]{2,1,0:T(8,128)S(1)} %get-tuple-element.52), channel_id=1, source_target_pairs={{4,0},{8,4},{12,8},{5,1},{9,5},{13,9},{6,2},{10,6},{14,10},{7,3},{... | collective-permute-start | bytes 196616 | tf_op jit(solution)/shard_map/ppermute | solution.py:428
  41.4 4.9 %collective-permute-done.8.refs_5_ = f32[4,32,128]{2,1,0:T(8,128)S(1)} collective-permute-done((f32[4,32,128]{2,1,0:T(8,128)S(1)}, f32[4,32,128]{2,1,0:T(8,128)S(1)}, u32[]{:S(2)}, u32[]{:S(2)}) %collective-permute-start.8) | collective-permute-done | bytes 65568 | tf_op jit(solution)/shard_map/ppermute | solution.py:428
  46.3 3.9 %velocity.3 = (f32[3,16,32,128]{3,2,1,0:T(8,128)S(1)}, f32[32,128]{1,0:T(8,128)S(1)}, f32[4,32,128]{2,1,0:T(8,128)S(1)}, f32[5,32,128]{2,1,0:T(8,128)S(1)}, f32[16,32,128]{2,1,0:T(8,128)S(1)}) custom-call(f32[3,16,32,128]{3,2,1,0:T(8,128)S(1)} %get-tuple-element.49.refs_0_, f32[6,16,32,128]{3,2,1,0:T(8,128)S(1)} %get-tuple-element.50.refs_1_, ...), custom_call_target="tpu_custom_call" | custom-call | flops 3932160 | bytes 4243616 | tf_op jit(solution)/shard_map/velocity/pallas_call | solution.py:411
  50.2 0.9 %copy-done.5 = f32[3,16,32,128]{3,2,1,0:T(8,128)} copy-done((f32[3,16,32,128]{3,2,1,0:T(8,128)}, f32[3,16,32,128]{3,2,1,0:T(8,128)S(1)}, u32[]{:S(2)}) %copy-start.5) | copy-done | bytes 786456
  51.1 1.5 %collective-permute-start.10 = (f32[32,128]{1,0:T(8,128)S(1)}, f32[32,128]{1,0:T(8,128)S(1)}, u32[]{:S(2)}, u32[]{:S(2)}) collective-permute-start(f32[32,128]{1,0:T(8,128)S(1)} %get-tuple-element.56.refs_0_), channel_id=1, source_target_pairs={{0,2},{2,0},{1,3},{3,1},{4,6},{6,4},{5,7},{7,5},{8,10},{10,8},{9,1... | collective-permute-start | bytes 49160 | tf_op jit(solution)/shard_map/ppermute | solution.py:428
  52.6 2.3 %collective-permute-done.10.refs_1_ = f32[32,128]{1,0:T(8,128)S(1)} collective-permute-done((f32[32,128]{1,0:T(8,128)S(1)}, f32[32,128]{1,0:T(8,128)S(1)}, u32[]{:S(2)}, u32[]{:S(2)}) %collective-permute-start.10) | collective-permute-done | bytes 16416 | tf_op jit(solution)/shard_map/ppermute | solution.py:428
  54.8 1.4 %fault.3 = (f32[2,16,128]{2,1,0:T(8,128)S(1)}, f32[16,128]{1,0:T(8,128)S(1)}, f32[4,32,128]{2,1,0:T(8,128)S(1)}, f32[5,32,128]{2,1,0:T(8,128)S(1)}, f32[16,32,128]{2,1,0:T(8,128)}) custom-call(f32[32,128]{1,0:T(8,128)S(1)} %get-tuple-element.56.refs_0_, f32[32,128]{1,0:T(8,128)S(1)} %collective-permute-done.10.refs_1_, ...), custom_call_target="tpu_custom_call" | custom-call | bytes 1032248 | tf_op jit(solution)/shard_map/fault/pallas_call | solution.py:411
  56.2 0.6 copy-done.15
  56.9 3.5 %collective-permute-start.11 = (f32[4,32,128]{2,1,0:T(8,128)}, f32[4,32,128]{2,1,0:T(8,128)S(1)}, u32[]{:S(2)}, u32[]{:S(2)}) collective-permute-start(f32[4,32,128]{2,1,0:T(8,128)} %copy-done.15), channel_id=1, source_target_pairs={{0,4},{4,8},{8,12},{1,5},{5,9},{9,13},{2,6},{6,10},{10,14},{3,7},{... | collective-permute-start | bytes 196616 | tf_op jit(solution)/shard_map/ppermute | solution.py:428
  60.4 1.3 %collective-permute-start.12 = (f32[5,32,128]{2,1,0:T(8,128)S(1)}, f32[5,32,128]{2,1,0:T(8,128)S(1)}, u32[]{:S(2)}, u32[]{:S(2)}) collective-permute-start(f32[5,32,128]{2,1,0:T(8,128)S(1)} %get-tuple-element.64), channel_id=1, source_target_pairs={{4,0},{8,4},{12,8},{5,1},{9,5},{13,9},{6,2},{10,6},{14,10},{7,3},{... | collective-permute-start | bytes 245768 | tf_op jit(solution)/shard_map/ppermute | solution.py:428
  61.7 0.6 constant_dynamic-slice_fusion
  62.3 0.4 collective-permute-done.11.refs_6_
  62.7 4.2 %collective-permute-done.12.refs_7_ = f32[5,32,128]{2,1,0:T(8,128)S(1)} collective-permute-done((f32[5,32,128]{2,1,0:T(8,128)S(1)}, f32[5,32,128]{2,1,0:T(8,128)S(1)}, u32[]{:S(2)}, u32[]{:S(2)}) %collective-permute-start.12) | collective-permute-done | bytes 81952 | tf_op jit(solution)/shard_map/ppermute | solution.py:428
  66.8 1.1 %copy-done.6 = f32[3,16,32,128]{3,2,1,0:T(8,128)S(1)} copy-done((f32[3,16,32,128]{3,2,1,0:T(8,128)S(1)}, f32[3,16,32,128]{3,2,1,0:T(8,128)}, u32[]{:S(2)}) %copy-start.6) | copy-done | bytes 786456
  68.0 5.4 %stress.5 = (f32[3,16,32,128]{3,2,1,0:T(8,128)}, f32[6,16,32,128]{3,2,1,0:T(8,128)}, f32[6,16,32,128]{3,2,1,0:T(8,128)}) custom-call(f32[3,16,32,128]{3,2,1,0:T(8,128)S(1)} %copy-done.6, f32[6,16,32,128]{3,2,1,0:T(8,128)S(1)} %get-tuple-element.50.refs_1_, f32[6,16,32,128]{3,2,1,0:T(8,128)S(1)} %get-tuple-element.55.refs_2_, s32[16,32,128]{2,1,0:T(8,128)S(1)} %copy-done.2, ...), custom_call_target="tpu_custom_call" | custom-call | flops 6553600 | bytes 8552608 | tf_op jit(solution)/shard_map/stress/pallas_call | solution.py:411
  (36 shorter events, 0.1 us)
Async XLA Ops:
  0.6 1.4 %copy-start = (f32[6,16,32,128]{3,2,1,0:T(8,128)S(1)}, f32[6,16,32,128]{3,2,1,0:T(8,128)}, u32[]{:S(2)}) copy-start(f32[6,16,32,128]{3,2,1,0:T(8,128)} %refs_1_.3) | copy-start | bytes 4718596
  2.0 12.8 %copy-start.2 = (s32[16,32,128]{2,1,0:T(8,128)S(1)}, s32[16,32,128]{2,1,0:T(8,128)}, u32[]{:S(2)}) copy-start(s32[16,32,128]{2,1,0:T(8,128)} %refs_3_.7) | copy-start | bytes 786436
  2.0 12.8 %copy-start.4 = (f32[3,16,32,128]{3,2,1,0:T(8,128)S(1)}, f32[3,16,32,128]{3,2,1,0:T(8,128)}, u32[]{:S(2)}) copy-start(f32[3,16,32,128]{3,2,1,0:T(8,128)} %refs_0_.1) | copy-start | bytes 2359300
  2.0 12.8 %copy-start.7 = (f32[5,8]{1,0:T(8,128)S(1)}, f32[5,8]{1,0:T(8,128)}, u32[]{:S(2)}) copy-start(f32[5,8]{1,0:T(8,128)} %refs_4_.3) | copy-start | bytes 484
  2.1 12.8 %copy-start.8 = (f32[8,2,128]{2,1,0:T(2,128)S(1)}, f32[8,2,128]{2,1,0:T(2,128)}, u32[]{:S(2)}) copy-start(f32[8,2,128]{2,1,0:T(2,128)} %refs_7_.1) | copy-start | bytes 24580
  2.1 12.8 %copy-start.10 = (f32[8,128]{1,0:T(8,128)S(1)}, f32[8,128]{1,0:T(8,128)}, u32[]{:S(2)}) copy-start(f32[8,128]{1,0:T(8,128)} %refs_8_.1) | copy-start | bytes 12292
  2.1 12.8 %copy-start.11 = (f32[8,128]{1,0:T(8,128)S(1)}, f32[8,128]{1,0:T(8,128)}, u32[]{:S(2)}) copy-start(f32[8,128]{1,0:T(8,128)} %refs_9_.1) | copy-start | bytes 12292
  2.1 12.8 %copy-start.12 = (s32[8,128]{1,0:T(8,128)S(1)}, s32[8,128]{1,0:T(8,128)}, u32[]{:S(2)}) copy-start(s32[8,128]{1,0:T(8,128)} %refs_10_.1) | copy-start | bytes 12292
  2.1 12.8 %copy-start.13 = (s32[8,128]{1,0:T(8,128)S(1)}, s32[8,128]{1,0:T(8,128)}, u32[]{:S(2)}) copy-start(s32[8,128]{1,0:T(8,128)} %refs_11_.1) | copy-start | bytes 12292
  3.3 19.6 %copy-start.9 = (f32[3,4]{1,0:T(4,128)S(1)}, f32[3,4]{1,0:T(4,128)}, u32[]{:S(2)}) copy-start(f32[3,4]{1,0:T(4,128)} %refs_5_.3) | copy-start | bytes 148
  3.3 19.6 %copy-start.14 = (s32[2]{0:T(128)S(1)}, s32[2]{0:T(128)}, u32[]{:S(2)}) copy-start(s32[2]{0:T(128)} %refs_6_.3) | copy-start | bytes 28
  3.3 11.5 %collective-permute-start.2 = (f32[16,32,128]{2,1,0:T(8,128)S(1)}, f32[16,32,128]{2,1,0:T(8,128)S(1)}, u32[]{:S(2)}, u32[]{:S(2)}) collective-permute-start(f32[16,32,128]{2,1,0:T(8,128)S(1)} %get-tuple-element.39), channel_id=1, source_target_pairs={{0,1},{1,0},{2,3},{3,2},{4,5},{5,4},{6,7},{7,6},{8,9},{9,8},{10,11... | collective-permute-start | bytes 786440 | tf_op jit(solution)/shard_map/ppermute | solution.py:428
  3.8 11.0 %collective-permute-start = (f32[5,32,128]{2,1,0:T(8,128)S(1)}, f32[5,32,128]{2,1,0:T(8,128)S(1)}, u32[]{:S(2)}, u32[]{:S(2)}) collective-permute-start(f32[5,32,128]{2,1,0:T(8,128)S(1)} %get-tuple-element.37), channel_id=1, source_target_pairs={{0,4},{4,8},{8,12},{1,5},{5,9},{9,13},{2,6},{6,10},{10,14},{3,7},{... | collective-permute-start | bytes 245768 | tf_op jit(solution)/shard_map/ppermute | solution.py:428
  8.3 23.2 %copy-start.1 = (f32[6,16,32,128]{3,2,1,0:T(8,128)S(1)}, f32[6,16,32,128]{3,2,1,0:T(8,128)}, u32[]{:S(2)}) copy-start(f32[6,16,32,128]{3,2,1,0:T(8,128)} %refs_1_.3) | copy-start | bytes 4718596
  8.4 23.1 %copy-start.3 = (f32[6,16,32,128]{3,2,1,0:T(8,128)S(1)}, f32[6,16,32,128]{3,2,1,0:T(8,128)}, u32[]{:S(2)}) copy-start(f32[6,16,32,128]{3,2,1,0:T(8,128)} %refs_2_.4) | copy-start | bytes 4718596
  8.4 6.4 %collective-permute-start.1 = (f32[4,32,128]{2,1,0:T(8,128)S(1)}, f32[4,32,128]{2,1,0:T(8,128)S(1)}, u32[]{:S(2)}, u32[]{:S(2)}) collective-permute-start(f32[4,32,128]{2,1,0:T(8,128)S(1)} %get-tuple-element.38), channel_id=1, source_target_pairs={{4,0},{8,4},{12,8},{5,1},{9,5},{13,9},{6,2},{10,6},{14,10},{7,3},{... | collective-permute-start | bytes 196616 | tf_op jit(solution)/shard_map/ppermute | solution.py:428
  18.8 4.2 %collective-permute-start.3 = (f32[96,128]{1,0:T(8,128)S(1)}, f32[96,128]{1,0:T(8,128)S(1)}, u32[]{:S(2)}, u32[]{:S(2)}) collective-permute-start(f32[96,128]{1,0:T(8,128)S(1)} %get-tuple-element.41.refs_0_.refs_8_), channel_id=1, source_target_pairs={{0,2},{2,0},{1,3},{3,1},{4,6},{6,4},{5,7},{7,5},{8,10},{10,8},{9,1... | collective-permute-start | bytes 147464 | tf_op jit(solution)/shard_map/ppermute | solution.py:428
  23.7 7.8 %collective-permute-start.6 = (f32[16,32,128]{2,1,0:T(8,128)S(1)}, f32[16,32,128]{2,1,0:T(8,128)S(1)}, u32[]{:S(2)}, u32[]{:S(2)}) collective-permute-start(f32[16,32,128]{2,1,0:T(8,128)S(1)} %get-tuple-element.48), channel_id=1, source_target_pairs={{0,1},{1,0},{2,3},{3,2},{4,5},{5,4},{6,7},{7,6},{8,9},{9,8},{10,11... | collective-permute-start | bytes 786440 | tf_op jit(solution)/shard_map/ppermute | solution.py:428
  23.8 7.7 %collective-permute-start.5 = (f32[5,32,128]{2,1,0:T(8,128)S(1)}, f32[5,32,128]{2,1,0:T(8,128)S(1)}, u32[]{:S(2)}, u32[]{:S(2)}) collective-permute-start(f32[5,32,128]{2,1,0:T(8,128)S(1)} %get-tuple-element.47), channel_id=1, source_target_pairs={{4,0},{8,4},{12,8},{5,1},{9,5},{13,9},{6,2},{10,6},{14,10},{7,3},{... | collective-permute-start | bytes 245768 | tf_op jit(solution)/shard_map/ppermute | solution.py:428
  25.1 6.4 %collective-permute-start.4 = (f32[4,32,128]{2,1,0:T(8,128)S(1)}, f32[4,32,128]{2,1,0:T(8,128)S(1)}, u32[]{:S(2)}, u32[]{:S(2)}) collective-permute-start(f32[4,32,128]{2,1,0:T(8,128)S(1)} %get-tuple-element.46), channel_id=1, source_target_pairs={{0,4},{4,8},{8,12},{1,5},{5,9},{9,13},{2,6},{6,10},{10,14},{3,7},{... | collective-permute-start | bytes 196616 | tf_op jit(solution)/shard_map/ppermute | solution.py:428
  35.8 10.5 %collective-permute-start.9 = (f32[16,32,128]{2,1,0:T(8,128)S(1)}, f32[16,32,128]{2,1,0:T(8,128)S(1)}, u32[]{:S(2)}, u32[]{:S(2)}) collective-permute-start(f32[16,32,128]{2,1,0:T(8,128)S(1)} %get-tuple-element.53), channel_id=1, source_target_pairs={{0,1},{1,0},{2,3},{3,2},{4,5},{5,4},{6,7},{7,6},{8,9},{9,8},{10,11... | collective-permute-start | bytes 786440 | tf_op jit(solution)/shard_map/ppermute | solution.py:428
  35.8 10.4 %collective-permute-start.7 = (f32[5,32,128]{2,1,0:T(8,128)S(1)}, f32[5,32,128]{2,1,0:T(8,128)S(1)}, u32[]{:S(2)}, u32[]{:S(2)}) collective-permute-start(f32[5,32,128]{2,1,0:T(8,128)S(1)} %get-tuple-element.51), channel_id=1, source_target_pairs={{0,4},{4,8},{8,12},{1,5},{5,9},{9,13},{2,6},{6,10},{10,14},{3,7},{... | collective-permute-start | bytes 245768 | tf_op jit(solution)/shard_map/ppermute | solution.py:428
  40.1 6.2 %collective-permute-start.8 = (f32[4,32,128]{2,1,0:T(8,128)S(1)}, f32[4,32,128]{2,1,0:T(8,128)S(1)}, u32[]{:S(2)}, u32[]{:S(2)}) collective-permute-start(f32[4,32,128]{2,1,0:T(8,128)S(1)} %get-tuple-element.52), channel_id=1, source_target_pairs={{4,0},{8,4},{12,8},{5,1},{9,5},{13,9},{6,2},{10,6},{14,10},{7,3},{... | collective-permute-start | bytes 196616 | tf_op jit(solution)/shard_map/ppermute | solution.py:428
  50.2 0.9 %copy-start.5 = (f32[3,16,32,128]{3,2,1,0:T(8,128)}, f32[3,16,32,128]{3,2,1,0:T(8,128)S(1)}, u32[]{:S(2)}) copy-start(f32[3,16,32,128]{3,2,1,0:T(8,128)S(1)} %get-tuple-element.54.refs_0_) | copy-start | bytes 2359300
  51.1 3.7 %collective-permute-start.10 = (f32[32,128]{1,0:T(8,128)S(1)}, f32[32,128]{1,0:T(8,128)S(1)}, u32[]{:S(2)}, u32[]{:S(2)}) collective-permute-start(f32[32,128]{1,0:T(8,128)S(1)} %get-tuple-element.56.refs_0_), channel_id=1, source_target_pairs={{0,2},{2,0},{1,3},{3,1},{4,6},{6,4},{5,7},{7,5},{8,10},{10,8},{9,1... | collective-permute-start | bytes 49160 | tf_op jit(solution)/shard_map/ppermute | solution.py:428
  56.2 0.6 copy-start.15
  56.9 10.0 %collective-permute-start.13 = (f32[16,32,128]{2,1,0:T(8,128)}, f32[16,32,128]{2,1,0:T(8,128)}, u32[]{:S(2)}, u32[]{:S(2)}) collective-permute-start(f32[16,32,128]{2,1,0:T(8,128)} %get-tuple-element.65), channel_id=1, source_target_pairs={{0,1},{1,0},{2,3},{3,2},{4,5},{5,4},{6,7},{7,6},{8,9},{9,8},{10,11... | collective-permute-start | bytes 786440 | tf_op jit(solution)/shard_map/ppermute | solution.py:428
  56.9 5.8 %collective-permute-start.11 = (f32[4,32,128]{2,1,0:T(8,128)}, f32[4,32,128]{2,1,0:T(8,128)S(1)}, u32[]{:S(2)}, u32[]{:S(2)}) collective-permute-start(f32[4,32,128]{2,1,0:T(8,128)} %copy-done.15), channel_id=1, source_target_pairs={{0,4},{4,8},{8,12},{1,5},{5,9},{9,13},{2,6},{6,10},{10,14},{3,7},{... | collective-permute-start | bytes 196616 | tf_op jit(solution)/shard_map/ppermute | solution.py:428
  60.4 6.5 %collective-permute-start.12 = (f32[5,32,128]{2,1,0:T(8,128)S(1)}, f32[5,32,128]{2,1,0:T(8,128)S(1)}, u32[]{:S(2)}, u32[]{:S(2)}) collective-permute-start(f32[5,32,128]{2,1,0:T(8,128)S(1)} %get-tuple-element.64), channel_id=1, source_target_pairs={{4,0},{8,4},{12,8},{5,1},{9,5},{13,9},{6,2},{10,6},{14,10},{7,3},{... | collective-permute-start | bytes 245768 | tf_op jit(solution)/shard_map/ppermute | solution.py:428
  66.8 1.1 %copy-start.6 = (f32[3,16,32,128]{3,2,1,0:T(8,128)S(1)}, f32[3,16,32,128]{3,2,1,0:T(8,128)}, u32[]{:S(2)}) copy-start(f32[3,16,32,128]{3,2,1,0:T(8,128)} %copy-done.5) | copy-start | bytes 2359300

commit v2 on v1

--- a/solution.py
+++ b/solution.py
@@ -127,19 +127,30 @@
 
 
 class Planes:
-    def __init__(self, ref, left, right, tail, head):
+    def __init__(self, ref, first, second, tail, head):
         self.ref = ref
         self.count = ref.shape[1]
-        self.left, self.right = left, right
+        self.first, self.second = first, second
         self.tail, self.head = tail, head
+        self.even = even_strike()
+        self.any_left = lax.axis_index("gx") > 0
+        self.any_right = lax.axis_index("gx") < lax.axis_size("gx") - 1
+
+    def left(self, i):
+        plane = jnp.where(self.even, self.second[i], self.first[i])
+        return jnp.where(self.any_left, plane, 0.0)
+
+    def right(self, i):
+        plane = jnp.where(self.even, self.first[i], self.second[i])
+        return jnp.where(self.any_right, plane, 0.0)
 
     def __call__(self, comp, x, offset=0):
         if isinstance(x, int):
             place = x + offset
             if place < 0:
-                return self.left[self.tail.index((comp, place))]
+                return self.left(self.tail.index((comp, place)))
             if place >= self.count:
-                return self.right[self.head.index((comp, place - self.count))]
+                return self.right(self.head.index((comp, place - self.count)))
         return self.ref[comp, x + offset]
 
     def forward_x(self, comp, x):
@@ -189,21 +200,30 @@
         body(x)
 
 
-def edge_planes(ref, planes, out):
+def even_strike():
+    return lax.axis_index("gx") % 2 == 0
+
+
+def edge_planes(ref, tail, head, first_out, second_out):
     count = ref.shape[1]
-    for i, (comp, place) in enumerate(planes):
-        out[i] = ref[comp, place % count]
+    even = even_strike()
+    for i in range(first_out.shape[0]):
+        comp, place = tail[min(i, len(tail) - 1)]
+        right = ref[comp, place % count]
+        comp, place = head[min(i, len(head) - 1)]
+        left = ref[comp, place % count]
+        first_out[i] = jnp.where(even, right, left)
+        second_out[i] = jnp.where(even, left, right)
 
 
 def fault_row(rows):
     return jnp.where(lax.axis_index("gy") == lax.axis_size("gy") // 2, 0, rows - 1)
 
 
-def pack_kernel(stress, tail_out, head_out, strip_out):
+def pack_kernel(stress, first_out, second_out, strip_out):
     count, rows, depths = stress.shape[1:]
     edges = Edges(rows, depths)
-    edge_planes(stress, STRESS_TAIL, tail_out)
-    edge_planes(stress, STRESS_HEAD, head_out)
+    edge_planes(stress, STRESS_TAIL, STRESS_HEAD, first_out, second_out)
 
     def body(x, carry):
         strip_out[x] = edges.packed([stress[c, x] for c in STRESS_SLOTS])
@@ -213,17 +233,17 @@
 
 
 def velocity_kernel(first, banded, *refs):
-    velocity, stress, material, table, left, right, strip = refs[:7]
+    velocity, stress, material, table, first_edge, second_edge, strip = refs[:7]
     refs = refs[7:]
     bands = ()
     if banded:
         bands, refs = refs[:2], refs[2:]
     if first and not banded:
         (prestress, normal, slip, zone, mask), refs = refs[:5], refs[5:]
-    out, face, tail_out, head_out, strip_out = refs
+    out, face, first_out, second_out, strip_out = refs
     count, rows, depths = velocity.shape[1:]
     edges = Edges(rows, depths)
-    planes = Planes(stress, left, right, STRESS_TAIL, STRESS_HEAD)
+    planes = Planes(stress, first_edge, second_edge, STRESS_TAIL, STRESS_HEAD)
     band = Bands(bands, STRESS_TAIL_Y, STRESS_HEAD_Y)
     fault = fault_row(rows)
 
@@ -257,8 +277,7 @@
             face[pl.ds(2 * count + x, 1), :] = looked_up(labels, table, 2, CLASSES)
 
     over_planes(count, body)
-    edge_planes(out, VEL_TAIL, tail_out)
-    edge_planes(out, VEL_HEAD, head_out)
+    edge_planes(out, VEL_TAIL, VEL_HEAD, first_out, second_out)
     if first and not banded:
         own = normal.shape[0]
         place = 3 * count
@@ -270,7 +289,7 @@
 
 
 def fault_kernel(first, banded, *refs):
-    (own_face, other_face, tail, head, strip, friction_table, anchor), refs = refs[:7], refs[7:]
+    (own_face, other_face, first_edge, second_edge, strip, friction_table, anchor), refs = refs[:7], refs[7:]
     if first:
         if banded:
             still, refs = refs[0], refs[1:]
@@ -278,7 +297,7 @@
         (still, own_first, other_first, slip), refs = refs[:4], refs[4:]
     if first:
         own_first, other_first = own_face, other_face
-    change, slip_out, tail_out, head_out, strip_out = refs[:5]
+    change, slip_out, first_out, second_out, strip_out = refs[:5]
     count, rows, depths = strip.shape
     middle = lax.axis_size("gy") // 2
     side = lax.axis_index("gy")
@@ -329,13 +348,18 @@
 
     fault = fault_row(rows)
     on_fault = lax.broadcasted_iota(jnp.int32, (rows, depths), 0) == fault
-    for planes, source, out in ((VEL_TAIL, tail, tail_out), (VEL_HEAD, head, head_out)):
-        for i, (comp, place) in enumerate(planes):
-            plane = source[i]
-            if comp != 1:
-                line = change[comp // 2, pl.ds(place % count, 1), :]
-                plane = plane + jnp.where(on_fault, line, 0.0)
-            out[i] = plane
+    even = even_strike()
+    still_line = jnp.zeros((1, depths), jnp.float32)
+
+    def line(planes, i):
+        comp, place = planes[min(i, len(planes) - 1)]
+        return still_line if comp == 1 else change[comp // 2, pl.ds(place % count, 1), :]
+
+    for i in range(first_out.shape[0]):
+        right, left = line(VEL_TAIL, i), line(VEL_HEAD, i)
+        one, two = jnp.where(even, right, left), jnp.where(even, left, right)
+        first_out[i] = first_edge[i] + jnp.where(on_fault, one, 0.0)
+        second_out[i] = second_edge[i] + jnp.where(on_fault, two, 0.0)
     flat = Edges(count, depths)
     ends = flat.packed([change_x, None, change_z])
     for x in range(count):
@@ -343,14 +367,14 @@
 
 
 def stress_kernel(last, banded, *refs):
-    velocity, stress, memory, material, table, change, left, right, strip = refs[:9]
+    velocity, stress, memory, material, table, change, first_edge, second_edge, strip = refs[:9]
     refs = refs[9:]
     bands = ()
     if banded:
         bands, refs = refs[:2], refs[2:]
     vel_out, stress_out, memory_out = refs[:3]
     if not last:
-        tail_out, head_out, strip_out = refs[3:]
+        first_out, second_out, strip_out = refs[3:]
     count, rows, depths = velocity.shape[1:]
     edges = Edges(rows, depths)
     on_fault = edges.row == fault_row(rows)
@@ -359,7 +383,7 @@
             line = change[c // 2, pl.ds(x, 1), :]
             vel_out[c, x] = velocity[c, x] + jnp.where(on_fault, line, 0.0)
         vel_out[1, x] = velocity[1, x]
-    planes = Planes(vel_out, left, right, VEL_TAIL, VEL_HEAD)
+    planes = Planes(vel_out, first_edge, second_edge, VEL_TAIL, VEL_HEAD)
     band = Bands(bands, VEL_TAIL_Y, VEL_HEAD_Y)
 
     def body(x):
@@ -397,8 +421,7 @@
 
     over_planes(count, body)
     if not last:
-        edge_planes(stress_out, STRESS_TAIL, tail_out)
-        edge_planes(stress_out, STRESS_HEAD, head_out)
+        edge_planes(stress_out, STRESS_TAIL, STRESS_HEAD, first_out, second_out)
 
 
 def call(kernel, name, operands, outs, scalars=(), cost=0):
@@ -422,6 +445,16 @@
 def along(axis, count, skip=()):
     up = [(i, i + 1) for i in range(count - 1) if i not in skip]
     return (axis, up), (axis, [(b, a) for a, b in up])
+
+
+def strike_swaps(count):
+    routes = []
+    for start in (0, 1):
+        partner = list(range(count))
+        for i in range(start, count - 1, 2):
+            partner[i], partner[i + 1] = i + 1, i
+        routes.append(("gx", list(enumerate(partner))))
+    return routes
 
 
 def sent(block, route):
@@ -452,13 +485,12 @@
     middle = sides // 2
     banded = sides > 2
     cells = count * rows * depths
-    up, down = along("gx", lax.axis_size("gx"))
+    swaps = strike_swaps(lax.axis_size("gx"))
     up_y, down_y = along("gy", sides, (middle - 1,))
     across = ("gy", [(middle - 1, middle), (middle, middle - 1)])
     deep = ("gz", [(0, 1), (1, 0)])
 
-    def strike_shape(planes):
-        return (len(planes), rows, depths)
+    edge_shape = (max(len(STRESS_TAIL), len(STRESS_HEAD)), rows, depths)
 
     strip_shape = (count, rows, depths)
     block = (count, rows, depths)
@@ -477,18 +509,18 @@
         )
         still = lax.all_gather(still, "gy", axis=1, tiled=True)
 
-    tail, head, strip = call(
+    one, two, strip = call(
         pack_kernel,
         "pack",
         [stress],
-        [strike_shape(STRESS_TAIL), strike_shape(STRESS_HEAD), strip_shape],
+        [edge_shape, edge_shape, strip_shape],
     )
     for step in range(STEPS):
         first, last = step == 0, step == STEPS - 1
         strip = sent(strip, deep)
-        left = sent(tail, up)
-        right = sent(head, down)
-        operands = [velocity, stress, material, material_table, left, right, strip]
+        one = sent(one, swaps[0])
+        two = sent(two, swaps[1])
+        operands = [velocity, stress, material, material_table, one, two, strip]
         if banded:
             operands += [
                 sent(edge_rows(stress, STRESS_TAIL_Y), up_y),
@@ -500,27 +532,27 @@
             if not banded:
                 operands += [prestress, normal_stress, slip_path, zone_label, fault_mask]
                 face_rows += 6 * normal_stress.shape[0]
-        free, face, tail, head, strip = call(
+        free, face, one, two, strip = call(
             functools.partial(velocity_kernel, first, banded),
             "velocity",
             operands,
             [
                 (3, *block),
                 (face_rows, depths),
-                strike_shape(VEL_TAIL),
-                strike_shape(VEL_HEAD),
+                edge_shape,
+                edge_shape,
                 strip_shape,
             ],
             scalars=(3,),
             cost=60 * cells,
         )
         other = sent(face, across)
-        operands = [face, other, tail, head, strip, friction_table, patch_anchor]
+        operands = [face, other, one, two, strip, friction_table, patch_anchor]
         outs = [
             (2, count, depths),
             (count, depths),
-            strike_shape(VEL_TAIL),
-            strike_shape(VEL_HEAD),
+            edge_shape,
+            edge_shape,
             strip_shape,
         ]
         if first:
@@ -538,14 +570,14 @@
             outs,
             scalars=(5, 6),
         )
-        change, slip, tail, head, strip = result[:5]
+        change, slip, one, two, strip = result[:5]
         if first and not banded:
             still = result[5]
         strip = sent(strip, deep)
-        left = sent(tail, up)
-        right = sent(head, down)
+        one = sent(one, swaps[0])
+        two = sent(two, swaps[1])
         operands = [free, stress, memory, material, material_table]
-        operands += [change, left, right, strip]
+        operands += [change, one, two, strip]
         if banded:
             operands += [
                 sent(edge_rows(free, VEL_TAIL_Y), up_y),
@@ -553,7 +585,7 @@
             ]
         outs = [(3, *block), (6, *block), (6, *block)]
         if not last:
-            outs += [strike_shape(STRESS_TAIL), strike_shape(STRESS_HEAD), strip_shape]
+            outs += [edge_shape, edge_shape, strip_shape]
         result = call(
             functools.partial(stress_kernel, last, banded),
             "stress",
@@ -564,7 +596,7 @@
         )
         velocity, stress, memory = result[:3]
         if not last:
-            tail, head, strip = result[3:]
+            one, two, strip = result[3:]
     side = lax.axis_index("gy")
     if banded:
         held = jnp.where(side == middle, slip, 0.0)

time: 73.7 us -> 62.7 us (0.85)
  waiting for transfers between devices: 21.1 us -> 13.8 us
  starting transfers between devices: 25.9 us -> 21.7 us
    ppermute x14, waiting for transfers between devices: 21.1 us -> 13.8 us  [sent(): return lax.ppermute(block, *route)]
    ppermute x14, starting transfers between devices: 25.9 us -> 21.7 us  [sent(): return lax.ppermute(block, *route)]
  transfers between devices with their start and end apart: 14 -> 14, of which waited for: 7 -> 6; matrix products, arithmetic and copies ran while one was open for 1% -> 1% of each run, Pallas kernels for 0% -> 0%
where the time goes in v2:
time: 62.7 us; the launch traced here: 61.8 us
  starting transfers between devices  21.7 us (35%)
  Pallas kernels  20.8 us (33%)
  waiting for transfers between devices  13.8 us (22%)
  local copies, waits for them, and re-layouts  4.69 us (7%)
  between operations  0.84 us (1%)
    ppermute x14, starting transfers between devices, sent(): return lax.ppermute(block, *route)  21.7 us
    pallas_call x7, Pallas kernels, call(): pl.pallas_call(kernel, out_shape=outs, in_specs=in_specs, out_specs=[pl.B...  20.8 us
    ppermute x14, waiting for transfers between devices, sent(): return lax.ppermute(block, *route)  13.8 us
    unnamed x32, local copies, waits for them, and re-layouts  4.09 us
  transfers between devices with their start and end apart: 14, of which 6 were waited for; matrix products, arithmetic and copies ran while one was open for 1% of the time, Pallas kernels for 0%

profile of v2, /device:TPU:0, one launch (start us, length us, event | category | flops | bytes accessed | tf_op | source)
XLA Modules:
  0.0 61.8 jit_solution(14652141899673798428)
XLA Ops:
  0.6 0.0 copy-start
  0.6 1.4 %copy-done = f32[6,16,32,128]{3,2,1,0:T(8,128)S(1)} copy-done((f32[6,16,32,128]{3,2,1,0:T(8,128)S(1)}, f32[6,16,32,128]{3,2,1,0:T(8,128)}, u32[]{:S(2)}) %copy-start) | copy-done | bytes 1572888
  2.1 1.2 %pack.1 = (f32[5,32,128]{2,1,0:T(8,128)S(1)}, f32[5,32,128]{2,1,0:T(8,128)S(1)}, f32[16,32,128]{2,1,0:T(8,128)S(1)}) custom-call(f32[6,16,32,128]{3,2,1,0:T(8,128)S(1)} %copy-done), custom_call_target="tpu_custom_call" | custom-call | bytes 1998848 | tf_op jit(solution)/shard_map/pack/pallas_call | solution.py:434
  3.3 0.5 collective-permute-start.2
  3.9 2.6 %collective-permute-start = (f32[5,32,128]{2,1,0:T(8,128)S(1)}, f32[5,32,128]{2,1,0:T(8,128)S(1)}, u32[]{:S(2)}, u32[]{:S(2)}) collective-permute-start(f32[5,32,128]{2,1,0:T(8,128)S(1)} %get-tuple-element.37), channel_id=1, source_target_pairs={{0,4},{4,0},{8,12},{12,8},{1,5},{5,1},{9,13},{13,9},{2,6},{6,2},{1... | collective-permute-start | bytes 245768 | tf_op jit(solution)/shard_map/ppermute | solution.py:461
  6.5 0.8 %collective-permute-start.1 = (f32[5,32,128]{2,1,0:T(8,128)S(1)}, f32[5,32,128]{2,1,0:T(8,128)S(1)}, u32[]{:S(2)}, u32[]{:S(2)}) collective-permute-start(f32[5,32,128]{2,1,0:T(8,128)S(1)} %get-tuple-element.38), channel_id=1, source_target_pairs={{0,0},{4,8},{8,4},{12,12},{1,1},{5,9},{9,5},{13,13},{2,2},{6,10},{... | collective-permute-start | bytes 245768 | tf_op jit(solution)/shard_map/ppermute | solution.py:461
  7.3 2.2 %collective-permute-done.refs_4_ = f32[5,32,128]{2,1,0:T(8,128)S(1)} collective-permute-done((f32[5,32,128]{2,1,0:T(8,128)S(1)}, f32[5,32,128]{2,1,0:T(8,128)S(1)}, u32[]{:S(2)}, u32[]{:S(2)}) %collective-permute-start) | collective-permute-done | bytes 81952 | tf_op jit(solution)/shard_map/ppermute | solution.py:461
  9.6 3.9 %velocity.2 = (f32[3,16,32,128]{3,2,1,0:T(8,128)S(1)}, f32[96,128]{1,0:T(8,128)S(1)}, f32[5,32,128]{2,1,0:T(8,128)S(1)}, f32[5,32,128]{2,1,0:T(8,128)S(1)}, f32[16,32,128]{2,1,0:T(8,128)S(1)}) custom-call(f32[3,16,32,128]{3,2,1,0:T(8,128)S(1)} %copy-done.4, f32[6,16,32,128]{3,2,1,0:T(8,128)S(1)} %copy-done, s32[16,32,128]{2,1,0:T(8,128)S(1)} %copy-done.2, ...), custom_call_target="tpu_custom_call" | custom-call | flops 3932160 | bytes 4333728 | tf_op jit(solution)/shard_map/velocity/pallas_call | solution.py:434
  13.6 1.7 %collective-permute-start.3 = (f32[96,128]{1,0:T(8,128)S(1)}, f32[96,128]{1,0:T(8,128)S(1)}, u32[]{:S(2)}, u32[]{:S(2)}) collective-permute-start(f32[96,128]{1,0:T(8,128)S(1)} %get-tuple-element.41.refs_0_.refs_8_), channel_id=1, source_target_pairs={{0,2},{2,0},{1,3},{3,1},{4,6},{6,4},{5,7},{7,5},{8,10},{10,8},{9,1... | collective-permute-start | bytes 147464 | tf_op jit(solution)/shard_map/ppermute | solution.py:461
  15.3 2.4 %collective-permute-done.3.refs_1_.refs_9_ = f32[96,128]{1,0:T(8,128)S(1)} collective-permute-done((f32[96,128]{1,0:T(8,128)S(1)}, f32[96,128]{1,0:T(8,128)S(1)}, u32[]{:S(2)}, u32[]{:S(2)}) %collective-permute-start.3) | collective-permute-done | bytes 49184 | tf_op jit(solution)/shard_map/ppermute | solution.py:461
  17.7 0.7 %fault.2 = (f32[2,16,128]{2,1,0:T(8,128)S(1)}, f32[16,128]{1,0:T(8,128)S(1)}, f32[5,32,128]{2,1,0:T(8,128)S(1)}, f32[5,32,128]{2,1,0:T(8,128)S(1)}, f32[16,32,12...) custom-call(f32[96,128]{1,0:T(8,128)S(1)} %get-tuple-element.41.refs_0_.refs_8_, ...), custom_call_target="tpu_custom_call" | custom-call | bytes 1024056 | tf_op jit(solution)/shard_map/fault/pallas_call | solution.py:434
  18.4 0.1 collective-permute-start.6
  18.5 5.1 %collective-permute-start.4 = (f32[5,32,128]{2,1,0:T(8,128)S(1)}, f32[5,32,128]{2,1,0:T(8,128)S(1)}, u32[]{:S(2)}, u32[]{:S(2)}) collective-permute-start(f32[5,32,128]{2,1,0:T(8,128)S(1)} %get-tuple-element.46), channel_id=1, source_target_pairs={{0,4},{4,0},{8,12},{12,8},{1,5},{5,1},{9,13},{13,9},{2,6},{6,2},{1... | collective-permute-start | bytes 245768 | tf_op jit(solution)/shard_map/ppermute | solution.py:461
  23.6 0.7 %collective-permute-start.5 = (f32[5,32,128]{2,1,0:T(8,128)S(1)}, f32[5,32,128]{2,1,0:T(8,128)S(1)}, u32[]{:S(2)}, u32[]{:S(2)}) collective-permute-start(f32[5,32,128]{2,1,0:T(8,128)S(1)} %get-tuple-element.47), channel_id=1, source_target_pairs={{0,0},{4,8},{8,4},{12,12},{1,1},{5,9},{9,5},{13,13},{2,2},{6,10},{... | collective-permute-start | bytes 245768 | tf_op jit(solution)/shard_map/ppermute | solution.py:461
  24.3 2.4 %collective-permute-done.4.refs_6_ = f32[5,32,128]{2,1,0:T(8,128)S(1)} collective-permute-done((f32[5,32,128]{2,1,0:T(8,128)S(1)}, f32[5,32,128]{2,1,0:T(8,128)S(1)}, u32[]{:S(2)}, u32[]{:S(2)}) %collective-permute-start.4) | collective-permute-done | bytes 81952 | tf_op jit(solution)/shard_map/ppermute | solution.py:461
  26.7 4.2 %stress.4 = (f32[3,16,32,128]{3,2,1,0:T(8,128)S(1)}, f32[6,16,32,128]{3,2,1,0:T(8,128)S(1)}, f32[6,16,32,128]{3,2,1,0:T(8,128)S(1)}, f32[5,32,128]{2,1,0:T(8,128...) custom-call(f32[3,16,32,128]{3,2,1,0:T(8,128)S(1)} %get-tuple-element.40.refs_0_, ...), custom_call_target="tpu_custom_call" | custom-call | flops 6553600 | bytes 8994976 | tf_op jit(solution)/shard_map/stress/pallas_call | solution.py:434
  30.9 0.1 collective-permute-start.9
  31.0 3.7 %collective-permute-start.7 = (f32[5,32,128]{2,1,0:T(8,128)S(1)}, f32[5,32,128]{2,1,0:T(8,128)S(1)}, u32[]{:S(2)}, u32[]{:S(2)}) collective-permute-start(f32[5,32,128]{2,1,0:T(8,128)S(1)} %get-tuple-element.51), channel_id=1, source_target_pairs={{0,4},{4,0},{8,12},{12,8},{1,5},{5,1},{9,13},{13,9},{2,6},{6,2},{1... | collective-permute-start | bytes 245768 | tf_op jit(solution)/shard_map/ppermute | solution.py:461
  34.7 0.7 %collective-permute-start.8 = (f32[5,32,128]{2,1,0:T(8,128)S(1)}, f32[5,32,128]{2,1,0:T(8,128)S(1)}, u32[]{:S(2)}, u32[]{:S(2)}) collective-permute-start(f32[5,32,128]{2,1,0:T(8,128)S(1)} %get-tuple-element.52), channel_id=1, source_target_pairs={{0,0},{4,8},{8,4},{12,12},{1,1},{5,9},{9,5},{13,13},{2,2},{6,10},{... | collective-permute-start | bytes 245768 | tf_op jit(solution)/shard_map/ppermute | solution.py:461
  35.3 2.4 %collective-permute-done.7.refs_4_ = f32[5,32,128]{2,1,0:T(8,128)S(1)} collective-permute-done((f32[5,32,128]{2,1,0:T(8,128)S(1)}, f32[5,32,128]{2,1,0:T(8,128)S(1)}, u32[]{:S(2)}, u32[]{:S(2)}) %collective-permute-start.7) | collective-permute-done | bytes 81952 | tf_op jit(solution)/shard_map/ppermute | solution.py:461
  37.7 3.9 %velocity.3 = (f32[3,16,32,128]{3,2,1,0:T(8,128)S(1)}, f32[32,128]{1,0:T(8,128)S(1)}, f32[5,32,128]{2,1,0:T(8,128)S(1)}, f32[5,32,128]{2,1,0:T(8,128)S(1)}, f32[16,32,128]{2,1,0:T(8,128)S(1)}) custom-call(f32[3,16,32,128]{3,2,1,0:T(8,128)S(1)} %get-tuple-element.49.refs_0_, f32[6,16,32,128]{3,2,1,0:T(8,128)S(1)} %get-tuple-element.50.refs_1_, ...), custom_call_target="tpu_custom_call" | custom-call | flops 3932160 | bytes 4276384 | tf_op jit(solution)/shard_map/velocity/pallas_call | solution.py:434
  41.7 0.9 %copy-done.5 = f32[3,16,32,128]{3,2,1,0:T(8,128)} copy-done((f32[3,16,32,128]{3,2,1,0:T(8,128)}, f32[3,16,32,128]{3,2,1,0:T(8,128)S(1)}, u32[]{:S(2)}) %copy-start.5) | copy-done | bytes 786456
  42.5 1.5 %collective-permute-start.10 = (f32[32,128]{1,0:T(8,128)S(1)}, f32[32,128]{1,0:T(8,128)S(1)}, u32[]{:S(2)}, u32[]{:S(2)}) collective-permute-start(f32[32,128]{1,0:T(8,128)S(1)} %get-tuple-element.56.refs_0_), channel_id=1, source_target_pairs={{0,2},{2,0},{1,3},{3,1},{4,6},{6,4},{5,7},{7,5},{8,10},{10,8},{9,1... | collective-permute-start | bytes 49160 | tf_op jit(solution)/shard_map/ppermute | solution.py:461
  44.0 2.3 %collective-permute-done.10.refs_1_ = f32[32,128]{1,0:T(8,128)S(1)} collective-permute-done((f32[32,128]{1,0:T(8,128)S(1)}, f32[32,128]{1,0:T(8,128)S(1)}, u32[]{:S(2)}, u32[]{:S(2)}) %collective-permute-start.10) | collective-permute-done | bytes 16416 | tf_op jit(solution)/shard_map/ppermute | solution.py:461
  46.3 1.4 %fault.3 = (f32[2,16,128]{2,1,0:T(8,128)S(1)}, f32[16,128]{1,0:T(8,128)S(1)}, f32[5,32,128]{2,1,0:T(8,128)S(1)}, f32[5,32,128]{2,1,0:T(8,128)S(1)}, f32[16,32,128]{2,1,0:T(8,128)}) custom-call(f32[32,128]{1,0:T(8,128)S(1)} %get-tuple-element.56.refs_0_, f32[32,128]{1,0:T(8,128)S(1)} %collective-permute-done.10.refs_1_, ...), custom_call_target="tpu_custom_call" | custom-call | bytes 1065016 | tf_op jit(solution)/shard_map/fault/pallas_call | solution.py:434
  47.7 0.6 %copy-done.15 = f32[5,32,128]{2,1,0:T(8,128)} copy-done((f32[5,32,128]{2,1,0:T(8,128)}, f32[5,32,128]{2,1,0:T(8,128)S(1)}, u32[]{:S(2)}) %copy-start.15) | copy-done | bytes 81944
  48.3 3.6 %collective-permute-start.11 = (f32[5,32,128]{2,1,0:T(8,128)}, f32[5,32,128]{2,1,0:T(8,128)S(1)}, u32[]{:S(2)}, u32[]{:S(2)}) collective-permute-start(f32[5,32,128]{2,1,0:T(8,128)} %copy-done.15), channel_id=1, source_target_pairs={{0,4},{4,0},{8,12},{12,8},{1,5},{5,1},{9,13},{13,9},{2,6},{6,2},{1... | collective-permute-start | bytes 245768 | tf_op jit(solution)/shard_map/ppermute | solution.py:461
  52.0 0.7 %collective-permute-start.12 = (f32[5,32,128]{2,1,0:T(8,128)S(1)}, f32[5,32,128]{2,1,0:T(8,128)S(1)}, u32[]{:S(2)}, u32[]{:S(2)}) collective-permute-start(f32[5,32,128]{2,1,0:T(8,128)S(1)} %get-tuple-element.64), channel_id=1, source_target_pairs={{0,0},{4,8},{8,4},{12,12},{1,1},{5,9},{9,5},{13,13},{2,2},{6,10},{... | collective-permute-start | bytes 245768 | tf_op jit(solution)/shard_map/ppermute | solution.py:461
  52.6 0.6 constant_dynamic-slice_fusion
  53.2 2.1 %collective-permute-done.11.refs_6_ = f32[5,32,128]{2,1,0:T(8,128)S(1)} collective-permute-done((f32[5,32,128]{2,1,0:T(8,128)}, f32[5,32,128]{2,1,0:T(8,128)S(1)}, u32[]{:S(2)}, u32[]{:S(2)}) %collective-permute-start.11) | collective-permute-done | bytes 81952 | tf_op jit(solution)/shard_map/ppermute | solution.py:461
  55.3 1.1 %copy-done.6 = f32[3,16,32,128]{3,2,1,0:T(8,128)S(1)} copy-done((f32[3,16,32,128]{3,2,1,0:T(8,128)S(1)}, f32[3,16,32,128]{3,2,1,0:T(8,128)}, u32[]{:S(2)}) %copy-start.6) | copy-done | bytes 786456
  56.4 5.4 %stress.5 = (f32[3,16,32,128]{3,2,1,0:T(8,128)}, f32[6,16,32,128]{3,2,1,0:T(8,128)}, f32[6,16,32,128]{3,2,1,0:T(8,128)}) custom-call(f32[3,16,32,128]{3,2,1,0:T(8,128)S(1)} %copy-done.6, f32[6,16,32,128]{3,2,1,0:T(8,128)S(1)} %get-tuple-element.50.refs_1_, f32[6,16,32,128]{3,2,1,0:T(8,128)S(1)} %get-tuple-element.55.refs_2_, s32[16,32,128]{2,1,0:T(8,128)S(1)} %copy-done.2, ...), custom_call_target="tpu_custom_call" | custom-call | flops 6553600 | bytes 8568992 | tf_op jit(solution)/shard_map/stress/pallas_call | solution.py:434
  (36 shorter events, 0.1 us)
Async XLA Ops:
  0.6 1.4 %copy-start = (f32[6,16,32,128]{3,2,1,0:T(8,128)S(1)}, f32[6,16,32,128]{3,2,1,0:T(8,128)}, u32[]{:S(2)}) copy-start(f32[6,16,32,128]{3,2,1,0:T(8,128)} %refs_1_.3) | copy-start | bytes 4718596
  2.0 7.5 %copy-start.2 = (s32[16,32,128]{2,1,0:T(8,128)S(1)}, s32[16,32,128]{2,1,0:T(8,128)}, u32[]{:S(2)}) copy-start(s32[16,32,128]{2,1,0:T(8,128)} %refs_3_.7) | copy-start | bytes 786436
  2.0 7.5 %copy-start.4 = (f32[3,16,32,128]{3,2,1,0:T(8,128)S(1)}, f32[3,16,32,128]{3,2,1,0:T(8,128)}, u32[]{:S(2)}) copy-start(f32[3,16,32,128]{3,2,1,0:T(8,128)} %refs_0_.1) | copy-start | bytes 2359300
  2.0 7.5 %copy-start.7 = (f32[5,8]{1,0:T(8,128)S(1)}, f32[5,8]{1,0:T(8,128)}, u32[]{:S(2)}) copy-start(f32[5,8]{1,0:T(8,128)} %refs_4_.3) | copy-start | bytes 484
  2.1 7.5 %copy-start.8 = (f32[8,2,128]{2,1,0:T(2,128)S(1)}, f32[8,2,128]{2,1,0:T(2,128)}, u32[]{:S(2)}) copy-start(f32[8,2,128]{2,1,0:T(2,128)} %refs_7_.1) | copy-start | bytes 24580
  2.1 7.5 %copy-start.10 = (f32[8,128]{1,0:T(8,128)S(1)}, f32[8,128]{1,0:T(8,128)}, u32[]{:S(2)}) copy-start(f32[8,128]{1,0:T(8,128)} %refs_8_.1) | copy-start | bytes 12292
  2.1 7.5 %copy-start.11 = (f32[8,128]{1,0:T(8,128)S(1)}, f32[8,128]{1,0:T(8,128)}, u32[]{:S(2)}) copy-start(f32[8,128]{1,0:T(8,128)} %refs_9_.1) | copy-start | bytes 12292
  2.1 7.5 %copy-start.12 = (s32[8,128]{1,0:T(8,128)S(1)}, s32[8,128]{1,0:T(8,128)}, u32[]{:S(2)}) copy-start(s32[8,128]{1,0:T(8,128)} %refs_10_.1) | copy-start | bytes 12292
  2.1 7.5 %copy-start.13 = (s32[8,128]{1,0:T(8,128)S(1)}, s32[8,128]{1,0:T(8,128)}, u32[]{:S(2)}) copy-start(s32[8,128]{1,0:T(8,128)} %refs_11_.1) | copy-start | bytes 12292
  3.3 14.4 %copy-start.9 = (f32[3,4]{1,0:T(4,128)S(1)}, f32[3,4]{1,0:T(4,128)}, u32[]{:S(2)}) copy-start(f32[3,4]{1,0:T(4,128)} %refs_5_.3) | copy-start | bytes 148
  3.3 14.4 %copy-start.14 = (s32[2]{0:T(128)S(1)}, s32[2]{0:T(128)}, u32[]{:S(2)}) copy-start(s32[2]{0:T(128)} %refs_6_.3) | copy-start | bytes 28
  3.3 6.2 %collective-permute-start.2 = (f32[16,32,128]{2,1,0:T(8,128)S(1)}, f32[16,32,128]{2,1,0:T(8,128)S(1)}, u32[]{:S(2)}, u32[]{:S(2)}) collective-permute-start(f32[16,32,128]{2,1,0:T(8,128)S(1)} %get-tuple-element.39), channel_id=1, source_target_pairs={{0,1},{1,0},{2,3},{3,2},{4,5},{5,4},{6,7},{7,6},{8,9},{9,8},{10,11... | collective-permute-start | bytes 786440 | tf_op jit(solution)/shard_map/ppermute | solution.py:461
  3.9 5.7 %collective-permute-start = (f32[5,32,128]{2,1,0:T(8,128)S(1)}, f32[5,32,128]{2,1,0:T(8,128)S(1)}, u32[]{:S(2)}, u32[]{:S(2)}) collective-permute-start(f32[5,32,128]{2,1,0:T(8,128)S(1)} %get-tuple-element.37), channel_id=1, source_target_pairs={{0,4},{4,0},{8,12},{12,8},{1,5},{5,1},{9,13},{13,9},{2,6},{6,2},{1... | collective-permute-start | bytes 245768 | tf_op jit(solution)/shard_map/ppermute | solution.py:461
  6.5 20.1 %copy-start.1 = (f32[6,16,32,128]{3,2,1,0:T(8,128)S(1)}, f32[6,16,32,128]{3,2,1,0:T(8,128)}, u32[]{:S(2)}) copy-start(f32[6,16,32,128]{3,2,1,0:T(8,128)} %refs_1_.3) | copy-start | bytes 4718596
  6.5 20.1 %copy-start.3 = (f32[6,16,32,128]{3,2,1,0:T(8,128)S(1)}, f32[6,16,32,128]{3,2,1,0:T(8,128)}, u32[]{:S(2)}) copy-start(f32[6,16,32,128]{3,2,1,0:T(8,128)} %refs_2_.4) | copy-start | bytes 4718596
  6.5 3.0 %collective-permute-start.1 = (f32[5,32,128]{2,1,0:T(8,128)S(1)}, f32[5,32,128]{2,1,0:T(8,128)S(1)}, u32[]{:S(2)}, u32[]{:S(2)}) collective-permute-start(f32[5,32,128]{2,1,0:T(8,128)S(1)} %get-tuple-element.38), channel_id=1, source_target_pairs={{0,0},{4,8},{8,4},{12,12},{1,1},{5,9},{9,5},{13,13},{2,2},{6,10},{... | collective-permute-start | bytes 245768 | tf_op jit(solution)/shard_map/ppermute | solution.py:461
  13.6 4.2 %collective-permute-start.3 = (f32[96,128]{1,0:T(8,128)S(1)}, f32[96,128]{1,0:T(8,128)S(1)}, u32[]{:S(2)}, u32[]{:S(2)}) collective-permute-start(f32[96,128]{1,0:T(8,128)S(1)} %get-tuple-element.41.refs_0_.refs_8_), channel_id=1, source_target_pairs={{0,2},{2,0},{1,3},{3,1},{4,6},{6,4},{5,7},{7,5},{8,10},{10,8},{9,1... | collective-permute-start | bytes 147464 | tf_op jit(solution)/shard_map/ppermute | solution.py:461
  18.4 8.2 %collective-permute-start.6 = (f32[16,32,128]{2,1,0:T(8,128)S(1)}, f32[16,32,128]{2,1,0:T(8,128)S(1)}, u32[]{:S(2)}, u32[]{:S(2)}) collective-permute-start(f32[16,32,128]{2,1,0:T(8,128)S(1)} %get-tuple-element.48), channel_id=1, source_target_pairs={{0,1},{1,0},{2,3},{3,2},{4,5},{5,4},{6,7},{7,6},{8,9},{9,8},{10,11... | collective-permute-start | bytes 786440 | tf_op jit(solution)/shard_map/ppermute | solution.py:461
  18.5 8.1 %collective-permute-start.4 = (f32[5,32,128]{2,1,0:T(8,128)S(1)}, f32[5,32,128]{2,1,0:T(8,128)S(1)}, u32[]{:S(2)}, u32[]{:S(2)}) collective-permute-start(f32[5,32,128]{2,1,0:T(8,128)S(1)} %get-tuple-element.46), channel_id=1, source_target_pairs={{0,4},{4,0},{8,12},{12,8},{1,5},{5,1},{9,13},{13,9},{2,6},{6,2},{1... | collective-permute-start | bytes 245768 | tf_op jit(solution)/shard_map/ppermute | solution.py:461
  23.6 3.0 %collective-permute-start.5 = (f32[5,32,128]{2,1,0:T(8,128)S(1)}, f32[5,32,128]{2,1,0:T(8,128)S(1)}, u32[]{:S(2)}, u32[]{:S(2)}) collective-permute-start(f32[5,32,128]{2,1,0:T(8,128)S(1)} %get-tuple-element.47), channel_id=1, source_target_pairs={{0,0},{4,8},{8,4},{12,12},{1,1},{5,9},{9,5},{13,13},{2,2},{6,10},{... | collective-permute-start | bytes 245768 | tf_op jit(solution)/shard_map/ppermute | solution.py:461
  30.9 6.8 %collective-permute-start.9 = (f32[16,32,128]{2,1,0:T(8,128)S(1)}, f32[16,32,128]{2,1,0:T(8,128)S(1)}, u32[]{:S(2)}, u32[]{:S(2)}) collective-permute-start(f32[16,32,128]{2,1,0:T(8,128)S(1)} %get-tuple-element.53), channel_id=1, source_target_pairs={{0,1},{1,0},{2,3},{3,2},{4,5},{5,4},{6,7},{7,6},{8,9},{9,8},{10,11... | collective-permute-start | bytes 786440 | tf_op jit(solution)/shard_map/ppermute | solution.py:461
  31.0 6.7 %collective-permute-start.7 = (f32[5,32,128]{2,1,0:T(8,128)S(1)}, f32[5,32,128]{2,1,0:T(8,128)S(1)}, u32[]{:S(2)}, u32[]{:S(2)}) collective-permute-start(f32[5,32,128]{2,1,0:T(8,128)S(1)} %get-tuple-element.51), channel_id=1, source_target_pairs={{0,4},{4,0},{8,12},{12,8},{1,5},{5,1},{9,13},{13,9},{2,6},{6,2},{1... | collective-permute-start | bytes 245768 | tf_op jit(solution)/shard_map/ppermute | solution.py:461
  34.7 3.0 %collective-permute-start.8 = (f32[5,32,128]{2,1,0:T(8,128)S(1)}, f32[5,32,128]{2,1,0:T(8,128)S(1)}, u32[]{:S(2)}, u32[]{:S(2)}) collective-permute-start(f32[5,32,128]{2,1,0:T(8,128)S(1)} %get-tuple-element.52), channel_id=1, source_target_pairs={{0,0},{4,8},{8,4},{12,12},{1,1},{5,9},{9,5},{13,13},{2,2},{6,10},{... | collective-permute-start | bytes 245768 | tf_op jit(solution)/shard_map/ppermute | solution.py:461
  41.7 0.9 %copy-start.5 = (f32[3,16,32,128]{3,2,1,0:T(8,128)}, f32[3,16,32,128]{3,2,1,0:T(8,128)S(1)}, u32[]{:S(2)}) copy-start(f32[3,16,32,128]{3,2,1,0:T(8,128)S(1)} %get-tuple-element.54.refs_0_) | copy-start | bytes 2359300
  42.5 3.7 %collective-permute-start.10 = (f32[32,128]{1,0:T(8,128)S(1)}, f32[32,128]{1,0:T(8,128)S(1)}, u32[]{:S(2)}, u32[]{:S(2)}) collective-permute-start(f32[32,128]{1,0:T(8,128)S(1)} %get-tuple-element.56.refs_0_), channel_id=1, source_target_pairs={{0,2},{2,0},{1,3},{3,1},{4,6},{6,4},{5,7},{7,5},{8,10},{10,8},{9,1... | collective-permute-start | bytes 49160 | tf_op jit(solution)/shard_map/ppermute | solution.py:461
  47.7 0.6 %copy-start.15 = (f32[5,32,128]{2,1,0:T(8,128)}, f32[5,32,128]{2,1,0:T(8,128)S(1)}, u32[]{:S(2)}) copy-start(f32[5,32,128]{2,1,0:T(8,128)S(1)} %get-tuple-element.63) | copy-start | bytes 245764
  48.3 7.0 %collective-permute-start.13 = (f32[16,32,128]{2,1,0:T(8,128)}, f32[16,32,128]{2,1,0:T(8,128)}, u32[]{:S(2)}, u32[]{:S(2)}) collective-permute-start(f32[16,32,128]{2,1,0:T(8,128)} %get-tuple-element.65), channel_id=1, source_target_pairs={{0,1},{1,0},{2,3},{3,2},{4,5},{5,4},{6,7},{7,6},{8,9},{9,8},{10,11... | collective-permute-start | bytes 786440 | tf_op jit(solution)/shard_map/ppermute | solution.py:461
  48.3 7.0 %collective-permute-start.11 = (f32[5,32,128]{2,1,0:T(8,128)}, f32[5,32,128]{2,1,0:T(8,128)S(1)}, u32[]{:S(2)}, u32[]{:S(2)}) collective-permute-start(f32[5,32,128]{2,1,0:T(8,128)} %copy-done.15), channel_id=1, source_target_pairs={{0,4},{4,0},{8,12},{12,8},{1,5},{5,1},{9,13},{13,9},{2,6},{6,2},{1... | collective-permute-start | bytes 245768 | tf_op jit(solution)/shard_map/ppermute | solution.py:461
  52.0 3.3 %collective-permute-start.12 = (f32[5,32,128]{2,1,0:T(8,128)S(1)}, f32[5,32,128]{2,1,0:T(8,128)S(1)}, u32[]{:S(2)}, u32[]{:S(2)}) collective-permute-start(f32[5,32,128]{2,1,0:T(8,128)S(1)} %get-tuple-element.64), channel_id=1, source_target_pairs={{0,0},{4,8},{8,4},{12,12},{1,1},{5,9},{9,5},{13,13},{2,2},{6,10},{... | collective-permute-start | bytes 245768 | tf_op jit(solution)/shard_map/ppermute | solution.py:461
  55.3 1.1 %copy-start.6 = (f32[3,16,32,128]{3,2,1,0:T(8,128)S(1)}, f32[3,16,32,128]{3,2,1,0:T(8,128)}, u32[]{:S(2)}) copy-start(f32[3,16,32,128]{3,2,1,0:T(8,128)} %copy-done.5) | copy-start | bytes 2359300

commit v3 on v2

v3 whole, which is shorter than its diff:
```python
import functools
import math
import types

import jax
import jax.numpy as jnp
from jax import lax
from jax.experimental import pallas as pl
from jax.experimental.pallas import tpu as pltpu
from jax.sharding import PartitionSpec as P

STEPS = 2
CLASSES = 8
ZONES = 4
PATCH = 8

NEAR = 9.0 / 8.0
FAR = -1.0 / 24.0
DT = 0.15

XX, YY, ZZ, XY, XZ, YZ = range(6)

STRESS_TAIL = ((XX, -1), (XY, -2), (XY, -1), (XZ, -2), (XZ, -1))
STRESS_HEAD = ((XX, 0), (XX, 1), (XY, 0), (XZ, 0))
VEL_TAIL = ((0, -2), (0, -1), (1, -1), (2, -1))
VEL_HEAD = ((0, 0), (1, 0), (1, 1), (2, 0), (2, 1))
STRESS_TAIL_Y = ((YY, -1), (XY, -2), (XY, -1), (YZ, -2), (YZ, -1))
STRESS_HEAD_Y = ((YY, 0), (YY, 1), (XY, 0), (YZ, 0))
VEL_TAIL_Y = ((1, -2), (1, -1), (0, -1), (2, -1))
VEL_HEAD_Y = ((1, 0), (0, 0), (0, 1), (2, 0), (2, 1))
STRESS_SLOTS = (XZ, YZ, ZZ)
VEL_SLOTS = (0, 1, 2)


def forward(before, here, after, after_2):
    return NEAR * (after - here) + FAR * (after_2 - before)


def backward(before_2, before, here, after):
    return NEAR * (here - before) + FAR * (after - before_2)


class Edges:
    def __init__(self, rows, depths):
        self.rows = rows
        self.depths = depths
        lane = lax.broadcasted_iota(jnp.int32, (rows, depths), 1)
        row = lax.broadcasted_iota(jnp.int32, (rows, depths), 0)
        self.row = row
        self.deep = lax.axis_index("gz")
        self.low = {1: lane < 1, 2: lane < 2}
        self.high = {1: lane >= depths - 1, 2: lane >= depths - 2}
        self.top = {1: row < 1, 2: row < 2}
        self.bottom = {1: row >= rows - 1, 2: row >= rows - 2}
        self.slots = [self.slot(lane, k) for k in range(3)]

    def slot(self, lane, k):
        first = jnp.where(self.deep == 0, self.depths - 2 - 8 * k, 8 * k)
        return (lane == first) | (lane == first + 1)

    def turn(self, k):
        return jnp.where(self.deep == 0, self.depths - 8 * k, 8 * k)

    def packed(self, fields):
        out = jnp.where(self.slots[0], fields[0], 0.0)
        for k in (1, 2):
            if fields[k] is not None:
                out = jnp.where(self.slots[k], pltpu.roll(fields[k], self.turn(k), 1), out)
        return out

    def ends(self, strip, k):
        return strip if k == 0 else pltpu.roll(strip, self.turn(k), 1)

    def shallower(self, field, halo, n):
        return pltpu.roll(jnp.where(self.high[n], halo, field), n, 1)

    def deeper(self, field, halo, n):
        return pltpu.roll(jnp.where(self.low[n], halo, field), self.depths - n, 1)

    def forward_z(self, field, strip, k):
        halo = self.ends(strip, k)
        return forward(
            self.shallower(field, halo, 1),
            field,
            self.deeper(field, halo, 1),
            self.deeper(field, halo, 2),
        )

    def backward_z(self, field, strip, k):
        halo = self.ends(strip, k)
        return backward(
            self.shallower(field, halo, 2),
            self.shallower(field, halo, 1),
            field,
            self.deeper(field, halo, 1),
        )

    def before(self, field, n, halo):
        moved = jnp.where(self.top[n], 0.0, pltpu.roll(field, n, 0))
        if halo:
            for i in range(n):
                moved = jnp.where(self.row == i, halo[n - 1 - i], moved)
        return moved

    def after(self, field, n, halo):
        moved = jnp.where(self.bottom[n], 0.0, pltpu.roll(field, self.rows - n, 0))
        if halo:
            for i in range(n):
                moved = jnp.where(self.row == self.rows - n + i, halo[i], moved)
        return moved

    def forward_y(self, field, halos):
        lower, upper = halos
        return forward(
            self.before(field, 1, lower),
            field,
            self.after(field, 1, upper),
            self.after(field, 2, upper),
        )

    def backward_y(self, field, halos):
        lower, upper = halos
        return backward(
            self.before(field, 2, lower),
            self.before(field, 1, lower),
            field,
            self.after(field, 1, upper),
        )


class Field:
    def __init__(self, count, *parts):
        self.count = count
        self.parts = parts

    def __call__(self, comp, x):
        if len(self.parts) == 1:
            return self.parts[0][comp, x]
        inner, edge = self.parts
        if x in inside(self.count):
            return inner[comp, x - 2]
        return edge[comp, ends_of(self.count).index(x)]


def inside(count):
    return range(2, count - 2)


def ends_of(count):
    return (0, 1, count - 2, count - 1)


class Planes:
    def __init__(self, field, tail, head, first=None, second=None):
        self.field = field
        self.count = field.count
        self.first, self.second = first, second
        self.tail, self.head = tail, head
        self.even = even_strike()
        self.any_left = lax.axis_index("gx") > 0
        self.any_right = lax.axis_index("gx") < lax.axis_size("gx") - 1

    def left(self, i):
        plane = jnp.where(self.even, self.second[i], self.first[i])
        return jnp.where(self.any_left, plane, 0.0)

    def right(self, i):
        plane = jnp.where(self.even, self.first[i], self.second[i])
        return jnp.where(self.any_right, plane, 0.0)

    def __call__(self, comp, place):
        if place < 0:
            return self.left(self.tail.index((comp, place)))
        if place >= self.count:
            return self.right(self.head.index((comp, place - self.count)))
        return self.field(comp, place)

    def forward_x(self, comp, x):
        return forward(self(comp, x - 1), self(comp, x), self(comp, x + 1), self(comp, x + 2))

    def backward_x(self, comp, x):
        return backward(self(comp, x - 2), self(comp, x - 1), self(comp, x), self(comp, x + 1))


class Bands:
    def __init__(self, lower, upper, tail, head):
        self.lower, self.upper = lower, upper
        self.tail, self.head = tail, head

    def __call__(self, comp, x):
        if self.lower is None:
            return (None, None)
        places = [i for i, (c, _) in enumerate(self.tail) if c == comp]
        before = [self.lower[i, pl.ds(x, 1), :] for i in reversed(places)]
        places = [i for i, (c, _) in enumerate(self.head) if c == comp]
        after = [self.upper[i, pl.ds(x, 1), :] for i in places]
        return (before, after)


def looked_up(labels, table, row, count):
    out = jnp.full(labels.shape, table[row, 0], jnp.float32)
    for k in range(1, count):
        out = jnp.where(labels == k, table[row, k], out)
    return out


def even_strike():
    return lax.axis_index("gx") % 2 == 0


def edge_planes(field, tail, head, first_out, second_out):
    even = even_strike()
    for i in range(first_out.shape[0]):
        comp, place = tail[min(i, len(tail) - 1)]
        right = field(comp, place % field.count)
        comp, place = head[min(i, len(head) - 1)]
        left = field(comp, place % field.count)
        first_out[i] = jnp.where(even, right, left)
        second_out[i] = jnp.where(even, left, right)


def fault_row(rows):
    return jnp.where(lax.axis_index("gy") == lax.axis_size("gy") // 2, 0, rows - 1)


def pack_kernel(r):
    count, rows, depths = r.stress.shape[1:]
    whole = [(comp, 0, count) for comp in STRESS_SLOTS]
    some = {}
    for comp, place in STRESS_TAIL + STRESS_HEAD:
        if comp not in STRESS_SLOTS:
            some.setdefault((comp, place < 0), []).append(place % count)
    some = [(comp, min(at), max(at) + 1) for (comp, _), at in some.items()]
    copies = []
    for i, (comp, start, stop) in enumerate(some + whole):
        span = pl.ds(start, stop - start)
        copy = pltpu.make_async_copy(r.stress.at[comp, span], r.held.at[comp, span], r.sems.at[i])
        copy.start()
        copies.append(copy)
    edges = Edges(rows, depths)
    for copy in copies:
        copy.wait()
    edge_planes(Field(count, r.held), STRESS_TAIL, STRESS_HEAD, r.one_out, r.two_out)
    for x in range(count):
        r.strip_out[x] = edges.packed([r.held[c, x] for c in STRESS_SLOTS])


def velocity_planes(r, xs, edges, planes, write):
    band = Bands(getattr(r, "lower", None), getattr(r, "upper", None), STRESS_TAIL_Y, STRESS_HEAD_Y)
    for x in xs:
        sxy, sxz, syz = planes(XY, x), planes(XZ, x), planes(YZ, x)
        push = DT * looked_up(r.material[x], r.table, 2, CLASSES)
        ends = r.strip[x]
        along_x = (
            planes.forward_x(XX, x)
            + edges.backward_y(sxy, band(XY, x))
            + edges.backward_z(sxz, ends, 0)
        )
        along_y = (
            planes.backward_x(XY, x)
            + edges.forward_y(planes(YY, x), band(YY, x))
            + edges.backward_z(syz, ends, 1)
        )
        along_z = (
            planes.backward_x(XZ, x)
            + edges.backward_y(syz, band(YZ, x))
            + edges.forward_z(planes(ZZ, x), ends, 2)
        )
        rates = (along_x, along_y, along_z)
        write(x, [r.velocity[c, x] + push * rate for c, rate in enumerate(rates)])


def velocity_inner(r):
    count, rows, depths = r.material.shape
    edges = Edges(rows, depths)
    planes = Planes(stress_of(r), STRESS_TAIL, STRESS_HEAD)

    def write(x, new):
        for c in range(3):
            r.inner_out[c, x - 2] = new[c]
        r.strip_inner_out[x - 2] = edges.packed(new)

    velocity_planes(r, inside(count), edges, planes, write)


def velocity_edge(first, r):
    count, rows, depths = r.material.shape
    edges = Edges(rows, depths)
    planes = Planes(stress_of(r), STRESS_TAIL, STRESS_HEAD, r.one, r.two)
    fault = fault_row(rows)
    places = ends_of(count)
    row = pl.ds(fault, 1)
    for x in inside(count):
        r.face_out[pl.ds(x, 1), :] = r.inner[0, x - 2, row, :]
        r.face_out[pl.ds(count + x, 1), :] = r.inner[2, x - 2, row, :]
        r.strip_out[x] = r.strip_inner[x - 2]
    if first:
        for x in range(count):
            labels = r.material[x, row, :]
            r.face_out[pl.ds(2 * count + x, 1), :] = looked_up(labels, r.table, 2, CLASSES)
    if hasattr(r, "prestress"):
        own = r.normal.shape[0]
        place = 3 * count
        for i in range(own):
            r.face_out[pl.ds(place + i, 1), :] = r.prestress[i, pl.ds(0, 1), :]
            r.face_out[pl.ds(place + own + i, 1), :] = r.prestress[i, pl.ds(1, 1), :]
        for i, field in enumerate((r.normal, r.slip, r.zone, r.mask)):
            r.face_out[pl.ds(place + (2 + i) * own, own), :] = field[...].astype(jnp.float32)

    def write(x, new):
        for c in range(3):
            r.edge_out[c, places.index(x)] = new[c]
        r.strip_out[x] = edges.packed(new)

    velocity_planes(r, places, edges, planes, write)
    for x in places:
        r.face_out[pl.ds(x, 1), :] = r.edge_out[0, places.index(x), row, :]
        r.face_out[pl.ds(count + x, 1), :] = r.edge_out[2, places.index(x), row, :]
    new = Field(count, r.inner, r.edge_out)
    edge_planes(new, VEL_TAIL, VEL_HEAD, r.one_out, r.two_out)


def stress_of(r):
    count = r.material.shape[0]
    if hasattr(r, "stress"):
        return Field(count, r.stress)
    return Field(count, r.stress_inner, r.stress_edge)


def memory_of(r):
    count = r.material.shape[0]
    if hasattr(r, "memory"):
        return Field(count, r.memory)
    return Field(count, r.memory_inner, r.memory_edge)


def fault_kernel(first, r):
    own_face, other_face = r.face, r.other
    own_first, other_first = (own_face, other_face) if first else (r.face_first, r.other_first)
    count, rows, depths = r.strip.shape
    middle = lax.axis_size("gy") // 2
    side = lax.axis_index("gy")
    plus = side == middle
    minus = side == middle - 1

    def pair(own, other, place):
        mine, theirs = own[pl.ds(place, count), :], other[pl.ds(place, count), :]
        return jnp.where(plus, theirs, mine), jnp.where(plus, mine, theirs)

    if hasattr(r, "still"):
        still = r.still
    else:
        still = r.still_out
        share = (own_face.shape[0] - 3 * count) // 6
        for i in range(6):
            mine = own_face[pl.ds(3 * count + i * share, share), :]
            theirs = other_face[pl.ds(3 * count + i * share, share), :]
            still[i, pl.ds(0, share), :] = jnp.where(plus, theirs, mine)
            still[i, pl.ds(share, share), :] = jnp.where(plus, mine, theirs)
    pre_x, pre_z, normal = still[0], still[1], still[2]
    slip = still[3] if first else r.slip[...]
    zone, mask = still[4], still[5]

    row = lax.broadcasted_iota(jnp.int32, (count, depths), 0) + lax.axis_index("gx") * count
    deep = lax.broadcasted_iota(jnp.int32, (count, depths), 1) + lax.axis_index("gz") * depths
    inside = (row >= r.anchor[0]) & (row < r.anchor[0] + 2 * PATCH)
    inside = inside & (deep >= r.anchor[1]) & (deep < r.anchor[1] + 2 * PATCH)
    dynamic = 0.4 * looked_up(zone, r.friction, 0, ZONES)
    static = jnp.where(
        inside, dynamic, dynamic + 0.5 * looked_up(zone, r.friction, 1, ZONES)
    )
    distance = 0.2 * looked_up(zone, r.friction, 2, ZONES)
    minus_x, plus_x = pair(own_face, other_face, 0)
    minus_z, plus_z = pair(own_face, other_face, count)
    minus_b, plus_b = pair(own_first, other_first, 2 * count)
    bsum = minus_b + plus_b
    trial_x = (plus_x - minus_x) / (DT * bsum) + pre_x
    trial_z = (plus_z - minus_z) / (DT * bsum) + pre_z
    size = jnp.sqrt(trial_x * trial_x + trial_z * trial_z)
    weaken = jnp.minimum(slip / distance, 1.0)
    strength = (static - (static - dynamic) * weaken) * normal
    factor = jnp.where(mask == 1.0, strength / jnp.maximum(size, strength), 1.0)
    r.slip_out[...] = slip + DT * DT * bsum * (size - size * factor)
    sign = jnp.where(minus, DT, 0.0) * minus_b - jnp.where(plus, DT, 0.0) * plus_b
    change_x = (trial_x * factor - pre_x) * sign
    change_z = (trial_z * factor - pre_z) * sign
    r.change_out[0] = change_x
    r.change_out[1] = change_z

    fault = fault_row(rows)
    on_fault = lax.broadcasted_iota(jnp.int32, (rows, depths), 0) == fault
    even = even_strike()
    still_line = jnp.zeros((1, depths), jnp.float32)

    def line(planes, i):
        comp, place = planes[min(i, len(planes) - 1)]
        return still_line if comp == 1 else r.change_out[comp // 2, pl.ds(place % count, 1), :]

    for i in range(r.one_out.shape[0]):
        right, left = line(VEL_TAIL, i), line(VEL_HEAD, i)
        one, two = jnp.where(even, right, left), jnp.where(even, left, right)
        r.one_out[i] = r.one[i] + jnp.where(on_fault, one, 0.0)
        r.two_out[i] = r.two[i] + jnp.where(on_fault, two, 0.0)
    flat = Edges(count, depths)
    ends = flat.packed([change_x, None, change_z])
    for x in range(count):
        r.strip_out[x] = r.strip[x] + jnp.where(on_fault, ends[x : x + 1, :], 0.0)


def stress_planes(r, xs, edges, planes, write):
    band = Bands(getattr(r, "lower", None), getattr(r, "upper", None), VEL_TAIL_Y, VEL_HEAD_Y)
    stress, memory = stress_of(r), memory_of(r)
    for x in xs:
        vx, vy, vz = planes(0, x), planes(1, x), planes(2, x)
        ends = r.strip[x]
        exx = planes.backward_x(0, x)
        eyy = edges.backward_y(vy, band(1, x))
        ezz = edges.backward_z(vz, ends, 2)
        exy = edges.forward_y(vx, band(0, x)) + planes.forward_x(1, x)
        exz = edges.forward_z(vx, ends, 0) + planes.forward_x(2, x)
        eyz = edges.forward_z(vy, ends, 1) + edges.forward_y(vz, band(2, x))
        labels = r.material[x]
        lame = looked_up(labels, r.table, 0, CLASSES)
        shear = looked_up(labels, r.table, 1, CLASSES)
        decay = jnp.exp(-DT / looked_up(labels, r.table, 3, CLASSES))
        gain = (1.0 - decay) * (0.3 * looked_up(labels, r.table, 4, CLASSES))
        bulk = lame * (exx + eyy + ezz)
        double = 2.0 * shear
        elastic = (
            bulk + double * exx,
            bulk + double * eyy,
            bulk + double * ezz,
            shear * exy,
            shear * exz,
            shear * eyz,
        )
        kept = [decay * memory(c, x) - gain * elastic[c] for c in range(6)]
        new = [stress(c, x) + DT * (elastic[c] + kept[c]) for c in range(6)]
        write(x, new, kept)


def stress_inner(last, r):
    count, rows, depths = r.material.shape
    edges = Edges(rows, depths)
    on_fault = edges.row == fault_row(rows)
    free = Field(count, r.inner, r.edge)
    for x in range(count):
        for c in (0, 2):
            line = r.change[c // 2, pl.ds(x, 1), :]
            r.velocity_out[c, x] = free(c, x) + jnp.where(on_fault, line, 0.0)
        r.velocity_out[1, x] = free(1, x)
    planes = Planes(Field(count, r.velocity_out), VEL_TAIL, VEL_HEAD)

    def write(x, new, kept):
        for c in range(6):
            r.stress_inner_out[c, x - 2] = new[c]
            r.memory_inner_out[c, x - 2] = kept[c]
        if not last:
            r.strip_inner_out[x - 2] = edges.packed([new[c] for c in STRESS_SLOTS])

    stress_planes(r, inside(count), edges, planes, write)


def stress_edge(last, r):
    count, rows, depths = r.material.shape
    edges = Edges(rows, depths)
    planes = Planes(Field(count, r.velocity), VEL_TAIL, VEL_HEAD, r.one, r.two)
    places = ends_of(count)
    copies = []

    def copy_out(source, out, span):
        copy = pltpu.make_async_copy(source, out.at[:, span], r.sems.at[len(copies)])
        copy.start()
        copies.append(copy)

    if last:
        copy_out(r.velocity, r.velocity_out, pl.ds(0, count))
        copy_out(r.new_stress_inner, r.stress_out, pl.ds(2, count - 4))
        copy_out(r.new_memory_inner, r.memory_out, pl.ds(2, count - 4))
        stress_out, memory_out = r.stress_held, r.memory_held
    else:
        stress_out, memory_out = r.stress_edge_out, r.memory_edge_out
        for x in inside(count):
            r.strip_out[x] = r.strip_inner[x - 2]

    def write(x, new, kept):
        for c in range(6):
            stress_out[c, places.index(x)] = new[c]
            memory_out[c, places.index(x)] = kept[c]
        if not last:
            r.strip_out[x] = edges.packed([new[c] for c in STRESS_SLOTS])

    stress_planes(r, places, edges, planes, write)
    if last:
        for held, out in ((stress_out, r.stress_out), (memory_out, r.memory_out)):
            copy_out(held.at[:, pl.ds(0, 2)], out, pl.ds(0, 2))
            copy_out(held.at[:, pl.ds(2, 2)], out, pl.ds(count - 2, 2))
        for copy in copies:
            copy.wait()
    else:
        new = Field(count, r.new_stress_inner, stress_out)
        edge_planes(new, STRESS_TAIL, STRESS_HEAD, r.one_out, r.two_out)


SCALARS = ("table", "friction", "anchor")


def call(kernel, name, ins, outs, scratch=None, apart=(), cost=0, vmem=14):
    scratch = scratch or {}
    names = [*ins, *(f"{key}_out" for key in outs), *scratch]

    def body(*refs):
        kernel(types.SimpleNamespace(**dict(zip(names, refs))))

    def place(key):
        if key in apart:
            return pl.BlockSpec(memory_space=pltpu.HBM)
        return pl.BlockSpec(memory_space=pltpu.SMEM if key in SCALARS else pltpu.VMEM)

    shapes = [jax.ShapeDtypeStruct(shape, jnp.float32) for shape in outs.values()]
    moved = 4 * (sum(a.size for a in ins.values()) + sum(math.prod(o.shape) for o in shapes))
    result = pl.pallas_call(
        body,
        out_shape=shapes,
        in_specs=[place(key) for key in ins],
        out_specs=[place(f"{key}_out") for key in outs],
        scratch_shapes=list(scratch.values()),
        name=name,
        cost_estimate=pl.CostEstimate(flops=cost, bytes_accessed=moved, transcendentals=0),
        compiler_params=pltpu.CompilerParams(vmem_limit_bytes=vmem * 2**20),
    )(*ins.values())
    return dict(zip(outs, result))


def along(axis, count, skip=()):
    up = [(i, i + 1) for i in range(count - 1) if i not in skip]
    return (axis, up), (axis, [(b, a) for a, b in up])


def strike_swaps(count):
    routes = []
    for start in (0, 1):
        partner = list(range(count))
        for i in range(start, count - 1, 2):
            partner[i], partner[i + 1] = i + 1, i
        routes.append(("gx", list(enumerate(partner))))
    return routes


def sent(block, route):
    return lax.ppermute(block, *route)


def whole(parts, name):
    if name in parts:
        return parts[name]
    inner, edge = parts[f"{name}_inner"], parts[f"{name}_edge"]
    return jnp.concatenate([edge[:, :2], inner, edge[:, 2:]], axis=1)


def edge_rows(field, rows):
    count = field.shape[2]
    return jnp.stack([field[c, :, place % count, :] for c, place in rows])


def shards(
    velocity,
    stress,
    memory,
    material,
    material_table,
    fault_mask,
    zone_label,
    patch_anchor,
    friction_table,
    prestress,
    normal_stress,
    slip_path,
):
    _, count, rows, depths = velocity.shape
    sides = lax.axis_size("gy")
    middle = sides // 2
    banded = sides > 2
    cells = count * rows * depths
    swaps = strike_swaps(lax.axis_size("gx"))
    up_y, down_y = along("gy", sides, (middle - 1,))
    across = ("gy", [(middle - 1, middle), (middle, middle - 1)])
    deep = ("gz", [(0, 1), (1, 0)])

    plane = (rows, depths)
    edge_shape = (max(len(STRESS_TAIL), len(STRESS_HEAD)), *plane)
    travelling = {"one": edge_shape, "two": edge_shape, "strip": (count, *plane)}
    inner, edge = (count - 4, *plane), (4, *plane)

    def travelled(packed):
        two = sent(packed["two"], swaps[1])
        one = sent(packed["one"], swaps[0])
        strip = sent(packed["strip"], deep)
        return {"strip": strip}, {"one": one, "two": two}

    def bands(field, tail, head):
        if not banded:
            return {}
        lower, upper = edge_rows(field, tail), edge_rows(field, head)
        return {"lower": sent(lower, up_y), "upper": sent(upper, down_y)}

    if banded:
        still = jnp.stack(
            [
                prestress[:, 0],
                prestress[:, 1],
                normal_stress,
                slip_path,
                zone_label.astype(jnp.float32),
                fault_mask.astype(jnp.float32),
            ]
        )
        still = {"still": lax.all_gather(still, "gy", axis=1, tiled=True)}
    else:
        still = {}

    parts = {"stress": stress, "memory": memory}
    props = {"material": material, "table": material_table}
    packed = call(
        pack_kernel,
        "pack",
        {"stress": stress},
        travelling,
        scratch={"held": pltpu.VMEM(stress.shape, jnp.float32), "sems": pltpu.SemaphoreType.DMA((8,))},
        apart=("stress",),
        vmem=14,
    )
    for step in range(STEPS):
        first, last = step == 0, step == STEPS - 1
        held_stress = {key: parts[key] for key in parts if key.startswith("stress")}
        strip, halos = travelled(packed)
        ins = {"velocity": velocity, **held_stress, **props, **strip}
        if banded:
            ins.update(bands(whole(parts, "stress"), STRESS_TAIL_Y, STRESS_HEAD_Y))
        free = call(
            velocity_inner,
            "velocity_inner",
            ins,
            {"inner": (3, *inner), "strip_inner": inner},
            cost=60 * cells,
        )
        face_rows = 2 * count
        ins = {**ins, **halos, **free}
        if first:
            face_rows += count
            if not banded:
                ins.update(prestress=prestress, normal=normal_stress, slip=slip_path)
                ins.update(zone=zone_label, mask=fault_mask)
                face_rows += 6 * normal_stress.shape[0]
        packed = call(
            functools.partial(velocity_edge, first),
            "velocity_edge",
            ins,
            {"edge": (3, *edge), "face": (face_rows, depths), **travelling},
            cost=20 * cells,
        )
        free = {"inner": free["inner"], "edge": packed["edge"]}
        face = packed["face"]
        other = sent(face, across)
        ins = {key: packed[key] for key in travelling}
        ins.update(face=face, other=other, friction=friction_table, anchor=patch_anchor, **still)
        if first:
            faces = {"face_first": face, "other_first": other}
        else:
            ins.update(slip=slip, **faces)
        outs = {"change": (2, count, depths), "slip": (count, depths), **travelling}
        if not still:
            outs["still"] = (6, count, depths)
        packed = call(functools.partial(fault_kernel, first), "fault", ins, outs)
        slip = packed["slip"]
        if not still:
            still = {"still": packed["still"]}
        strip, halos = travelled(packed)
        ins = {**free, "change": packed["change"], **parts, **props, **strip}
        if banded:
            joined = jnp.concatenate(
                [free["edge"][:, :2], free["inner"], free["edge"][:, 2:]], axis=1
            )
            band = bands(joined, VEL_TAIL_Y, VEL_HEAD_Y)
        else:
            band = {}
        outs = {"velocity": velocity.shape, "stress_inner": (6, *inner), "memory_inner": (6, *inner)}
        if not last:
            outs["strip_inner"] = inner
        done = call(
            functools.partial(stress_inner, last), "stress_inner", {**ins, **band}, outs, cost=100 * cells
        )
        velocity = done["velocity"]
        ins = {"velocity": velocity, **parts, **props, **strip, **halos, **band}
        ins["new_stress_inner"] = done["stress_inner"]
        if last:
            ins["new_memory_inner"] = done["memory_inner"]
            held = pltpu.VMEM((6, *edge), jnp.float32)
            packed = call(
                functools.partial(stress_edge, last),
                "stress_edge",
                ins,
                {"velocity": velocity.shape, "stress": stress.shape, "memory": memory.shape},
                scratch={
                    "stress_held": held,
                    "memory_held": held,
                    "sems": pltpu.SemaphoreType.DMA((7,)),
                },
                apart=("velocity_out", "stress_out", "memory_out"),
            )
            velocity, stress, memory = packed["velocity"], packed["stress"], packed["memory"]
        else:
            ins["strip_inner"] = done["strip_inner"]
            packed = call(
                functools.partial(stress_edge, last),
                "stress_edge",
                ins,
                {"stress_edge": (6, *edge), "memory_edge": (6, *edge), **travelling},
                cost=30 * cells,
            )
            parts = {
                "stress_inner": done["stress_inner"],
                "stress_edge": packed["stress_edge"],
                "memory_inner": done["memory_inner"],
                "memory_edge": packed["memory_edge"],
            }
    side = lax.axis_index("gy")
    if banded:
        held = jnp.where(side == middle, slip, 0.0)
        new_slip = lax.psum_scatter(held, "gy", scatter_dimension=0, tiled=True)
    else:
        share = count // sides
        new_slip = lax.dynamic_slice_in_dim(slip, side * share, share, axis=0)
    return (velocity, stress, memory, new_slip)


def solution(mesh):
    in_specs = (
        P(None, ("ens", "gx"), "gy", "gz"),
        P(None, ("ens", "gx"), "gy", "gz"),
        P(None, ("ens", "gx"), "gy", "gz"),
        P(("ens", "gx"), "gy", "gz"),
        P(None, "ens"),
        P(("ens", "gx", "gy"), "gz"),
        P(("ens", "gx", "gy"), "gz"),
        P("ens"),
        P(None, "ens"),
        P(("ens", "gx", "gy"), None, "gz"),
        P(("ens", "gx", "gy"), "gz"),
        P(("ens", "gx", "gy"), "gz"),
    )
    out_specs = (
        P(None, ("ens", "gx"), "gy", "gz"),
        P(None, ("ens", "gx"), "gy", "gz"),
        P(None, ("ens", "gx"), "gy", "gz"),
        P(("ens", "gx", "gy"), "gz"),
    )
    return jax.shard_map(shards, mesh=mesh, in_specs=in_specs, out_specs=out_specs, check_vma=False)
```

time: 62.7 us -> 51.4 us (0.82)
  waiting for transfers between devices: 13.8 us -> 4.89 us
  starting transfers between devices: 21.7 us -> 19.3 us
    ppermute x14, waiting for transfers between devices: 13.8 us -> 4.89 us  [sent(): return lax.ppermute(block, *route)]
    ppermute x14, starting transfers between devices: 21.7 us -> 19.3 us  [sent(): return lax.ppermute(block, *route)]
    pallas_call x7 -> x11, Pallas kernels: 20.8 us -> 21.1 us  [call(): pl.pallas_call(body, out_shape=shapes, in_specs=[place(key) for key in in...]
    unnamed x32 -> x36, local copies, waits for them, and re-layouts: 4.09 us -> 4.12 us
  transfers between devices with their start and end apart: 14 -> 14, of which waited for: 6 -> 2; matrix products, arithmetic and copies ran while one was open for 1% -> 1% of each run, Pallas kernels for 0% -> 24%
where the time goes in v3:
time: 51.4 us; the launch traced here: 51 us
  Pallas kernels  21.1 us (41%)
  starting transfers between devices  19.3 us (38%)
  waiting for transfers between devices  4.89 us (10%)
  local copies, waits for them, and re-layouts  4.72 us (9%)
  between operations  0.97 us (2%)
    pallas_call x11, Pallas kernels, call(): pl.pallas_call(body, out_shape=shapes, in_specs=[place(key) for key in in...  21.1 us
    ppermute x14, starting transfers between devices, sent(): return lax.ppermute(block, *route)  19.3 us
    ppermute x14, waiting for transfers between devices, sent(): return lax.ppermute(block, *route)  4.89 us
    unnamed x36, local copies, waits for them, and re-layouts  4.12 us
  transfers between devices with their start and end apart: 14, of which 2 were waited for; matrix products, arithmetic and copies ran while one was open for 1% of the time, Pallas kernels for 24%

profile of v3, /device:TPU:0, one launch (start us, length us, event | category | flops | bytes accessed | tf_op | source)
XLA Modules:
  0.0 51.0 jit_solution(10380226512170353522)
XLA Ops:
  0.6 1.4 %copy-done = f32[6,16,32,128]{3,2,1,0:T(8,128)S(1)} copy-done((f32[6,16,32,128]{3,2,1,0:T(8,128)S(1)}, f32[6,16,32,128]{3,2,1,0:T(8,128)}, u32[]{:S(2)}) %copy-start) | copy-done | bytes 1572888
  2.0 0.5 pack.1
  2.5 0.0 copy-start.12
  2.6 0.5 %collective-permute-start = (f32[16,32,128]{2,1,0:T(8,128)S(1)}, f32[16,32,128]{2,1,0:T(8,128)S(1)}, u32[]{:S(2)}, u32[]{:S(2)}) collective-permute-start(f32[16,32,128]{2,1,0:T(8,128)S(1)} %get-tuple-element.47), channel_id=1, source_target_pairs={{0,1},{1,0},{2,3},{3,2},{4,5},{5,4},{6,7},{7,6},{8,9},{9,8},{10,11... | collective-permute-start | bytes 786440 | tf_op jit(solution)/shard_map/ppermute | solution.py:551
  3.1 2.6 %collective-permute-start.1 = (f32[5,32,128]{2,1,0:T(8,128)S(1)}, f32[5,32,128]{2,1,0:T(8,128)S(1)}, u32[]{:S(2)}, u32[]{:S(2)}) collective-permute-start(f32[5,32,128]{2,1,0:T(8,128)S(1)} %get-tuple-element.49), channel_id=1, source_target_pairs={{0,4},{4,0},{8,12},{12,8},{1,5},{5,1},{9,13},{13,9},{2,6},{6,2},{1... | collective-permute-start | bytes 245768 | tf_op jit(solution)/shard_map/ppermute | solution.py:551
  5.8 0.7 %collective-permute-start.2 = (f32[5,32,128]{2,1,0:T(8,128)S(1)}, f32[5,32,128]{2,1,0:T(8,128)S(1)}, u32[]{:S(2)}, u32[]{:S(2)}) collective-permute-start(f32[5,32,128]{2,1,0:T(8,128)S(1)} %get-tuple-element.50), channel_id=1, source_target_pairs={{0,0},{4,8},{8,4},{12,12},{1,1},{5,9},{9,5},{13,13},{2,2},{6,10},{... | collective-permute-start | bytes 245768 | tf_op jit(solution)/shard_map/ppermute | solution.py:551
  6.5 3.0 %velocity_inner.2 = (f32[3,12,32,128]{3,2,1,0:T(8,128)S(1)}, f32[12,32,128]{2,1,0:T(8,128)S(1)}) custom-call(f32[3,16,32,128]{3,2,1,0:T(8,128)S(1)} %copy-done.4, f32[6,16,32,128]{3,2,1,0:T(8,128)S(1)} %copy-done, s32[16,32,128]{2,1,0:T(8,128)S(1)} %copy-done.2, f32[5,8]{1,0:T(8,128)S(1)} %copy-done.7, f32[16,32,128]{2,1,0:T(8,128)S(1)} %collective-permute-done.refs_4_), custom_call_target="tpu_custom_call" | custom-call | flops 3932160 | bytes 3670176 | tf_op jit(solution)/shard_map/velocity_inner/pallas_call | solution.py:522
  9.6 1.1 %velocity_edge.2 = (f32[3,4,32,128]{3,2,1,0:T(8,128)S(1)}, f32[96,128]{1,0:T(8,128)S(1)}, f32[5,32,128]{2,1,0:T(8,128)S(1)}, f32[5,32,128]{2,1,0:T(8,128)S(1)}, f32[16,32,128]{2,1,0:T(8,128)S(1)}) custom-call(f32[3,16,32,128]{3,2,1,0:T(8,128)S(1)} %copy-done.4, f32[6,16,32,128]{3,2,1,0:T(8,128)S(1)} %copy-done, s32[16,32,128]{2,1,0:T(8,128)S(1)} %copy-done.2, ...), custom_call_target="tpu_custom_call" | custom-call | flops 1310720 | bytes 4530336 | tf_op jit(solution)/shard_map/velocity_edge/pallas_call | solution.py:522
  10.6 1.6 %collective-permute-start.3 = (f32[96,128]{1,0:T(8,128)S(1)}, f32[96,128]{1,0:T(8,128)S(1)}, u32[]{:S(2)}, u32[]{:S(2)}) collective-permute-start(f32[96,128]{1,0:T(8,128)S(1)} %get-tuple-element.56.refs_3_.refs_9_), channel_id=1, source_target_pairs={{0,2},{2,0},{1,3},{3,1},{4,6},{6,4},{5,7},{7,5},{8,10},{10,8},{9,1... | collective-permute-start | bytes 147464 | tf_op jit(solution)/shard_map/ppermute | solution.py:551
  12.2 2.6 %collective-permute-done.3.refs_4_.refs_10_ = f32[96,128]{1,0:T(8,128)S(1)} collective-permute-done((f32[96,128]{1,0:T(8,128)S(1)}, f32[96,128]{1,0:T(8,128)S(1)}, u32[]{:S(2)}, u32[]{:S(2)}) %collective-permute-start.3) | collective-permute-done | bytes 49184 | tf_op jit(solution)/shard_map/ppermute | solution.py:551
  14.8 0.7 %fault.2 = (f32[2,16,128]{2,1,0:T(8,128)S(1)}, f32[16,128]{1,0:T(8,128)S(1)}, f32[5,32,128]{2,1,0:T(8,128)S(1)}, f32[5,32,128]{2,1,0:T(8,128)S(1)}, f32[16,32,12...) custom-call(f32[5,32,128]{2,1,0:T(8,128)S(1)} %get-tuple-element.53.refs_0_, f32[5,32,128]{2,1,0:T(8,128)S(1)} %get-tuple-element.54.refs_1_, ...), custom_call_target="tpu_custom_call" | custom-call | bytes 1024056 | tf_op jit(solution)/shard_map/fault/pallas_call | solution.py:522
  15.5 0.1 collective-permute-start.4
  15.6 4.5 %collective-permute-start.5 = (f32[5,32,128]{2,1,0:T(8,128)S(1)}, f32[5,32,128]{2,1,0:T(8,128)S(1)}, u32[]{:S(2)}, u32[]{:S(2)}) collective-permute-start(f32[5,32,128]{2,1,0:T(8,128)S(1)} %get-tuple-element.61), channel_id=1, source_target_pairs={{0,4},{4,0},{8,12},{12,8},{1,5},{5,1},{9,13},{13,9},{2,6},{6,2},{1... | collective-permute-start | bytes 245768 | tf_op jit(solution)/shard_map/ppermute | solution.py:551
  20.0 0.7 %collective-permute-start.6 = (f32[5,32,128]{2,1,0:T(8,128)S(1)}, f32[5,32,128]{2,1,0:T(8,128)S(1)}, u32[]{:S(2)}, u32[]{:S(2)}) collective-permute-start(f32[5,32,128]{2,1,0:T(8,128)S(1)} %get-tuple-element.62), channel_id=1, source_target_pairs={{0,0},{4,8},{8,4},{12,12},{1,1},{5,9},{9,5},{13,13},{2,2},{6,10},{... | collective-permute-start | bytes 245768 | tf_op jit(solution)/shard_map/ppermute | solution.py:551
  20.7 3.2 %stress_inner.2 = (f32[3,16,32,128]{3,2,1,0:T(8,128)S(1)}, f32[6,12,32,128]{3,2,1,0:T(8,128)S(1)}, f32[6,12,32,128]{3,2,1,0:T(8,128)S(1)}, f32[12,32,128]{2,1,0:T(8,128)S(1)}) custom-call(f32[3,12,32,128]{3,2,1,0:T(8,128)S(1)} %get-tuple-element.48.refs_7_.refs_0_, f32[3,4,32,128]{3,2,1,0:T(8,128)S(1)} %get-tuple-element.52.refs_1_, ...), custom_call_target="tpu_custom_call" | custom-call | flops 6553600 | bytes 7815328 | tf_op jit(solution)/shard_map/stress_inner/pallas_call | solution.py:522
  24.0 1.1 %stress_edge.2 = (f32[6,4,32,128]{3,2,1,0:T(8,128)S(1)}, f32[6,4,32,128]{3,2,1,0:T(8,128)S(1)}, f32[5,32,128]{2,1,0:T(8,128)S(1)}, f32[5,32,128]{2,1,0:T(8,128)S(1)}, f32[16,32,128]{2,1,0:T(8,128)S(1)}) custom-call(f32[3,16,32,128]{3,2,1,0:T(8,128)S(1)} %get-tuple-element.59.refs_0_, f32[6,16,32,128]{3,2,1,0:T(8,128)S(1)} %copy-done.1, ...), custom_call_target="tpu_custom_call" | custom-call | flops 1966080 | bytes 7209120 | tf_op jit(solution)/shard_map/stress_edge/pallas_call | solution.py:522
  25.1 0.2 collective-permute-start.7
  25.3 2.7 %collective-permute-start.8 = (f32[5,32,128]{2,1,0:T(8,128)S(1)}, f32[5,32,128]{2,1,0:T(8,128)S(1)}, u32[]{:S(2)}, u32[]{:S(2)}) collective-permute-start(f32[5,32,128]{2,1,0:T(8,128)S(1)} %get-tuple-element.67), channel_id=1, source_target_pairs={{0,4},{4,0},{8,12},{12,8},{1,5},{5,1},{9,13},{13,9},{2,6},{6,2},{1... | collective-permute-start | bytes 245768 | tf_op jit(solution)/shard_map/ppermute | solution.py:551
  28.0 0.7 %collective-permute-start.9 = (f32[5,32,128]{2,1,0:T(8,128)S(1)}, f32[5,32,128]{2,1,0:T(8,128)S(1)}, u32[]{:S(2)}, u32[]{:S(2)}) collective-permute-start(f32[5,32,128]{2,1,0:T(8,128)S(1)} %get-tuple-element.68), channel_id=1, source_target_pairs={{0,0},{4,8},{8,4},{12,12},{1,1},{5,9},{9,5},{13,13},{2,2},{6,10},{... | collective-permute-start | bytes 245768 | tf_op jit(solution)/shard_map/ppermute | solution.py:551
  28.7 3.0 %velocity_inner.3 = (f32[3,12,32,128]{3,2,1,0:T(8,128)S(1)}, f32[12,32,128]{2,1,0:T(8,128)S(1)}) custom-call(f32[3,16,32,128]{3,2,1,0:T(8,128)S(1)} %get-tuple-element.59.refs_0_, f32[6,12,32,128]{3,2,1,0:T(8,128)S(1)} %get-tuple-element.60.refs_8_.refs_1_.refs_3_, f32[6,4,32,128]{3,2,1,0:T(8,128)S(1)} %get-tuple-element.64.refs_2_.refs_4_, ...), custom_call_target="tpu_custom_call" | custom-call | flops 3932160 | bytes 3670176 | tf_op jit(solution)/shard_map/velocity_inner/pallas_call | solution.py:522
  31.7 1.0 %velocity_edge.3 = (f32[3,4,32,128]{3,2,1,0:T(8,128)S(1)}, f32[32,128]{1,0:T(8,128)S(1)}, f32[5,32,128]{2,1,0:T(8,128)S(1)}, f32[5,32,128]{2,1,0:T(8,128)S(1)}, f32[16,32,128]{2,1,0:T(8,128)S(1)}) custom-call(f32[3,16,32,128]{3,2,1,0:T(8,128)S(1)} %get-tuple-element.59.refs_0_, f32[6,12,32,128]{3,2,1,0:T(8,128)S(1)} %get-tuple-element.60.refs_8_.refs_1_.refs_3_, ...), custom_call_target="tpu_custom_call" | custom-call | flops 1310720 | bytes 4472992 | tf_op jit(solution)/shard_map/velocity_edge/pallas_call | solution.py:522
  32.7 1.5 %collective-permute-start.10 = (f32[32,128]{1,0:T(8,128)S(1)}, f32[32,128]{1,0:T(8,128)S(1)}, u32[]{:S(2)}, u32[]{:S(2)}) collective-permute-start(f32[32,128]{1,0:T(8,128)S(1)} %get-tuple-element.74.refs_3_), channel_id=1, source_target_pairs={{0,2},{2,0},{1,3},{3,1},{4,6},{6,4},{5,7},{7,5},{8,10},{10,8},{9,1... | collective-permute-start | bytes 49160 | tf_op jit(solution)/shard_map/ppermute | solution.py:551
  34.3 2.3 %collective-permute-done.10.refs_4_ = f32[32,128]{1,0:T(8,128)S(1)} collective-permute-done((f32[32,128]{1,0:T(8,128)S(1)}, f32[32,128]{1,0:T(8,128)S(1)}, u32[]{:S(2)}, u32[]{:S(2)}) %collective-permute-start.10) | collective-permute-done | bytes 16416 | tf_op jit(solution)/shard_map/ppermute | solution.py:551
  36.5 1.4 %fault.3 = (f32[2,16,128]{2,1,0:T(8,128)S(1)}, f32[16,128]{1,0:T(8,128)S(1)}, f32[5,32,128]{2,1,0:T(8,128)S(1)}, f32[5,32,128]{2,1,0:T(8,128)S(1)}, f32[16,32,128]{2,1,0:T(8,128)}) custom-call(f32[5,32,128]{2,1,0:T(8,128)S(1)} %get-tuple-element.71.refs_0_, f32[5,32,128]{2,1,0:T(8,128)S(1)} %get-tuple-element.72.refs_1_, ...), custom_call_target="tpu_custom_call" | custom-call | bytes 1065016 | tf_op jit(solution)/shard_map/fault/pallas_call | solution.py:522
  38.0 0.6 %copy-done.17 = f32[5,32,128]{2,1,0:T(8,128)} copy-done((f32[5,32,128]{2,1,0:T(8,128)}, f32[5,32,128]{2,1,0:T(8,128)S(1)}, u32[]{:S(2)}) %copy-start.17) | copy-done | bytes 81944
  38.6 3.0 %collective-permute-start.12 = (f32[5,32,128]{2,1,0:T(8,128)}, f32[5,32,128]{2,1,0:T(8,128)S(1)}, u32[]{:S(2)}, u32[]{:S(2)}) collective-permute-start(f32[5,32,128]{2,1,0:T(8,128)} %copy-done.17), channel_id=1, source_target_pairs={{0,4},{4,0},{8,12},{12,8},{1,5},{5,1},{9,13},{13,9},{2,6},{6,2},{1... | collective-permute-start | bytes 245768 | tf_op jit(solution)/shard_map/ppermute | solution.py:551
  41.6 0.7 %collective-permute-start.13 = (f32[5,32,128]{2,1,0:T(8,128)S(1)}, f32[5,32,128]{2,1,0:T(8,128)S(1)}, u32[]{:S(2)}, u32[]{:S(2)}) collective-permute-start(f32[5,32,128]{2,1,0:T(8,128)S(1)} %get-tuple-element.83), channel_id=1, source_target_pairs={{0,0},{4,8},{8,4},{12,12},{1,1},{5,9},{9,5},{13,13},{2,2},{6,10},{... | collective-permute-start | bytes 245768 | tf_op jit(solution)/shard_map/ppermute | solution.py:551
  42.2 0.6 %constant_dynamic-slice_fusion = f32[8,128]{1,0:T(8,128)} fusion(f32[16,128]{1,0:T(8,128)S(1)} %get-tuple-element.89, s32[]{:T(128)S(6)} %select_n.3), kind=kLoop, calls=%fused_computation | loop fusion | bytes 8196 | tf_op jit(solution)/shard_map/dynamic_slice | solution.py:733
  42.9 1.1 %copy-done.6 = f32[3,12,32,128]{3,2,1,0:T(8,128)S(1)} copy-done((f32[3,12,32,128]{3,2,1,0:T(8,128)S(1)}, f32[3,12,32,128]{3,2,1,0:T(8,128)}, u32[]{:S(2)}) %copy-start.6) | copy-done | bytes 589848
  43.9 0.9 %copy-done.9 = f32[3,4,32,128]{3,2,1,0:T(8,128)S(1)} copy-done((f32[3,4,32,128]{3,2,1,0:T(8,128)S(1)}, f32[3,4,32,128]{3,2,1,0:T(8,128)}, u32[]{:S(2)}) %copy-start.9) | copy-done | bytes 196632
  44.8 2.9 %stress_inner.3 = (f32[3,16,32,128]{3,2,1,0:T(8,128)S(1)}, f32[6,12,32,128]{3,2,1,0:T(8,128)S(1)}, f32[6,12,32,128]{3,2,1,0:T(8,128)S(1)}) custom-call(f32[3,12,32,128]{3,2,1,0:T(8,128)S(1)} %copy-done.6, f32[3,4,32,128]{3,2,1,0:T(8,128)S(1)} %copy-done.9, f32[2,16,128]{2,1,0:T(8,128)S(1)} %get-tuple-element.77.refs_2_, ...), custom_call_target="tpu_custom_call" | custom-call | flops 6553600 | bytes 7618720 | tf_op jit(solution)/shard_map/stress_inner/pallas_call | solution.py:522
  47.7 3.3 %stress_edge.3 = (f32[3,16,32,128]{3,2,1,0:T(8,128)}, f32[6,16,32,128]{3,2,1,0:T(8,128)}, f32[6,16,32,128]{3,2,1,0:T(8,128)}) custom-call(f32[3,16,32,128]{3,2,1,0:T(8,128)S(1)} %get-tuple-element.81.refs_0_, f32[6,12,32,128]{3,2,1,0:T(8,128)S(1)} %get-tuple-element.60.refs_8_.refs_1_.refs_3_, f32[6,4,32,128]{3,2,1,0:T(8,128)S(1)} %get-tuple-element.64.refs_2_.refs_4_, ...), custom_call_target="tpu_custom_call" | custom-call | bytes 10911904 | tf_op jit(solution)/shard_map/stress_edge/pallas_call | solution.py:522
  (44 shorter events, 0.1 us)
Async XLA Ops:
  0.6 1.4 %copy-start = (f32[6,16,32,128]{3,2,1,0:T(8,128)S(1)}, f32[6,16,32,128]{3,2,1,0:T(8,128)}, u32[]{:S(2)}) copy-start(f32[6,16,32,128]{3,2,1,0:T(8,128)} %refs_1_.5) | copy-start | bytes 4718596
  2.0 4.4 %copy-start.2 = (s32[16,32,128]{2,1,0:T(8,128)S(1)}, s32[16,32,128]{2,1,0:T(8,128)}, u32[]{:S(2)}) copy-start(s32[16,32,128]{2,1,0:T(8,128)} %refs_5_.7) | copy-start | bytes 786436
  2.0 4.4 %copy-start.4 = (f32[3,16,32,128]{3,2,1,0:T(8,128)S(1)}, f32[3,16,32,128]{3,2,1,0:T(8,128)}, u32[]{:S(2)}) copy-start(f32[3,16,32,128]{3,2,1,0:T(8,128)} %refs_0_.5) | copy-start | bytes 2359300
  2.0 4.4 %copy-start.7 = (f32[5,8]{1,0:T(8,128)S(1)}, f32[5,8]{1,0:T(8,128)}, u32[]{:S(2)}) copy-start(f32[5,8]{1,0:T(8,128)} %refs_6_.7) | copy-start | bytes 484
  2.5 6.9 %copy-start.10 = (f32[8,2,128]{2,1,0:T(2,128)S(1)}, f32[8,2,128]{2,1,0:T(2,128)}, u32[]{:S(2)}) copy-start(f32[8,2,128]{2,1,0:T(2,128)} %refs_9_.1) | copy-start | bytes 24580
  2.5 6.9 %copy-start.12 = (f32[8,128]{1,0:T(8,128)S(1)}, f32[8,128]{1,0:T(8,128)}, u32[]{:S(2)}) copy-start(f32[8,128]{1,0:T(8,128)} %refs_10_.1) | copy-start | bytes 12292
  2.6 6.9 %copy-start.13 = (f32[8,128]{1,0:T(8,128)S(1)}, f32[8,128]{1,0:T(8,128)}, u32[]{:S(2)}) copy-start(f32[8,128]{1,0:T(8,128)} %refs_11_.1) | copy-start | bytes 12292
  2.6 6.9 %copy-start.14 = (s32[8,128]{1,0:T(8,128)S(1)}, s32[8,128]{1,0:T(8,128)}, u32[]{:S(2)}) copy-start(s32[8,128]{1,0:T(8,128)} %refs_12_.1) | copy-start | bytes 12292
  2.6 6.9 %copy-start.15 = (s32[8,128]{1,0:T(8,128)S(1)}, s32[8,128]{1,0:T(8,128)}, u32[]{:S(2)}) copy-start(s32[8,128]{1,0:T(8,128)} %refs_13_.1) | copy-start | bytes 12292
  2.6 3.8 %collective-permute-start = (f32[16,32,128]{2,1,0:T(8,128)S(1)}, f32[16,32,128]{2,1,0:T(8,128)S(1)}, u32[]{:S(2)}, u32[]{:S(2)}) collective-permute-start(f32[16,32,128]{2,1,0:T(8,128)S(1)} %get-tuple-element.47), channel_id=1, source_target_pairs={{0,1},{1,0},{2,3},{3,2},{4,5},{5,4},{6,7},{7,6},{8,9},{9,8},{10,11... | collective-permute-start | bytes 786440 | tf_op jit(solution)/shard_map/ppermute | solution.py:551
  3.1 6.3 %collective-permute-start.1 = (f32[5,32,128]{2,1,0:T(8,128)S(1)}, f32[5,32,128]{2,1,0:T(8,128)S(1)}, u32[]{:S(2)}, u32[]{:S(2)}) collective-permute-start(f32[5,32,128]{2,1,0:T(8,128)S(1)} %get-tuple-element.49), channel_id=1, source_target_pairs={{0,4},{4,0},{8,12},{12,8},{1,5},{5,1},{9,13},{13,9},{2,6},{6,2},{1... | collective-permute-start | bytes 245768 | tf_op jit(solution)/shard_map/ppermute | solution.py:551
  5.8 3.7 %collective-permute-start.2 = (f32[5,32,128]{2,1,0:T(8,128)S(1)}, f32[5,32,128]{2,1,0:T(8,128)S(1)}, u32[]{:S(2)}, u32[]{:S(2)}) collective-permute-start(f32[5,32,128]{2,1,0:T(8,128)S(1)} %get-tuple-element.50), channel_id=1, source_target_pairs={{0,0},{4,8},{8,4},{12,12},{1,1},{5,9},{9,5},{13,13},{2,2},{6,10},{... | collective-permute-start | bytes 245768 | tf_op jit(solution)/shard_map/ppermute | solution.py:551
  9.5 5.3 %copy-start.11 = (f32[3,4]{1,0:T(4,128)S(1)}, f32[3,4]{1,0:T(4,128)}, u32[]{:S(2)}) copy-start(f32[3,4]{1,0:T(4,128)} %refs_5_.6) | copy-start | bytes 148
  9.5 5.2 %copy-start.16 = (s32[2]{0:T(128)S(1)}, s32[2]{0:T(128)}, u32[]{:S(2)}) copy-start(s32[2]{0:T(128)} %refs_6_.6) | copy-start | bytes 28
  9.6 11.2 %copy-start.1 = (f32[6,16,32,128]{3,2,1,0:T(8,128)S(1)}, f32[6,16,32,128]{3,2,1,0:T(8,128)}, u32[]{:S(2)}) copy-start(f32[6,16,32,128]{3,2,1,0:T(8,128)} %refs_1_.5) | copy-start | bytes 4718596
  9.6 11.2 %copy-start.3 = (f32[6,16,32,128]{3,2,1,0:T(8,128)S(1)}, f32[6,16,32,128]{3,2,1,0:T(8,128)}, u32[]{:S(2)}) copy-start(f32[6,16,32,128]{3,2,1,0:T(8,128)} %refs_2_.5) | copy-start | bytes 4718596
  10.6 4.2 %collective-permute-start.3 = (f32[96,128]{1,0:T(8,128)S(1)}, f32[96,128]{1,0:T(8,128)S(1)}, u32[]{:S(2)}, u32[]{:S(2)}) collective-permute-start(f32[96,128]{1,0:T(8,128)S(1)} %get-tuple-element.56.refs_3_.refs_9_), channel_id=1, source_target_pairs={{0,2},{2,0},{1,3},{3,1},{4,6},{6,4},{5,7},{7,5},{8,10},{10,8},{9,1... | collective-permute-start | bytes 147464 | tf_op jit(solution)/shard_map/ppermute | solution.py:551
  15.5 5.2 %collective-permute-start.4 = (f32[16,32,128]{2,1,0:T(8,128)S(1)}, f32[16,32,128]{2,1,0:T(8,128)S(1)}, u32[]{:S(2)}, u32[]{:S(2)}) collective-permute-start(f32[16,32,128]{2,1,0:T(8,128)S(1)} %get-tuple-element.58), channel_id=1, source_target_pairs={{0,1},{1,0},{2,3},{3,2},{4,5},{5,4},{6,7},{7,6},{8,9},{9,8},{10,11... | collective-permute-start | bytes 786440 | tf_op jit(solution)/shard_map/ppermute | solution.py:551
  15.6 8.4 %collective-permute-start.5 = (f32[5,32,128]{2,1,0:T(8,128)S(1)}, f32[5,32,128]{2,1,0:T(8,128)S(1)}, u32[]{:S(2)}, u32[]{:S(2)}) collective-permute-start(f32[5,32,128]{2,1,0:T(8,128)S(1)} %get-tuple-element.61), channel_id=1, source_target_pairs={{0,4},{4,0},{8,12},{12,8},{1,5},{5,1},{9,13},{13,9},{2,6},{6,2},{1... | collective-permute-start | bytes 245768 | tf_op jit(solution)/shard_map/ppermute | solution.py:551
  20.0 3.9 %collective-permute-start.6 = (f32[5,32,128]{2,1,0:T(8,128)S(1)}, f32[5,32,128]{2,1,0:T(8,128)S(1)}, u32[]{:S(2)}, u32[]{:S(2)}) collective-permute-start(f32[5,32,128]{2,1,0:T(8,128)S(1)} %get-tuple-element.62), channel_id=1, source_target_pairs={{0,0},{4,8},{8,4},{12,12},{1,1},{5,9},{9,5},{13,13},{2,2},{6,10},{... | collective-permute-start | bytes 245768 | tf_op jit(solution)/shard_map/ppermute | solution.py:551
  25.1 3.6 %collective-permute-start.7 = (f32[16,32,128]{2,1,0:T(8,128)S(1)}, f32[16,32,128]{2,1,0:T(8,128)S(1)}, u32[]{:S(2)}, u32[]{:S(2)}) collective-permute-start(f32[16,32,128]{2,1,0:T(8,128)S(1)} %get-tuple-element.65), channel_id=1, source_target_pairs={{0,1},{1,0},{2,3},{3,2},{4,5},{5,4},{6,7},{7,6},{8,9},{9,8},{10,11... | collective-permute-start | bytes 786440 | tf_op jit(solution)/shard_map/ppermute | solution.py:551
  25.3 6.4 %collective-permute-start.8 = (f32[5,32,128]{2,1,0:T(8,128)S(1)}, f32[5,32,128]{2,1,0:T(8,128)S(1)}, u32[]{:S(2)}, u32[]{:S(2)}) collective-permute-start(f32[5,32,128]{2,1,0:T(8,128)S(1)} %get-tuple-element.67), channel_id=1, source_target_pairs={{0,4},{4,0},{8,12},{12,8},{1,5},{5,1},{9,13},{13,9},{2,6},{6,2},{1... | collective-permute-start | bytes 245768 | tf_op jit(solution)/shard_map/ppermute | solution.py:551
  28.0 3.7 %collective-permute-start.9 = (f32[5,32,128]{2,1,0:T(8,128)S(1)}, f32[5,32,128]{2,1,0:T(8,128)S(1)}, u32[]{:S(2)}, u32[]{:S(2)}) collective-permute-start(f32[5,32,128]{2,1,0:T(8,128)S(1)} %get-tuple-element.68), channel_id=1, source_target_pairs={{0,0},{4,8},{8,4},{12,12},{1,1},{5,9},{9,5},{13,13},{2,2},{6,10},{... | collective-permute-start | bytes 245768 | tf_op jit(solution)/shard_map/ppermute | solution.py:551
  31.7 1.1 %copy-start.5 = (f32[3,12,32,128]{3,2,1,0:T(8,128)}, f32[3,12,32,128]{3,2,1,0:T(8,128)S(1)}, u32[]{:S(2)}) copy-start(f32[3,12,32,128]{3,2,1,0:T(8,128)S(1)} %get-tuple-element.66.refs_8_.refs_0_) | copy-start | bytes 1769476
  32.7 5.2 %copy-start.8 = (f32[3,4,32,128]{3,2,1,0:T(8,128)}, f32[3,4,32,128]{3,2,1,0:T(8,128)S(1)}, u32[]{:S(2)}) copy-start(f32[3,4,32,128]{3,2,1,0:T(8,128)S(1)} %get-tuple-element.70.refs_1_) | copy-start | bytes 589828
  32.7 3.8 %collective-permute-start.10 = (f32[32,128]{1,0:T(8,128)S(1)}, f32[32,128]{1,0:T(8,128)S(1)}, u32[]{:S(2)}, u32[]{:S(2)}) collective-permute-start(f32[32,128]{1,0:T(8,128)S(1)} %get-tuple-element.74.refs_3_), channel_id=1, source_target_pairs={{0,2},{2,0},{1,3},{3,1},{4,6},{6,4},{5,7},{7,5},{8,10},{10,8},{9,1... | collective-permute-start | bytes 49160 | tf_op jit(solution)/shard_map/ppermute | solution.py:551
  38.0 0.7 %copy-start.17 = (f32[5,32,128]{2,1,0:T(8,128)}, f32[5,32,128]{2,1,0:T(8,128)S(1)}, u32[]{:S(2)}) copy-start(f32[5,32,128]{2,1,0:T(8,128)S(1)} %get-tuple-element.82) | copy-start | bytes 245764
  38.6 4.2 %collective-permute-start.11 = (f32[16,32,128]{2,1,0:T(8,128)}, f32[16,32,128]{2,1,0:T(8,128)}, u32[]{:S(2)}, u32[]{:S(2)}) collective-permute-start(f32[16,32,128]{2,1,0:T(8,128)} %get-tuple-element.80), channel_id=1, source_target_pairs={{0,1},{1,0},{2,3},{3,2},{4,5},{5,4},{6,7},{7,6},{8,9},{9,8},{10,11... | collective-permute-start | bytes 786440 | tf_op jit(solution)/shard_map/ppermute | solution.py:551
  38.6 9.1 %collective-permute-start.12 = (f32[5,32,128]{2,1,0:T(8,128)}, f32[5,32,128]{2,1,0:T(8,128)S(1)}, u32[]{:S(2)}, u32[]{:S(2)}) collective-permute-start(f32[5,32,128]{2,1,0:T(8,128)} %copy-done.17), channel_id=1, source_target_pairs={{0,4},{4,0},{8,12},{12,8},{1,5},{5,1},{9,13},{13,9},{2,6},{6,2},{1... | collective-permute-start | bytes 245768 | tf_op jit(solution)/shard_map/ppermute | solution.py:551
  41.6 6.1 %collective-permute-start.13 = (f32[5,32,128]{2,1,0:T(8,128)S(1)}, f32[5,32,128]{2,1,0:T(8,128)S(1)}, u32[]{:S(2)}, u32[]{:S(2)}) collective-permute-start(f32[5,32,128]{2,1,0:T(8,128)S(1)} %get-tuple-element.83), channel_id=1, source_target_pairs={{0,0},{4,8},{8,4},{12,12},{1,1},{5,9},{9,5},{13,13},{2,2},{6,10},{... | collective-permute-start | bytes 245768 | tf_op jit(solution)/shard_map/ppermute | solution.py:551
  42.9 1.1 %copy-start.6 = (f32[3,12,32,128]{3,2,1,0:T(8,128)S(1)}, f32[3,12,32,128]{3,2,1,0:T(8,128)}, u32[]{:S(2)}) copy-start(f32[3,12,32,128]{3,2,1,0:T(8,128)} %copy-done.5) | copy-start | bytes 1769476
  43.9 0.9 %copy-start.9 = (f32[3,4,32,128]{3,2,1,0:T(8,128)S(1)}, f32[3,4,32,128]{3,2,1,0:T(8,128)}, u32[]{:S(2)}) copy-start(f32[3,4,32,128]{3,2,1,0:T(8,128)} %copy-done.8) | copy-start | bytes 589828

commit v4 on v3

--- a/solution.py
+++ b/solution.py
@@ -17,6 +17,7 @@
 NEAR = 9.0 / 8.0
 FAR = -1.0 / 24.0
 DT = 0.15
+TILE = 8
 
 XX, YY, ZZ, XY, XZ, YZ = range(6)
 
@@ -45,31 +46,30 @@
         self.rows = rows
         self.depths = depths
         lane = lax.broadcasted_iota(jnp.int32, (rows, depths), 1)
-        row = lax.broadcasted_iota(jnp.int32, (rows, depths), 0)
-        self.row = row
+        row = lax.broadcasted_iota(jnp.int32, (TILE, depths), 0)
+        self.row = lax.broadcasted_iota(jnp.int32, (rows, depths), 0)
+        self.tile_row = row
         self.deep = lax.axis_index("gz")
-        self.low = {1: lane < 1, 2: lane < 2}
-        self.high = {1: lane >= depths - 1, 2: lane >= depths - 2}
-        self.top = {1: row < 1, 2: row < 2}
-        self.bottom = {1: row >= rows - 1, 2: row >= rows - 2}
-        self.slots = [self.slot(lane, k) for k in range(3)]
-
-    def slot(self, lane, k):
-        first = jnp.where(self.deep == 0, self.depths - 2 - 8 * k, 8 * k)
-        return (lane == first) | (lane == first + 1)
-
-    def turn(self, k):
-        return jnp.where(self.deep == 0, self.depths - 8 * k, 8 * k)
-
-    def packed(self, fields):
-        out = jnp.where(self.slots[0], fields[0], 0.0)
-        for k in (1, 2):
-            if fields[k] is not None:
-                out = jnp.where(self.slots[k], pltpu.roll(fields[k], self.turn(k), 1), out)
-        return out
-
-    def ends(self, strip, k):
-        return strip if k == 0 else pltpu.roll(strip, self.turn(k), 1)
+        self.upper = jnp.where(self.deep == 0, 1.0, 0.0)
+        self.zero = jnp.minimum(self.deep, 0)
+        self.pair = lane // 2
+        self.low = {n: lane < n for n in (1, 2)}
+        self.high = {n: lane >= depths - n for n in (1, 2)}
+        self.top = {n: row < n for n in (1, 2)}
+        self.bottom = {n: row >= TILE - n for n in (1, 2)}
+
+    def packed(self, strip, x, fields):
+        first = jnp.where(self.deep == 0, 2, 0)
+        for k, field in enumerate(fields):
+            turn = lax.rem(first + 8 * x + 2 * k, self.depths)
+            strip = jnp.where(self.pair == 4 * x + k, pltpu.roll(field, turn, 1), strip)
+        return strip
+
+    def ends(self, strip, x, k):
+        back = self.depths - 8 * x - 2 * k
+        turn = jnp.where(self.deep == 0, back % self.depths, back - 2)
+        halo = pltpu.roll(strip, turn, 1)
+        return halo * self.upper, halo * (1.0 - self.upper)
 
     def shallower(self, field, halo, n):
         return pltpu.roll(jnp.where(self.high[n], halo, field), n, 1)
@@ -77,54 +77,57 @@
     def deeper(self, field, halo, n):
         return pltpu.roll(jnp.where(self.low[n], halo, field), self.depths - n, 1)
 
-    def forward_z(self, field, strip, k):
-        halo = self.ends(strip, k)
+    def forward_z(self, field, halos):
+        after, before = halos
         return forward(
-            self.shallower(field, halo, 1),
+            self.shallower(field, before, 1),
             field,
-            self.deeper(field, halo, 1),
-            self.deeper(field, halo, 2),
-        )
-
-    def backward_z(self, field, strip, k):
-        halo = self.ends(strip, k)
+            self.deeper(field, after, 1),
+            self.deeper(field, after, 2),
+        )
+
+    def backward_z(self, field, halos):
+        after, before = halos
         return backward(
-            self.shallower(field, halo, 2),
-            self.shallower(field, halo, 1),
+            self.shallower(field, before, 2),
+            self.shallower(field, before, 1),
             field,
-            self.deeper(field, halo, 1),
-        )
-
-    def before(self, field, n, halo):
-        moved = jnp.where(self.top[n], 0.0, pltpu.roll(field, n, 0))
+            self.deeper(field, after, 1),
+        )
+
+    def before(self, field, load, n, halo):
+        top = jnp.where(self.top[n], 0.0, pltpu.roll(field[:TILE], n, 0))
         if halo:
             for i in range(n):
-                moved = jnp.where(self.row == i, halo[n - 1 - i], moved)
-        return moved
-
-    def after(self, field, n, halo):
-        moved = jnp.where(self.bottom[n], 0.0, pltpu.roll(field, self.rows - n, 0))
+                top = jnp.where(self.tile_row == i, halo[n - 1 - i], top)
+        return jnp.concatenate([top, load(self.zero + (TILE - n), self.rows - TILE)], axis=0)
+
+    def after(self, field, load, n, halo):
+        bottom = pltpu.roll(field[self.rows - TILE :], TILE - n, 0)
+        bottom = jnp.where(self.bottom[n], 0.0, bottom)
         if halo:
             for i in range(n):
-                moved = jnp.where(self.row == self.rows - n + i, halo[i], moved)
-        return moved
-
-    def forward_y(self, field, halos):
+                bottom = jnp.where(self.tile_row == TILE - n + i, halo[i], bottom)
+        return jnp.concatenate([load(self.zero + n, self.rows - TILE), bottom], axis=0)
+
+    def forward_y(self, planes, comp, x, halos):
+        field, load = planes(comp, x), planes.rows(comp, x)
         lower, upper = halos
         return forward(
-            self.before(field, 1, lower),
+            self.before(field, load, 1, lower),
             field,
-            self.after(field, 1, upper),
-            self.after(field, 2, upper),
-        )
-
-    def backward_y(self, field, halos):
+            self.after(field, load, 1, upper),
+            self.after(field, load, 2, upper),
+        )
+
+    def backward_y(self, planes, comp, x, halos):
+        field, load = planes(comp, x), planes.rows(comp, x)
         lower, upper = halos
         return backward(
-            self.before(field, 2, lower),
-            self.before(field, 1, lower),
+            self.before(field, load, 2, lower),
+            self.before(field, load, 1, lower),
             field,
-            self.after(field, 1, upper),
+            self.after(field, load, 1, upper),
         )
 
 
@@ -133,13 +136,21 @@
         self.count = count
         self.parts = parts
 
-    def __call__(self, comp, x):
+    def place(self, x):
         if len(self.parts) == 1:
-            return self.parts[0][comp, x]
+            return self.parts[0], x
         inner, edge = self.parts
         if x in inside(self.count):
-            return inner[comp, x - 2]
-        return edge[comp, ends_of(self.count).index(x)]
+            return inner, x - 2
+        return edge, ends_of(self.count).index(x)
+
+    def __call__(self, comp, x):
+        ref, at = self.place(x)
+        return ref[comp, at]
+
+    def rows(self, comp, x):
+        ref, at = self.place(x)
+        return lambda start, size: ref[comp, at, pl.ds(start, size), :]
 
 
 def inside(count):
@@ -174,6 +185,9 @@
         if place >= self.count:
             return self.right(self.head.index((comp, place - self.count)))
         return self.field(comp, place)
+
+    def rows(self, comp, x):
+        return self.field.rows(comp, x)
 
     def forward_x(self, comp, x):
         return forward(self(comp, x - 1), self(comp, x), self(comp, x + 1), self(comp, x + 2))
@@ -241,30 +255,31 @@
     for copy in copies:
         copy.wait()
     edge_planes(Field(count, r.held), STRESS_TAIL, STRESS_HEAD, r.one_out, r.two_out)
+    strip = jnp.zeros((rows, depths), jnp.float32)
     for x in range(count):
-        r.strip_out[x] = edges.packed([r.held[c, x] for c in STRESS_SLOTS])
+        strip = edges.packed(strip, x, [r.held[c, x] for c in STRESS_SLOTS])
+    r.strip_out[...] = strip
 
 
 def velocity_planes(r, xs, edges, planes, write):
     band = Bands(getattr(r, "lower", None), getattr(r, "upper", None), STRESS_TAIL_Y, STRESS_HEAD_Y)
+    strip = r.strip[...]
     for x in xs:
-        sxy, sxz, syz = planes(XY, x), planes(XZ, x), planes(YZ, x)
         push = DT * looked_up(r.material[x], r.table, 2, CLASSES)
-        ends = r.strip[x]
         along_x = (
             planes.forward_x(XX, x)
-            + edges.backward_y(sxy, band(XY, x))
-            + edges.backward_z(sxz, ends, 0)
+            + edges.backward_y(planes, XY, x, band(XY, x))
+            + edges.backward_z(planes(XZ, x), edges.ends(strip, x, 0))
         )
         along_y = (
             planes.backward_x(XY, x)
-            + edges.forward_y(planes(YY, x), band(YY, x))
-            + edges.backward_z(syz, ends, 1)
+            + edges.forward_y(planes, YY, x, band(YY, x))
+            + edges.backward_z(planes(YZ, x), edges.ends(strip, x, 1))
         )
         along_z = (
             planes.backward_x(XZ, x)
-            + edges.backward_y(syz, band(YZ, x))
-            + edges.forward_z(planes(ZZ, x), ends, 2)
+            + edges.backward_y(planes, YZ, x, band(YZ, x))
+            + edges.forward_z(planes(ZZ, x), edges.ends(strip, x, 2))
         )
         rates = (along_x, along_y, along_z)
         write(x, [r.velocity[c, x] + push * rate for c, rate in enumerate(rates)])
@@ -274,13 +289,15 @@
     count, rows, depths = r.material.shape
     edges = Edges(rows, depths)
     planes = Planes(stress_of(r), STRESS_TAIL, STRESS_HEAD)
+    packed = [jnp.zeros((rows, depths), jnp.float32)]
 
     def write(x, new):
         for c in range(3):
             r.inner_out[c, x - 2] = new[c]
-        r.strip_inner_out[x - 2] = edges.packed(new)
+        packed[0] = edges.packed(packed[0], x, new)
 
     velocity_planes(r, inside(count), edges, planes, write)
+    r.strip_inner_out[...] = packed[0]
 
 
 def velocity_edge(first, r):
@@ -293,7 +310,6 @@
     for x in inside(count):
         r.face_out[pl.ds(x, 1), :] = r.inner[0, x - 2, row, :]
         r.face_out[pl.ds(count + x, 1), :] = r.inner[2, x - 2, row, :]
-        r.strip_out[x] = r.strip_inner[x - 2]
     if first:
         for x in range(count):
             labels = r.material[x, row, :]
@@ -307,12 +323,15 @@
         for i, field in enumerate((r.normal, r.slip, r.zone, r.mask)):
             r.face_out[pl.ds(place + (2 + i) * own, own), :] = field[...].astype(jnp.float32)
 
+    packed = [r.strip_inner[...]]
+
     def write(x, new):
         for c in range(3):
             r.edge_out[c, places.index(x)] = new[c]
-        r.strip_out[x] = edges.packed(new)
+        packed[0] = edges.packed(packed[0], x, new)
 
     velocity_planes(r, places, edges, planes, write)
+    r.strip_out[...] = packed[0]
     for x in places:
         r.face_out[pl.ds(x, 1), :] = r.edge_out[0, places.index(x), row, :]
         r.face_out[pl.ds(count + x, 1), :] = r.edge_out[2, places.index(x), row, :]
@@ -337,7 +356,8 @@
 def fault_kernel(first, r):
     own_face, other_face = r.face, r.other
     own_first, other_first = (own_face, other_face) if first else (r.face_first, r.other_first)
-    count, rows, depths = r.strip.shape
+    rows, depths = r.strip.shape
+    count = r.change_out.shape[1]
     middle = lax.axis_size("gy") // 2
     side = lax.axis_index("gy")
     plus = side == middle
@@ -380,7 +400,12 @@
     weaken = jnp.minimum(slip / distance, 1.0)
     strength = (static - (static - dynamic) * weaken) * normal
     factor = jnp.where(mask == 1.0, strength / jnp.maximum(size, strength), 1.0)
-    r.slip_out[...] = slip + DT * DT * bsum * (size - size * factor)
+    new_slip = slip + DT * DT * bsum * (size - size * factor)
+    if r.slip_out.shape[0] == count:
+        r.slip_out[...] = new_slip
+    else:
+        half = r.slip_out.shape[0]
+        r.slip_out[...] = jnp.where(plus, new_slip[half:], new_slip[:half])
     sign = jnp.where(minus, DT, 0.0) * minus_b - jnp.where(plus, DT, 0.0) * plus_b
     change_x = (trial_x * factor - pre_x) * sign
     change_z = (trial_z * factor - pre_z) * sign
@@ -401,24 +426,30 @@
         one, two = jnp.where(even, right, left), jnp.where(even, left, right)
         r.one_out[i] = r.one[i] + jnp.where(on_fault, one, 0.0)
         r.two_out[i] = r.two[i] + jnp.where(on_fault, two, 0.0)
-    flat = Edges(count, depths)
-    ends = flat.packed([change_x, None, change_z])
-    for x in range(count):
-        r.strip_out[x] = r.strip[x] + jnp.where(on_fault, ends[x : x + 1, :], 0.0)
+    ends = jnp.zeros((count, depths), jnp.float32)
+    pair = lax.broadcasted_iota(jnp.int32, (count, depths), 1) // 2
+    place = 4 * lax.broadcasted_iota(jnp.int32, (count, depths), 0)
+    upper = lax.axis_index("gz") == 0
+    for k, field in ((0, change_x), (2, change_z)):
+        turned = jnp.where(upper, pltpu.roll(field, 2, 1), field)
+        turned = pltpu.roll(turned, 2 * k, 1, stride=8, stride_axis=0)
+        ends = jnp.where(pair == place + k, turned, ends)
+    line = jnp.sum(ends, axis=0, keepdims=True)
+    r.strip_out[...] = r.strip[...] + jnp.where(on_fault, line, 0.0)
 
 
 def stress_planes(r, xs, edges, planes, write):
     band = Bands(getattr(r, "lower", None), getattr(r, "upper", None), VEL_TAIL_Y, VEL_HEAD_Y)
     stress, memory = stress_of(r), memory_of(r)
+    strip = r.strip[...]
     for x in xs:
-        vx, vy, vz = planes(0, x), planes(1, x), planes(2, x)
-        ends = r.strip[x]
+        in_x, in_y, in_z = [edges.ends(strip, x, k) for k in range(3)]
         exx = planes.backward_x(0, x)
-        eyy = edges.backward_y(vy, band(1, x))
-        ezz = edges.backward_z(vz, ends, 2)
-        exy = edges.forward_y(vx, band(0, x)) + planes.forward_x(1, x)
-        exz = edges.forward_z(vx, ends, 0) + planes.forward_x(2, x)
-        eyz = edges.forward_z(vy, ends, 1) + edges.forward_y(vz, band(2, x))
+        eyy = edges.backward_y(planes, 1, x, band(1, x))
+        ezz = edges.backward_z(planes(2, x), in_z)
+        exy = edges.forward_y(planes, 0, x, band(0, x)) + planes.forward_x(1, x)
+        exz = edges.forward_z(planes(0, x), in_x) + planes.forward_x(2, x)
+        eyz = edges.forward_z(planes(1, x), in_y) + edges.forward_y(planes, 2, x, band(2, x))
         labels = r.material[x]
         lame = looked_up(labels, r.table, 0, CLASSES)
         shear = looked_up(labels, r.table, 1, CLASSES)
@@ -450,15 +481,25 @@
             r.velocity_out[c, x] = free(c, x) + jnp.where(on_fault, line, 0.0)
         r.velocity_out[1, x] = free(1, x)
     planes = Planes(Field(count, r.velocity_out), VEL_TAIL, VEL_HEAD)
+    packed = [jnp.zeros((rows, depths), jnp.float32)]
+    if last:
+        velocity_copy = pltpu.make_async_copy(
+            r.velocity_out, r.new_velocity_out, r.sems.at[0]
+        )
+        velocity_copy.start()
 
     def write(x, new, kept):
         for c in range(6):
             r.stress_inner_out[c, x - 2] = new[c]
             r.memory_inner_out[c, x - 2] = kept[c]
         if not last:
-            r.strip_inner_out[x - 2] = edges.packed([new[c] for c in STRESS_SLOTS])
+            packed[0] = edges.packed(packed[0], x, [new[c] for c in STRESS_SLOTS])
 
     stress_planes(r, inside(count), edges, planes, write)
+    if last:
+        velocity_copy.wait()
+    else:
+        r.strip_inner_out[...] = packed[0]
 
 
 def stress_edge(last, r):
@@ -474,21 +515,19 @@
         copies.append(copy)
 
     if last:
-        copy_out(r.velocity, r.velocity_out, pl.ds(0, count))
         copy_out(r.new_stress_inner, r.stress_out, pl.ds(2, count - 4))
         copy_out(r.new_memory_inner, r.memory_out, pl.ds(2, count - 4))
         stress_out, memory_out = r.stress_held, r.memory_held
     else:
         stress_out, memory_out = r.stress_edge_out, r.memory_edge_out
-        for x in inside(count):
-            r.strip_out[x] = r.strip_inner[x - 2]
+        packed = [r.strip_inner[...]]
 
     def write(x, new, kept):
         for c in range(6):
             stress_out[c, places.index(x)] = new[c]
             memory_out[c, places.index(x)] = kept[c]
         if not last:
-            r.strip_out[x] = edges.packed([new[c] for c in STRESS_SLOTS])
+            packed[0] = edges.packed(packed[0], x, [new[c] for c in STRESS_SLOTS])
 
     stress_planes(r, places, edges, planes, write)
     if last:
@@ -498,6 +537,7 @@
         for copy in copies:
             copy.wait()
     else:
+        r.strip_out[...] = packed[0]
         new = Field(count, r.new_stress_inner, stress_out)
         edge_planes(new, STRESS_TAIL, STRESS_HEAD, r.one_out, r.two_out)
 
@@ -505,7 +545,7 @@
 SCALARS = ("table", "friction", "anchor")
 
 
-def call(kernel, name, ins, outs, scratch=None, apart=(), cost=0, vmem=14):
+def call(kernel, name, ins, outs, scratch=None, apart=(), cost=0, vmem=6):
     scratch = scratch or {}
     names = [*ins, *(f"{key}_out" for key in outs), *scratch]
 
@@ -589,7 +629,7 @@
 
     plane = (rows, depths)
     edge_shape = (max(len(STRESS_TAIL), len(STRESS_HEAD)), *plane)
-    travelling = {"one": edge_shape, "two": edge_shape, "strip": (count, *plane)}
+    travelling = {"one": edge_shape, "two": edge_shape, "strip": plane}
     inner, edge = (count - 4, *plane), (4, *plane)
 
     def travelled(packed):
@@ -628,7 +668,7 @@
         travelling,
         scratch={"held": pltpu.VMEM(stress.shape, jnp.float32), "sems": pltpu.SemaphoreType.DMA((8,))},
         apart=("stress",),
-        vmem=14,
+        vmem=6,
     )
     for step in range(STEPS):
         first, last = step == 0, step == STEPS - 1
@@ -641,7 +681,7 @@
             velocity_inner,
             "velocity_inner",
             ins,
-            {"inner": (3, *inner), "strip_inner": inner},
+            {"inner": (3, *inner), "strip_inner": plane},
             cost=60 * cells,
         )
         face_rows = 2 * count
@@ -669,9 +709,11 @@
         else:
             ins.update(slip=slip, **faces)
         outs = {"change": (2, count, depths), "slip": (count, depths), **travelling}
+        if last and not banded:
+            outs["slip"] = (count // sides, depths)
         if not still:
             outs["still"] = (6, count, depths)
-        packed = call(functools.partial(fault_kernel, first), "fault", ins, outs)
+        packed = call(functools.partial(fault_kernel, first), "fault", ins, outs, vmem=2)
         slip = packed["slip"]
         if not still:
             still = {"still": packed["still"]}
@@ -685,10 +727,20 @@
         else:
             band = {}
         outs = {"velocity": velocity.shape, "stress_inner": (6, *inner), "memory_inner": (6, *inner)}
-        if not last:
-            outs["strip_inner"] = inner
+        extra = {}
+        if last:
+            outs["new_velocity"] = velocity.shape
+            extra = {"scratch": {"sems": pltpu.SemaphoreType.DMA((1,))}, "apart": ("new_velocity_out",)}
+        else:
+            outs["strip_inner"] = plane
         done = call(
-            functools.partial(stress_inner, last), "stress_inner", {**ins, **band}, outs, cost=100 * cells
+            functools.partial(stress_inner, last),
+            "stress_inner",
+            {**ins, **band},
+            outs,
+            cost=100 * cells,
+            vmem=10,
+            **extra,
         )
         velocity = done["velocity"]
         ins = {"velocity": velocity, **parts, **props, **strip, **halos, **band}
@@ -700,15 +752,17 @@
                 functools.partial(stress_edge, last),
                 "stress_edge",
                 ins,
-                {"velocity": velocity.shape, "stress": stress.shape, "memory": memory.shape},
+                {"stress": stress.shape, "memory": memory.shape},
                 scratch={
                     "stress_held": held,
                     "memory_held": held,
-                    "sems": pltpu.SemaphoreType.DMA((7,)),
+                    "sems": pltpu.SemaphoreType.DMA((6,)),
                 },
-                apart=("velocity_out", "stress_out", "memory_out"),
+                apart=("stress_out", "memory_out"),
+                vmem=10,
             )
-            velocity, stress, memory = packed["velocity"], packed["stress"], packed["memory"]
+            velocity = done["new_velocity"]
+            stress, memory = packed["stress"], packed["memory"]
         else:
             ins["strip_inner"] = done["strip_inner"]
             packed = call(
@@ -717,6 +771,7 @@
                 ins,
                 {"stress_edge": (6, *edge), "memory_edge": (6, *edge), **travelling},
                 cost=30 * cells,
+                vmem=10,
             )
             parts = {
                 "stress_inner": done["stress_inner"],
@@ -724,14 +779,10 @@
                 "memory_inner": done["memory_inner"],
                 "memory_edge": packed["memory_edge"],
             }
-    side = lax.axis_index("gy")
     if banded:
-        held = jnp.where(side == middle, slip, 0.0)
-        new_slip = lax.psum_scatter(held, "gy", scatter_dimension=0, tiled=True)
-    else:
-        share = count // sides
-        new_slip = lax.dynamic_slice_in_dim(slip, side * share, share, axis=0)
-    return (velocity, stress, memory, new_slip)
+        held = jnp.where(lax.axis_index("gy") == middle, slip, 0.0)
+        slip = lax.psum_scatter(held, "gy", scatter_dimension=0, tiled=True)
+    return (velocity, stress, memory, slip)
 
 
 def solution(mesh):

time: 51.4 us -> 52.5 us (1.021)
  waiting for transfers between devices: 4.89 us -> 9.58 us
  local copies, waits for them, and re-layouts: 4.72 us -> 1.47 us
  starting transfers between devices: 19.3 us -> 18.1 us
  Pallas kernels: 21.1 us -> 22.2 us
    ppermute x14, waiting for transfers between devices: 4.89 us -> 9.58 us  [sent(): return lax.ppermute(block, *route)]
    unnamed x36 -> x26, local copies, waits for them, and re-layouts: 4.12 us -> 1.47 us
    ppermute x14, starting transfers between devices: 19.3 us -> 18.1 us  [sent(): return lax.ppermute(block, *route)]
    pallas_call x11, Pallas kernels: 21.1 us -> 22.2 us  [call(): pl.pallas_call(body, out_shape=shapes, in_specs=[place(key) for key in in...]
    dynamic_slice x1 -> x0, local copies, waits for them, and re-layouts: 0.6 us -> none  [shards(): new_slip = lax.dynamic_slice_in_dim(slip, side * share, share, axis=0)]
  transfers between devices with their start and end apart: 14 -> 14, of which waited for: 2 -> 6; matrix products, arithmetic and copies ran while one was open for 1% -> 0% of each run, Pallas kernels for 24% -> 25%
where the time goes in v4:
time: 52.5 us; the launch traced here: 52.2 us
  Pallas kernels  22.2 us (42%)
  starting transfers between devices  18.1 us (34%)
  waiting for transfers between devices  9.58 us (18%)
  local copies, waits for them, and re-layouts  1.47 us (3%)
  between operations  0.9 us (2%)
    pallas_call x11, Pallas kernels, call(): pl.pallas_call(body, out_shape=shapes, in_specs=[place(key) for key in in...  22.2 us
    ppermute x14, starting transfers between devices, sent(): return lax.ppermute(block, *route)  18.1 us
    ppermute x14, waiting for transfers between devices, sent(): return lax.ppermute(block, *route)  9.58 us
    unnamed x26, local copies, waits for them, and re-layouts  1.47 us
  transfers between devices with their start and end apart: 14, of which 6 were waited for; matrix products, arithmetic and copies ran while one was open for 0% of the time, Pallas kernels for 25%

profile of v4, /device:TPU:0, one launch (start us, length us, event | category | flops | bytes accessed | tf_op | source)
XLA Modules:
  0.0 52.2 jit_solution(18049898886487310977)
XLA Ops:
  0.6 1.4 %copy-done = f32[6,16,32,128]{3,2,1,0:T(8,128)S(1)} copy-done((f32[6,16,32,128]{3,2,1,0:T(8,128)S(1)}, f32[6,16,32,128]{3,2,1,0:T(8,128)}, u32[]{:S(2)}) %copy-start) | copy-done | bytes 1572888
  2.0 0.5 %pack.1 = (f32[5,32,128]{2,1,0:T(8,128)S(1)}, f32[5,32,128]{2,1,0:T(8,128)S(1)}, f32[32,128]{1,0:T(8,128)S(1)}) custom-call(f32[6,16,32,128]{3,2,1,0:T(8,128)S(1)} %copy-done), custom_call_target="tpu_custom_call" | custom-call | bytes 1753088 | tf_op jit(solution)/shard_map/pack/pallas_call | solution.py:562
  2.7 3.1 %collective-permute-start.1 = (f32[5,32,128]{2,1,0:T(8,128)S(1)}, f32[5,32,128]{2,1,0:T(8,128)S(1)}, u32[]{:S(2)}, u32[]{:S(2)}) collective-permute-start(f32[5,32,128]{2,1,0:T(8,128)S(1)} %get-tuple-element.49), channel_id=1, source_target_pairs={{0,4},{4,0},{8,12},{12,8},{1,5},{5,1},{9,13},{13,9},{2,6},{6,2},{1... | collective-permute-start | bytes 245768 | tf_op jit(solution)/shard_map/ppermute | solution.py:591
  5.7 0.7 %collective-permute-start.2 = (f32[5,32,128]{2,1,0:T(8,128)S(1)}, f32[5,32,128]{2,1,0:T(8,128)S(1)}, u32[]{:S(2)}, u32[]{:S(2)}) collective-permute-start(f32[5,32,128]{2,1,0:T(8,128)S(1)} %get-tuple-element.50), channel_id=1, source_target_pairs={{0,0},{4,8},{8,4},{12,12},{1,1},{5,9},{9,5},{13,13},{2,2},{6,10},{... | collective-permute-start | bytes 245768 | tf_op jit(solution)/shard_map/ppermute | solution.py:591
  6.4 0.1 collective-permute-start
  6.5 1.2 %collective-permute-done.refs_4_ = f32[32,128]{1,0:T(8,128)S(1)} collective-permute-done((f32[32,128]{1,0:T(8,128)S(1)}, f32[32,128]{1,0:T(8,128)S(1)}, u32[]{:S(2)}, u32[]{:S(2)}) %collective-permute-start) | collective-permute-done | bytes 16416 | tf_op jit(solution)/shard_map/ppermute | solution.py:591
  7.7 3.8 %velocity_inner.2 = (f32[3,12,32,128]{3,2,1,0:T(8,128)S(1)}, f32[32,128]{1,0:T(8,128)S(1)}) custom-call(f32[3,16,32,128]{3,2,1,0:T(8,128)S(1)} %copy-done.4, f32[6,16,32,128]{3,2,1,0:T(8,128)S(1)} %copy-done, s32[16,32,128]{2,1,0:T(8,128)S(1)} %copy-done.2, f32[5,8]{1,0:T(8,128)S(1)} %copy-done.5, f32[32,128]{1,0:T(8,128)S(1)} %collective-permute-done.refs_4_), custom_call_target="tpu_custom_call" | custom-call | flops 3932160 | bytes 3244192 | tf_op jit(solution)/shard_map/velocity_inner/pallas_call | solution.py:562
  11.5 1.2 %velocity_edge.2 = (f32[3,4,32,128]{3,2,1,0:T(8,128)S(1)}, f32[96,128]{1,0:T(8,128)S(1)}, f32[5,32,128]{2,1,0:T(8,128)S(1)}, f32[5,32,128]{2,1,0:T(8,128)S(1)}, f32[32,128]{1,0:T(8,128)S(1)}) custom-call(f32[3,16,32,128]{3,2,1,0:T(8,128)S(1)} %copy-done.4, f32[6,16,32,128]{3,2,1,0:T(8,128)S(1)} %copy-done, s32[16,32,128]{2,1,0:T(8,128)S(1)} %copy-done.2, ...), custom_call_target="tpu_custom_call" | custom-call | flops 1310720 | bytes 3858592 | tf_op jit(solution)/shard_map/velocity_edge/pallas_call | solution.py:562
  12.8 1.5 %collective-permute-start.3 = (f32[96,128]{1,0:T(8,128)S(1)}, f32[96,128]{1,0:T(8,128)S(1)}, u32[]{:S(2)}, u32[]{:S(2)}) collective-permute-start(f32[96,128]{1,0:T(8,128)S(1)} %get-tuple-element.56.refs_3_.refs_9_), channel_id=1, source_target_pairs={{0,2},{2,0},{1,3},{3,1},{4,6},{6,4},{5,7},{7,5},{8,10},{10,8},{9,1... | collective-permute-start | bytes 147464 | tf_op jit(solution)/shard_map/ppermute | solution.py:591
  14.3 2.6 %collective-permute-done.3.refs_4_.refs_10_ = f32[96,128]{1,0:T(8,128)S(1)} collective-permute-done((f32[96,128]{1,0:T(8,128)S(1)}, f32[96,128]{1,0:T(8,128)S(1)}, u32[]{:S(2)}, u32[]{:S(2)}) %collective-permute-start.3) | collective-permute-done | bytes 49184 | tf_op jit(solution)/shard_map/ppermute | solution.py:591
  16.9 0.8 %fault.2 = (f32[2,16,128]{2,1,0:T(8,128)S(1)}, f32[16,128]{1,0:T(8,128)S(1)}, f32[5,32,128]{2,1,0:T(8,128)S(1)}, f32[5,32,128]{2,1,0:T(8,128)S(1)}, f32[32,128]{1,0:T(8,128)S(1)}, /*index=5*/f32[6,16,128]{2,1,0:T(8,128)S(1)}) custom-call(f32[5,32,128]{2,1,0:T(8,128)S(1)} %get-tuple-element.53.refs_0_, f32[5,32,128]{2,1,0:T(8,128)S(1)} %get-tuple-element.54.refs_1_, ...), custom_call_target="tpu_custom_call" | custom-call | bytes 532536 | tf_op jit(solution)/shard_map/fault/pallas_call | solution.py:562
  17.7 4.5 %collective-permute-start.5 = (f32[5,32,128]{2,1,0:T(8,128)S(1)}, f32[5,32,128]{2,1,0:T(8,128)S(1)}, u32[]{:S(2)}, u32[]{:S(2)}) collective-permute-start(f32[5,32,128]{2,1,0:T(8,128)S(1)} %get-tuple-element.61), channel_id=1, source_target_pairs={{0,4},{4,0},{8,12},{12,8},{1,5},{5,1},{9,13},{13,9},{2,6},{6,2},{1... | collective-permute-start | bytes 245768 | tf_op jit(solution)/shard_map/ppermute | solution.py:591
  22.1 0.7 %collective-permute-start.6 = (f32[5,32,128]{2,1,0:T(8,128)S(1)}, f32[5,32,128]{2,1,0:T(8,128)S(1)}, u32[]{:S(2)}, u32[]{:S(2)}) collective-permute-start(f32[5,32,128]{2,1,0:T(8,128)S(1)} %get-tuple-element.62), channel_id=1, source_target_pairs={{0,0},{4,8},{8,4},{12,12},{1,1},{5,9},{9,5},{13,13},{2,2},{6,10},{... | collective-permute-start | bytes 245768 | tf_op jit(solution)/shard_map/ppermute | solution.py:591
  22.8 0.1 collective-permute-start.4
  22.9 1.2 %collective-permute-done.4.refs_7_.refs_5_ = f32[32,128]{1,0:T(8,128)S(1)} collective-permute-done((f32[32,128]{1,0:T(8,128)S(1)}, f32[32,128]{1,0:T(8,128)S(1)}, u32[]{:S(2)}, u32[]{:S(2)}) %collective-permute-start.4) | collective-permute-done | bytes 16416 | tf_op jit(solution)/shard_map/ppermute | solution.py:591
  24.0 2.8 %stress_inner.2 = (f32[3,16,32,128]{3,2,1,0:T(8,128)S(1)}, f32[6,12,32,128]{3,2,1,0:T(8,128)S(1)}, f32[6,12,32,128]{3,2,1,0:T(8,128)S(1)}, f32[32,128]{1,0:T(8,128)S(1)}) custom-call(f32[3,12,32,128]{3,2,1,0:T(8,128)S(1)} %get-tuple-element.48.refs_7_.refs_0_, f32[3,4,32,128]{3,2,1,0:T(8,128)S(1)} %get-tuple-element.52.refs_1_, ...), custom_call_target="tpu_custom_call" | custom-call | flops 6553600 | bytes 7389344 | tf_op jit(solution)/shard_map/stress_inner/pallas_call | solution.py:562
  26.9 1.2 %stress_edge.2 = (f32[6,4,32,128]{3,2,1,0:T(8,128)S(1)}, f32[6,4,32,128]{3,2,1,0:T(8,128)S(1)}, f32[5,32,128]{2,1,0:T(8,128)S(1)}, f32[5,32,128]{2,1,0:T(8,128)S(1)}, f32[32,128]{1,0:T(8,128)S(1)}) custom-call(f32[3,16,32,128]{3,2,1,0:T(8,128)S(1)} %get-tuple-element.59.refs_0_, f32[6,16,32,128]{3,2,1,0:T(8,128)S(1)} %copy-done.1, ...), custom_call_target="tpu_custom_call" | custom-call | flops 1966080 | bytes 6537376 | tf_op jit(solution)/shard_map/stress_edge/pallas_call | solution.py:562
  28.1 1.7 %collective-permute-start.8 = (f32[5,32,128]{2,1,0:T(8,128)S(1)}, f32[5,32,128]{2,1,0:T(8,128)S(1)}, u32[]{:S(2)}, u32[]{:S(2)}) collective-permute-start(f32[5,32,128]{2,1,0:T(8,128)S(1)} %get-tuple-element.67), channel_id=1, source_target_pairs={{0,4},{4,0},{8,12},{12,8},{1,5},{5,1},{9,13},{13,9},{2,6},{6,2},{1... | collective-permute-start | bytes 245768 | tf_op jit(solution)/shard_map/ppermute | solution.py:591
  29.7 0.7 %collective-permute-start.9 = (f32[5,32,128]{2,1,0:T(8,128)S(1)}, f32[5,32,128]{2,1,0:T(8,128)S(1)}, u32[]{:S(2)}, u32[]{:S(2)}) collective-permute-start(f32[5,32,128]{2,1,0:T(8,128)S(1)} %get-tuple-element.68), channel_id=1, source_target_pairs={{0,0},{4,8},{8,4},{12,12},{1,1},{5,9},{9,5},{13,13},{2,2},{6,10},{... | collective-permute-start | bytes 245768 | tf_op jit(solution)/shard_map/ppermute | solution.py:591
  30.4 0.1 collective-permute-start.7
  30.5 1.2 %collective-permute-done.7.refs_5_ = f32[32,128]{1,0:T(8,128)S(1)} collective-permute-done((f32[32,128]{1,0:T(8,128)S(1)}, f32[32,128]{1,0:T(8,128)S(1)}, u32[]{:S(2)}, u32[]{:S(2)}) %collective-permute-start.7) | collective-permute-done | bytes 16416 | tf_op jit(solution)/shard_map/ppermute | solution.py:591
  31.6 3.8 %velocity_inner.3 = (f32[3,12,32,128]{3,2,1,0:T(8,128)S(1)}, f32[32,128]{1,0:T(8,128)S(1)}) custom-call(f32[3,16,32,128]{3,2,1,0:T(8,128)S(1)} %get-tuple-element.59.refs_0_, f32[6,12,32,128]{3,2,1,0:T(8,128)S(1)} %get-tuple-element.60.refs_8_.refs_1_.refs_3_, f32[6,4,32,128]{3,2,1,0:T(8,128)S(1)} %get-tuple-element.64.refs_2_.refs_4_, ...), custom_call_target="tpu_custom_call" | custom-call | flops 3932160 | bytes 3244192 | tf_op jit(solution)/shard_map/velocity_inner/pallas_call | solution.py:562
  35.4 1.2 %velocity_edge.3 = (f32[3,4,32,128]{3,2,1,0:T(8,128)S(1)}, f32[32,128]{1,0:T(8,128)S(1)}, f32[5,32,128]{2,1,0:T(8,128)S(1)}, f32[5,32,128]{2,1,0:T(8,128)S(1)}, f32[32,128]{1,0:T(8,128)S(1)}) custom-call(f32[3,16,32,128]{3,2,1,0:T(8,128)S(1)} %get-tuple-element.59.refs_0_, f32[6,12,32,128]{3,2,1,0:T(8,128)S(1)} %get-tuple-element.60.refs_8_.refs_1_.refs_3_, ...), custom_call_target="tpu_custom_call" | custom-call | flops 1310720 | bytes 3801248 | tf_op jit(solution)/shard_map/velocity_edge/pallas_call | solution.py:562
  36.6 1.5 %collective-permute-start.10 = (f32[32,128]{1,0:T(8,128)S(1)}, f32[32,128]{1,0:T(8,128)S(1)}, u32[]{:S(2)}, u32[]{:S(2)}) collective-permute-start(f32[32,128]{1,0:T(8,128)S(1)} %get-tuple-element.74.refs_3_), channel_id=1, source_target_pairs={{0,2},{2,0},{1,3},{3,1},{4,6},{6,4},{5,7},{7,5},{8,10},{10,8},{9,1... | collective-permute-start | bytes 49160 | tf_op jit(solution)/shard_map/ppermute | solution.py:591
  38.1 2.3 %collective-permute-done.10.refs_4_ = f32[32,128]{1,0:T(8,128)S(1)} collective-permute-done((f32[32,128]{1,0:T(8,128)S(1)}, f32[32,128]{1,0:T(8,128)S(1)}, u32[]{:S(2)}, u32[]{:S(2)}) %collective-permute-start.10) | collective-permute-done | bytes 16416 | tf_op jit(solution)/shard_map/ppermute | solution.py:591
  40.4 1.3 %fault.3 = (f32[2,16,128]{2,1,0:T(8,128)S(1)}, f32[8,128]{1,0:T(8,128)}, f32[5,32,128]{2,1,0:T(8,128)S(1)}, f32[5,32,128]{2,1,0:T(8,128)S(1)}, f32[32,128]{1,0:T(8,128)S(1)}) custom-call(f32[5,32,128]{2,1,0:T(8,128)S(1)} %get-tuple-element.71.refs_0_, f32[5,32,128]{2,1,0:T(8,128)S(1)} %get-tuple-element.72.refs_1_, f32[32,128]{1,0:T(8,128)S(1)} %get-tuple-element.73.refs_2_, ...), custom_call_target="tpu_custom_call" | custom-call | bytes 569400 | tf_op jit(solution)/shard_map/fault/pallas_call | solution.py:562
  41.7 3.0 %collective-permute-start.12 = (f32[5,32,128]{2,1,0:T(8,128)S(1)}, f32[5,32,128]{2,1,0:T(8,128)S(1)}, u32[]{:S(2)}, u32[]{:S(2)}) collective-permute-start(f32[5,32,128]{2,1,0:T(8,128)S(1)} %get-tuple-element.83), channel_id=1, source_target_pairs={{0,4},{4,0},{8,12},{12,8},{1,5},{5,1},{9,13},{13,9},{2,6},{6,2},{1... | collective-permute-start | bytes 245768 | tf_op jit(solution)/shard_map/ppermute | solution.py:591
  44.6 0.7 %collective-permute-start.13 = (f32[5,32,128]{2,1,0:T(8,128)S(1)}, f32[5,32,128]{2,1,0:T(8,128)S(1)}, u32[]{:S(2)}, u32[]{:S(2)}) collective-permute-start(f32[5,32,128]{2,1,0:T(8,128)S(1)} %get-tuple-element.84), channel_id=1, source_target_pairs={{0,0},{4,8},{8,4},{12,12},{1,1},{5,9},{9,5},{13,13},{2,2},{6,10},{... | collective-permute-start | bytes 245768 | tf_op jit(solution)/shard_map/ppermute | solution.py:591
  45.3 0.1 collective-permute-start.11
  45.4 1.2 %collective-permute-done.11.refs_9_.refs_7_ = f32[32,128]{1,0:T(8,128)S(1)} collective-permute-done((f32[32,128]{1,0:T(8,128)S(1)}, f32[32,128]{1,0:T(8,128)S(1)}, u32[]{:S(2)}, u32[]{:S(2)}) %collective-permute-start.11) | collective-permute-done | bytes 16416 | tf_op jit(solution)/shard_map/ppermute | solution.py:591
  46.5 2.9 %stress_inner.3 = (f32[3,16,32,128]{3,2,1,0:T(8,128)S(1)}, f32[6,12,32,128]{3,2,1,0:T(8,128)S(1)}, f32[6,12,32,128]{3,2,1,0:T(8,128)S(1)}, f32[3,16,32,128]{3,2,1,0:T(8,128)}) custom-call(f32[3,12,32,128]{3,2,1,0:T(8,128)S(1)} %get-tuple-element.66.refs_8_.refs_0_, f32[3,4,32,128]{3,2,1,0:T(8,128)S(1)} %get-tuple-element.70.refs_1_, ...), custom_call_target="tpu_custom_call" | custom-call | flops 6553600 | bytes 8159392 | tf_op jit(solution)/shard_map/stress_inner/pallas_call | solution.py:562
  49.5 2.7 %stress_edge.3 = (f32[6,16,32,128]{3,2,1,0:T(8,128)}, f32[6,16,32,128]{3,2,1,0:T(8,128)}) custom-call(f32[3,16,32,128]{3,2,1,0:T(8,128)S(1)} %get-tuple-element.82.refs_0_, f32[6,12,32,128]{3,2,1,0:T(8,128)S(1)} %get-tuple-element.60.refs_8_.refs_1_.refs_3_, f32[6,4,32,128]{3,2,1,0:T(8,128)S(1)} %get-tuple-element.64.refs_2_.refs_4_, ...), custom_call_target="tpu_custom_call" | custom-call | bytes 9879712 | tf_op jit(solution)/shard_map/stress_edge/pallas_call | solution.py:562
  (33 shorter events, 0.1 us)
Async XLA Ops:
  0.6 1.4 %copy-start = (f32[6,16,32,128]{3,2,1,0:T(8,128)S(1)}, f32[6,16,32,128]{3,2,1,0:T(8,128)}, u32[]{:S(2)}) copy-start(f32[6,16,32,128]{3,2,1,0:T(8,128)} %refs_1_.5) | copy-start | bytes 4718596
  2.0 5.6 %copy-start.2 = (s32[16,32,128]{2,1,0:T(8,128)S(1)}, s32[16,32,128]{2,1,0:T(8,128)}, u32[]{:S(2)}) copy-start(s32[16,32,128]{2,1,0:T(8,128)} %refs_5_.7) | copy-start | bytes 786436
  2.0 5.6 %copy-start.4 = (f32[3,16,32,128]{3,2,1,0:T(8,128)S(1)}, f32[3,16,32,128]{3,2,1,0:T(8,128)}, u32[]{:S(2)}) copy-start(f32[3,16,32,128]{3,2,1,0:T(8,128)} %refs_0_.5) | copy-start | bytes 2359300
  2.0 5.6 %copy-start.5 = (f32[5,8]{1,0:T(8,128)S(1)}, f32[5,8]{1,0:T(8,128)}, u32[]{:S(2)}) copy-start(f32[5,8]{1,0:T(8,128)} %refs_6_.7) | copy-start | bytes 484
  2.6 8.9 %copy-start.6 = (f32[8,2,128]{2,1,0:T(2,128)S(1)}, f32[8,2,128]{2,1,0:T(2,128)}, u32[]{:S(2)}) copy-start(f32[8,2,128]{2,1,0:T(2,128)} %refs_9_.1) | copy-start | bytes 24580
  2.6 8.9 %copy-start.8 = (f32[8,128]{1,0:T(8,128)S(1)}, f32[8,128]{1,0:T(8,128)}, u32[]{:S(2)}) copy-start(f32[8,128]{1,0:T(8,128)} %refs_10_.1) | copy-start | bytes 12292
  2.6 8.8 %copy-start.9 = (f32[8,128]{1,0:T(8,128)S(1)}, f32[8,128]{1,0:T(8,128)}, u32[]{:S(2)}) copy-start(f32[8,128]{1,0:T(8,128)} %refs_11_.1) | copy-start | bytes 12292
  2.6 8.8 %copy-start.10 = (s32[8,128]{1,0:T(8,128)S(1)}, s32[8,128]{1,0:T(8,128)}, u32[]{:S(2)}) copy-start(s32[8,128]{1,0:T(8,128)} %refs_12_.1) | copy-start | bytes 12292
  2.6 8.8 %copy-start.11 = (s32[8,128]{1,0:T(8,128)S(1)}, s32[8,128]{1,0:T(8,128)}, u32[]{:S(2)}) copy-start(s32[8,128]{1,0:T(8,128)} %refs_13_.1) | copy-start | bytes 12292
  2.7 8.8 %collective-permute-start.1 = (f32[5,32,128]{2,1,0:T(8,128)S(1)}, f32[5,32,128]{2,1,0:T(8,128)S(1)}, u32[]{:S(2)}, u32[]{:S(2)}) collective-permute-start(f32[5,32,128]{2,1,0:T(8,128)S(1)} %get-tuple-element.49), channel_id=1, source_target_pairs={{0,4},{4,0},{8,12},{12,8},{1,5},{5,1},{9,13},{13,9},{2,6},{6,2},{1... | collective-permute-start | bytes 245768 | tf_op jit(solution)/shard_map/ppermute | solution.py:591
  5.7 5.7 %collective-permute-start.2 = (f32[5,32,128]{2,1,0:T(8,128)S(1)}, f32[5,32,128]{2,1,0:T(8,128)S(1)}, u32[]{:S(2)}, u32[]{:S(2)}) collective-permute-start(f32[5,32,128]{2,1,0:T(8,128)S(1)} %get-tuple-element.50), channel_id=1, source_target_pairs={{0,0},{4,8},{8,4},{12,12},{1,1},{5,9},{9,5},{13,13},{2,2},{6,10},{... | collective-permute-start | bytes 245768 | tf_op jit(solution)/shard_map/ppermute | solution.py:591
  6.4 1.2 %collective-permute-start = (f32[32,128]{1,0:T(8,128)S(1)}, f32[32,128]{1,0:T(8,128)S(1)}, u32[]{:S(2)}, u32[]{:S(2)}) collective-permute-start(f32[32,128]{1,0:T(8,128)S(1)} %get-tuple-element.47), channel_id=1, source_target_pairs={{0,1},{1,0},{2,3},{3,2},{4,5},{5,4},{6,7},{7,6},{8,9},{9,8},{10,11... | collective-permute-start | bytes 49160 | tf_op jit(solution)/shard_map/ppermute | solution.py:591
  11.5 5.4 %copy-start.7 = (f32[3,4]{1,0:T(4,128)S(1)}, f32[3,4]{1,0:T(4,128)}, u32[]{:S(2)}) copy-start(f32[3,4]{1,0:T(4,128)} %refs_5_.6) | copy-start | bytes 148
  11.5 5.4 %copy-start.12 = (s32[2]{0:T(128)S(1)}, s32[2]{0:T(128)}, u32[]{:S(2)}) copy-start(s32[2]{0:T(128)} %refs_6_.6) | copy-start | bytes 28
  11.5 12.5 %copy-start.1 = (f32[6,16,32,128]{3,2,1,0:T(8,128)S(1)}, f32[6,16,32,128]{3,2,1,0:T(8,128)}, u32[]{:S(2)}) copy-start(f32[6,16,32,128]{3,2,1,0:T(8,128)} %refs_1_.5) | copy-start | bytes 4718596
  11.5 12.5 %copy-start.3 = (f32[6,16,32,128]{3,2,1,0:T(8,128)S(1)}, f32[6,16,32,128]{3,2,1,0:T(8,128)}, u32[]{:S(2)}) copy-start(f32[6,16,32,128]{3,2,1,0:T(8,128)} %refs_2_.5) | copy-start | bytes 4718596
  12.8 4.1 %collective-permute-start.3 = (f32[96,128]{1,0:T(8,128)S(1)}, f32[96,128]{1,0:T(8,128)S(1)}, u32[]{:S(2)}, u32[]{:S(2)}) collective-permute-start(f32[96,128]{1,0:T(8,128)S(1)} %get-tuple-element.56.refs_3_.refs_9_), channel_id=1, source_target_pairs={{0,2},{2,0},{1,3},{3,1},{4,6},{6,4},{5,7},{7,5},{8,10},{10,8},{9,1... | collective-permute-start | bytes 147464 | tf_op jit(solution)/shard_map/ppermute | solution.py:591
  17.7 9.2 %collective-permute-start.5 = (f32[5,32,128]{2,1,0:T(8,128)S(1)}, f32[5,32,128]{2,1,0:T(8,128)S(1)}, u32[]{:S(2)}, u32[]{:S(2)}) collective-permute-start(f32[5,32,128]{2,1,0:T(8,128)S(1)} %get-tuple-element.61), channel_id=1, source_target_pairs={{0,4},{4,0},{8,12},{12,8},{1,5},{5,1},{9,13},{13,9},{2,6},{6,2},{1... | collective-permute-start | bytes 245768 | tf_op jit(solution)/shard_map/ppermute | solution.py:591
  22.1 4.7 %collective-permute-start.6 = (f32[5,32,128]{2,1,0:T(8,128)S(1)}, f32[5,32,128]{2,1,0:T(8,128)S(1)}, u32[]{:S(2)}, u32[]{:S(2)}) collective-permute-start(f32[5,32,128]{2,1,0:T(8,128)S(1)} %get-tuple-element.62), channel_id=1, source_target_pairs={{0,0},{4,8},{8,4},{12,12},{1,1},{5,9},{9,5},{13,13},{2,2},{6,10},{... | collective-permute-start | bytes 245768 | tf_op jit(solution)/shard_map/ppermute | solution.py:591
  22.8 1.2 %collective-permute-start.4 = (f32[32,128]{1,0:T(8,128)S(1)}, f32[32,128]{1,0:T(8,128)S(1)}, u32[]{:S(2)}, u32[]{:S(2)}) collective-permute-start(f32[32,128]{1,0:T(8,128)S(1)} %get-tuple-element.58), channel_id=1, source_target_pairs={{0,1},{1,0},{2,3},{3,2},{4,5},{5,4},{6,7},{7,6},{8,9},{9,8},{10,11... | collective-permute-start | bytes 49160 | tf_op jit(solution)/shard_map/ppermute | solution.py:591
  28.1 7.3 %collective-permute-start.8 = (f32[5,32,128]{2,1,0:T(8,128)S(1)}, f32[5,32,128]{2,1,0:T(8,128)S(1)}, u32[]{:S(2)}, u32[]{:S(2)}) collective-permute-start(f32[5,32,128]{2,1,0:T(8,128)S(1)} %get-tuple-element.67), channel_id=1, source_target_pairs={{0,4},{4,0},{8,12},{12,8},{1,5},{5,1},{9,13},{13,9},{2,6},{6,2},{1... | collective-permute-start | bytes 245768 | tf_op jit(solution)/shard_map/ppermute | solution.py:591
  29.7 5.7 %collective-permute-start.9 = (f32[5,32,128]{2,1,0:T(8,128)S(1)}, f32[5,32,128]{2,1,0:T(8,128)S(1)}, u32[]{:S(2)}, u32[]{:S(2)}) collective-permute-start(f32[5,32,128]{2,1,0:T(8,128)S(1)} %get-tuple-element.68), channel_id=1, source_target_pairs={{0,0},{4,8},{8,4},{12,12},{1,1},{5,9},{9,5},{13,13},{2,2},{6,10},{... | collective-permute-start | bytes 245768 | tf_op jit(solution)/shard_map/ppermute | solution.py:591
  30.4 1.2 %collective-permute-start.7 = (f32[32,128]{1,0:T(8,128)S(1)}, f32[32,128]{1,0:T(8,128)S(1)}, u32[]{:S(2)}, u32[]{:S(2)}) collective-permute-start(f32[32,128]{1,0:T(8,128)S(1)} %get-tuple-element.65), channel_id=1, source_target_pairs={{0,1},{1,0},{2,3},{3,2},{4,5},{5,4},{6,7},{7,6},{8,9},{9,8},{10,11... | collective-permute-start | bytes 49160 | tf_op jit(solution)/shard_map/ppermute | solution.py:591
  36.6 3.8 %collective-permute-start.10 = (f32[32,128]{1,0:T(8,128)S(1)}, f32[32,128]{1,0:T(8,128)S(1)}, u32[]{:S(2)}, u32[]{:S(2)}) collective-permute-start(f32[32,128]{1,0:T(8,128)S(1)} %get-tuple-element.74.refs_3_), channel_id=1, source_target_pairs={{0,2},{2,0},{1,3},{3,1},{4,6},{6,4},{5,7},{7,5},{8,10},{10,8},{9,1... | collective-permute-start | bytes 49160 | tf_op jit(solution)/shard_map/ppermute | solution.py:591
  41.7 7.8 %collective-permute-start.12 = (f32[5,32,128]{2,1,0:T(8,128)S(1)}, f32[5,32,128]{2,1,0:T(8,128)S(1)}, u32[]{:S(2)}, u32[]{:S(2)}) collective-permute-start(f32[5,32,128]{2,1,0:T(8,128)S(1)} %get-tuple-element.83), channel_id=1, source_target_pairs={{0,4},{4,0},{8,12},{12,8},{1,5},{5,1},{9,13},{13,9},{2,6},{6,2},{1... | collective-permute-start | bytes 245768 | tf_op jit(solution)/shard_map/ppermute | solution.py:591
  44.6 4.9 %collective-permute-start.13 = (f32[5,32,128]{2,1,0:T(8,128)S(1)}, f32[5,32,128]{2,1,0:T(8,128)S(1)}, u32[]{:S(2)}, u32[]{:S(2)}) collective-permute-start(f32[5,32,128]{2,1,0:T(8,128)S(1)} %get-tuple-element.84), channel_id=1, source_target_pairs={{0,0},{4,8},{8,4},{12,12},{1,1},{5,9},{9,5},{13,13},{2,2},{6,10},{... | collective-permute-start | bytes 245768 | tf_op jit(solution)/shard_map/ppermute | solution.py:591
  45.3 1.2 %collective-permute-start.11 = (f32[32,128]{1,0:T(8,128)S(1)}, f32[32,128]{1,0:T(8,128)S(1)}, u32[]{:S(2)}, u32[]{:S(2)}) collective-permute-start(f32[32,128]{1,0:T(8,128)S(1)} %get-tuple-element.80), channel_id=1, source_target_pairs={{0,1},{1,0},{2,3},{3,2},{4,5},{5,4},{6,7},{7,6},{8,9},{9,8},{10,11... | collective-permute-start | bytes 49160 | tf_op jit(solution)/shard_map/ppermute | solution.py:591

commit v5 on v4

--- a/solution.py
+++ b/solution.py
@@ -1,5 +1,4 @@
 import functools
-import math
 import types
 
 import jax
@@ -18,6 +17,7 @@
 FAR = -1.0 / 24.0
 DT = 0.15
 TILE = 8
+STRIP_PLANES = 6
 
 XX, YY, ZZ, XY, XZ, YZ = range(6)
 
@@ -42,7 +42,7 @@
 
 
 class Edges:
-    def __init__(self, rows, depths):
+    def __init__(self, rows, depths, by_loads=False):
         self.rows = rows
         self.depths = depths
         lane = lax.broadcasted_iota(jnp.int32, (rows, depths), 1)
@@ -50,8 +50,10 @@
         self.row = lax.broadcasted_iota(jnp.int32, (rows, depths), 0)
         self.tile_row = row
         self.deep = lax.axis_index("gz")
-        self.upper = jnp.where(self.deep == 0, 1.0, 0.0)
+        near = (self.deep == 0) & (lane < 2) | (self.deep == 1) & (lane >= depths - 2)
+        self.near = jnp.where(near, 1.0, 0.0)
         self.zero = jnp.minimum(self.deep, 0)
+        self.by_loads = by_loads
         self.pair = lane // 2
         self.low = {n: lane < n for n in (1, 2)}
         self.high = {n: lane >= depths - n for n in (1, 2)}
@@ -68,8 +70,7 @@
     def ends(self, strip, x, k):
         back = self.depths - 8 * x - 2 * k
         turn = jnp.where(self.deep == 0, back % self.depths, back - 2)
-        halo = pltpu.roll(strip, turn, 1)
-        return halo * self.upper, halo * (1.0 - self.upper)
+        return pltpu.roll(strip, turn, 1) * self.near
 
     def shallower(self, field, halo, n):
         return pltpu.roll(jnp.where(self.high[n], halo, field), n, 1)
@@ -77,22 +78,20 @@
     def deeper(self, field, halo, n):
         return pltpu.roll(jnp.where(self.low[n], halo, field), self.depths - n, 1)
 
-    def forward_z(self, field, halos):
-        after, before = halos
+    def forward_z(self, field, halo):
         return forward(
-            self.shallower(field, before, 1),
+            self.shallower(field, halo, 1),
             field,
-            self.deeper(field, after, 1),
-            self.deeper(field, after, 2),
-        )
-
-    def backward_z(self, field, halos):
-        after, before = halos
+            self.deeper(field, halo, 1),
+            self.deeper(field, halo, 2),
+        )
+
+    def backward_z(self, field, halo):
         return backward(
-            self.shallower(field, before, 2),
-            self.shallower(field, before, 1),
+            self.shallower(field, halo, 2),
+            self.shallower(field, halo, 1),
             field,
-            self.deeper(field, after, 1),
+            self.deeper(field, halo, 1),
         )
 
     def before(self, field, load, n, halo):
@@ -100,7 +99,11 @@
         if halo:
             for i in range(n):
                 top = jnp.where(self.tile_row == i, halo[n - 1 - i], top)
-        return jnp.concatenate([top, load(self.zero + (TILE - n), self.rows - TILE)], axis=0)
+        if load:
+            rest = load(self.zero + (TILE - n), self.rows - TILE)
+        else:
+            rest = pltpu.roll(field, n, 0)[TILE:]
+        return jnp.concatenate([top, rest], axis=0)
 
     def after(self, field, load, n, halo):
         bottom = pltpu.roll(field[self.rows - TILE :], TILE - n, 0)
@@ -108,10 +111,15 @@
         if halo:
             for i in range(n):
                 bottom = jnp.where(self.tile_row == TILE - n + i, halo[i], bottom)
-        return jnp.concatenate([load(self.zero + n, self.rows - TILE), bottom], axis=0)
+        if load:
+            rest = load(self.zero + n, self.rows - TILE)
+        else:
+            rest = pltpu.roll(field, self.rows - n, 0)[: self.rows - TILE]
+        return jnp.concatenate([rest, bottom], axis=0)
 
     def forward_y(self, planes, comp, x, halos):
-        field, load = planes(comp, x), planes.rows(comp, x)
+        field = planes(comp, x)
+        load = planes.rows(comp, x) if self.by_loads else None
         lower, upper = halos
         return forward(
             self.before(field, load, 1, lower),
@@ -121,7 +129,8 @@
         )
 
     def backward_y(self, planes, comp, x, halos):
-        field, load = planes(comp, x), planes.rows(comp, x)
+        field = planes(comp, x)
+        load = planes.rows(comp, x) if self.by_loads else None
         lower, upper = halos
         return backward(
             self.before(field, load, 2, lower),
@@ -258,46 +267,70 @@
     strip = jnp.zeros((rows, depths), jnp.float32)
     for x in range(count):
         strip = edges.packed(strip, x, [r.held[c, x] for c in STRESS_SLOTS])
-    r.strip_out[...] = strip
+    set_strip(r, strip)
+
+
+def grouped(xs, size):
+    return [xs[i : i + size] for i in range(0, len(xs), size)]
+
+
+def set_strip(r, strip):
+    r.strip_out[0] = strip
+    for i in range(1, STRIP_PLANES):
+        r.strip_out[i] = jnp.zeros_like(strip)
+
+
+def unpack(r, xs, edges):
+    strip = r.strip[0]
+    for i, x in enumerate(xs):
+        for k in range(3):
+            r.ends[i, k] = edges.ends(strip, x, k)
 
 
 def velocity_planes(r, xs, edges, planes, write):
     band = Bands(getattr(r, "lower", None), getattr(r, "upper", None), STRESS_TAIL_Y, STRESS_HEAD_Y)
-    strip = r.strip[...]
-    for x in xs:
+    unpack(r, xs, edges)
+
+    def new(x):
         push = DT * looked_up(r.material[x], r.table, 2, CLASSES)
+        ends = [r.ends[xs.index(x), k] for k in range(3)]
         along_x = (
             planes.forward_x(XX, x)
             + edges.backward_y(planes, XY, x, band(XY, x))
-            + edges.backward_z(planes(XZ, x), edges.ends(strip, x, 0))
+            + edges.backward_z(planes(XZ, x), ends[0])
         )
         along_y = (
             planes.backward_x(XY, x)
             + edges.forward_y(planes, YY, x, band(YY, x))
-            + edges.backward_z(planes(YZ, x), edges.ends(strip, x, 1))
+            + edges.backward_z(planes(YZ, x), ends[1])
         )
         along_z = (
             planes.backward_x(XZ, x)
             + edges.backward_y(planes, YZ, x, band(YZ, x))
-            + edges.forward_z(planes(ZZ, x), edges.ends(strip, x, 2))
+            + edges.forward_z(planes(ZZ, x), ends[2])
         )
         rates = (along_x, along_y, along_z)
-        write(x, [r.velocity[c, x] + push * rate for c, rate in enumerate(rates)])
+        return [r.velocity[c, x] + push * rate for c, rate in enumerate(rates)]
+
+    for group in grouped(xs, 3 if len(xs) % 3 == 0 else 2):
+        for x, values in [(x, new(x)) for x in group]:
+            write(x, values)
 
 
 def velocity_inner(r):
     count, rows, depths = r.material.shape
     edges = Edges(rows, depths)
     planes = Planes(stress_of(r), STRESS_TAIL, STRESS_HEAD)
-    packed = [jnp.zeros((rows, depths), jnp.float32)]
 
     def write(x, new):
         for c in range(3):
             r.inner_out[c, x - 2] = new[c]
-        packed[0] = edges.packed(packed[0], x, new)
 
     velocity_planes(r, inside(count), edges, planes, write)
-    r.strip_inner_out[...] = packed[0]
+    strip = jnp.zeros((rows, depths), jnp.float32)
+    for x in inside(count):
+        strip = edges.packed(strip, x, [r.inner_out[c, x - 2] for c in VEL_SLOTS])
+    r.strip_inner_out[...] = strip
 
 
 def velocity_edge(first, r):
@@ -323,15 +356,16 @@
         for i, field in enumerate((r.normal, r.slip, r.zone, r.mask)):
             r.face_out[pl.ds(place + (2 + i) * own, own), :] = field[...].astype(jnp.float32)
 
-    packed = [r.strip_inner[...]]
 
     def write(x, new):
         for c in range(3):
             r.edge_out[c, places.index(x)] = new[c]
-        packed[0] = edges.packed(packed[0], x, new)
 
     velocity_planes(r, places, edges, planes, write)
-    r.strip_out[...] = packed[0]
+    strip = r.strip_inner[...]
+    for i, x in enumerate(places):
+        strip = edges.packed(strip, x, [r.edge_out[c, i] for c in VEL_SLOTS])
+    set_strip(r, strip)
     for x in places:
         r.face_out[pl.ds(x, 1), :] = r.edge_out[0, places.index(x), row, :]
         r.face_out[pl.ds(count + x, 1), :] = r.edge_out[2, places.index(x), row, :]
@@ -356,7 +390,7 @@
 def fault_kernel(first, r):
     own_face, other_face = r.face, r.other
     own_first, other_first = (own_face, other_face) if first else (r.face_first, r.other_first)
-    rows, depths = r.strip.shape
+    rows, depths = r.strip.shape[1:]
     count = r.change_out.shape[1]
     middle = lax.axis_size("gy") // 2
     side = lax.axis_index("gy")
@@ -435,15 +469,16 @@
         turned = pltpu.roll(turned, 2 * k, 1, stride=8, stride_axis=0)
         ends = jnp.where(pair == place + k, turned, ends)
     line = jnp.sum(ends, axis=0, keepdims=True)
-    r.strip_out[...] = r.strip[...] + jnp.where(on_fault, line, 0.0)
+    set_strip(r, r.strip[0] + jnp.where(on_fault, line, 0.0))
 
 
 def stress_planes(r, xs, edges, planes, write):
     band = Bands(getattr(r, "lower", None), getattr(r, "upper", None), VEL_TAIL_Y, VEL_HEAD_Y)
     stress, memory = stress_of(r), memory_of(r)
-    strip = r.strip[...]
-    for x in xs:
-        in_x, in_y, in_z = [edges.ends(strip, x, k) for k in range(3)]
+    unpack(r, xs, edges)
+
+    def rates(x):
+        in_x, in_y, in_z = [r.ends[xs.index(x), k] for k in range(3)]
         exx = planes.backward_x(0, x)
         eyy = edges.backward_y(planes, 1, x, band(1, x))
         ezz = edges.backward_z(planes(2, x), in_z)
@@ -451,13 +486,10 @@
         exz = edges.forward_z(planes(0, x), in_x) + planes.forward_x(2, x)
         eyz = edges.forward_z(planes(1, x), in_y) + edges.forward_y(planes, 2, x, band(2, x))
         labels = r.material[x]
-        lame = looked_up(labels, r.table, 0, CLASSES)
+        bulk = looked_up(labels, r.table, 0, CLASSES) * (exx + eyy + ezz)
         shear = looked_up(labels, r.table, 1, CLASSES)
-        decay = jnp.exp(-DT / looked_up(labels, r.table, 3, CLASSES))
-        gain = (1.0 - decay) * (0.3 * looked_up(labels, r.table, 4, CLASSES))
-        bulk = lame * (exx + eyy + ezz)
         double = 2.0 * shear
-        elastic = (
+        return (
             bulk + double * exx,
             bulk + double * eyy,
             bulk + double * ezz,
@@ -465,14 +497,22 @@
             shear * exz,
             shear * eyz,
         )
+
+    def new(x, elastic):
+        labels = r.material[x]
+        decay = jnp.exp(-DT / looked_up(labels, r.table, 3, CLASSES))
+        gain = (1.0 - decay) * (0.3 * looked_up(labels, r.table, 4, CLASSES))
         kept = [decay * memory(c, x) - gain * elastic[c] for c in range(6)]
-        new = [stress(c, x) + DT * (elastic[c] + kept[c]) for c in range(6)]
-        write(x, new, kept)
+        return [stress(c, x) + DT * (elastic[c] + kept[c]) for c in range(6)], kept
+
+    for group in grouped(xs, 2):
+        for x, elastic in [(x, rates(x)) for x in group]:
+            write(x, *new(x, elastic))
 
 
 def stress_inner(last, r):
     count, rows, depths = r.material.shape
-    edges = Edges(rows, depths)
+    edges = Edges(rows, depths, by_loads=True)
     on_fault = edges.row == fault_row(rows)
     free = Field(count, r.inner, r.edge)
     for x in range(count):
@@ -481,7 +521,6 @@
             r.velocity_out[c, x] = free(c, x) + jnp.where(on_fault, line, 0.0)
         r.velocity_out[1, x] = free(1, x)
     planes = Planes(Field(count, r.velocity_out), VEL_TAIL, VEL_HEAD)
-    packed = [jnp.zeros((rows, depths), jnp.float32)]
     if last:
         velocity_copy = pltpu.make_async_copy(
             r.velocity_out, r.new_velocity_out, r.sems.at[0]
@@ -492,19 +531,20 @@
         for c in range(6):
             r.stress_inner_out[c, x - 2] = new[c]
             r.memory_inner_out[c, x - 2] = kept[c]
-        if not last:
-            packed[0] = edges.packed(packed[0], x, [new[c] for c in STRESS_SLOTS])
 
     stress_planes(r, inside(count), edges, planes, write)
     if last:
         velocity_copy.wait()
     else:
-        r.strip_inner_out[...] = packed[0]
+        strip = jnp.zeros((rows, depths), jnp.float32)
+        for x in inside(count):
+            strip = edges.packed(strip, x, [r.stress_inner_out[c, x - 2] for c in STRESS_SLOTS])
+        r.strip_inner_out[...] = strip
 
 
 def stress_edge(last, r):
     count, rows, depths = r.material.shape
-    edges = Edges(rows, depths)
+    edges = Edges(rows, depths, by_loads=True)
     planes = Planes(Field(count, r.velocity), VEL_TAIL, VEL_HEAD, r.one, r.two)
     places = ends_of(count)
     copies = []
@@ -520,14 +560,11 @@
         stress_out, memory_out = r.stress_held, r.memory_held
     else:
         stress_out, memory_out = r.stress_edge_out, r.memory_edge_out
-        packed = [r.strip_inner[...]]
 
     def write(x, new, kept):
         for c in range(6):
             stress_out[c, places.index(x)] = new[c]
             memory_out[c, places.index(x)] = kept[c]
-        if not last:
-            packed[0] = edges.packed(packed[0], x, [new[c] for c in STRESS_SLOTS])
 
     stress_planes(r, places, edges, planes, write)
     if last:
@@ -537,7 +574,10 @@
         for copy in copies:
             copy.wait()
     else:
-        r.strip_out[...] = packed[0]
+        strip = r.strip_inner[...]
+        for i, x in enumerate(places):
+            strip = edges.packed(strip, x, [stress_out[c, i] for c in STRESS_SLOTS])
+        set_strip(r, strip)
         new = Field(count, r.new_stress_inner, stress_out)
         edge_planes(new, STRESS_TAIL, STRESS_HEAD, r.one_out, r.two_out)
 
@@ -545,7 +585,7 @@
 SCALARS = ("table", "friction", "anchor")
 
 
-def call(kernel, name, ins, outs, scratch=None, apart=(), cost=0, vmem=6):
+def call(kernel, name, ins, outs, scratch=None, apart=(), micros=1, vmem=6):
     scratch = scratch or {}
     names = [*ins, *(f"{key}_out" for key in outs), *scratch]
 
@@ -558,7 +598,6 @@
         return pl.BlockSpec(memory_space=pltpu.SMEM if key in SCALARS else pltpu.VMEM)
 
     shapes = [jax.ShapeDtypeStruct(shape, jnp.float32) for shape in outs.values()]
-    moved = 4 * (sum(a.size for a in ins.values()) + sum(math.prod(o.shape) for o in shapes))
     result = pl.pallas_call(
         body,
         out_shape=shapes,
@@ -566,7 +605,9 @@
         out_specs=[place(f"{key}_out") for key in outs],
         scratch_shapes=list(scratch.values()),
         name=name,
-        cost_estimate=pl.CostEstimate(flops=cost, bytes_accessed=moved, transcendentals=0),
+        cost_estimate=pl.CostEstimate(
+            flops=0, bytes_accessed=micros * 3_690_000, transcendentals=0
+        ),
         compiler_params=pltpu.CompilerParams(vmem_limit_bytes=vmem * 2**20),
     )(*ins.values())
     return dict(zip(outs, result))
@@ -621,7 +662,6 @@
     sides = lax.axis_size("gy")
     middle = sides // 2
     banded = sides > 2
-    cells = count * rows * depths
     swaps = strike_swaps(lax.axis_size("gx"))
     up_y, down_y = along("gy", sides, (middle - 1,))
     across = ("gy", [(middle - 1, middle), (middle, middle - 1)])
@@ -629,14 +669,16 @@
 
     plane = (rows, depths)
     edge_shape = (max(len(STRESS_TAIL), len(STRESS_HEAD)), *plane)
-    travelling = {"one": edge_shape, "two": edge_shape, "strip": plane}
+    travelling = {"one": edge_shape, "two": edge_shape, "strip": (STRIP_PLANES, *plane)}
     inner, edge = (count - 4, *plane), (4, *plane)
+    inner_ends = {"ends": pltpu.VMEM((count - 4, 3, *plane), jnp.float32)}
+    edge_ends = {"ends": pltpu.VMEM((4, 3, *plane), jnp.float32)}
 
     def travelled(packed):
         two = sent(packed["two"], swaps[1])
         one = sent(packed["one"], swaps[0])
         strip = sent(packed["strip"], deep)
-        return {"strip": strip}, {"one": one, "two": two}
+        return {"strip": strip}, {"two": two, "one": one}
 
     def bands(field, tail, head):
         if not banded:
@@ -682,7 +724,8 @@
             "velocity_inner",
             ins,
             {"inner": (3, *inner), "strip_inner": plane},
-            cost=60 * cells,
+            scratch=inner_ends,
+            micros=3,
         )
         face_rows = 2 * count
         ins = {**ins, **halos, **free}
@@ -697,7 +740,7 @@
             "velocity_edge",
             ins,
             {"edge": (3, *edge), "face": (face_rows, depths), **travelling},
-            cost=20 * cells,
+            scratch=edge_ends,
         )
         free = {"inner": free["inner"], "edge": packed["edge"]}
         face = packed["face"]
@@ -727,10 +770,11 @@
         else:
             band = {}
         outs = {"velocity": velocity.shape, "stress_inner": (6, *inner), "memory_inner": (6, *inner)}
-        extra = {}
+        extra = {"scratch": inner_ends}
         if last:
             outs["new_velocity"] = velocity.shape
-            extra = {"scratch": {"sems": pltpu.SemaphoreType.DMA((1,))}, "apart": ("new_velocity_out",)}
+            extra["scratch"] = {"sems": pltpu.SemaphoreType.DMA((1,)), **inner_ends}
+            extra["apart"] = ("new_velocity_out",)
         else:
             outs["strip_inner"] = plane
         done = call(
@@ -738,8 +782,8 @@
             "stress_inner",
             {**ins, **band},
             outs,
-            cost=100 * cells,
-            vmem=10,
+            micros=3,
+            vmem=11,
             **extra,
         )
         velocity = done["velocity"]
@@ -757,6 +801,7 @@
                     "stress_held": held,
                     "memory_held": held,
                     "sems": pltpu.SemaphoreType.DMA((6,)),
+                    **edge_ends,
                 },
                 apart=("stress_out", "memory_out"),
                 vmem=10,
@@ -770,7 +815,7 @@
                 "stress_edge",
                 ins,
                 {"stress_edge": (6, *edge), "memory_edge": (6, *edge), **travelling},
-                cost=30 * cells,
+                scratch=edge_ends,
                 vmem=10,
             )
             parts = {

time: 52.5 us -> 50.7 us (0.966)
  Pallas kernels: 22.2 us -> 16.6 us
  starting transfers between devices: 18.1 us -> 23.5 us
  waiting for transfers between devices: 9.58 us -> 8.04 us
    pallas_call x11, Pallas kernels: 22.2 us -> 16.6 us  [call(): pl.pallas_call(body, out_shape=shapes, in_specs=[place(key) for key in in...]
    ppermute x14, starting transfers between devices: 18.1 us -> 23.5 us  [sent(): return lax.ppermute(block, *route)]
    ppermute x14, waiting for transfers between devices: 9.58 us -> 8.04 us  [sent(): return lax.ppermute(block, *route)]
  transfers between devices with their start and end apart: 14 -> 14, of which waited for: 6 -> 5; matrix products, arithmetic and copies ran while one was open for 0% -> 0% of each run, Pallas kernels for 25% -> 16%
where the time goes in v5:
time: 50.7 us; the launch traced here: 50.5 us
  starting transfers between devices  23.5 us (46%)
  Pallas kernels  16.6 us (33%)
  waiting for transfers between devices  8.04 us (16%)
  local copies, waits for them, and re-layouts  1.47 us (3%)
  between operations  0.88 us (2%)
    ppermute x14, starting transfers between devices, sent(): return lax.ppermute(block, *route)  23.5 us
    pallas_call x11, Pallas kernels, call(): pl.pallas_call(body, out_shape=shapes, in_specs=[place(key) for key in in...  16.6 us
    ppermute x14, waiting for transfers between devices, sent(): return lax.ppermute(block, *route)  8.04 us
    unnamed x26, local copies, waits for them, and re-layouts  1.47 us
  transfers between devices with their start and end apart: 14, of which 5 were waited for; matrix products, arithmetic and copies ran while one was open for 0% of the time, Pallas kernels for 16%

profile of v5, /device:TPU:0, one launch (start us, length us, event | category | flops | bytes accessed | tf_op | source)
XLA Modules:
  0.0 50.5 jit_solution(5845196429378691270)
XLA Ops:
  0.6 0.0 copy-start
  0.6 1.4 %copy-done = f32[6,16,32,128]{3,2,1,0:T(8,128)S(1)} copy-done((f32[6,16,32,128]{3,2,1,0:T(8,128)S(1)}, f32[6,16,32,128]{3,2,1,0:T(8,128)}, u32[]{:S(2)}) %copy-start) | copy-done | bytes 1572888
  2.0 0.5 %pack.1 = (f32[5,32,128]{2,1,0:T(8,128)S(1)}, f32[5,32,128]{2,1,0:T(8,128)S(1)}, f32[6,32,128]{2,1,0:T(8,128)S(1)}) custom-call(f32[6,16,32,128]{3,2,1,0:T(8,128)S(1)} %copy-done), custom_call_target="tpu_custom_call" | custom-call | bytes 3690000 | tf_op jit(solution)/shard_map/pack/pallas_call | solution.py:601
  2.6 0.0 copy-start.9
  2.7 0.5 %collective-permute-start = (f32[6,32,128]{2,1,0:T(8,128)S(1)}, f32[6,32,128]{2,1,0:T(8,128)S(1)}, u32[]{:S(2)}, u32[]{:S(2)}) collective-permute-start(f32[6,32,128]{2,1,0:T(8,128)S(1)} %get-tuple-element.47), channel_id=1, source_target_pairs={{0,1},{1,0},{2,3},{3,2},{4,5},{5,4},{6,7},{7,6},{8,9},{9,8},{10,11... | collective-permute-start | bytes 294920 | tf_op jit(solution)/shard_map/ppermute | solution.py:632
  3.2 0.7 %collective-permute-start.1 = (f32[5,32,128]{2,1,0:T(8,128)S(1)}, f32[5,32,128]{2,1,0:T(8,128)S(1)}, u32[]{:S(2)}, u32[]{:S(2)}) collective-permute-start(f32[5,32,128]{2,1,0:T(8,128)S(1)} %get-tuple-element.49), channel_id=1, source_target_pairs={{0,0},{4,8},{8,4},{12,12},{1,1},{5,9},{9,5},{13,13},{2,2},{6,10},{... | collective-permute-start | bytes 245768 | tf_op jit(solution)/shard_map/ppermute | solution.py:632
  3.8 5.5 %collective-permute-start.2 = (f32[5,32,128]{2,1,0:T(8,128)S(1)}, f32[5,32,128]{2,1,0:T(8,128)S(1)}, u32[]{:S(2)}, u32[]{:S(2)}) collective-permute-start(f32[5,32,128]{2,1,0:T(8,128)S(1)} %get-tuple-element.50), channel_id=1, source_target_pairs={{0,4},{4,0},{8,12},{12,8},{1,5},{5,1},{9,13},{13,9},{2,6},{6,2},{1... | collective-permute-start | bytes 245768 | tf_op jit(solution)/shard_map/ppermute | solution.py:632
  9.3 1.6 %velocity_inner.2 = (f32[3,12,32,128]{3,2,1,0:T(8,128)S(1)}, f32[32,128]{1,0:T(8,128)S(1)}) custom-call(f32[3,16,32,128]{3,2,1,0:T(8,128)S(1)} %copy-done.4, f32[6,16,32,128]{3,2,1,0:T(8,128)S(1)} %copy-done, s32[16,32,128]{2,1,0:T(8,128)S(1)} %copy-done.2, f32[5,8]{1,0:T(8,128)S(1)} %copy-done.5, f32[6,32,128]{2,1,0:T(8,128)S(1)} %collective-permute-done.refs_4_), custom_call_target="tpu_custom_call" | custom-call | bytes 11070000 | tf_op jit(solution)/shard_map/velocity_inner/pallas_call | solution.py:601
  10.9 1.2 %collective-permute-done.2.refs_6_ = f32[5,32,128]{2,1,0:T(8,128)S(1)} collective-permute-done((f32[5,32,128]{2,1,0:T(8,128)S(1)}, f32[5,32,128]{2,1,0:T(8,128)S(1)}, u32[]{:S(2)}, u32[]{:S(2)}) %collective-permute-start.2) | collective-permute-done | bytes 81952 | tf_op jit(solution)/shard_map/ppermute | solution.py:632
  12.2 1.1 %velocity_edge.2 = (f32[3,4,32,128]{3,2,1,0:T(8,128)S(1)}, f32[96,128]{1,0:T(8,128)S(1)}, f32[5,32,128]{2,1,0:T(8,128)S(1)}, f32[5,32,128]{2,1,0:T(8,128)S(1)}, f32[6,32,128]{2,1,0:T(8,128)S(1)}) custom-call(f32[3,16,32,128]{3,2,1,0:T(8,128)S(1)} %copy-done.4, f32[6,16,32,128]{3,2,1,0:T(8,128)S(1)} %copy-done, s32[16,32,128]{2,1,0:T(8,128)S(1)} %copy-done.2, ...), custom_call_target="tpu_custom_call" | custom-call | bytes 3690000 | tf_op jit(solution)/shard_map/velocity_edge/pallas_call | solution.py:601
  13.3 1.5 %collective-permute-start.3 = (f32[96,128]{1,0:T(8,128)S(1)}, f32[96,128]{1,0:T(8,128)S(1)}, u32[]{:S(2)}, u32[]{:S(2)}) collective-permute-start(f32[96,128]{1,0:T(8,128)S(1)} %get-tuple-element.56.refs_3_.refs_9_), channel_id=1, source_target_pairs={{0,2},{2,0},{1,3},{3,1},{4,6},{6,4},{5,7},{7,5},{8,10},{10,8},{9,1... | collective-permute-start | bytes 147464 | tf_op jit(solution)/shard_map/ppermute | solution.py:632
  14.8 2.6 %collective-permute-done.3.refs_4_.refs_10_ = f32[96,128]{1,0:T(8,128)S(1)} collective-permute-done((f32[96,128]{1,0:T(8,128)S(1)}, f32[96,128]{1,0:T(8,128)S(1)}, u32[]{:S(2)}, u32[]{:S(2)}) %collective-permute-start.3) | collective-permute-done | bytes 49184 | tf_op jit(solution)/shard_map/ppermute | solution.py:632
  17.4 0.8 %fault.2 = (f32[2,16,128]{2,1,0:T(8,128)S(1)}, f32[16,128]{1,0:T(8,128)S(1)}, f32[5,32,128]{2,1,0:T(8,128)S(1)}, f32[5,32,128]{2,1,0:T(8,128)S(1)}, f32[6,32,128...) custom-call(f32[5,32,128]{2,1,0:T(8,128)S(1)} %get-tuple-element.53.refs_0_, f32[5,32,128]{2,1,0:T(8,128)S(1)} %get-tuple-element.54.refs_1_, ...), custom_call_target="tpu_custom_call" | custom-call | bytes 3690000 | tf_op jit(solution)/shard_map/fault/pallas_call | solution.py:601
  18.2 0.1 collective-permute-start.4
  18.3 0.7 %collective-permute-start.5 = (f32[5,32,128]{2,1,0:T(8,128)S(1)}, f32[5,32,128]{2,1,0:T(8,128)S(1)}, u32[]{:S(2)}, u32[]{:S(2)}) collective-permute-start(f32[5,32,128]{2,1,0:T(8,128)S(1)} %get-tuple-element.61), channel_id=1, source_target_pairs={{0,0},{4,8},{8,4},{12,12},{1,1},{5,9},{9,5},{13,13},{2,2},{6,10},{... | collective-permute-start | bytes 245768 | tf_op jit(solution)/shard_map/ppermute | solution.py:632
  18.9 3.5 %collective-permute-start.6 = (f32[5,32,128]{2,1,0:T(8,128)S(1)}, f32[5,32,128]{2,1,0:T(8,128)S(1)}, u32[]{:S(2)}, u32[]{:S(2)}) collective-permute-start(f32[5,32,128]{2,1,0:T(8,128)S(1)} %get-tuple-element.62), channel_id=1, source_target_pairs={{0,4},{4,0},{8,12},{12,8},{1,5},{5,1},{9,13},{13,9},{2,6},{6,2},{1... | collective-permute-start | bytes 245768 | tf_op jit(solution)/shard_map/ppermute | solution.py:632
  22.4 2.1 %stress_inner.2 = (f32[3,16,32,128]{3,2,1,0:T(8,128)S(1)}, f32[6,12,32,128]{3,2,1,0:T(8,128)S(1)}, f32[6,12,32,128]{3,2,1,0:T(8,128)S(1)}, f32[32,128]{1,0:T(8,128)S(1)}) custom-call(f32[3,12,32,128]{3,2,1,0:T(8,128)S(1)} %get-tuple-element.48.refs_7_.refs_0_, f32[3,4,32,128]{3,2,1,0:T(8,128)S(1)} %get-tuple-element.52.refs_1_, ...), custom_call_target="tpu_custom_call" | custom-call | bytes 11070000 | tf_op jit(solution)/shard_map/stress_inner/pallas_call | solution.py:601
  24.5 0.7 %collective-permute-done.6.refs_7_ = f32[5,32,128]{2,1,0:T(8,128)S(1)} collective-permute-done((f32[5,32,128]{2,1,0:T(8,128)S(1)}, f32[5,32,128]{2,1,0:T(8,128)S(1)}, u32[]{:S(2)}, u32[]{:S(2)}) %collective-permute-start.6) | collective-permute-done | bytes 81952 | tf_op jit(solution)/shard_map/ppermute | solution.py:632
  25.3 1.2 %stress_edge.2 = (f32[6,4,32,128]{3,2,1,0:T(8,128)S(1)}, f32[6,4,32,128]{3,2,1,0:T(8,128)S(1)}, f32[5,32,128]{2,1,0:T(8,128)S(1)}, f32[5,32,128]{2,1,0:T(8,128)S(1)}, f32[6,32,128]{2,1,0:T(8,128)S(1)}) custom-call(f32[3,16,32,128]{3,2,1,0:T(8,128)S(1)} %get-tuple-element.59.refs_0_, f32[6,16,32,128]{3,2,1,0:T(8,128)S(1)} %copy-done.1, ...), custom_call_target="tpu_custom_call" | custom-call | bytes 3690000 | tf_op jit(solution)/shard_map/stress_edge/pallas_call | solution.py:601
  26.4 0.1 collective-permute-start.7
  26.5 0.7 %collective-permute-start.8 = (f32[5,32,128]{2,1,0:T(8,128)S(1)}, f32[5,32,128]{2,1,0:T(8,128)S(1)}, u32[]{:S(2)}, u32[]{:S(2)}) collective-permute-start(f32[5,32,128]{2,1,0:T(8,128)S(1)} %get-tuple-element.67), channel_id=1, source_target_pairs={{0,0},{4,8},{8,4},{12,12},{1,1},{5,9},{9,5},{13,13},{2,2},{6,10},{... | collective-permute-start | bytes 245768 | tf_op jit(solution)/shard_map/ppermute | solution.py:632
  27.2 4.6 %collective-permute-start.9 = (f32[5,32,128]{2,1,0:T(8,128)S(1)}, f32[5,32,128]{2,1,0:T(8,128)S(1)}, u32[]{:S(2)}, u32[]{:S(2)}) collective-permute-start(f32[5,32,128]{2,1,0:T(8,128)S(1)} %get-tuple-element.68), channel_id=1, source_target_pairs={{0,4},{4,0},{8,12},{12,8},{1,5},{5,1},{9,13},{13,9},{2,6},{6,2},{1... | collective-permute-start | bytes 245768 | tf_op jit(solution)/shard_map/ppermute | solution.py:632
  31.8 1.6 %velocity_inner.3 = (f32[3,12,32,128]{3,2,1,0:T(8,128)S(1)}, f32[32,128]{1,0:T(8,128)S(1)}) custom-call(f32[3,16,32,128]{3,2,1,0:T(8,128)S(1)} %get-tuple-element.59.refs_0_, f32[6,12,32,128]{3,2,1,0:T(8,128)S(1)} %get-tuple-element.60.refs_8_.refs_1_.refs_3_, f32[6,4,32,128]{3,2,1,0:T(8,128)S(1)} %get-tuple-element.64.refs_2_.refs_4_, ...), custom_call_target="tpu_custom_call" | custom-call | bytes 11070000 | tf_op jit(solution)/shard_map/velocity_inner/pallas_call | solution.py:601
  33.4 1.2 %collective-permute-done.9.refs_7_ = f32[5,32,128]{2,1,0:T(8,128)S(1)} collective-permute-done((f32[5,32,128]{2,1,0:T(8,128)S(1)}, f32[5,32,128]{2,1,0:T(8,128)S(1)}, u32[]{:S(2)}, u32[]{:S(2)}) %collective-permute-start.9) | collective-permute-done | bytes 81952 | tf_op jit(solution)/shard_map/ppermute | solution.py:632
  34.6 1.0 %velocity_edge.3 = (f32[3,4,32,128]{3,2,1,0:T(8,128)S(1)}, f32[32,128]{1,0:T(8,128)S(1)}, f32[5,32,128]{2,1,0:T(8,128)S(1)}, f32[5,32,128]{2,1,0:T(8,128)S(1)}, f32[6,32,128]{2,1,0:T(8,128)S(1)}) custom-call(f32[3,16,32,128]{3,2,1,0:T(8,128)S(1)} %get-tuple-element.59.refs_0_, f32[6,12,32,128]{3,2,1,0:T(8,128)S(1)} %get-tuple-element.60.refs_8_.refs_1_.refs_3_, ...), custom_call_target="tpu_custom_call" | custom-call | bytes 3690000 | tf_op jit(solution)/shard_map/velocity_edge/pallas_call | solution.py:601
  35.6 1.5 %collective-permute-start.10 = (f32[32,128]{1,0:T(8,128)S(1)}, f32[32,128]{1,0:T(8,128)S(1)}, u32[]{:S(2)}, u32[]{:S(2)}) collective-permute-start(f32[32,128]{1,0:T(8,128)S(1)} %get-tuple-element.74.refs_3_), channel_id=1, source_target_pairs={{0,2},{2,0},{1,3},{3,1},{4,6},{6,4},{5,7},{7,5},{8,10},{10,8},{9,1... | collective-permute-start | bytes 49160 | tf_op jit(solution)/shard_map/ppermute | solution.py:632
  37.2 2.3 %collective-permute-done.10.refs_4_ = f32[32,128]{1,0:T(8,128)S(1)} collective-permute-done((f32[32,128]{1,0:T(8,128)S(1)}, f32[32,128]{1,0:T(8,128)S(1)}, u32[]{:S(2)}, u32[]{:S(2)}) %collective-permute-start.10) | collective-permute-done | bytes 16416 | tf_op jit(solution)/shard_map/ppermute | solution.py:632
  39.4 1.3 %fault.3 = (f32[2,16,128]{2,1,0:T(8,128)S(1)}, f32[8,128]{1,0:T(8,128)}, f32[5,32,128]{2,1,0:T(8,128)S(1)}, f32[5,32,128]{2,1,0:T(8,128)S(1)}, f32[6,32,128]{2,1,0:T(8,128)S(1)}) custom-call(f32[5,32,128]{2,1,0:T(8,128)S(1)} %get-tuple-element.71.refs_0_, f32[5,32,128]{2,1,0:T(8,128)S(1)} %get-tuple-element.72.refs_1_, ...), custom_call_target="tpu_custom_call" | custom-call | bytes 3690000 | tf_op jit(solution)/shard_map/fault/pallas_call | solution.py:601
  40.7 0.7 %collective-permute-start.12 = (f32[5,32,128]{2,1,0:T(8,128)S(1)}, f32[5,32,128]{2,1,0:T(8,128)S(1)}, u32[]{:S(2)}, u32[]{:S(2)}) collective-permute-start(f32[5,32,128]{2,1,0:T(8,128)S(1)} %get-tuple-element.83), channel_id=1, source_target_pairs={{0,0},{4,8},{8,4},{12,12},{1,1},{5,9},{9,5},{13,13},{2,2},{6,10},{... | collective-permute-start | bytes 245768 | tf_op jit(solution)/shard_map/ppermute | solution.py:632
  41.4 3.5 %collective-permute-start.13 = (f32[5,32,128]{2,1,0:T(8,128)S(1)}, f32[5,32,128]{2,1,0:T(8,128)S(1)}, u32[]{:S(2)}, u32[]{:S(2)}) collective-permute-start(f32[5,32,128]{2,1,0:T(8,128)S(1)} %get-tuple-element.84), channel_id=1, source_target_pairs={{0,4},{4,0},{8,12},{12,8},{1,5},{5,1},{9,13},{13,9},{2,6},{6,2},{1... | collective-permute-start | bytes 245768 | tf_op jit(solution)/shard_map/ppermute | solution.py:632
  44.9 2.9 %stress_inner.3 = (f32[3,16,32,128]{3,2,1,0:T(8,128)S(1)}, f32[6,12,32,128]{3,2,1,0:T(8,128)S(1)}, f32[6,12,32,128]{3,2,1,0:T(8,128)S(1)}, f32[3,16,32,128]{3,2,1,0:T(8,128)}) custom-call(f32[3,12,32,128]{3,2,1,0:T(8,128)S(1)} %get-tuple-element.66.refs_8_.refs_0_, f32[3,4,32,128]{3,2,1,0:T(8,128)S(1)} %get-tuple-element.70.refs_1_, ...), custom_call_target="tpu_custom_call" | custom-call | bytes 11070000 | tf_op jit(solution)/shard_map/stress_inner/pallas_call | solution.py:601
  47.8 2.7 %stress_edge.3 = (f32[6,16,32,128]{3,2,1,0:T(8,128)}, f32[6,16,32,128]{3,2,1,0:T(8,128)}) custom-call(f32[3,16,32,128]{3,2,1,0:T(8,128)S(1)} %get-tuple-element.82.refs_0_, f32[6,12,32,128]{3,2,1,0:T(8,128)S(1)} %get-tuple-element.60.refs_8_.refs_1_.refs_3_, f32[6,4,32,128]{3,2,1,0:T(8,128)S(1)} %get-tuple-element.64.refs_2_.refs_4_, ...), custom_call_target="tpu_custom_call" | custom-call | bytes 3690000 | tf_op jit(solution)/shard_map/stress_edge/pallas_call | solution.py:601
  (33 shorter events, 0.1 us)
Async XLA Ops:
  0.6 1.4 %copy-start = (f32[6,16,32,128]{3,2,1,0:T(8,128)S(1)}, f32[6,16,32,128]{3,2,1,0:T(8,128)}, u32[]{:S(2)}) copy-start(f32[6,16,32,128]{3,2,1,0:T(8,128)} %refs_1_.5) | copy-start | bytes 4718596
  2.0 7.3 %copy-start.2 = (s32[16,32,128]{2,1,0:T(8,128)S(1)}, s32[16,32,128]{2,1,0:T(8,128)}, u32[]{:S(2)}) copy-start(s32[16,32,128]{2,1,0:T(8,128)} %refs_5_.7) | copy-start | bytes 786436
  2.0 7.3 %copy-start.4 = (f32[3,16,32,128]{3,2,1,0:T(8,128)S(1)}, f32[3,16,32,128]{3,2,1,0:T(8,128)}, u32[]{:S(2)}) copy-start(f32[3,16,32,128]{3,2,1,0:T(8,128)} %refs_0_.5) | copy-start | bytes 2359300
  2.0 7.3 %copy-start.5 = (f32[5,8]{1,0:T(8,128)S(1)}, f32[5,8]{1,0:T(8,128)}, u32[]{:S(2)}) copy-start(f32[5,8]{1,0:T(8,128)} %refs_6_.7) | copy-start | bytes 484
  2.6 9.5 %copy-start.6 = (f32[8,2,128]{2,1,0:T(2,128)S(1)}, f32[8,2,128]{2,1,0:T(2,128)}, u32[]{:S(2)}) copy-start(f32[8,2,128]{2,1,0:T(2,128)} %refs_9_.1) | copy-start | bytes 24580
  2.6 9.5 %copy-start.8 = (f32[8,128]{1,0:T(8,128)S(1)}, f32[8,128]{1,0:T(8,128)}, u32[]{:S(2)}) copy-start(f32[8,128]{1,0:T(8,128)} %refs_10_.1) | copy-start | bytes 12292
  2.6 9.5 %copy-start.9 = (f32[8,128]{1,0:T(8,128)S(1)}, f32[8,128]{1,0:T(8,128)}, u32[]{:S(2)}) copy-start(f32[8,128]{1,0:T(8,128)} %refs_11_.1) | copy-start | bytes 12292
  2.6 9.5 %copy-start.10 = (s32[8,128]{1,0:T(8,128)S(1)}, s32[8,128]{1,0:T(8,128)}, u32[]{:S(2)}) copy-start(s32[8,128]{1,0:T(8,128)} %refs_12_.1) | copy-start | bytes 12292
  2.6 9.5 %copy-start.11 = (s32[8,128]{1,0:T(8,128)S(1)}, s32[8,128]{1,0:T(8,128)}, u32[]{:S(2)}) copy-start(s32[8,128]{1,0:T(8,128)} %refs_13_.1) | copy-start | bytes 12292
  2.7 6.7 %collective-permute-start = (f32[6,32,128]{2,1,0:T(8,128)S(1)}, f32[6,32,128]{2,1,0:T(8,128)S(1)}, u32[]{:S(2)}, u32[]{:S(2)}) collective-permute-start(f32[6,32,128]{2,1,0:T(8,128)S(1)} %get-tuple-element.47), channel_id=1, source_target_pairs={{0,1},{1,0},{2,3},{3,2},{4,5},{5,4},{6,7},{7,6},{8,9},{9,8},{10,11... | collective-permute-start | bytes 294920 | tf_op jit(solution)/shard_map/ppermute | solution.py:632
  3.2 7.7 %collective-permute-start.1 = (f32[5,32,128]{2,1,0:T(8,128)S(1)}, f32[5,32,128]{2,1,0:T(8,128)S(1)}, u32[]{:S(2)}, u32[]{:S(2)}) collective-permute-start(f32[5,32,128]{2,1,0:T(8,128)S(1)} %get-tuple-element.49), channel_id=1, source_target_pairs={{0,0},{4,8},{8,4},{12,12},{1,1},{5,9},{9,5},{13,13},{2,2},{6,10},{... | collective-permute-start | bytes 245768 | tf_op jit(solution)/shard_map/ppermute | solution.py:632
  3.8 8.3 %collective-permute-start.2 = (f32[5,32,128]{2,1,0:T(8,128)S(1)}, f32[5,32,128]{2,1,0:T(8,128)S(1)}, u32[]{:S(2)}, u32[]{:S(2)}) collective-permute-start(f32[5,32,128]{2,1,0:T(8,128)S(1)} %get-tuple-element.50), channel_id=1, source_target_pairs={{0,4},{4,0},{8,12},{12,8},{1,5},{5,1},{9,13},{13,9},{2,6},{6,2},{1... | collective-permute-start | bytes 245768 | tf_op jit(solution)/shard_map/ppermute | solution.py:632
  12.2 5.3 %copy-start.7 = (f32[3,4]{1,0:T(4,128)S(1)}, f32[3,4]{1,0:T(4,128)}, u32[]{:S(2)}) copy-start(f32[3,4]{1,0:T(4,128)} %refs_5_.6) | copy-start | bytes 148
  12.2 5.2 %copy-start.12 = (s32[2]{0:T(128)S(1)}, s32[2]{0:T(128)}, u32[]{:S(2)}) copy-start(s32[2]{0:T(128)} %refs_6_.6) | copy-start | bytes 28
  12.2 10.3 %copy-start.1 = (f32[6,16,32,128]{3,2,1,0:T(8,128)S(1)}, f32[6,16,32,128]{3,2,1,0:T(8,128)}, u32[]{:S(2)}) copy-start(f32[6,16,32,128]{3,2,1,0:T(8,128)} %refs_1_.5) | copy-start | bytes 4718596
  12.2 10.3 %copy-start.3 = (f32[6,16,32,128]{3,2,1,0:T(8,128)S(1)}, f32[6,16,32,128]{3,2,1,0:T(8,128)}, u32[]{:S(2)}) copy-start(f32[6,16,32,128]{3,2,1,0:T(8,128)} %refs_2_.5) | copy-start | bytes 4718596
  13.3 4.1 %collective-permute-start.3 = (f32[96,128]{1,0:T(8,128)S(1)}, f32[96,128]{1,0:T(8,128)S(1)}, u32[]{:S(2)}, u32[]{:S(2)}) collective-permute-start(f32[96,128]{1,0:T(8,128)S(1)} %get-tuple-element.56.refs_3_.refs_9_), channel_id=1, source_target_pairs={{0,2},{2,0},{1,3},{3,1},{4,6},{6,4},{5,7},{7,5},{8,10},{10,8},{9,1... | collective-permute-start | bytes 147464 | tf_op jit(solution)/shard_map/ppermute | solution.py:632
  18.2 4.3 %collective-permute-start.4 = (f32[6,32,128]{2,1,0:T(8,128)S(1)}, f32[6,32,128]{2,1,0:T(8,128)S(1)}, u32[]{:S(2)}, u32[]{:S(2)}) collective-permute-start(f32[6,32,128]{2,1,0:T(8,128)S(1)} %get-tuple-element.58), channel_id=1, source_target_pairs={{0,1},{1,0},{2,3},{3,2},{4,5},{5,4},{6,7},{7,6},{8,9},{9,8},{10,11... | collective-permute-start | bytes 294920 | tf_op jit(solution)/shard_map/ppermute | solution.py:632
  18.3 6.3 %collective-permute-start.5 = (f32[5,32,128]{2,1,0:T(8,128)S(1)}, f32[5,32,128]{2,1,0:T(8,128)S(1)}, u32[]{:S(2)}, u32[]{:S(2)}) collective-permute-start(f32[5,32,128]{2,1,0:T(8,128)S(1)} %get-tuple-element.61), channel_id=1, source_target_pairs={{0,0},{4,8},{8,4},{12,12},{1,1},{5,9},{9,5},{13,13},{2,2},{6,10},{... | collective-permute-start | bytes 245768 | tf_op jit(solution)/shard_map/ppermute | solution.py:632
  18.9 6.3 %collective-permute-start.6 = (f32[5,32,128]{2,1,0:T(8,128)S(1)}, f32[5,32,128]{2,1,0:T(8,128)S(1)}, u32[]{:S(2)}, u32[]{:S(2)}) collective-permute-start(f32[5,32,128]{2,1,0:T(8,128)S(1)} %get-tuple-element.62), channel_id=1, source_target_pairs={{0,4},{4,0},{8,12},{12,8},{1,5},{5,1},{9,13},{13,9},{2,6},{6,2},{1... | collective-permute-start | bytes 245768 | tf_op jit(solution)/shard_map/ppermute | solution.py:632
  26.4 5.4 %collective-permute-start.7 = (f32[6,32,128]{2,1,0:T(8,128)S(1)}, f32[6,32,128]{2,1,0:T(8,128)S(1)}, u32[]{:S(2)}, u32[]{:S(2)}) collective-permute-start(f32[6,32,128]{2,1,0:T(8,128)S(1)} %get-tuple-element.65), channel_id=1, source_target_pairs={{0,1},{1,0},{2,3},{3,2},{4,5},{5,4},{6,7},{7,6},{8,9},{9,8},{10,11... | collective-permute-start | bytes 294920 | tf_op jit(solution)/shard_map/ppermute | solution.py:632
  26.5 6.9 %collective-permute-start.8 = (f32[5,32,128]{2,1,0:T(8,128)S(1)}, f32[5,32,128]{2,1,0:T(8,128)S(1)}, u32[]{:S(2)}, u32[]{:S(2)}) collective-permute-start(f32[5,32,128]{2,1,0:T(8,128)S(1)} %get-tuple-element.67), channel_id=1, source_target_pairs={{0,0},{4,8},{8,4},{12,12},{1,1},{5,9},{9,5},{13,13},{2,2},{6,10},{... | collective-permute-start | bytes 245768 | tf_op jit(solution)/shard_map/ppermute | solution.py:632
  27.2 7.4 %collective-permute-start.9 = (f32[5,32,128]{2,1,0:T(8,128)S(1)}, f32[5,32,128]{2,1,0:T(8,128)S(1)}, u32[]{:S(2)}, u32[]{:S(2)}) collective-permute-start(f32[5,32,128]{2,1,0:T(8,128)S(1)} %get-tuple-element.68), channel_id=1, source_target_pairs={{0,4},{4,0},{8,12},{12,8},{1,5},{5,1},{9,13},{13,9},{2,6},{6,2},{1... | collective-permute-start | bytes 245768 | tf_op jit(solution)/shard_map/ppermute | solution.py:632
  35.6 3.8 %collective-permute-start.10 = (f32[32,128]{1,0:T(8,128)S(1)}, f32[32,128]{1,0:T(8,128)S(1)}, u32[]{:S(2)}, u32[]{:S(2)}) collective-permute-start(f32[32,128]{1,0:T(8,128)S(1)} %get-tuple-element.74.refs_3_), channel_id=1, source_target_pairs={{0,2},{2,0},{1,3},{3,1},{4,6},{6,4},{5,7},{7,5},{8,10},{10,8},{9,1... | collective-permute-start | bytes 49160 | tf_op jit(solution)/shard_map/ppermute | solution.py:632
  40.7 4.2 %collective-permute-start.11 = (f32[6,32,128]{2,1,0:T(8,128)S(1)}, f32[6,32,128]{2,1,0:T(8,128)S(1)}, u32[]{:S(2)}, u32[]{:S(2)}) collective-permute-start(f32[6,32,128]{2,1,0:T(8,128)S(1)} %get-tuple-element.80), channel_id=1, source_target_pairs={{0,1},{1,0},{2,3},{3,2},{4,5},{5,4},{6,7},{7,6},{8,9},{9,8},{10,11... | collective-permute-start | bytes 294920 | tf_op jit(solution)/shard_map/ppermute | solution.py:632
  40.7 7.0 %collective-permute-start.12 = (f32[5,32,128]{2,1,0:T(8,128)S(1)}, f32[5,32,128]{2,1,0:T(8,128)S(1)}, u32[]{:S(2)}, u32[]{:S(2)}) collective-permute-start(f32[5,32,128]{2,1,0:T(8,128)S(1)} %get-tuple-element.83), channel_id=1, source_target_pairs={{0,0},{4,8},{8,4},{12,12},{1,1},{5,9},{9,5},{13,13},{2,2},{6,10},{... | collective-permute-start | bytes 245768 | tf_op jit(solution)/shard_map/ppermute | solution.py:632
  41.4 6.4 %collective-permute-start.13 = (f32[5,32,128]{2,1,0:T(8,128)S(1)}, f32[5,32,128]{2,1,0:T(8,128)S(1)}, u32[]{:S(2)}, u32[]{:S(2)}) collective-permute-start(f32[5,32,128]{2,1,0:T(8,128)S(1)} %get-tuple-element.84), channel_id=1, source_target_pairs={{0,4},{4,0},{8,12},{12,8},{1,5},{5,1},{9,13},{13,9},{2,6},{6,2},{1... | collective-permute-start | bytes 245768 | tf_op jit(solution)/shard_map/ppermute | solution.py:632

commit v6 on v5

--- a/solution.py
+++ b/solution.py
@@ -233,13 +233,16 @@
 
 def edge_planes(field, tail, head, first_out, second_out):
     even = even_strike()
+    pairs = []
     for i in range(first_out.shape[0]):
         comp, place = tail[min(i, len(tail) - 1)]
         right = field(comp, place % field.count)
         comp, place = head[min(i, len(head) - 1)]
         left = field(comp, place % field.count)
-        first_out[i] = jnp.where(even, right, left)
-        second_out[i] = jnp.where(even, left, right)
+        pairs.append((jnp.where(even, right, left), jnp.where(even, left, right)))
+    for i, (one, two) in enumerate(pairs):
+        first_out[i] = one
+        second_out[i] = two
 
 
 def fault_row(rows):
@@ -340,21 +343,20 @@
     fault = fault_row(rows)
     places = ends_of(count)
     row = pl.ds(fault, 1)
-    for x in inside(count):
-        r.face_out[pl.ds(x, 1), :] = r.inner[0, x - 2, row, :]
-        r.face_out[pl.ds(count + x, 1), :] = r.inner[2, x - 2, row, :]
     if first:
-        for x in range(count):
-            labels = r.material[x, row, :]
-            r.face_out[pl.ds(2 * count + x, 1), :] = looked_up(labels, r.table, 2, CLASSES)
+        labels = [r.material[x, row, :] for x in range(count)]
+        lines = [looked_up(label, r.table, 2, CLASSES) for label in labels]
+        for x, line in enumerate(lines):
+            r.face_out[pl.ds(2 * count + x, 1), :] = line
     if hasattr(r, "prestress"):
         own = r.normal.shape[0]
         place = 3 * count
-        for i in range(own):
-            r.face_out[pl.ds(place + i, 1), :] = r.prestress[i, pl.ds(0, 1), :]
-            r.face_out[pl.ds(place + own + i, 1), :] = r.prestress[i, pl.ds(1, 1), :]
-        for i, field in enumerate((r.normal, r.slip, r.zone, r.mask)):
-            r.face_out[pl.ds(place + (2 + i) * own, own), :] = field[...].astype(jnp.float32)
+        lines = [r.prestress[i, pl.ds(c, 1), :] for c in (0, 1) for i in range(own)]
+        fields = [field[...] for field in (r.normal, r.slip, r.zone, r.mask)]
+        for i, line in enumerate(lines):
+            r.face_out[pl.ds(place + i, 1), :] = line
+        for i, field in enumerate(fields):
+            r.face_out[pl.ds(place + (2 + i) * own, own), :] = field.astype(jnp.float32)
 
 
     def write(x, new):
@@ -366,10 +368,10 @@
     for i, x in enumerate(places):
         strip = edges.packed(strip, x, [r.edge_out[c, i] for c in VEL_SLOTS])
     set_strip(r, strip)
-    for x in places:
-        r.face_out[pl.ds(x, 1), :] = r.edge_out[0, places.index(x), row, :]
-        r.face_out[pl.ds(count + x, 1), :] = r.edge_out[2, places.index(x), row, :]
     new = Field(count, r.inner, r.edge_out)
+    lines = [new.rows(c, x)(fault, 1) for c in (0, 2) for x in range(count)]
+    for i, line in enumerate(lines):
+        r.face_out[pl.ds(i, 1), :] = line
     edge_planes(new, VEL_TAIL, VEL_HEAD, r.one_out, r.two_out)
 
 
@@ -435,11 +437,10 @@
     strength = (static - (static - dynamic) * weaken) * normal
     factor = jnp.where(mask == 1.0, strength / jnp.maximum(size, strength), 1.0)
     new_slip = slip + DT * DT * bsum * (size - size * factor)
-    if r.slip_out.shape[0] == count:
-        r.slip_out[...] = new_slip
-    else:
-        half = r.slip_out.shape[0]
-        r.slip_out[...] = jnp.where(plus, new_slip[half:], new_slip[:half])
+    half = r.slip_out.shape[0]
+    if half < count:
+        new_slip = jnp.where(plus, new_slip[half:], new_slip[:half])
+    r.slip_out[...] = new_slip
     sign = jnp.where(minus, DT, 0.0) * minus_b - jnp.where(plus, DT, 0.0) * plus_b
     change_x = (trial_x * factor - pre_x) * sign
     change_z = (trial_z * factor - pre_z) * sign
@@ -455,11 +456,15 @@
         comp, place = planes[min(i, len(planes) - 1)]
         return still_line if comp == 1 else r.change_out[comp // 2, pl.ds(place % count, 1), :]
 
+    pairs = []
     for i in range(r.one_out.shape[0]):
         right, left = line(VEL_TAIL, i), line(VEL_HEAD, i)
         one, two = jnp.where(even, right, left), jnp.where(even, left, right)
-        r.one_out[i] = r.one[i] + jnp.where(on_fault, one, 0.0)
-        r.two_out[i] = r.two[i] + jnp.where(on_fault, two, 0.0)
+        one = r.one[i] + jnp.where(on_fault, one, 0.0)
+        pairs.append((one, r.two[i] + jnp.where(on_fault, two, 0.0)))
+    for i, (one, two) in enumerate(pairs):
+        r.one_out[i] = one
+        r.two_out[i] = two
     ends = jnp.zeros((count, depths), jnp.float32)
     pair = lax.broadcasted_iota(jnp.int32, (count, depths), 1) // 2
     place = 4 * lax.broadcasted_iota(jnp.int32, (count, depths), 0)
@@ -521,20 +526,34 @@
             r.velocity_out[c, x] = free(c, x) + jnp.where(on_fault, line, 0.0)
         r.velocity_out[1, x] = free(1, x)
     planes = Planes(Field(count, r.velocity_out), VEL_TAIL, VEL_HEAD)
+    copies = []
+
+    def copy_out(source, out):
+        copy = pltpu.make_async_copy(source, out, r.sems.at[len(copies)])
+        copy.start()
+        copies.append(copy)
+
     if last:
-        velocity_copy = pltpu.make_async_copy(
-            r.velocity_out, r.new_velocity_out, r.sems.at[0]
-        )
-        velocity_copy.start()
+        copy_out(r.velocity_out, r.new_velocity_out)
+        if hasattr(r, "slip"):
+            copy_out(r.slip, r.new_slip_out)
+        stress_out, memory_out = r.stress_held, r.memory_held
+    else:
+        stress_out, memory_out = r.stress_inner_out, r.memory_inner_out
 
     def write(x, new, kept):
         for c in range(6):
-            r.stress_inner_out[c, x - 2] = new[c]
-            r.memory_inner_out[c, x - 2] = kept[c]
+            stress_out[c, x - 2] = new[c]
+            memory_out[c, x - 2] = kept[c]
+        if last and x % 2 == 1:
+            held, out = pl.ds(x - 3, 2), pl.ds(x - 1, 2)
+            copy_out(stress_out.at[:, held], r.stress_out.at[:, out])
+            copy_out(memory_out.at[:, held], r.memory_out.at[:, out])
 
     stress_planes(r, inside(count), edges, planes, write)
     if last:
-        velocity_copy.wait()
+        for copy in copies:
+            copy.wait()
     else:
         strip = jnp.zeros((rows, depths), jnp.float32)
         for x in inside(count):
@@ -555,8 +574,6 @@
         copies.append(copy)
 
     if last:
-        copy_out(r.new_stress_inner, r.stress_out, pl.ds(2, count - 4))
-        copy_out(r.new_memory_inner, r.memory_out, pl.ds(2, count - 4))
         stress_out, memory_out = r.stress_held, r.memory_held
     else:
         stress_out, memory_out = r.stress_edge_out, r.memory_edge_out
@@ -585,7 +602,7 @@
 SCALARS = ("table", "friction", "anchor")
 
 
-def call(kernel, name, ins, outs, scratch=None, apart=(), micros=1, vmem=6):
+def call(kernel, name, ins, outs, scratch=None, apart=(), onto=(), micros=1, vmem=6):
     scratch = scratch or {}
     names = [*ins, *(f"{key}_out" for key in outs), *scratch]
 
@@ -605,6 +622,9 @@
         out_specs=[place(f"{key}_out") for key in outs],
         scratch_shapes=list(scratch.values()),
         name=name,
+        input_output_aliases={
+            list(ins).index(key): list(outs).index(onto[key]) for key in onto
+        },
         cost_estimate=pl.CostEstimate(
             flops=0, bytes_accessed=micros * 3_690_000, transcendentals=0
         ),
@@ -678,7 +698,7 @@
         two = sent(packed["two"], swaps[1])
         one = sent(packed["one"], swaps[0])
         strip = sent(packed["strip"], deep)
-        return {"strip": strip}, {"two": two, "one": one}
+        return {"strip": strip}, {"one": one, "two": two}
 
     def bands(field, tail, head):
         if not banded:
@@ -769,14 +789,20 @@
             band = bands(joined, VEL_TAIL_Y, VEL_HEAD_Y)
         else:
             band = {}
-        outs = {"velocity": velocity.shape, "stress_inner": (6, *inner), "memory_inner": (6, *inner)}
+        outs = {"velocity": velocity.shape}
         extra = {"scratch": inner_ends}
         if last:
-            outs["new_velocity"] = velocity.shape
-            extra["scratch"] = {"sems": pltpu.SemaphoreType.DMA((1,)), **inner_ends}
-            extra["apart"] = ("new_velocity_out",)
+            outs.update(new_velocity=velocity.shape, stress=stress.shape, memory=memory.shape)
+            extra["apart"] = ["new_velocity_out", "stress_out", "memory_out"]
+            if not banded:
+                ins["slip"] = slip
+                outs["new_slip"] = slip.shape
+                extra["apart"].append("new_slip_out")
+            held = pltpu.VMEM((6, *inner), jnp.float32)
+            sems = pltpu.SemaphoreType.DMA((count,))
+            extra["scratch"] = {"stress_held": held, "memory_held": held, "sems": sems, **inner_ends}
         else:
-            outs["strip_inner"] = plane
+            outs.update(stress_inner=(6, *inner), memory_inner=(6, *inner), strip_inner=plane)
         done = call(
             functools.partial(stress_inner, last),
             "stress_inner",
@@ -788,9 +814,8 @@
         )
         velocity = done["velocity"]
         ins = {"velocity": velocity, **parts, **props, **strip, **halos, **band}
-        ins["new_stress_inner"] = done["stress_inner"]
         if last:
-            ins["new_memory_inner"] = done["memory_inner"]
+            ins.update(stress_done=done["stress"], memory_done=done["memory"])
             held = pltpu.VMEM((6, *edge), jnp.float32)
             packed = call(
                 functools.partial(stress_edge, last),
@@ -800,16 +825,18 @@
                 scratch={
                     "stress_held": held,
                     "memory_held": held,
-                    "sems": pltpu.SemaphoreType.DMA((6,)),
+                    "sems": pltpu.SemaphoreType.DMA((4,)),
                     **edge_ends,
                 },
-                apart=("stress_out", "memory_out"),
+                apart=("stress_done", "memory_done", "stress_out", "memory_out"),
+                onto={"stress_done": "stress", "memory_done": "memory"},
                 vmem=10,
             )
             velocity = done["new_velocity"]
             stress, memory = packed["stress"], packed["memory"]
+            slip = done.get("new_slip", slip)
         else:
-            ins["strip_inner"] = done["strip_inner"]
+            ins.update(new_stress_inner=done["stress_inner"], strip_inner=done["strip_inner"])
             packed = call(
                 functools.partial(stress_edge, last),
                 "stress_edge",

time: 50.7 us -> 46.4 us (0.915)
  starting transfers between devices: 23.5 us -> 21.5 us
  waiting for transfers between devices: 8.04 us -> 6.51 us
  Pallas kernels: 16.6 us -> 15.4 us
    ppermute x14, starting transfers between devices: 23.5 us -> 21.5 us  [sent(): return lax.ppermute(block, *route)]
    ppermute x14, waiting for transfers between devices: 8.04 us -> 6.51 us  [sent(): return lax.ppermute(block, *route)]
    pallas_call x11, Pallas kernels: 16.6 us -> 15.4 us  [call(): pl.pallas_call(body, out_shape=shapes, in_specs=[place(key) for key in in...]
  transfers between devices with their start and end apart: 14 -> 14, of which waited for: 5 -> 5; matrix products, arithmetic and copies ran while one was open for 0% -> 0% of each run, Pallas kernels for 16% -> 18%
where the time goes in v6:
time: 46.4 us; the launch traced here: 45.8 us
  starting transfers between devices  21.5 us (46%)
  Pallas kernels  15.4 us (33%)
  waiting for transfers between devices  6.51 us (14%)
  local copies, waits for them, and re-layouts  1.47 us (3%)
  between operations  0.93 us (2%)
    ppermute x14, starting transfers between devices, sent(): return lax.ppermute(block, *route)  21.5 us
    pallas_call x11, Pallas kernels, call(): pl.pallas_call(body, out_shape=shapes, in_specs=[place(key) for key in in...  15.4 us
    ppermute x14, waiting for transfers between devices, sent(): return lax.ppermute(block, *route)  6.51 us
    unnamed x26, local copies, waits for them, and re-layouts  1.47 us
  transfers between devices with their start and end apart: 14, of which 5 were waited for; matrix products, arithmetic and copies ran while one was open for 0% of the time, Pallas kernels for 18%

profile of v6, /device:TPU:0, one launch (start us, length us, event | category | flops | bytes accessed | tf_op | source)
XLA Modules:
  0.0 45.8 jit_solution(14193969391859353617)
XLA Ops:
  0.6 0.0 copy-start
  0.6 1.4 %copy-done = f32[6,16,32,128]{3,2,1,0:T(8,128)S(1)} copy-done((f32[6,16,32,128]{3,2,1,0:T(8,128)S(1)}, f32[6,16,32,128]{3,2,1,0:T(8,128)}, u32[]{:S(2)}) %copy-start) | copy-done | bytes 1572888
  2.0 0.5 %pack.1 = (f32[5,32,128]{2,1,0:T(8,128)S(1)}, f32[5,32,128]{2,1,0:T(8,128)S(1)}, f32[6,32,128]{2,1,0:T(8,128)S(1)}) custom-call(f32[6,16,32,128]{3,2,1,0:T(8,128)S(1)} %copy-done), custom_call_target="tpu_custom_call" | custom-call | bytes 3690000 | tf_op jit(solution)/shard_map/pack/pallas_call | solution.py:618
  2.7 0.5 %collective-permute-start = (f32[6,32,128]{2,1,0:T(8,128)S(1)}, f32[6,32,128]{2,1,0:T(8,128)S(1)}, u32[]{:S(2)}, u32[]{:S(2)}) collective-permute-start(f32[6,32,128]{2,1,0:T(8,128)S(1)} %get-tuple-element.48), channel_id=1, source_target_pairs={{0,1},{1,0},{2,3},{3,2},{4,5},{5,4},{6,7},{7,6},{8,9},{9,8},{10,11... | collective-permute-start | bytes 294920 | tf_op jit(solution)/shard_map/ppermute | solution.py:652
  3.2 2.6 %collective-permute-start.1 = (f32[5,32,128]{2,1,0:T(8,128)S(1)}, f32[5,32,128]{2,1,0:T(8,128)S(1)}, u32[]{:S(2)}, u32[]{:S(2)}) collective-permute-start(f32[5,32,128]{2,1,0:T(8,128)S(1)} %get-tuple-element.50), channel_id=1, source_target_pairs={{0,4},{4,0},{8,12},{12,8},{1,5},{5,1},{9,13},{13,9},{2,6},{6,2},{1... | collective-permute-start | bytes 245768 | tf_op jit(solution)/shard_map/ppermute | solution.py:652
  5.8 0.7 %collective-permute-start.2 = (f32[5,32,128]{2,1,0:T(8,128)S(1)}, f32[5,32,128]{2,1,0:T(8,128)S(1)}, u32[]{:S(2)}, u32[]{:S(2)}) collective-permute-start(f32[5,32,128]{2,1,0:T(8,128)S(1)} %get-tuple-element.51), channel_id=1, source_target_pairs={{0,0},{4,8},{8,4},{12,12},{1,1},{5,9},{9,5},{13,13},{2,2},{6,10},{... | collective-permute-start | bytes 245768 | tf_op jit(solution)/shard_map/ppermute | solution.py:652
  6.5 1.6 %velocity_inner.2 = (f32[3,12,32,128]{3,2,1,0:T(8,128)S(1)}, f32[32,128]{1,0:T(8,128)S(1)}) custom-call(f32[3,16,32,128]{3,2,1,0:T(8,128)S(1)} %copy-done.4, f32[6,16,32,128]{3,2,1,0:T(8,128)S(1)} %copy-done, s32[16,32,128]{2,1,0:T(8,128)S(1)} %copy-done.2, f32[5,8]{1,0:T(8,128)S(1)} %copy-done.5, f32[6,32,128]{2,1,0:T(8,128)S(1)} %collective-permute-done.refs_4_), custom_call_target="tpu_custom_call" | custom-call | bytes 11070000 | tf_op jit(solution)/shard_map/velocity_inner/pallas_call | solution.py:618
  8.1 0.8 %collective-permute-done.1.refs_5_ = f32[5,32,128]{2,1,0:T(8,128)S(1)} collective-permute-done((f32[5,32,128]{2,1,0:T(8,128)S(1)}, f32[5,32,128]{2,1,0:T(8,128)S(1)}, u32[]{:S(2)}, u32[]{:S(2)}) %collective-permute-start.1) | collective-permute-done | bytes 81952 | tf_op jit(solution)/shard_map/ppermute | solution.py:652
  9.0 1.1 %velocity_edge.2 = (f32[3,4,32,128]{3,2,1,0:T(8,128)S(1)}, f32[96,128]{1,0:T(8,128)S(1)}, f32[5,32,128]{2,1,0:T(8,128)S(1)}, f32[5,32,128]{2,1,0:T(8,128)S(1)}, f32[6,32,128]{2,1,0:T(8,128)S(1)}) custom-call(f32[3,16,32,128]{3,2,1,0:T(8,128)S(1)} %copy-done.4, f32[6,16,32,128]{3,2,1,0:T(8,128)S(1)} %copy-done, s32[16,32,128]{2,1,0:T(8,128)S(1)} %copy-done.2, ...), custom_call_target="tpu_custom_call" | custom-call | bytes 3690000 | tf_op jit(solution)/shard_map/velocity_edge/pallas_call | solution.py:618
  10.0 1.7 %collective-permute-start.3 = (f32[96,128]{1,0:T(8,128)S(1)}, f32[96,128]{1,0:T(8,128)S(1)}, u32[]{:S(2)}, u32[]{:S(2)}) collective-permute-start(f32[96,128]{1,0:T(8,128)S(1)} %get-tuple-element.57.refs_3_.refs_9_), channel_id=1, source_target_pairs={{0,2},{2,0},{1,3},{3,1},{4,6},{6,4},{5,7},{7,5},{8,10},{10,8},{9,1... | collective-permute-start | bytes 147464 | tf_op jit(solution)/shard_map/ppermute | solution.py:652
  11.7 2.4 %collective-permute-done.3.refs_4_.refs_10_ = f32[96,128]{1,0:T(8,128)S(1)} collective-permute-done((f32[96,128]{1,0:T(8,128)S(1)}, f32[96,128]{1,0:T(8,128)S(1)}, u32[]{:S(2)}, u32[]{:S(2)}) %collective-permute-start.3) | collective-permute-done | bytes 49184 | tf_op jit(solution)/shard_map/ppermute | solution.py:652
  14.2 0.8 %fault.2 = (f32[2,16,128]{2,1,0:T(8,128)S(1)}, f32[16,128]{1,0:T(8,128)S(1)}, f32[5,32,128]{2,1,0:T(8,128)S(1)}, f32[5,32,128]{2,1,0:T(8,128)S(1)}, f32[6,32,128...) custom-call(f32[5,32,128]{2,1,0:T(8,128)S(1)} %get-tuple-element.54.refs_0_, f32[5,32,128]{2,1,0:T(8,128)S(1)} %get-tuple-element.55.refs_1_, ...), custom_call_target="tpu_custom_call" | custom-call | bytes 3690000 | tf_op jit(solution)/shard_map/fault/pallas_call | solution.py:618
  14.9 0.1 collective-permute-start.4
  15.0 4.8 %collective-permute-start.5 = (f32[5,32,128]{2,1,0:T(8,128)S(1)}, f32[5,32,128]{2,1,0:T(8,128)S(1)}, u32[]{:S(2)}, u32[]{:S(2)}) collective-permute-start(f32[5,32,128]{2,1,0:T(8,128)S(1)} %get-tuple-element.62), channel_id=1, source_target_pairs={{0,4},{4,0},{8,12},{12,8},{1,5},{5,1},{9,13},{13,9},{2,6},{6,2},{1... | collective-permute-start | bytes 245768 | tf_op jit(solution)/shard_map/ppermute | solution.py:652
  19.8 0.7 %collective-permute-start.6 = (f32[5,32,128]{2,1,0:T(8,128)S(1)}, f32[5,32,128]{2,1,0:T(8,128)S(1)}, u32[]{:S(2)}, u32[]{:S(2)}) collective-permute-start(f32[5,32,128]{2,1,0:T(8,128)S(1)} %get-tuple-element.63), channel_id=1, source_target_pairs={{0,0},{4,8},{8,4},{12,12},{1,1},{5,9},{9,5},{13,13},{2,2},{6,10},{... | collective-permute-start | bytes 245768 | tf_op jit(solution)/shard_map/ppermute | solution.py:652
  20.5 2.1 %stress_inner.2 = (f32[3,16,32,128]{3,2,1,0:T(8,128)S(1)}, f32[6,12,32,128]{3,2,1,0:T(8,128)S(1)}, f32[6,12,32,128]{3,2,1,0:T(8,128)S(1)}, f32[32,128]{1,0:T(8,128)S(1)}) custom-call(f32[3,12,32,128]{3,2,1,0:T(8,128)S(1)} %get-tuple-element.49.refs_7_.refs_0_, f32[3,4,32,128]{3,2,1,0:T(8,128)S(1)} %get-tuple-element.53.refs_1_, ...), custom_call_target="tpu_custom_call" | custom-call | bytes 11070000 | tf_op jit(solution)/shard_map/stress_inner/pallas_call | solution.py:618
  22.6 0.3 collective-permute-done.5.refs_6_
  22.9 1.2 %stress_edge.2 = (f32[6,4,32,128]{3,2,1,0:T(8,128)S(1)}, f32[6,4,32,128]{3,2,1,0:T(8,128)S(1)}, f32[5,32,128]{2,1,0:T(8,128)S(1)}, f32[5,32,128]{2,1,0:T(8,128)S(1)}, f32[6,32,128]{2,1,0:T(8,128)S(1)}) custom-call(f32[3,16,32,128]{3,2,1,0:T(8,128)S(1)} %get-tuple-element.60.refs_0_, f32[6,16,32,128]{3,2,1,0:T(8,128)S(1)} %copy-done.1, ...), custom_call_target="tpu_custom_call" | custom-call | bytes 3690000 | tf_op jit(solution)/shard_map/stress_edge/pallas_call | solution.py:618
  24.1 0.1 collective-permute-start.7
  24.1 3.7 %collective-permute-start.8 = (f32[5,32,128]{2,1,0:T(8,128)S(1)}, f32[5,32,128]{2,1,0:T(8,128)S(1)}, u32[]{:S(2)}, u32[]{:S(2)}) collective-permute-start(f32[5,32,128]{2,1,0:T(8,128)S(1)} %get-tuple-element.68), channel_id=1, source_target_pairs={{0,4},{4,0},{8,12},{12,8},{1,5},{5,1},{9,13},{13,9},{2,6},{6,2},{1... | collective-permute-start | bytes 245768 | tf_op jit(solution)/shard_map/ppermute | solution.py:652
  27.8 0.7 %collective-permute-start.9 = (f32[5,32,128]{2,1,0:T(8,128)S(1)}, f32[5,32,128]{2,1,0:T(8,128)S(1)}, u32[]{:S(2)}, u32[]{:S(2)}) collective-permute-start(f32[5,32,128]{2,1,0:T(8,128)S(1)} %get-tuple-element.69), channel_id=1, source_target_pairs={{0,0},{4,8},{8,4},{12,12},{1,1},{5,9},{9,5},{13,13},{2,2},{6,10},{... | collective-permute-start | bytes 245768 | tf_op jit(solution)/shard_map/ppermute | solution.py:652
  28.5 1.6 %velocity_inner.3 = (f32[3,12,32,128]{3,2,1,0:T(8,128)S(1)}, f32[32,128]{1,0:T(8,128)S(1)}) custom-call(f32[3,16,32,128]{3,2,1,0:T(8,128)S(1)} %get-tuple-element.60.refs_0_, f32[6,12,32,128]{3,2,1,0:T(8,128)S(1)} %get-tuple-element.61.refs_8_.refs_1_.refs_3_, f32[6,4,32,128]{3,2,1,0:T(8,128)S(1)} %get-tuple-element.65.refs_2_.refs_4_, ...), custom_call_target="tpu_custom_call" | custom-call | bytes 11070000 | tf_op jit(solution)/shard_map/velocity_inner/pallas_call | solution.py:618
  30.1 0.8 %collective-permute-done.8.refs_6_ = f32[5,32,128]{2,1,0:T(8,128)S(1)} collective-permute-done((f32[5,32,128]{2,1,0:T(8,128)S(1)}, f32[5,32,128]{2,1,0:T(8,128)S(1)}, u32[]{:S(2)}, u32[]{:S(2)}) %collective-permute-start.8) | collective-permute-done | bytes 81952 | tf_op jit(solution)/shard_map/ppermute | solution.py:652
  30.9 1.0 %velocity_edge.3 = (f32[3,4,32,128]{3,2,1,0:T(8,128)S(1)}, f32[32,128]{1,0:T(8,128)S(1)}, f32[5,32,128]{2,1,0:T(8,128)S(1)}, f32[5,32,128]{2,1,0:T(8,128)S(1)}, f32[6,32,128]{2,1,0:T(8,128)S(1)}) custom-call(f32[3,16,32,128]{3,2,1,0:T(8,128)S(1)} %get-tuple-element.60.refs_0_, f32[6,12,32,128]{3,2,1,0:T(8,128)S(1)} %get-tuple-element.61.refs_8_.refs_1_.refs_3_, ...), custom_call_target="tpu_custom_call" | custom-call | bytes 3690000 | tf_op jit(solution)/shard_map/velocity_edge/pallas_call | solution.py:618
  31.9 1.5 %collective-permute-start.10 = (f32[32,128]{1,0:T(8,128)S(1)}, f32[32,128]{1,0:T(8,128)S(1)}, u32[]{:S(2)}, u32[]{:S(2)}) collective-permute-start(f32[32,128]{1,0:T(8,128)S(1)} %get-tuple-element.75.refs_3_), channel_id=1, source_target_pairs={{0,2},{2,0},{1,3},{3,1},{4,6},{6,4},{5,7},{7,5},{8,10},{10,8},{9,1... | collective-permute-start | bytes 49160 | tf_op jit(solution)/shard_map/ppermute | solution.py:652
  33.4 2.3 %collective-permute-done.10.refs_4_ = f32[32,128]{1,0:T(8,128)S(1)} collective-permute-done((f32[32,128]{1,0:T(8,128)S(1)}, f32[32,128]{1,0:T(8,128)S(1)}, u32[]{:S(2)}, u32[]{:S(2)}) %collective-permute-start.10) | collective-permute-done | bytes 16416 | tf_op jit(solution)/shard_map/ppermute | solution.py:652
  35.7 0.8 %fault.3 = (f32[2,16,128]{2,1,0:T(8,128)S(1)}, f32[8,128]{1,0:T(8,128)S(1)}, f32[5,32,128]{2,1,0:T(8,128)S(1)}, f32[5,32,128]{2,1,0:T(8,128)S(1)}, f32[6,32,128]{2,1,0:T(8,128)S(1)}) custom-call(f32[5,32,128]{2,1,0:T(8,128)S(1)} %get-tuple-element.72.refs_0_, f32[5,32,128]{2,1,0:T(8,128)S(1)} %get-tuple-element.73.refs_1_, ...), custom_call_target="tpu_custom_call" | custom-call | bytes 3690000 | tf_op jit(solution)/shard_map/fault/pallas_call | solution.py:618
  36.5 0.1 collective-permute-start.11
  36.5 3.7 %collective-permute-start.12 = (f32[5,32,128]{2,1,0:T(8,128)S(1)}, f32[5,32,128]{2,1,0:T(8,128)S(1)}, u32[]{:S(2)}, u32[]{:S(2)}) collective-permute-start(f32[5,32,128]{2,1,0:T(8,128)S(1)} %get-tuple-element.85), channel_id=1, source_target_pairs={{0,4},{4,0},{8,12},{12,8},{1,5},{5,1},{9,13},{13,9},{2,6},{6,2},{1... | collective-permute-start | bytes 245768 | tf_op jit(solution)/shard_map/ppermute | solution.py:652
  40.3 0.7 %collective-permute-start.13 = (f32[5,32,128]{2,1,0:T(8,128)S(1)}, f32[5,32,128]{2,1,0:T(8,128)S(1)}, u32[]{:S(2)}, u32[]{:S(2)}) collective-permute-start(f32[5,32,128]{2,1,0:T(8,128)S(1)} %get-tuple-element.86), channel_id=1, source_target_pairs={{0,0},{4,8},{8,4},{12,12},{1,1},{5,9},{9,5},{13,13},{2,2},{6,10},{... | collective-permute-start | bytes 245768 | tf_op jit(solution)/shard_map/ppermute | solution.py:652
  40.9 2.9 %stress_inner.3 = (f32[3,16,32,128]{3,2,1,0:T(8,128)S(1)}, f32[3,16,32,128]{3,2,1,0:T(8,128)}, f32[6,16,32,128]{3,2,1,0:T(8,128)}, f32[6,16,32,128]{3,2,1,0:T(8,128)}, f32[8,128]{1,0:T(8,128)}) custom-call(f32[3,12,32,128]{3,2,1,0:T(8,128)S(1)} %get-tuple-element.67.refs_8_.refs_0_, f32[3,4,32,128]{3,2,1,0:T(8,128)S(1)} %get-tuple-element.71.refs_1_, ...), custom_call_target="tpu_custom_call" | custom-call | bytes 11070000 | tf_op jit(solution)/shard_map/stress_inner/pallas_call | solution.py:618
  43.8 2.0 %stress_edge.3 = (f32[6,16,32,128]{3,2,1,0:T(8,128)}, f32[6,16,32,128]{3,2,1,0:T(8,128)}) custom-call(f32[3,16,32,128]{3,2,1,0:T(8,128)S(1)} %get-tuple-element.84.refs_0_, f32[6,12,32,128]{3,2,1,0:T(8,128)S(1)} %get-tuple-element.61.refs_8_.refs_1_.refs_3_, ...), custom_call_target="tpu_custom_call", output_to_operand_aliasing={{0}: (10, {}), {1}: (11, {})} | custom-call | bytes 3690000 | tf_op jit(solution)/shard_map/stress_edge/pallas_call | solution.py:618
  (33 shorter events, 0.1 us)
Async XLA Ops:
  0.6 1.4 %copy-start = (f32[6,16,32,128]{3,2,1,0:T(8,128)S(1)}, f32[6,16,32,128]{3,2,1,0:T(8,128)}, u32[]{:S(2)}) copy-start(f32[6,16,32,128]{3,2,1,0:T(8,128)} %refs_1_.5) | copy-start | bytes 4718596
  2.0 4.5 %copy-start.2 = (s32[16,32,128]{2,1,0:T(8,128)S(1)}, s32[16,32,128]{2,1,0:T(8,128)}, u32[]{:S(2)}) copy-start(s32[16,32,128]{2,1,0:T(8,128)} %refs_5_.7) | copy-start | bytes 786436
  2.0 4.5 %copy-start.4 = (f32[3,16,32,128]{3,2,1,0:T(8,128)S(1)}, f32[3,16,32,128]{3,2,1,0:T(8,128)}, u32[]{:S(2)}) copy-start(f32[3,16,32,128]{3,2,1,0:T(8,128)} %refs_0_.5) | copy-start | bytes 2359300
  2.0 4.5 %copy-start.5 = (f32[5,8]{1,0:T(8,128)S(1)}, f32[5,8]{1,0:T(8,128)}, u32[]{:S(2)}) copy-start(f32[5,8]{1,0:T(8,128)} %refs_6_.7) | copy-start | bytes 484
  2.6 6.3 %copy-start.6 = (f32[8,2,128]{2,1,0:T(2,128)S(1)}, f32[8,2,128]{2,1,0:T(2,128)}, u32[]{:S(2)}) copy-start(f32[8,2,128]{2,1,0:T(2,128)} %refs_9_.1) | copy-start | bytes 24580
  2.6 6.3 %copy-start.8 = (f32[8,128]{1,0:T(8,128)S(1)}, f32[8,128]{1,0:T(8,128)}, u32[]{:S(2)}) copy-start(f32[8,128]{1,0:T(8,128)} %refs_10_.1) | copy-start | bytes 12292
  2.6 6.3 %copy-start.9 = (f32[8,128]{1,0:T(8,128)S(1)}, f32[8,128]{1,0:T(8,128)}, u32[]{:S(2)}) copy-start(f32[8,128]{1,0:T(8,128)} %refs_11_.1) | copy-start | bytes 12292
  2.6 6.3 %copy-start.10 = (s32[8,128]{1,0:T(8,128)S(1)}, s32[8,128]{1,0:T(8,128)}, u32[]{:S(2)}) copy-start(s32[8,128]{1,0:T(8,128)} %refs_12_.1) | copy-start | bytes 12292
  2.6 6.3 %copy-start.11 = (s32[8,128]{1,0:T(8,128)S(1)}, s32[8,128]{1,0:T(8,128)}, u32[]{:S(2)}) copy-start(s32[8,128]{1,0:T(8,128)} %refs_13_.1) | copy-start | bytes 12292
  2.7 3.8 %collective-permute-start = (f32[6,32,128]{2,1,0:T(8,128)S(1)}, f32[6,32,128]{2,1,0:T(8,128)S(1)}, u32[]{:S(2)}, u32[]{:S(2)}) collective-permute-start(f32[6,32,128]{2,1,0:T(8,128)S(1)} %get-tuple-element.48), channel_id=1, source_target_pairs={{0,1},{1,0},{2,3},{3,2},{4,5},{5,4},{6,7},{7,6},{8,9},{9,8},{10,11... | collective-permute-start | bytes 294920 | tf_op jit(solution)/shard_map/ppermute | solution.py:652
  3.2 5.7 %collective-permute-start.1 = (f32[5,32,128]{2,1,0:T(8,128)S(1)}, f32[5,32,128]{2,1,0:T(8,128)S(1)}, u32[]{:S(2)}, u32[]{:S(2)}) collective-permute-start(f32[5,32,128]{2,1,0:T(8,128)S(1)} %get-tuple-element.50), channel_id=1, source_target_pairs={{0,4},{4,0},{8,12},{12,8},{1,5},{5,1},{9,13},{13,9},{2,6},{6,2},{1... | collective-permute-start | bytes 245768 | tf_op jit(solution)/shard_map/ppermute | solution.py:652
  5.8 3.0 %collective-permute-start.2 = (f32[5,32,128]{2,1,0:T(8,128)S(1)}, f32[5,32,128]{2,1,0:T(8,128)S(1)}, u32[]{:S(2)}, u32[]{:S(2)}) collective-permute-start(f32[5,32,128]{2,1,0:T(8,128)S(1)} %get-tuple-element.51), channel_id=1, source_target_pairs={{0,0},{4,8},{8,4},{12,12},{1,1},{5,9},{9,5},{13,13},{2,2},{6,10},{... | collective-permute-start | bytes 245768 | tf_op jit(solution)/shard_map/ppermute | solution.py:652
  8.9 5.3 %copy-start.7 = (f32[3,4]{1,0:T(4,128)S(1)}, f32[3,4]{1,0:T(4,128)}, u32[]{:S(2)}) copy-start(f32[3,4]{1,0:T(4,128)} %refs_5_.6) | copy-start | bytes 148
  8.9 5.2 %copy-start.12 = (s32[2]{0:T(128)S(1)}, s32[2]{0:T(128)}, u32[]{:S(2)}) copy-start(s32[2]{0:T(128)} %refs_6_.6) | copy-start | bytes 28
  8.9 11.6 %copy-start.1 = (f32[6,16,32,128]{3,2,1,0:T(8,128)S(1)}, f32[6,16,32,128]{3,2,1,0:T(8,128)}, u32[]{:S(2)}) copy-start(f32[6,16,32,128]{3,2,1,0:T(8,128)} %refs_1_.5) | copy-start | bytes 4718596
  8.9 11.6 %copy-start.3 = (f32[6,16,32,128]{3,2,1,0:T(8,128)S(1)}, f32[6,16,32,128]{3,2,1,0:T(8,128)}, u32[]{:S(2)}) copy-start(f32[6,16,32,128]{3,2,1,0:T(8,128)} %refs_2_.5) | copy-start | bytes 4718596
  10.0 4.1 %collective-permute-start.3 = (f32[96,128]{1,0:T(8,128)S(1)}, f32[96,128]{1,0:T(8,128)S(1)}, u32[]{:S(2)}, u32[]{:S(2)}) collective-permute-start(f32[96,128]{1,0:T(8,128)S(1)} %get-tuple-element.57.refs_3_.refs_9_), channel_id=1, source_target_pairs={{0,2},{2,0},{1,3},{3,1},{4,6},{6,4},{5,7},{7,5},{8,10},{10,8},{9,1... | collective-permute-start | bytes 147464 | tf_op jit(solution)/shard_map/ppermute | solution.py:652
  14.9 5.6 %collective-permute-start.4 = (f32[6,32,128]{2,1,0:T(8,128)S(1)}, f32[6,32,128]{2,1,0:T(8,128)S(1)}, u32[]{:S(2)}, u32[]{:S(2)}) collective-permute-start(f32[6,32,128]{2,1,0:T(8,128)S(1)} %get-tuple-element.59), channel_id=1, source_target_pairs={{0,1},{1,0},{2,3},{3,2},{4,5},{5,4},{6,7},{7,6},{8,9},{9,8},{10,11... | collective-permute-start | bytes 294920 | tf_op jit(solution)/shard_map/ppermute | solution.py:652
  15.0 7.9 %collective-permute-start.5 = (f32[5,32,128]{2,1,0:T(8,128)S(1)}, f32[5,32,128]{2,1,0:T(8,128)S(1)}, u32[]{:S(2)}, u32[]{:S(2)}) collective-permute-start(f32[5,32,128]{2,1,0:T(8,128)S(1)} %get-tuple-element.62), channel_id=1, source_target_pairs={{0,4},{4,0},{8,12},{12,8},{1,5},{5,1},{9,13},{13,9},{2,6},{6,2},{1... | collective-permute-start | bytes 245768 | tf_op jit(solution)/shard_map/ppermute | solution.py:652
  19.8 3.0 %collective-permute-start.6 = (f32[5,32,128]{2,1,0:T(8,128)S(1)}, f32[5,32,128]{2,1,0:T(8,128)S(1)}, u32[]{:S(2)}, u32[]{:S(2)}) collective-permute-start(f32[5,32,128]{2,1,0:T(8,128)S(1)} %get-tuple-element.63), channel_id=1, source_target_pairs={{0,0},{4,8},{8,4},{12,12},{1,1},{5,9},{9,5},{13,13},{2,2},{6,10},{... | collective-permute-start | bytes 245768 | tf_op jit(solution)/shard_map/ppermute | solution.py:652
  24.1 4.5 %collective-permute-start.7 = (f32[6,32,128]{2,1,0:T(8,128)S(1)}, f32[6,32,128]{2,1,0:T(8,128)S(1)}, u32[]{:S(2)}, u32[]{:S(2)}) collective-permute-start(f32[6,32,128]{2,1,0:T(8,128)S(1)} %get-tuple-element.66), channel_id=1, source_target_pairs={{0,1},{1,0},{2,3},{3,2},{4,5},{5,4},{6,7},{7,6},{8,9},{9,8},{10,11... | collective-permute-start | bytes 294920 | tf_op jit(solution)/shard_map/ppermute | solution.py:652
  24.1 6.7 %collective-permute-start.8 = (f32[5,32,128]{2,1,0:T(8,128)S(1)}, f32[5,32,128]{2,1,0:T(8,128)S(1)}, u32[]{:S(2)}, u32[]{:S(2)}) collective-permute-start(f32[5,32,128]{2,1,0:T(8,128)S(1)} %get-tuple-element.68), channel_id=1, source_target_pairs={{0,4},{4,0},{8,12},{12,8},{1,5},{5,1},{9,13},{13,9},{2,6},{6,2},{1... | collective-permute-start | bytes 245768 | tf_op jit(solution)/shard_map/ppermute | solution.py:652
  27.8 3.0 %collective-permute-start.9 = (f32[5,32,128]{2,1,0:T(8,128)S(1)}, f32[5,32,128]{2,1,0:T(8,128)S(1)}, u32[]{:S(2)}, u32[]{:S(2)}) collective-permute-start(f32[5,32,128]{2,1,0:T(8,128)S(1)} %get-tuple-element.69), channel_id=1, source_target_pairs={{0,0},{4,8},{8,4},{12,12},{1,1},{5,9},{9,5},{13,13},{2,2},{6,10},{... | collective-permute-start | bytes 245768 | tf_op jit(solution)/shard_map/ppermute | solution.py:652
  31.9 3.8 %collective-permute-start.10 = (f32[32,128]{1,0:T(8,128)S(1)}, f32[32,128]{1,0:T(8,128)S(1)}, u32[]{:S(2)}, u32[]{:S(2)}) collective-permute-start(f32[32,128]{1,0:T(8,128)S(1)} %get-tuple-element.75.refs_3_), channel_id=1, source_target_pairs={{0,2},{2,0},{1,3},{3,1},{4,6},{6,4},{5,7},{7,5},{8,10},{10,8},{9,1... | collective-permute-start | bytes 49160 | tf_op jit(solution)/shard_map/ppermute | solution.py:652
  36.5 4.5 %collective-permute-start.11 = (f32[6,32,128]{2,1,0:T(8,128)S(1)}, f32[6,32,128]{2,1,0:T(8,128)S(1)}, u32[]{:S(2)}, u32[]{:S(2)}) collective-permute-start(f32[6,32,128]{2,1,0:T(8,128)S(1)} %get-tuple-element.81), channel_id=1, source_target_pairs={{0,1},{1,0},{2,3},{3,2},{4,5},{5,4},{6,7},{7,6},{8,9},{9,8},{10,11... | collective-permute-start | bytes 294920 | tf_op jit(solution)/shard_map/ppermute | solution.py:652
  36.5 7.3 %collective-permute-start.12 = (f32[5,32,128]{2,1,0:T(8,128)S(1)}, f32[5,32,128]{2,1,0:T(8,128)S(1)}, u32[]{:S(2)}, u32[]{:S(2)}) collective-permute-start(f32[5,32,128]{2,1,0:T(8,128)S(1)} %get-tuple-element.85), channel_id=1, source_target_pairs={{0,4},{4,0},{8,12},{12,8},{1,5},{5,1},{9,13},{13,9},{2,6},{6,2},{1... | collective-permute-start | bytes 245768 | tf_op jit(solution)/shard_map/ppermute | solution.py:652
  40.3 3.6 %collective-permute-start.13 = (f32[5,32,128]{2,1,0:T(8,128)S(1)}, f32[5,32,128]{2,1,0:T(8,128)S(1)}, u32[]{:S(2)}, u32[]{:S(2)}) collective-permute-start(f32[5,32,128]{2,1,0:T(8,128)S(1)} %get-tuple-element.86), channel_id=1, source_target_pairs={{0,0},{4,8},{8,4},{12,12},{1,1},{5,9},{9,5},{13,13},{2,2},{6,10},{... | collective-permute-start | bytes 245768 | tf_op jit(solution)/shard_map/ppermute | solution.py:652

commit v7 on v6

--- a/solution.py
+++ b/solution.py
@@ -639,12 +639,17 @@
 
 
 def strike_swaps(count):
+    halves = lax.axis_size("gz")
     routes = []
     for start in (0, 1):
-        partner = list(range(count))
+        partner = {}
         for i in range(start, count - 1, 2):
-            partner[i], partner[i + 1] = i + 1, i
-        routes.append(("gx", list(enumerate(partner))))
+            for half in range(halves):
+                one, other = i * halves + half, (i + 1) * halves + half
+                partner[one], partner[other] = other, one
+        for i in range(count * halves):
+            partner.setdefault(i, i ^ 1)
+        routes.append((("gx", "gz"), sorted(partner.items())))
     return routes
 
 

time: 46.4 us -> 39.8 us (0.86)
  starting transfers between devices: 21.5 us -> 13.9 us
  waiting for transfers between devices: 6.51 us -> 8.05 us
    ppermute x14, starting transfers between devices: 21.5 us -> 13.9 us  [sent(): return lax.ppermute(block, *route)]
    ppermute x14, waiting for transfers between devices: 6.51 us -> 8.05 us  [sent(): return lax.ppermute(block, *route)]
  transfers between devices with their start and end apart: 14 -> 14, of which waited for: 5 -> 5; matrix products, arithmetic and copies ran while one was open for 0% -> 0% of each run, Pallas kernels for 18% -> 20%
where the time goes in v7:
time: 39.8 us; the launch traced here: 39.7 us
  Pallas kernels  15.4 us (39%)
  starting transfers between devices  13.9 us (35%)
  waiting for transfers between devices  8.05 us (20%)
  local copies, waits for them, and re-layouts  1.47 us (4%)
  between operations  0.85 us (2%)
    pallas_call x11, Pallas kernels, call(): pl.pallas_call(body, out_shape=shapes, in_specs=[place(key) for key in in...  15.4 us
    ppermute x14, starting transfers between devices, sent(): return lax.ppermute(block, *route)  13.9 us
    ppermute x14, waiting for transfers between devices, sent(): return lax.ppermute(block, *route)  8.05 us
    unnamed x26, local copies, waits for them, and re-layouts  1.47 us
  transfers between devices with their start and end apart: 14, of which 5 were waited for; matrix products, arithmetic and copies ran while one was open for 0% of the time, Pallas kernels for 20%

profile of v7, /device:TPU:0, one launch (start us, length us, event | category | flops | bytes accessed | tf_op | source)
XLA Modules:
  0.0 39.7 jit_solution(1848510842085971585)
XLA Ops:
  0.6 0.0 copy-start
  0.6 1.4 %copy-done = f32[6,16,32,128]{3,2,1,0:T(8,128)S(1)} copy-done((f32[6,16,32,128]{3,2,1,0:T(8,128)S(1)}, f32[6,16,32,128]{3,2,1,0:T(8,128)}, u32[]{:S(2)}) %copy-start) | copy-done | bytes 1572888
  2.0 0.5 %pack.1 = (f32[5,32,128]{2,1,0:T(8,128)S(1)}, f32[5,32,128]{2,1,0:T(8,128)S(1)}, f32[6,32,128]{2,1,0:T(8,128)S(1)}) custom-call(f32[6,16,32,128]{3,2,1,0:T(8,128)S(1)} %copy-done), custom_call_target="tpu_custom_call" | custom-call | bytes 3690000 | tf_op jit(solution)/shard_map/pack/pallas_call | solution.py:618
  2.7 0.5 %collective-permute-start = (f32[6,32,128]{2,1,0:T(8,128)S(1)}, f32[6,32,128]{2,1,0:T(8,128)S(1)}, u32[]{:S(2)}, u32[]{:S(2)}) collective-permute-start(f32[6,32,128]{2,1,0:T(8,128)S(1)} %get-tuple-element.48), channel_id=1, source_target_pairs={{0,1},{1,0},{2,3},{3,2},{4,5},{5,4},{6,7},{7,6},{8,9},{9,8},{10,11... | collective-permute-start | bytes 294920 | tf_op jit(solution)/shard_map/ppermute | solution.py:657
  3.2 2.6 %collective-permute-start.1 = (f32[5,32,128]{2,1,0:T(8,128)S(1)}, f32[5,32,128]{2,1,0:T(8,128)S(1)}, u32[]{:S(2)}, u32[]{:S(2)}) collective-permute-start(f32[5,32,128]{2,1,0:T(8,128)S(1)} %get-tuple-element.50), channel_id=1, source_target_pairs={{0,4},{1,5},{4,0},{5,1},{8,12},{9,13},{12,8},{13,9},{2,6},{3,7},{6... | collective-permute-start | bytes 245768 | tf_op jit(solution)/shard_map/ppermute | solution.py:657
  5.8 0.2 collective-permute-start.2
  6.0 1.6 %velocity_inner.2 = (f32[3,12,32,128]{3,2,1,0:T(8,128)S(1)}, f32[32,128]{1,0:T(8,128)S(1)}) custom-call(f32[3,16,32,128]{3,2,1,0:T(8,128)S(1)} %copy-done.4, f32[6,16,32,128]{3,2,1,0:T(8,128)S(1)} %copy-done, s32[16,32,128]{2,1,0:T(8,128)S(1)} %copy-done.2, f32[5,8]{1,0:T(8,128)S(1)} %copy-done.5, f32[6,32,128]{2,1,0:T(8,128)S(1)} %collective-permute-done.refs_4_), custom_call_target="tpu_custom_call" | custom-call | bytes 11070000 | tf_op jit(solution)/shard_map/velocity_inner/pallas_call | solution.py:618
  7.6 1.3 %collective-permute-done.1.refs_5_ = f32[5,32,128]{2,1,0:T(8,128)S(1)} collective-permute-done((f32[5,32,128]{2,1,0:T(8,128)S(1)}, f32[5,32,128]{2,1,0:T(8,128)S(1)}, u32[]{:S(2)}, u32[]{:S(2)}) %collective-permute-start.1) | collective-permute-done | bytes 81952 | tf_op jit(solution)/shard_map/ppermute | solution.py:657
  9.0 1.1 %velocity_edge.2 = (f32[3,4,32,128]{3,2,1,0:T(8,128)S(1)}, f32[96,128]{1,0:T(8,128)S(1)}, f32[5,32,128]{2,1,0:T(8,128)S(1)}, f32[5,32,128]{2,1,0:T(8,128)S(1)}, f32[6,32,128]{2,1,0:T(8,128)S(1)}) custom-call(f32[3,16,32,128]{3,2,1,0:T(8,128)S(1)} %copy-done.4, f32[6,16,32,128]{3,2,1,0:T(8,128)S(1)} %copy-done, s32[16,32,128]{2,1,0:T(8,128)S(1)} %copy-done.2, ...), custom_call_target="tpu_custom_call" | custom-call | bytes 3690000 | tf_op jit(solution)/shard_map/velocity_edge/pallas_call | solution.py:618
  10.0 1.7 %collective-permute-start.3 = (f32[96,128]{1,0:T(8,128)S(1)}, f32[96,128]{1,0:T(8,128)S(1)}, u32[]{:S(2)}, u32[]{:S(2)}) collective-permute-start(f32[96,128]{1,0:T(8,128)S(1)} %get-tuple-element.57.refs_3_.refs_9_), channel_id=1, source_target_pairs={{0,2},{2,0},{1,3},{3,1},{4,6},{6,4},{5,7},{7,5},{8,10},{10,8},{9,1... | collective-permute-start | bytes 147464 | tf_op jit(solution)/shard_map/ppermute | solution.py:657
  11.7 2.4 %collective-permute-done.3.refs_4_.refs_10_ = f32[96,128]{1,0:T(8,128)S(1)} collective-permute-done((f32[96,128]{1,0:T(8,128)S(1)}, f32[96,128]{1,0:T(8,128)S(1)}, u32[]{:S(2)}, u32[]{:S(2)}) %collective-permute-start.3) | collective-permute-done | bytes 49184 | tf_op jit(solution)/shard_map/ppermute | solution.py:657
  14.2 0.8 %fault.2 = (f32[2,16,128]{2,1,0:T(8,128)S(1)}, f32[16,128]{1,0:T(8,128)S(1)}, f32[5,32,128]{2,1,0:T(8,128)S(1)}, f32[5,32,128]{2,1,0:T(8,128)S(1)}, f32[6,32,128...) custom-call(f32[5,32,128]{2,1,0:T(8,128)S(1)} %get-tuple-element.54.refs_0_, f32[5,32,128]{2,1,0:T(8,128)S(1)} %get-tuple-element.55.refs_1_, ...), custom_call_target="tpu_custom_call" | custom-call | bytes 3690000 | tf_op jit(solution)/shard_map/fault/pallas_call | solution.py:618
  14.9 0.1 collective-permute-start.4
  15.0 2.9 %collective-permute-start.5 = (f32[5,32,128]{2,1,0:T(8,128)S(1)}, f32[5,32,128]{2,1,0:T(8,128)S(1)}, u32[]{:S(2)}, u32[]{:S(2)}) collective-permute-start(f32[5,32,128]{2,1,0:T(8,128)S(1)} %get-tuple-element.62), channel_id=1, source_target_pairs={{0,4},{1,5},{4,0},{5,1},{8,12},{9,13},{12,8},{13,9},{2,6},{3,7},{6... | collective-permute-start | bytes 245768 | tf_op jit(solution)/shard_map/ppermute | solution.py:657
  17.9 0.2 collective-permute-start.6
  18.1 2.1 %stress_inner.2 = (f32[3,16,32,128]{3,2,1,0:T(8,128)S(1)}, f32[6,12,32,128]{3,2,1,0:T(8,128)S(1)}, f32[6,12,32,128]{3,2,1,0:T(8,128)S(1)}, f32[32,128]{1,0:T(8,128)S(1)}) custom-call(f32[3,12,32,128]{3,2,1,0:T(8,128)S(1)} %get-tuple-element.49.refs_7_.refs_0_, f32[3,4,32,128]{3,2,1,0:T(8,128)S(1)} %get-tuple-element.53.refs_1_, ...), custom_call_target="tpu_custom_call" | custom-call | bytes 11070000 | tf_op jit(solution)/shard_map/stress_inner/pallas_call | solution.py:618
  20.2 0.8 %collective-permute-done.5.refs_6_ = f32[5,32,128]{2,1,0:T(8,128)S(1)} collective-permute-done((f32[5,32,128]{2,1,0:T(8,128)S(1)}, f32[5,32,128]{2,1,0:T(8,128)S(1)}, u32[]{:S(2)}, u32[]{:S(2)}) %collective-permute-start.5) | collective-permute-done | bytes 81952 | tf_op jit(solution)/shard_map/ppermute | solution.py:657
  21.0 1.2 %stress_edge.2 = (f32[6,4,32,128]{3,2,1,0:T(8,128)S(1)}, f32[6,4,32,128]{3,2,1,0:T(8,128)S(1)}, f32[5,32,128]{2,1,0:T(8,128)S(1)}, f32[5,32,128]{2,1,0:T(8,128)S(1)}, f32[6,32,128]{2,1,0:T(8,128)S(1)}) custom-call(f32[3,16,32,128]{3,2,1,0:T(8,128)S(1)} %get-tuple-element.60.refs_0_, f32[6,16,32,128]{3,2,1,0:T(8,128)S(1)} %copy-done.1, ...), custom_call_target="tpu_custom_call" | custom-call | bytes 3690000 | tf_op jit(solution)/shard_map/stress_edge/pallas_call | solution.py:618
  22.2 0.1 collective-permute-start.7
  22.2 1.8 %collective-permute-start.8 = (f32[5,32,128]{2,1,0:T(8,128)S(1)}, f32[5,32,128]{2,1,0:T(8,128)S(1)}, u32[]{:S(2)}, u32[]{:S(2)}) collective-permute-start(f32[5,32,128]{2,1,0:T(8,128)S(1)} %get-tuple-element.68), channel_id=1, source_target_pairs={{0,4},{1,5},{4,0},{5,1},{8,12},{9,13},{12,8},{13,9},{2,6},{3,7},{6... | collective-permute-start | bytes 245768 | tf_op jit(solution)/shard_map/ppermute | solution.py:657
  24.1 0.2 collective-permute-start.9
  24.2 1.6 %velocity_inner.3 = (f32[3,12,32,128]{3,2,1,0:T(8,128)S(1)}, f32[32,128]{1,0:T(8,128)S(1)}) custom-call(f32[3,16,32,128]{3,2,1,0:T(8,128)S(1)} %get-tuple-element.60.refs_0_, f32[6,12,32,128]{3,2,1,0:T(8,128)S(1)} %get-tuple-element.61.refs_8_.refs_1_.refs_3_, f32[6,4,32,128]{3,2,1,0:T(8,128)S(1)} %get-tuple-element.65.refs_2_.refs_4_, ...), custom_call_target="tpu_custom_call" | custom-call | bytes 11070000 | tf_op jit(solution)/shard_map/velocity_inner/pallas_call | solution.py:618
  25.8 1.3 %collective-permute-done.8.refs_6_ = f32[5,32,128]{2,1,0:T(8,128)S(1)} collective-permute-done((f32[5,32,128]{2,1,0:T(8,128)S(1)}, f32[5,32,128]{2,1,0:T(8,128)S(1)}, u32[]{:S(2)}, u32[]{:S(2)}) %collective-permute-start.8) | collective-permute-done | bytes 81952 | tf_op jit(solution)/shard_map/ppermute | solution.py:657
  27.1 1.0 %velocity_edge.3 = (f32[3,4,32,128]{3,2,1,0:T(8,128)S(1)}, f32[32,128]{1,0:T(8,128)S(1)}, f32[5,32,128]{2,1,0:T(8,128)S(1)}, f32[5,32,128]{2,1,0:T(8,128)S(1)}, f32[6,32,128]{2,1,0:T(8,128)S(1)}) custom-call(f32[3,16,32,128]{3,2,1,0:T(8,128)S(1)} %get-tuple-element.60.refs_0_, f32[6,12,32,128]{3,2,1,0:T(8,128)S(1)} %get-tuple-element.61.refs_8_.refs_1_.refs_3_, ...), custom_call_target="tpu_custom_call" | custom-call | bytes 3690000 | tf_op jit(solution)/shard_map/velocity_edge/pallas_call | solution.py:618
  28.1 1.5 %collective-permute-start.10 = (f32[32,128]{1,0:T(8,128)S(1)}, f32[32,128]{1,0:T(8,128)S(1)}, u32[]{:S(2)}, u32[]{:S(2)}) collective-permute-start(f32[32,128]{1,0:T(8,128)S(1)} %get-tuple-element.75.refs_3_), channel_id=1, source_target_pairs={{0,2},{2,0},{1,3},{3,1},{4,6},{6,4},{5,7},{7,5},{8,10},{10,8},{9,1... | collective-permute-start | bytes 49160 | tf_op jit(solution)/shard_map/ppermute | solution.py:657
  29.7 2.3 %collective-permute-done.10.refs_4_ = f32[32,128]{1,0:T(8,128)S(1)} collective-permute-done((f32[32,128]{1,0:T(8,128)S(1)}, f32[32,128]{1,0:T(8,128)S(1)}, u32[]{:S(2)}, u32[]{:S(2)}) %collective-permute-start.10) | collective-permute-done | bytes 16416 | tf_op jit(solution)/shard_map/ppermute | solution.py:657
  31.9 0.8 %fault.3 = (f32[2,16,128]{2,1,0:T(8,128)S(1)}, f32[8,128]{1,0:T(8,128)S(1)}, f32[5,32,128]{2,1,0:T(8,128)S(1)}, f32[5,32,128]{2,1,0:T(8,128)S(1)}, f32[6,32,128]{2,1,0:T(8,128)S(1)}) custom-call(f32[5,32,128]{2,1,0:T(8,128)S(1)} %get-tuple-element.72.refs_0_, f32[5,32,128]{2,1,0:T(8,128)S(1)} %get-tuple-element.73.refs_1_, ...), custom_call_target="tpu_custom_call" | custom-call | bytes 3690000 | tf_op jit(solution)/shard_map/fault/pallas_call | solution.py:618
  32.7 0.1 collective-permute-start.11
  32.8 1.8 %collective-permute-start.12 = (f32[5,32,128]{2,1,0:T(8,128)S(1)}, f32[5,32,128]{2,1,0:T(8,128)S(1)}, u32[]{:S(2)}, u32[]{:S(2)}) collective-permute-start(f32[5,32,128]{2,1,0:T(8,128)S(1)} %get-tuple-element.85), channel_id=1, source_target_pairs={{0,4},{1,5},{4,0},{5,1},{8,12},{9,13},{12,8},{13,9},{2,6},{3,7},{6... | collective-permute-start | bytes 245768 | tf_op jit(solution)/shard_map/ppermute | solution.py:657
  34.6 0.2 collective-permute-start.13
  34.8 2.9 %stress_inner.3 = (f32[3,16,32,128]{3,2,1,0:T(8,128)S(1)}, f32[3,16,32,128]{3,2,1,0:T(8,128)}, f32[6,16,32,128]{3,2,1,0:T(8,128)}, f32[6,16,32,128]{3,2,1,0:T(8,128)}, f32[8,128]{1,0:T(8,128)}) custom-call(f32[3,12,32,128]{3,2,1,0:T(8,128)S(1)} %get-tuple-element.67.refs_8_.refs_0_, f32[3,4,32,128]{3,2,1,0:T(8,128)S(1)} %get-tuple-element.71.refs_1_, ...), custom_call_target="tpu_custom_call" | custom-call | bytes 11070000 | tf_op jit(solution)/shard_map/stress_inner/pallas_call | solution.py:618
  37.7 2.0 %stress_edge.3 = (f32[6,16,32,128]{3,2,1,0:T(8,128)}, f32[6,16,32,128]{3,2,1,0:T(8,128)}) custom-call(f32[3,16,32,128]{3,2,1,0:T(8,128)S(1)} %get-tuple-element.84.refs_0_, f32[6,12,32,128]{3,2,1,0:T(8,128)S(1)} %get-tuple-element.61.refs_8_.refs_1_.refs_3_, ...), custom_call_target="tpu_custom_call", output_to_operand_aliasing={{0}: (10, {}), {1}: (11, {})} | custom-call | bytes 3690000 | tf_op jit(solution)/shard_map/stress_edge/pallas_call | solution.py:618
  (33 shorter events, 0.1 us)
Async XLA Ops:
  0.6 1.4 %copy-start = (f32[6,16,32,128]{3,2,1,0:T(8,128)S(1)}, f32[6,16,32,128]{3,2,1,0:T(8,128)}, u32[]{:S(2)}) copy-start(f32[6,16,32,128]{3,2,1,0:T(8,128)} %refs_1_.5) | copy-start | bytes 4718596
  2.0 4.0 %copy-start.2 = (s32[16,32,128]{2,1,0:T(8,128)S(1)}, s32[16,32,128]{2,1,0:T(8,128)}, u32[]{:S(2)}) copy-start(s32[16,32,128]{2,1,0:T(8,128)} %refs_5_.7) | copy-start | bytes 786436
  2.0 4.0 %copy-start.4 = (f32[3,16,32,128]{3,2,1,0:T(8,128)S(1)}, f32[3,16,32,128]{3,2,1,0:T(8,128)}, u32[]{:S(2)}) copy-start(f32[3,16,32,128]{3,2,1,0:T(8,128)} %refs_0_.5) | copy-start | bytes 2359300
  2.0 4.0 %copy-start.5 = (f32[5,8]{1,0:T(8,128)S(1)}, f32[5,8]{1,0:T(8,128)}, u32[]{:S(2)}) copy-start(f32[5,8]{1,0:T(8,128)} %refs_6_.7) | copy-start | bytes 484
  2.6 6.3 %copy-start.6 = (f32[8,2,128]{2,1,0:T(2,128)S(1)}, f32[8,2,128]{2,1,0:T(2,128)}, u32[]{:S(2)}) copy-start(f32[8,2,128]{2,1,0:T(2,128)} %refs_9_.1) | copy-start | bytes 24580
  2.6 6.3 %copy-start.8 = (f32[8,128]{1,0:T(8,128)S(1)}, f32[8,128]{1,0:T(8,128)}, u32[]{:S(2)}) copy-start(f32[8,128]{1,0:T(8,128)} %refs_10_.1) | copy-start | bytes 12292
  2.6 6.3 %copy-start.9 = (f32[8,128]{1,0:T(8,128)S(1)}, f32[8,128]{1,0:T(8,128)}, u32[]{:S(2)}) copy-start(f32[8,128]{1,0:T(8,128)} %refs_11_.1) | copy-start | bytes 12292
  2.6 6.3 %copy-start.10 = (s32[8,128]{1,0:T(8,128)S(1)}, s32[8,128]{1,0:T(8,128)}, u32[]{:S(2)}) copy-start(s32[8,128]{1,0:T(8,128)} %refs_12_.1) | copy-start | bytes 12292
  2.6 6.3 %copy-start.11 = (s32[8,128]{1,0:T(8,128)S(1)}, s32[8,128]{1,0:T(8,128)}, u32[]{:S(2)}) copy-start(s32[8,128]{1,0:T(8,128)} %refs_13_.1) | copy-start | bytes 12292
  2.7 3.3 %collective-permute-start = (f32[6,32,128]{2,1,0:T(8,128)S(1)}, f32[6,32,128]{2,1,0:T(8,128)S(1)}, u32[]{:S(2)}, u32[]{:S(2)}) collective-permute-start(f32[6,32,128]{2,1,0:T(8,128)S(1)} %get-tuple-element.48), channel_id=1, source_target_pairs={{0,1},{1,0},{2,3},{3,2},{4,5},{5,4},{6,7},{7,6},{8,9},{9,8},{10,11... | collective-permute-start | bytes 294920 | tf_op jit(solution)/shard_map/ppermute | solution.py:657
  3.2 5.7 %collective-permute-start.1 = (f32[5,32,128]{2,1,0:T(8,128)S(1)}, f32[5,32,128]{2,1,0:T(8,128)S(1)}, u32[]{:S(2)}, u32[]{:S(2)}) collective-permute-start(f32[5,32,128]{2,1,0:T(8,128)S(1)} %get-tuple-element.50), channel_id=1, source_target_pairs={{0,4},{1,5},{4,0},{5,1},{8,12},{9,13},{12,8},{13,9},{2,6},{3,7},{6... | collective-permute-start | bytes 245768 | tf_op jit(solution)/shard_map/ppermute | solution.py:657
  5.8 3.0 %collective-permute-start.2 = (f32[5,32,128]{2,1,0:T(8,128)S(1)}, f32[5,32,128]{2,1,0:T(8,128)S(1)}, u32[]{:S(2)}, u32[]{:S(2)}) collective-permute-start(f32[5,32,128]{2,1,0:T(8,128)S(1)} %get-tuple-element.51), channel_id=1, source_target_pairs={{0,1},{1,0},{4,8},{5,9},{8,4},{9,5},{12,13},{13,12},{2,3},{3,2},{6... | collective-permute-start | bytes 245768 | tf_op jit(solution)/shard_map/ppermute | solution.py:657
  8.9 5.3 %copy-start.7 = (f32[3,4]{1,0:T(4,128)S(1)}, f32[3,4]{1,0:T(4,128)}, u32[]{:S(2)}) copy-start(f32[3,4]{1,0:T(4,128)} %refs_5_.6) | copy-start | bytes 148
  8.9 5.2 %copy-start.12 = (s32[2]{0:T(128)S(1)}, s32[2]{0:T(128)}, u32[]{:S(2)}) copy-start(s32[2]{0:T(128)} %refs_6_.6) | copy-start | bytes 28
  8.9 9.2 %copy-start.1 = (f32[6,16,32,128]{3,2,1,0:T(8,128)S(1)}, f32[6,16,32,128]{3,2,1,0:T(8,128)}, u32[]{:S(2)}) copy-start(f32[6,16,32,128]{3,2,1,0:T(8,128)} %refs_1_.5) | copy-start | bytes 4718596
  8.9 9.2 %copy-start.3 = (f32[6,16,32,128]{3,2,1,0:T(8,128)S(1)}, f32[6,16,32,128]{3,2,1,0:T(8,128)}, u32[]{:S(2)}) copy-start(f32[6,16,32,128]{3,2,1,0:T(8,128)} %refs_2_.5) | copy-start | bytes 4718596
  10.0 4.1 %collective-permute-start.3 = (f32[96,128]{1,0:T(8,128)S(1)}, f32[96,128]{1,0:T(8,128)S(1)}, u32[]{:S(2)}, u32[]{:S(2)}) collective-permute-start(f32[96,128]{1,0:T(8,128)S(1)} %get-tuple-element.57.refs_3_.refs_9_), channel_id=1, source_target_pairs={{0,2},{2,0},{1,3},{3,1},{4,6},{6,4},{5,7},{7,5},{8,10},{10,8},{9,1... | collective-permute-start | bytes 147464 | tf_op jit(solution)/shard_map/ppermute | solution.py:657
  14.9 3.2 %collective-permute-start.4 = (f32[6,32,128]{2,1,0:T(8,128)S(1)}, f32[6,32,128]{2,1,0:T(8,128)S(1)}, u32[]{:S(2)}, u32[]{:S(2)}) collective-permute-start(f32[6,32,128]{2,1,0:T(8,128)S(1)} %get-tuple-element.59), channel_id=1, source_target_pairs={{0,1},{1,0},{2,3},{3,2},{4,5},{5,4},{6,7},{7,6},{8,9},{9,8},{10,11... | collective-permute-start | bytes 294920 | tf_op jit(solution)/shard_map/ppermute | solution.py:657
  15.0 6.0 %collective-permute-start.5 = (f32[5,32,128]{2,1,0:T(8,128)S(1)}, f32[5,32,128]{2,1,0:T(8,128)S(1)}, u32[]{:S(2)}, u32[]{:S(2)}) collective-permute-start(f32[5,32,128]{2,1,0:T(8,128)S(1)} %get-tuple-element.62), channel_id=1, source_target_pairs={{0,4},{1,5},{4,0},{5,1},{8,12},{9,13},{12,8},{13,9},{2,6},{3,7},{6... | collective-permute-start | bytes 245768 | tf_op jit(solution)/shard_map/ppermute | solution.py:657
  17.9 3.0 %collective-permute-start.6 = (f32[5,32,128]{2,1,0:T(8,128)S(1)}, f32[5,32,128]{2,1,0:T(8,128)S(1)}, u32[]{:S(2)}, u32[]{:S(2)}) collective-permute-start(f32[5,32,128]{2,1,0:T(8,128)S(1)} %get-tuple-element.63), channel_id=1, source_target_pairs={{0,1},{1,0},{4,8},{5,9},{8,4},{9,5},{12,13},{13,12},{2,3},{3,2},{6... | collective-permute-start | bytes 245768 | tf_op jit(solution)/shard_map/ppermute | solution.py:657
  22.2 2.1 %collective-permute-start.7 = (f32[6,32,128]{2,1,0:T(8,128)S(1)}, f32[6,32,128]{2,1,0:T(8,128)S(1)}, u32[]{:S(2)}, u32[]{:S(2)}) collective-permute-start(f32[6,32,128]{2,1,0:T(8,128)S(1)} %get-tuple-element.66), channel_id=1, source_target_pairs={{0,1},{1,0},{2,3},{3,2},{4,5},{5,4},{6,7},{7,6},{8,9},{9,8},{10,11... | collective-permute-start | bytes 294920 | tf_op jit(solution)/shard_map/ppermute | solution.py:657
  22.2 4.9 %collective-permute-start.8 = (f32[5,32,128]{2,1,0:T(8,128)S(1)}, f32[5,32,128]{2,1,0:T(8,128)S(1)}, u32[]{:S(2)}, u32[]{:S(2)}) collective-permute-start(f32[5,32,128]{2,1,0:T(8,128)S(1)} %get-tuple-element.68), channel_id=1, source_target_pairs={{0,4},{1,5},{4,0},{5,1},{8,12},{9,13},{12,8},{13,9},{2,6},{3,7},{6... | collective-permute-start | bytes 245768 | tf_op jit(solution)/shard_map/ppermute | solution.py:657
  24.1 3.0 %collective-permute-start.9 = (f32[5,32,128]{2,1,0:T(8,128)S(1)}, f32[5,32,128]{2,1,0:T(8,128)S(1)}, u32[]{:S(2)}, u32[]{:S(2)}) collective-permute-start(f32[5,32,128]{2,1,0:T(8,128)S(1)} %get-tuple-element.69), channel_id=1, source_target_pairs={{0,1},{1,0},{4,8},{5,9},{8,4},{9,5},{12,13},{13,12},{2,3},{3,2},{6... | collective-permute-start | bytes 245768 | tf_op jit(solution)/shard_map/ppermute | solution.py:657
  28.1 3.8 %collective-permute-start.10 = (f32[32,128]{1,0:T(8,128)S(1)}, f32[32,128]{1,0:T(8,128)S(1)}, u32[]{:S(2)}, u32[]{:S(2)}) collective-permute-start(f32[32,128]{1,0:T(8,128)S(1)} %get-tuple-element.75.refs_3_), channel_id=1, source_target_pairs={{0,2},{2,0},{1,3},{3,1},{4,6},{6,4},{5,7},{7,5},{8,10},{10,8},{9,1... | collective-permute-start | bytes 49160 | tf_op jit(solution)/shard_map/ppermute | solution.py:657
  32.7 2.1 %collective-permute-start.11 = (f32[6,32,128]{2,1,0:T(8,128)S(1)}, f32[6,32,128]{2,1,0:T(8,128)S(1)}, u32[]{:S(2)}, u32[]{:S(2)}) collective-permute-start(f32[6,32,128]{2,1,0:T(8,128)S(1)} %get-tuple-element.81), channel_id=1, source_target_pairs={{0,1},{1,0},{2,3},{3,2},{4,5},{5,4},{6,7},{7,6},{8,9},{9,8},{10,11... | collective-permute-start | bytes 294920 | tf_op jit(solution)/shard_map/ppermute | solution.py:657
  32.8 4.9 %collective-permute-start.12 = (f32[5,32,128]{2,1,0:T(8,128)S(1)}, f32[5,32,128]{2,1,0:T(8,128)S(1)}, u32[]{:S(2)}, u32[]{:S(2)}) collective-permute-start(f32[5,32,128]{2,1,0:T(8,128)S(1)} %get-tuple-element.85), channel_id=1, source_target_pairs={{0,4},{1,5},{4,0},{5,1},{8,12},{9,13},{12,8},{13,9},{2,6},{3,7},{6... | collective-permute-start | bytes 245768 | tf_op jit(solution)/shard_map/ppermute | solution.py:657
  34.6 3.1 %collective-permute-start.13 = (f32[5,32,128]{2,1,0:T(8,128)S(1)}, f32[5,32,128]{2,1,0:T(8,128)S(1)}, u32[]{:S(2)}, u32[]{:S(2)}) collective-permute-start(f32[5,32,128]{2,1,0:T(8,128)S(1)} %get-tuple-element.86), channel_id=1, source_target_pairs={{0,1},{1,0},{4,8},{5,9},{8,4},{9,5},{12,13},{13,12},{2,3},{3,2},{6... | collective-permute-start | bytes 245768 | tf_op jit(solution)/shard_map/ppermute | solution.py:657

commit v8 on v7

--- a/solution.py
+++ b/solution.py
@@ -17,7 +17,7 @@
 FAR = -1.0 / 24.0
 DT = 0.15
 TILE = 8
-STRIP_PLANES = 6
+ENS, GX, GY, GZ = "ens", "gx", "gy", "gz"
 
 XX, YY, ZZ, XY, XZ, YZ = range(6)
 
@@ -49,7 +49,7 @@
         row = lax.broadcasted_iota(jnp.int32, (TILE, depths), 0)
         self.row = lax.broadcasted_iota(jnp.int32, (rows, depths), 0)
         self.tile_row = row
-        self.deep = lax.axis_index("gz")
+        self.deep = lax.axis_index(GZ)
         near = (self.deep == 0) & (lane < 2) | (self.deep == 1) & (lane >= depths - 2)
         self.near = jnp.where(near, 1.0, 0.0)
         self.zero = jnp.minimum(self.deep, 0)
@@ -171,28 +171,36 @@
 
 
 class Planes:
-    def __init__(self, field, tail, head, first=None, second=None):
+    def __init__(self, field, tail, head, first=None, second=None, change=None, on_fault=None):
+        self.change, self.on_fault = change, on_fault
         self.field = field
         self.count = field.count
         self.first, self.second = first, second
         self.tail, self.head = tail, head
         self.even = even_strike()
-        self.any_left = lax.axis_index("gx") > 0
-        self.any_right = lax.axis_index("gx") < lax.axis_size("gx") - 1
+        self.any_left = lax.axis_index(GX) > 0
+        self.any_right = lax.axis_index(GX) < lax.axis_size(GX) - 1
 
     def left(self, i):
-        plane = jnp.where(self.even, self.second[i], self.first[i])
-        return jnp.where(self.any_left, plane, 0.0)
+        return jnp.where(self.even, self.second[i], self.first[i])
 
     def right(self, i):
-        plane = jnp.where(self.even, self.first[i], self.second[i])
-        return jnp.where(self.any_right, plane, 0.0)
+        return jnp.where(self.even, self.first[i], self.second[i])
+
+    def changed(self, plane, comp, node):
+        if self.change is None or comp == 1:
+            return plane
+        line = self.change[comp // 2, pl.ds(node, 1), :]
+        return plane + jnp.where(self.on_fault, line, 0.0)
 
     def __call__(self, comp, place):
         if place < 0:
-            return self.left(self.tail.index((comp, place)))
+            plane = self.left(self.tail.index((comp, place)))
+            return jnp.where(self.any_left, self.changed(plane, comp, place + 2), 0.0)
         if place >= self.count:
-            return self.right(self.head.index((comp, place - self.count)))
+            beyond = place - self.count
+            plane = self.right(self.head.index((comp, beyond)))
+            return jnp.where(self.any_right, self.changed(plane, comp, beyond + 2), 0.0)
         return self.field(comp, place)
 
     def rows(self, comp, x):
@@ -228,13 +236,13 @@
 
 
 def even_strike():
-    return lax.axis_index("gx") % 2 == 0
+    return lax.axis_index(GX) % 2 == 0
 
 
 def edge_planes(field, tail, head, first_out, second_out):
     even = even_strike()
     pairs = []
-    for i in range(first_out.shape[0]):
+    for i in range(max(len(tail), len(head))):
         comp, place = tail[min(i, len(tail) - 1)]
         right = field(comp, place % field.count)
         comp, place = head[min(i, len(head) - 1)]
@@ -246,7 +254,7 @@
 
 
 def fault_row(rows):
-    return jnp.where(lax.axis_index("gy") == lax.axis_size("gy") // 2, 0, rows - 1)
+    return jnp.where(lax.axis_index(GY) == lax.axis_size(GY) // 2, 0, rows - 1)
 
 
 def pack_kernel(r):
@@ -277,9 +285,16 @@
     return [xs[i : i + size] for i in range(0, len(xs), size)]
 
 
-def set_strip(r, strip):
+def set_strip(r, strip, face=None):
+    rows = strip.shape[0]
+    filled = 1
     r.strip_out[0] = strip
-    for i in range(1, STRIP_PLANES):
+    if face is not None:
+        filled += face.shape[0] // rows
+        faces = [face[pl.ds(i * rows, rows), :] for i in range(filled - 1)]
+        for i, part in enumerate(faces):
+            r.strip_out[1 + i] = part
+    for i in range(filled, r.strip_out.shape[0]):
         r.strip_out[i] = jnp.zeros_like(strip)
 
 
@@ -336,28 +351,26 @@
     r.strip_inner_out[...] = strip
 
 
-def velocity_edge(first, r):
+def velocity_edge(r):
     count, rows, depths = r.material.shape
     edges = Edges(rows, depths)
     planes = Planes(stress_of(r), STRESS_TAIL, STRESS_HEAD, r.one, r.two)
     fault = fault_row(rows)
     places = ends_of(count)
     row = pl.ds(fault, 1)
-    if first:
-        labels = [r.material[x, row, :] for x in range(count)]
-        lines = [looked_up(label, r.table, 2, CLASSES) for label in labels]
-        for x, line in enumerate(lines):
-            r.face_out[pl.ds(2 * count + x, 1), :] = line
-    if hasattr(r, "prestress"):
+    labels = [r.material[x, row, :] for x in range(count)]
+    push = [looked_up(label, r.table, 2, CLASSES) for label in labels]
+    lines = dict(enumerate(push, 2 * count))
+    halves = hasattr(r, "prestress")
+    if halves:
         own = r.normal.shape[0]
-        place = 3 * count
-        lines = [r.prestress[i, pl.ds(c, 1), :] for c in (0, 1) for i in range(own)]
-        fields = [field[...] for field in (r.normal, r.slip, r.zone, r.mask)]
-        for i, line in enumerate(lines):
-            r.face_out[pl.ds(place + i, 1), :] = line
-        for i, field in enumerate(fields):
-            r.face_out[pl.ds(place + (2 + i) * own, own), :] = field.astype(jnp.float32)
-
+        still = [[r.prestress[i, pl.ds(c, 1), :] for i in range(own)] for c in (0, 1)]
+        for field in (r.normal, r.slip, r.zone, r.mask):
+            still.append([field[pl.ds(i, 1), :].astype(jnp.float32) for i in range(own)])
+        lines.update(enumerate(sum(still, []), 3 * count))
+    else:
+        still = [[r.still[i, pl.ds(x, 1), :] for x in range(count)] for i in range(6)]
+        still[3] = [r.slip[pl.ds(x, 1), :] for x in range(count)]
 
     def write(x, new):
         for c in range(3):
@@ -367,12 +380,29 @@
     strip = r.strip_inner[...]
     for i, x in enumerate(places):
         strip = edges.packed(strip, x, [r.edge_out[c, i] for c in VEL_SLOTS])
-    set_strip(r, strip)
     new = Field(count, r.inner, r.edge_out)
-    lines = [new.rows(c, x)(fault, 1) for c in (0, 2) for x in range(count)]
-    for i, line in enumerate(lines):
+    faces = [[new.rows(c, x)(fault, 1) for x in range(count)] for c in (0, 2)]
+    lines.update(enumerate(sum(faces, [])))
+    for i in range(len(lines), r.face_out.shape[0]):
+        lines[i] = jnp.zeros((1, depths), jnp.float32)
+    for i, line in lines.items():
         r.face_out[pl.ds(i, 1), :] = line
+    set_strip(r, strip, r.face_out)
     edge_planes(new, VEL_TAIL, VEL_HEAD, r.one_out, r.two_out)
+
+    even = even_strike()
+    fields = [*faces, push, *still]
+    for i, field in enumerate(fields):
+        for j in (0, 1):
+            tail, head = field[len(field) - 2 + j], field[j]
+            at = pl.ds(2 * i + j, 1)
+            one, two = jnp.where(even, tail, head), jnp.where(even, head, tail)
+            for line, plane, alone in (
+                (one, r.one_out, r.line_one_out),
+                (two, r.two_out, r.line_two_out),
+            ):
+                plane[plane.shape[0] - 1, at, :] = line
+                alone[at, :] = line
 
 
 def stress_of(r):
@@ -389,36 +419,14 @@
     return Field(count, r.memory_inner, r.memory_edge)
 
 
-def fault_kernel(first, r):
-    own_face, other_face = r.face, r.other
-    own_first, other_first = (own_face, other_face) if first else (r.face_first, r.other_first)
-    rows, depths = r.strip.shape[1:]
-    count = r.change_out.shape[1]
-    middle = lax.axis_size("gy") // 2
-    side = lax.axis_index("gy")
+def slipped(r, own, other, still, slip, row, deep):
+    middle = lax.axis_size(GY) // 2
+    side = lax.axis_index(GY)
     plus = side == middle
     minus = side == middle - 1
-
-    def pair(own, other, place):
-        mine, theirs = own[pl.ds(place, count), :], other[pl.ds(place, count), :]
-        return jnp.where(plus, theirs, mine), jnp.where(plus, mine, theirs)
-
-    if hasattr(r, "still"):
-        still = r.still
-    else:
-        still = r.still_out
-        share = (own_face.shape[0] - 3 * count) // 6
-        for i in range(6):
-            mine = own_face[pl.ds(3 * count + i * share, share), :]
-            theirs = other_face[pl.ds(3 * count + i * share, share), :]
-            still[i, pl.ds(0, share), :] = jnp.where(plus, theirs, mine)
-            still[i, pl.ds(share, share), :] = jnp.where(plus, mine, theirs)
-    pre_x, pre_z, normal = still[0], still[1], still[2]
-    slip = still[3] if first else r.slip[...]
-    zone, mask = still[4], still[5]
-
-    row = lax.broadcasted_iota(jnp.int32, (count, depths), 0) + lax.axis_index("gx") * count
-    deep = lax.broadcasted_iota(jnp.int32, (count, depths), 1) + lax.axis_index("gz") * depths
+    minus_x, minus_z, minus_b = [jnp.where(plus, b, a) for a, b in zip(own, other)]
+    plus_x, plus_z, plus_b = [jnp.where(plus, a, b) for a, b in zip(own, other)]
+    pre_x, pre_z, normal, _, zone, mask = still
     inside = (row >= r.anchor[0]) & (row < r.anchor[0] + 2 * PATCH)
     inside = inside & (deep >= r.anchor[1]) & (deep < r.anchor[1] + 2 * PATCH)
     dynamic = 0.4 * looked_up(zone, r.friction, 0, ZONES)
@@ -426,9 +434,6 @@
         inside, dynamic, dynamic + 0.5 * looked_up(zone, r.friction, 1, ZONES)
     )
     distance = 0.2 * looked_up(zone, r.friction, 2, ZONES)
-    minus_x, plus_x = pair(own_face, other_face, 0)
-    minus_z, plus_z = pair(own_face, other_face, count)
-    minus_b, plus_b = pair(own_first, other_first, 2 * count)
     bsum = minus_b + plus_b
     trial_x = (plus_x - minus_x) / (DT * bsum) + pre_x
     trial_z = (plus_z - minus_z) / (DT * bsum) + pre_z
@@ -437,44 +442,96 @@
     strength = (static - (static - dynamic) * weaken) * normal
     factor = jnp.where(mask == 1.0, strength / jnp.maximum(size, strength), 1.0)
     new_slip = slip + DT * DT * bsum * (size - size * factor)
-    half = r.slip_out.shape[0]
-    if half < count:
-        new_slip = jnp.where(plus, new_slip[half:], new_slip[:half])
+    sign = jnp.where(minus, DT, 0.0) * minus_b - jnp.where(plus, DT, 0.0) * plus_b
+    return (trial_x * factor - pre_x) * sign, (trial_z * factor - pre_z) * sign, new_slip
+
+
+def fault_kernel(count, r):
+    rows, depths = r.strip.shape[1:]
+    plus = lax.axis_index(GY) == lax.axis_size(GY) // 2
+
+    def beside(place, size):
+        return r.strip[1 + place // rows, pl.ds(place % rows, size), :]
+
+    def nodes(source, source_beside, place, size):
+        return source[pl.ds(place, size), :], source_beside(place, size)
+
+    def cross(place, size):
+        return r.cross[pl.ds(place, size), :]
+
+    own = [jnp.concatenate(nodes(r.face, beside, i * count, count)) for i in range(3)]
+    other = [jnp.concatenate(nodes(r.other, cross, i * count, count)) for i in range(3)]
+    if hasattr(r, "still"):
+        still = [r.still[i] for i in range(6)]
+    else:
+        share = count // 2
+        still = []
+        for i in range(6):
+            place = 3 * count + i * share
+            mine = nodes(r.face, beside, place, share)
+            theirs = nodes(r.other, cross, place, share)
+            halves = []
+            for a, b in zip(mine, theirs):
+                halves += [jnp.where(plus, b, a), jnp.where(plus, a, b)]
+            still.append(jnp.concatenate(halves))
+        for i in range(6):
+            r.still_out[i] = still[i]
+    slip = r.slip[...] if hasattr(r, "slip") else still[3]
+    deep = lax.axis_index(GZ)
+    row = lax.broadcasted_iota(jnp.int32, (2 * count, depths), 0)
+    lane = lax.broadcasted_iota(jnp.int32, (2 * count, depths), 1)
+    lane = lane + jnp.where(row < count, deep, 1 - deep) * depths
+    row = row % count
+    place = row + lax.axis_index(GX) * count
+    change_x, change_z, new_slip = slipped(r, own, other, still, slip, place, lane)
     r.slip_out[...] = new_slip
-    sign = jnp.where(minus, DT, 0.0) * minus_b - jnp.where(plus, DT, 0.0) * plus_b
-    change_x = (trial_x * factor - pre_x) * sign
-    change_z = (trial_z * factor - pre_z) * sign
+    if hasattr(r, "new_slip_out"):
+        half = r.new_slip_out.shape[0]
+        r.new_slip_out[...] = jnp.where(plus, new_slip[half : 2 * half], new_slip[:half])
     r.change_out[0] = change_x
     r.change_out[1] = change_z
 
-    fault = fault_row(rows)
-    on_fault = lax.broadcasted_iota(jnp.int32, (rows, depths), 0) == fault
-    even = even_strike()
-    still_line = jnp.zeros((1, depths), jnp.float32)
-
-    def line(planes, i):
-        comp, place = planes[min(i, len(planes) - 1)]
-        return still_line if comp == 1 else r.change_out[comp // 2, pl.ds(place % count, 1), :]
-
-    pairs = []
-    for i in range(r.one_out.shape[0]):
-        right, left = line(VEL_TAIL, i), line(VEL_HEAD, i)
-        one, two = jnp.where(even, right, left), jnp.where(even, left, right)
-        one = r.one[i] + jnp.where(on_fault, one, 0.0)
-        pairs.append((one, r.two[i] + jnp.where(on_fault, two, 0.0)))
-    for i, (one, two) in enumerate(pairs):
-        r.one_out[i] = one
-        r.two_out[i] = two
+    on_fault = lax.broadcasted_iota(jnp.int32, (rows, depths), 0) == fault_row(rows)
     ends = jnp.zeros((count, depths), jnp.float32)
     pair = lax.broadcasted_iota(jnp.int32, (count, depths), 1) // 2
-    place = 4 * lax.broadcasted_iota(jnp.int32, (count, depths), 0)
-    upper = lax.axis_index("gz") == 0
-    for k, field in ((0, change_x), (2, change_z)):
-        turned = jnp.where(upper, pltpu.roll(field, 2, 1), field)
+    first = 4 * lax.broadcasted_iota(jnp.int32, (count, depths), 0)
+    for k, field in ((0, change_x[count:]), (2, change_z[count:])):
+        turned = jnp.where(deep == 0, field, pltpu.roll(field, 2, 1))
         turned = pltpu.roll(turned, 2 * k, 1, stride=8, stride_axis=0)
-        ends = jnp.where(pair == place + k, turned, ends)
+        ends = jnp.where(pair == first + k, turned, ends)
     line = jnp.sum(ends, axis=0, keepdims=True)
-    set_strip(r, r.strip[0] + jnp.where(on_fault, line, 0.0))
+    r.strip_out[0] = r.strip[0] + jnp.where(on_fault, line, 0.0)
+
+
+def end_changes(count, r):
+    depths = r.line_one.shape[1]
+    middle = lax.axis_size(GY) // 2
+    side = lax.axis_index(GY)
+    even = even_strike()
+    last = r.one.shape[0] - 1
+    pieces = []
+    for i in range(9):
+        at = pl.ds(2 * i, 2)
+        one, two = r.one[last, at, :], r.two[last, at, :]
+        far_one, far_two = r.line_one[at, :], r.line_two[at, :]
+        left, right = jnp.where(even, two, one), jnp.where(even, one, two)
+        far_left, far_right = jnp.where(even, far_two, far_one), jnp.where(even, far_one, far_two)
+        if i < 3:
+            pieces += [(i, left, right), (3 + i, far_left, far_right)]
+        else:
+            left = jnp.where(side == middle, left, far_left)
+            right = jnp.where(side == middle, far_right, right)
+            pieces.append((3 + i, left, right))
+    for i, left, right in pieces:
+        r.nodes[i, pl.ds(0, 2), :] = left
+        r.nodes[i, pl.ds(2, 2), :] = right
+    held = [r.nodes[i, pl.ds(0, 4), :] for i in range(12)]
+    row = lax.broadcasted_iota(jnp.int32, (4, depths), 0)
+    lane = lax.broadcasted_iota(jnp.int32, (4, depths), 1) + lax.axis_index(GZ) * depths
+    place = jnp.where(row < 2, row - 2, count + row - 2) + lax.axis_index(GX) * count
+    change = slipped(r, held[:3], held[3:6], held[6:], held[9], place, lane)
+    for i in range(2):
+        r.nodes[i, pl.ds(0, 4), :] = change[i]
 
 
 def stress_planes(r, xs, edges, planes, write):
@@ -564,7 +621,10 @@
 def stress_edge(last, r):
     count, rows, depths = r.material.shape
     edges = Edges(rows, depths, by_loads=True)
-    planes = Planes(Field(count, r.velocity), VEL_TAIL, VEL_HEAD, r.one, r.two)
+    end_changes(count, r)
+    on_fault = edges.row == fault_row(rows)
+    field = Field(count, r.velocity)
+    planes = Planes(field, VEL_TAIL, VEL_HEAD, r.one, r.two, r.nodes, on_fault)
     places = ends_of(count)
     copies = []
 
@@ -639,7 +699,7 @@
 
 
 def strike_swaps(count):
-    halves = lax.axis_size("gz")
+    halves = lax.axis_size(GZ)
     routes = []
     for start in (0, 1):
         partner = {}
@@ -649,8 +709,33 @@
                 partner[one], partner[other] = other, one
         for i in range(count * halves):
             partner.setdefault(i, i ^ 1)
-        routes.append((("gx", "gz"), sorted(partner.items())))
+        routes.append(((GX, GZ), sorted(partner.items())))
     return routes
+
+
+def fault_swaps(pair, sides):
+    across, cross = [], []
+    for side in range(sides):
+        for half in (0, 1):
+            place, over = 2 * side + half, 2 * (sum(pair) - side) + half
+            if side not in pair:
+                over = place ^ 1
+            across.append((place, over))
+            cross.append((place, over ^ 1 if side in pair else over))
+    return ((GY, GZ), across), ((GY, GZ), cross)
+
+
+def far_swap(route, pair, sides):
+    pairs = []
+    for place, partner in route[1]:
+        for side in range(sides):
+            here = ((place // 2) * sides + side) * 2 + place % 2
+            if place // 2 == partner // 2 or side not in pair:
+                there = here ^ 1
+            else:
+                there = ((partner // 2) * sides + sum(pair) - side) * 2 + partner % 2
+            pairs.append((here, there))
+    return (GX, GY, GZ), sorted(pairs)
 
 
 def sent(block, route):
@@ -684,19 +769,25 @@
     slip_path,
 ):
     _, count, rows, depths = velocity.shape
-    sides = lax.axis_size("gy")
+    sides = lax.axis_size(GY)
     middle = sides // 2
     banded = sides > 2
-    swaps = strike_swaps(lax.axis_size("gx"))
-    up_y, down_y = along("gy", sides, (middle - 1,))
-    across = ("gy", [(middle - 1, middle), (middle, middle - 1)])
-    deep = ("gz", [(0, 1), (1, 0)])
+    swaps = strike_swaps(lax.axis_size(GX))
+    up_y, down_y = along(GY, sides, (middle - 1,))
+    deep = (GZ, [(0, 1), (1, 0)])
+    pair = (middle - 1, middle)
+    across, cross = fault_swaps(pair, sides)
+    far = [far_swap(route, pair, sides) for route in swaps]
 
     plane = (rows, depths)
-    edge_shape = (max(len(STRESS_TAIL), len(STRESS_HEAD)), *plane)
-    travelling = {"one": edge_shape, "two": edge_shape, "strip": (STRIP_PLANES, *plane)}
+    edge_planes = max(len(STRESS_TAIL), len(STRESS_HEAD))
+
+    def travelling(planes):
+        return {"one": (planes, *plane), "two": (planes, *plane), "strip": (planes + 1, *plane)}
+
     inner, edge = (count - 4, *plane), (4, *plane)
     inner_ends = {"ends": pltpu.VMEM((count - 4, 3, *plane), jnp.float32)}
+    nodes = pltpu.VMEM((12, TILE, depths), jnp.float32)
     edge_ends = {"ends": pltpu.VMEM((4, 3, *plane), jnp.float32)}
 
     def travelled(packed):
@@ -722,7 +813,9 @@
                 fault_mask.astype(jnp.float32),
             ]
         )
-        still = {"still": lax.all_gather(still, "gy", axis=1, tiled=True)}
+        still = lax.all_gather(still, GY, axis=1, tiled=True)
+        still = jnp.concatenate([still, sent(still, deep)], axis=1)
+        still, slip = {"still": still}, still[3]
     else:
         still = {}
 
@@ -732,7 +825,7 @@
         pack_kernel,
         "pack",
         {"stress": stress},
-        travelling,
+        travelling(edge_planes),
         scratch={"held": pltpu.VMEM(stress.shape, jnp.float32), "sems": pltpu.SemaphoreType.DMA((8,))},
         apart=("stress",),
         vmem=6,
@@ -752,40 +845,44 @@
             scratch=inner_ends,
             micros=3,
         )
-        face_rows = 2 * count
+        face_rows = 3 * count
         ins = {**ins, **halos, **free}
-        if first:
-            face_rows += count
-            if not banded:
-                ins.update(prestress=prestress, normal=normal_stress, slip=slip_path)
-                ins.update(zone=zone_label, mask=fault_mask)
-                face_rows += 6 * normal_stress.shape[0]
+        if still:
+            ins.update(slip=slip, **still)
+        else:
+            ins.update(prestress=prestress, normal=normal_stress, slip=slip_path)
+            ins.update(zone=zone_label, mask=fault_mask)
+            face_rows += 6 * normal_stress.shape[0]
+        face_rows = -(-face_rows // rows) * rows
+        outs = {"edge": (3, *edge), "face": (face_rows, depths), "line_one": plane, "line_two": plane}
         packed = call(
-            functools.partial(velocity_edge, first),
+            velocity_edge,
             "velocity_edge",
             ins,
-            {"edge": (3, *edge), "face": (face_rows, depths), **travelling},
+            {**outs, **travelling(edge_planes + 1)},
             scratch=edge_ends,
         )
         free = {"inner": free["inner"], "edge": packed["edge"]}
+        strip, halos = travelled(packed)
         face = packed["face"]
-        other = sent(face, across)
-        ins = {key: packed[key] for key in travelling}
-        ins.update(face=face, other=other, friction=friction_table, anchor=patch_anchor, **still)
-        if first:
-            faces = {"face_first": face, "other_first": other}
-        else:
-            ins.update(slip=slip, **faces)
-        outs = {"change": (2, count, depths), "slip": (count, depths), **travelling}
+        rules = {"friction": friction_table, "anchor": patch_anchor}
+        ins = {"face": face, "other": sent(face, across), "cross": sent(face, cross), **strip}
+        ins.update(rules)
+        halos["line_one"] = sent(packed["line_one"], far[0])
+        halos["line_two"] = sent(packed["line_two"], far[1])
+        halos.update(rules)
+        if still:
+            ins.update(slip=slip, **still)
+        outs = {"change": (2, 2 * count, depths), "slip": (2 * count, depths), "strip": (1, *plane)}
         if last and not banded:
-            outs["slip"] = (count // sides, depths)
+            outs["new_slip"] = (count // sides, depths)
         if not still:
-            outs["still"] = (6, count, depths)
-        packed = call(functools.partial(fault_kernel, first), "fault", ins, outs, vmem=2)
+            outs["still"] = (6, 2 * count, depths)
+        packed = call(functools.partial(fault_kernel, count), "fault", ins, outs, vmem=3)
         slip = packed["slip"]
         if not still:
             still = {"still": packed["still"]}
-        strip, halos = travelled(packed)
+        strip = {"strip": packed["strip"]}
         ins = {**free, "change": packed["change"], **parts, **props, **strip}
         if banded:
             joined = jnp.concatenate(
@@ -800,8 +897,8 @@
             outs.update(new_velocity=velocity.shape, stress=stress.shape, memory=memory.shape)
             extra["apart"] = ["new_velocity_out", "stress_out", "memory_out"]
             if not banded:
-                ins["slip"] = slip
-                outs["new_slip"] = slip.shape
+                ins["slip"] = packed["new_slip"]
+                outs["new_slip"] = packed["new_slip"].shape
                 extra["apart"].append("new_slip_out")
             held = pltpu.VMEM((6, *inner), jnp.float32)
             sems = pltpu.SemaphoreType.DMA((count,))
@@ -831,6 +928,7 @@
                     "stress_held": held,
                     "memory_held": held,
                     "sems": pltpu.SemaphoreType.DMA((4,)),
+                    "nodes": nodes,
                     **edge_ends,
                 },
                 apart=("stress_done", "memory_done", "stress_out", "memory_out"),
@@ -846,8 +944,12 @@
                 functools.partial(stress_edge, last),
                 "stress_edge",
                 ins,
-                {"stress_edge": (6, *edge), "memory_edge": (6, *edge), **travelling},
-                scratch=edge_ends,
+                {
+                    "stress_edge": (6, *edge),
+                    "memory_edge": (6, *edge),
+                    **travelling(edge_planes),
+                },
+                scratch={"nodes": nodes, **edge_ends},
                 vmem=10,
             )
             parts = {
@@ -857,30 +959,30 @@
                 "memory_edge": packed["memory_edge"],
             }
     if banded:
-        held = jnp.where(lax.axis_index("gy") == middle, slip, 0.0)
-        slip = lax.psum_scatter(held, "gy", scatter_dimension=0, tiled=True)
+        held = jnp.where(lax.axis_index(GY) == middle, slip[:count], 0.0)
+        slip = lax.psum_scatter(held, GY, scatter_dimension=0, tiled=True)
     return (velocity, stress, memory, slip)
 
 
 def solution(mesh):
     in_specs = (
-        P(None, ("ens", "gx"), "gy", "gz"),
-        P(None, ("ens", "gx"), "gy", "gz"),
-        P(None, ("ens", "gx"), "gy", "gz"),
-        P(("ens", "gx"), "gy", "gz"),
-        P(None, "ens"),
-        P(("ens", "gx", "gy"), "gz"),
-        P(("ens", "gx", "gy"), "gz"),
-        P("ens"),
-        P(None, "ens"),
-        P(("ens", "gx", "gy"), None, "gz"),
-        P(("ens", "gx", "gy"), "gz"),
-        P(("ens", "gx", "gy"), "gz"),
+        P(None, (ENS, GX), GY, GZ),
+        P(None, (ENS, GX), GY, GZ),
+        P(None, (ENS, GX), GY, GZ),
+        P((ENS, GX), GY, GZ),
+        P(None, ENS),
+        P((ENS, GX, GY), GZ),
+        P((ENS, GX, GY), GZ),
+        P(ENS),
+        P(None, ENS),
+        P((ENS, GX, GY), None, GZ),
+        P((ENS, GX, GY), GZ),
+        P((ENS, GX, GY), GZ),
     )
     out_specs = (
-        P(None, ("ens", "gx"), "gy", "gz"),
-        P(None, ("ens", "gx"), "gy", "gz"),
-        P(None, ("ens", "gx"), "gy", "gz"),
-        P(("ens", "gx", "gy"), "gz"),
+        P(None, (ENS, GX), GY, GZ),
+        P(None, (ENS, GX), GY, GZ),
+        P(None, (ENS, GX), GY, GZ),
+        P((ENS, GX, GY), GZ),
     )
     return jax.shard_map(shards, mesh=mesh, in_specs=in_specs, out_specs=out_specs, check_vma=False)

time: 39.8 us -> 44.3 us (1.11)
  starting transfers between devices: 13.9 us -> 19.7 us
  waiting for transfers between devices: 8.05 us -> 5.72 us
  Pallas kernels: 15.4 us -> 16.3 us
    ppermute x14 -> x20, starting transfers between devices: 13.9 us -> 19.7 us  [sent(): return lax.ppermute(block, *route)]
    ppermute x14 -> x20, waiting for transfers between devices: 8.05 us -> 5.72 us  [sent(): return lax.ppermute(block, *route)]
    pallas_call x11, Pallas kernels: 15.4 us -> 16.3 us  [call(): pl.pallas_call(body, out_shape=shapes, in_specs=[place(key) for key in in...]
  transfers between devices with their start and end apart: 14 -> 20, of which waited for: 5 -> 5; matrix products, arithmetic and copies ran while one was open for 0% -> 0% of each run, Pallas kernels for 20% -> 23%
where the time goes in v8:
time: 44.3 us; the launch traced here: 44.1 us
  starting transfers between devices  19.7 us (44%)
  Pallas kernels  16.3 us (37%)
  waiting for transfers between devices  5.72 us (13%)
  local copies, waits for them, and re-layouts  1.47 us (3%)
  between operations  0.92 us (2%)
    ppermute x20, starting transfers between devices, sent(): return lax.ppermute(block, *route)  19.7 us
    pallas_call x11, Pallas kernels, call(): pl.pallas_call(body, out_shape=shapes, in_specs=[place(key) for key in in...  16.3 us
    ppermute x20, waiting for transfers between devices, sent(): return lax.ppermute(block, *route)  5.72 us
    unnamed x26, local copies, waits for them, and re-layouts  1.47 us
  transfers between devices with their start and end apart: 20, of which 5 were waited for; matrix products, arithmetic and copies ran while one was open for 0% of the time, Pallas kernels for 23%

profile of v8, /device:TPU:0, one launch (start us, length us, event | category | flops | bytes accessed | tf_op | source)
XLA Modules:
  0.0 44.1 jit_solution(14870610348897501132)
XLA Ops:
  0.6 1.4 %copy-done = f32[6,16,32,128]{3,2,1,0:T(8,128)S(1)} copy-done((f32[6,16,32,128]{3,2,1,0:T(8,128)S(1)}, f32[6,16,32,128]{3,2,1,0:T(8,128)}, u32[]{:S(2)}) %copy-start) | copy-done | bytes 1572888
  2.0 0.5 %pack.1 = (f32[5,32,128]{2,1,0:T(8,128)S(1)}, f32[5,32,128]{2,1,0:T(8,128)S(1)}, f32[6,32,128]{2,1,0:T(8,128)S(1)}) custom-call(f32[6,16,32,128]{3,2,1,0:T(8,128)S(1)} %copy-done), custom_call_target="tpu_custom_call" | custom-call | bytes 3690000 | tf_op jit(solution)/shard_map/pack/pallas_call | solution.py:678
  2.7 0.5 %collective-permute-start = (f32[6,32,128]{2,1,0:T(8,128)S(1)}, f32[6,32,128]{2,1,0:T(8,128)S(1)}, u32[]{:S(2)}, u32[]{:S(2)}) collective-permute-start(f32[6,32,128]{2,1,0:T(8,128)S(1)} %get-tuple-element.48), channel_id=1, source_target_pairs={{0,1},{1,0},{2,3},{3,2},{4,5},{5,4},{6,7},{7,6},{8,9},{9,8},{10,11... | collective-permute-start | bytes 294920 | tf_op jit(solution)/shard_map/ppermute | solution.py:742
  3.2 2.6 %collective-permute-start.1 = (f32[5,32,128]{2,1,0:T(8,128)S(1)}, f32[5,32,128]{2,1,0:T(8,128)S(1)}, u32[]{:S(2)}, u32[]{:S(2)}) collective-permute-start(f32[5,32,128]{2,1,0:T(8,128)S(1)} %get-tuple-element.50), channel_id=1, source_target_pairs={{0,4},{1,5},{4,0},{5,1},{8,12},{9,13},{12,8},{13,9},{2,6},{3,7},{6... | collective-permute-start | bytes 245768 | tf_op jit(solution)/shard_map/ppermute | solution.py:742
  5.8 0.2 collective-permute-start.2
  6.0 1.6 %velocity_inner.2 = (f32[3,12,32,128]{3,2,1,0:T(8,128)S(1)}, f32[32,128]{1,0:T(8,128)S(1)}) custom-call(f32[3,16,32,128]{3,2,1,0:T(8,128)S(1)} %copy-done.4, f32[6,16,32,128]{3,2,1,0:T(8,128)S(1)} %copy-done, s32[16,32,128]{2,1,0:T(8,128)S(1)} %copy-done.2, f32[5,8]{1,0:T(8,128)S(1)} %copy-done.5, f32[6,32,128]{2,1,0:T(8,128)S(1)} %collective-permute-done.refs_4_), custom_call_target="tpu_custom_call" | custom-call | bytes 11070000 | tf_op jit(solution)/shard_map/velocity_inner/pallas_call | solution.py:678
  7.6 1.3 %collective-permute-done.1.refs_5_ = f32[5,32,128]{2,1,0:T(8,128)S(1)} collective-permute-done((f32[5,32,128]{2,1,0:T(8,128)S(1)}, f32[5,32,128]{2,1,0:T(8,128)S(1)}, u32[]{:S(2)}, u32[]{:S(2)}) %collective-permute-start.1) | collective-permute-done | bytes 81952 | tf_op jit(solution)/shard_map/ppermute | solution.py:742
  9.0 1.1 %velocity_edge.2 = (f32[3,4,32,128]{3,2,1,0:T(8,128)S(1)}, f32[96,128]{1,0:T(8,128)S(1)}, f32[32,128]{1,0:T(8,128)S(1)}, f32[32,128]{1,0:T(8,128)S(1)}, f32[6,32...) custom-call(f32[3,16,32,128]{3,2,1,0:T(8,128)S(1)} %copy-done.4, ...), custom_call_target="tpu_custom_call" | custom-call | bytes 3690000 | tf_op jit(solution)/shard_map/velocity_edge/pallas_call | solution.py:678
  10.1 2.9 %collective-permute-start.6 = (f32[6,32,128]{2,1,0:T(8,128)S(1)}, f32[6,32,128]{2,1,0:T(8,128)S(1)}, u32[]{:S(2)}, u32[]{:S(2)}) collective-permute-start(f32[6,32,128]{2,1,0:T(8,128)S(1)} %get-tuple-element.60), channel_id=1, source_target_pairs={{0,4},{1,5},{4,0},{5,1},{8,12},{9,13},{12,8},{13,9},{2,6},{3,7},{6... | collective-permute-start | bytes 294920 | tf_op jit(solution)/shard_map/ppermute | solution.py:742
  13.0 0.2 collective-permute-start.7
  13.2 1.4 %collective-permute-start.4 = (f32[96,128]{1,0:T(8,128)S(1)}, f32[96,128]{1,0:T(8,128)S(1)}, u32[]{:S(2)}, u32[]{:S(2)}) collective-permute-start(f32[96,128]{1,0:T(8,128)S(1)} %get-tuple-element.54.refs_0_), channel_id=1, source_target_pairs={{0,3},{1,2},{2,1},{3,0},{4,7},{5,6},{6,5},{7,4},{8,11},{9,10},{10,... | collective-permute-start | bytes 147464 | tf_op jit(solution)/shard_map/ppermute | solution.py:742
  14.6 0.5 %collective-permute-start.3 = (f32[96,128]{1,0:T(8,128)S(1)}, f32[96,128]{1,0:T(8,128)S(1)}, u32[]{:S(2)}, u32[]{:S(2)}) collective-permute-start(f32[96,128]{1,0:T(8,128)S(1)} %get-tuple-element.54.refs_0_), channel_id=1, source_target_pairs={{0,2},{1,3},{2,0},{3,1},{4,6},{5,7},{6,4},{7,5},{8,10},{9,11},{10,... | collective-permute-start | bytes 147464 | tf_op jit(solution)/shard_map/ppermute | solution.py:742
  15.2 1.5 %collective-permute-done.4.refs_2_ = f32[96,128]{1,0:T(8,128)S(1)} collective-permute-done((f32[96,128]{1,0:T(8,128)S(1)}, f32[96,128]{1,0:T(8,128)S(1)}, u32[]{:S(2)}, u32[]{:S(2)}) %collective-permute-start.4) | collective-permute-done | bytes 49184 | tf_op jit(solution)/shard_map/ppermute | solution.py:742
  16.7 3.2 %collective-permute-start.8 = (f32[32,128]{1,0:T(8,128)S(1)}, f32[32,128]{1,0:T(8,128)S(1)}, u32[]{:S(2)}, u32[]{:S(2)}) collective-permute-start(f32[32,128]{1,0:T(8,128)S(1)} %get-tuple-element.62), channel_id=1, source_target_pairs={{0,6},{1,7},{2,4},{3,5},{4,2},{5,3},{6,0},{7,1},{8,14},{9,15},{10,... | collective-permute-start | bytes 49160 | tf_op jit(solution)/shard_map/ppermute | solution.py:742
  20.0 0.8 %fault.2 = (f32[2,32,128]{2,1,0:T(8,128)S(1)}, f32[32,128]{1,0:T(8,128)S(1)}, f32[1,32,128]{2,1,0:T(8,128)S(1)}, f32[6,32,128]{2,1,0:T(8,128)S(1)}) custom-call(f32[96,128]{1,0:T(8,128)S(1)} %get-tuple-element.54.refs_0_, f32[96,128]{1,0:T(8,128)S(1)} %collective-permute-done.3.refs_1_, f32[96,128]{1,0:T(8,128)S(1)} %collective-permute-done.4.refs_2_, ...), custom_call_target="tpu_custom_call" | custom-call | bytes 3690000 | tf_op jit(solution)/shard_map/fault/pallas_call | solution.py:678
  20.8 2.1 %stress_inner.2 = (f32[3,16,32,128]{3,2,1,0:T(8,128)S(1)}, f32[6,12,32,128]{3,2,1,0:T(8,128)S(1)}, f32[6,12,32,128]{3,2,1,0:T(8,128)S(1)}, f32[32,128]{1,0:T(8,128)S(1)}) custom-call(f32[3,12,32,128]{3,2,1,0:T(8,128)S(1)} %get-tuple-element.49.refs_7_.refs_0_, f32[3,4,32,128]{3,2,1,0:T(8,128)S(1)} %get-tuple-element.53.refs_1_, ...), custom_call_target="tpu_custom_call" | custom-call | bytes 11070000 | tf_op jit(solution)/shard_map/stress_inner/pallas_call | solution.py:678
  22.9 1.2 %stress_edge.2 = (f32[6,4,32,128]{3,2,1,0:T(8,128)S(1)}, f32[6,4,32,128]{3,2,1,0:T(8,128)S(1)}, f32[5,32,128]{2,1,0:T(8,128)S(1)}, f32[5,32,128]{2,1,0:T(8,128)S(1)}, f32[6,32,128]{2,1,0:T(8,128)S(1)}) custom-call(f32[3,16,32,128]{3,2,1,0:T(8,128)S(1)} %get-tuple-element.58.refs_0_, f32[6,16,32,128]{3,2,1,0:T(8,128)S(1)} %copy-done.1, ...), custom_call_target="tpu_custom_call" | custom-call | bytes 3690000 | tf_op jit(solution)/shard_map/stress_edge/pallas_call | solution.py:678
  24.2 0.6 %collective-permute-start.10 = (f32[6,32,128]{2,1,0:T(8,128)S(1)}, f32[6,32,128]{2,1,0:T(8,128)S(1)}, u32[]{:S(2)}, u32[]{:S(2)}) collective-permute-start(f32[6,32,128]{2,1,0:T(8,128)S(1)} %get-tuple-element.66), channel_id=1, source_target_pairs={{0,1},{1,0},{2,3},{3,2},{4,5},{5,4},{6,7},{7,6},{8,9},{9,8},{10,11... | collective-permute-start | bytes 294920 | tf_op jit(solution)/shard_map/ppermute | solution.py:742
  24.7 1.6 %collective-permute-start.11 = (f32[5,32,128]{2,1,0:T(8,128)S(1)}, f32[5,32,128]{2,1,0:T(8,128)S(1)}, u32[]{:S(2)}, u32[]{:S(2)}) collective-permute-start(f32[5,32,128]{2,1,0:T(8,128)S(1)} %get-tuple-element.68), channel_id=1, source_target_pairs={{0,4},{1,5},{4,0},{5,1},{8,12},{9,13},{12,8},{13,9},{2,6},{3,7},{6... | collective-permute-start | bytes 245768 | tf_op jit(solution)/shard_map/ppermute | solution.py:742
  26.5 1.6 %velocity_inner.3 = (f32[3,12,32,128]{3,2,1,0:T(8,128)S(1)}, f32[32,128]{1,0:T(8,128)S(1)}) custom-call(f32[3,16,32,128]{3,2,1,0:T(8,128)S(1)} %get-tuple-element.58.refs_0_, f32[6,12,32,128]{3,2,1,0:T(8,128)S(1)} %get-tuple-element.59.refs_12_.refs_1_.refs_3_, f32[6,4,32,128]{3,2,1,0:T(8,128)S(1)} %get-tuple-element.65.refs_2_.refs_4_, ...), custom_call_target="tpu_custom_call" | custom-call | bytes 11070000 | tf_op jit(solution)/shard_map/velocity_inner/pallas_call | solution.py:678
  28.1 1.3 %collective-permute-done.11.refs_6_ = f32[5,32,128]{2,1,0:T(8,128)S(1)} collective-permute-done((f32[5,32,128]{2,1,0:T(8,128)S(1)}, f32[5,32,128]{2,1,0:T(8,128)S(1)}, u32[]{:S(2)}, u32[]{:S(2)}) %collective-permute-start.11) | collective-permute-done | bytes 81952 | tf_op jit(solution)/shard_map/ppermute | solution.py:742
  29.4 1.1 %velocity_edge.3 = (f32[3,4,32,128]{3,2,1,0:T(8,128)S(1)}, f32[64,128]{1,0:T(8,128)S(1)}, f32[32,128]{1,0:T(8,128)S(1)}, f32[32,128]{1,0:T(8,128)S(1)}, f32[6,32...) custom-call(f32[3,16,32,128]{3,2,1,0:T(8,128)S(1)} %get-tuple-element.58.refs_0_, ...), custom_call_target="tpu_custom_call" | custom-call | bytes 3690000 | tf_op jit(solution)/shard_map/velocity_edge/pallas_call | solution.py:678
  30.5 1.9 %collective-permute-start.16 = (f32[6,32,128]{2,1,0:T(8,128)S(1)}, f32[6,32,128]{2,1,0:T(8,128)S(1)}, u32[]{:S(2)}, u32[]{:S(2)}) collective-permute-start(f32[6,32,128]{2,1,0:T(8,128)S(1)} %get-tuple-element.83), channel_id=1, source_target_pairs={{0,4},{1,5},{4,0},{5,1},{8,12},{9,13},{12,8},{13,9},{2,6},{3,7},{6... | collective-permute-start | bytes 294920 | tf_op jit(solution)/shard_map/ppermute | solution.py:742
  32.4 0.2 collective-permute-start.17
  32.6 1.2 %collective-permute-start.14 = (f32[64,128]{1,0:T(8,128)S(1)}, f32[64,128]{1,0:T(8,128)S(1)}, u32[]{:S(2)}, u32[]{:S(2)}) collective-permute-start(f32[64,128]{1,0:T(8,128)S(1)} %get-tuple-element.74.refs_0_), channel_id=1, source_target_pairs={{0,3},{1,2},{2,1},{3,0},{4,7},{5,6},{6,5},{7,4},{8,11},{9,10},{10,... | collective-permute-start | bytes 98312 | tf_op jit(solution)/shard_map/ppermute | solution.py:742
  33.8 0.8 %collective-permute-start.13 = (f32[64,128]{1,0:T(8,128)S(1)}, f32[64,128]{1,0:T(8,128)S(1)}, u32[]{:S(2)}, u32[]{:S(2)}) collective-permute-start(f32[64,128]{1,0:T(8,128)S(1)} %get-tuple-element.74.refs_0_), channel_id=1, source_target_pairs={{0,2},{1,3},{2,0},{3,1},{4,6},{5,7},{6,4},{7,5},{8,10},{9,11},{10,... | collective-permute-start | bytes 98312 | tf_op jit(solution)/shard_map/ppermute | solution.py:742
  34.5 1.4 %collective-permute-done.14.refs_2_ = f32[64,128]{1,0:T(8,128)S(1)} collective-permute-done((f32[64,128]{1,0:T(8,128)S(1)}, f32[64,128]{1,0:T(8,128)S(1)}, u32[]{:S(2)}, u32[]{:S(2)}) %collective-permute-start.14) | collective-permute-done | bytes 32800 | tf_op jit(solution)/shard_map/ppermute | solution.py:742
  35.9 1.5 %collective-permute-start.18 = (f32[32,128]{1,0:T(8,128)S(1)}, f32[32,128]{1,0:T(8,128)S(1)}, u32[]{:S(2)}, u32[]{:S(2)}) collective-permute-start(f32[32,128]{1,0:T(8,128)S(1)} %get-tuple-element.85), channel_id=1, source_target_pairs={{0,6},{1,7},{2,4},{3,5},{4,2},{5,3},{6,0},{7,1},{8,14},{9,15},{10,... | collective-permute-start | bytes 49160 | tf_op jit(solution)/shard_map/ppermute | solution.py:742
  37.5 0.2 collective-permute-done.13.refs_1_
  37.7 1.3 %fault.3 = (f32[2,32,128]{2,1,0:T(8,128)S(1)}, f32[32,128]{1,0:T(8,128)}, f32[1,32,128]{2,1,0:T(8,128)S(1)}, f32[8,128]{1,0:T(8,128)S(1)}) custom-call(f32[64,128]{1,0:T(8,128)S(1)} %get-tuple-element.74.refs_0_, f32[64,128]{1,0:T(8,128)S(1)} %collective-permute-done.13.refs_1_, f32[64,128]{1,0:T(8,128)S(1)} %collective-permute-done.14.refs_2_, ...), custom_call_target="tpu_custom_call" | custom-call | bytes 3690000 | tf_op jit(solution)/shard_map/fault/pallas_call | solution.py:678
  39.0 2.9 %stress_inner.3 = (f32[3,16,32,128]{3,2,1,0:T(8,128)S(1)}, f32[3,16,32,128]{3,2,1,0:T(8,128)}, f32[6,16,32,128]{3,2,1,0:T(8,128)}, f32[6,16,32,128]{3,2,1,0:T(8,128)}, f32[8,128]{1,0:T(8,128)}) custom-call(f32[3,12,32,128]{3,2,1,0:T(8,128)S(1)} %get-tuple-element.67.refs_8_.refs_0_, f32[3,4,32,128]{3,2,1,0:T(8,128)S(1)} %get-tuple-element.73.refs_1_, ...), custom_call_target="tpu_custom_call" | custom-call | bytes 11070000 | tf_op jit(solution)/shard_map/stress_inner/pallas_call | solution.py:678
  42.0 2.1 %stress_edge.3 = (f32[6,16,32,128]{3,2,1,0:T(8,128)}, f32[6,16,32,128]{3,2,1,0:T(8,128)}) custom-call(f32[3,16,32,128]{3,2,1,0:T(8,128)S(1)} %get-tuple-element.82.refs_0_, f32[6,12,32,128]{3,2,1,0:T(8,128)S(1)} %get-tuple-element.59.refs_12_.refs_1_.refs_3_, ...), custom_call_target="tpu_custom_call", output_to_operand_aliasing={{0}: (14, {}), {1}: (15, {})} | custom-call | bytes 3690000 | tf_op jit(solution)/shard_map/stress_edge/pallas_call | solution.py:678
  (45 shorter events, 0.4 us)
Async XLA Ops:
  2.0 4.0 %copy-start.2 = (s32[16,32,128]{2,1,0:T(8,128)S(1)}, s32[16,32,128]{2,1,0:T(8,128)}, u32[]{:S(2)}) copy-start(s32[16,32,128]{2,1,0:T(8,128)} %refs_5_.7) | copy-start | bytes 786436
  2.0 4.0 %copy-start.4 = (f32[3,16,32,128]{3,2,1,0:T(8,128)S(1)}, f32[3,16,32,128]{3,2,1,0:T(8,128)}, u32[]{:S(2)}) copy-start(f32[3,16,32,128]{3,2,1,0:T(8,128)} %refs_0_.5) | copy-start | bytes 2359300
  2.0 4.0 %copy-start.5 = (f32[5,8]{1,0:T(8,128)S(1)}, f32[5,8]{1,0:T(8,128)}, u32[]{:S(2)}) copy-start(f32[5,8]{1,0:T(8,128)} %refs_6_.3) | copy-start | bytes 484
  2.6 6.3 %copy-start.7 = (f32[8,2,128]{2,1,0:T(2,128)S(1)}, f32[8,2,128]{2,1,0:T(2,128)}, u32[]{:S(2)}) copy-start(f32[8,2,128]{2,1,0:T(2,128)} %refs_9_.1) | copy-start | bytes 24580
  2.6 6.3 %copy-start.9 = (f32[8,128]{1,0:T(8,128)S(1)}, f32[8,128]{1,0:T(8,128)}, u32[]{:S(2)}) copy-start(f32[8,128]{1,0:T(8,128)} %refs_10_.2) | copy-start | bytes 12292
  2.6 6.3 %copy-start.10 = (f32[8,128]{1,0:T(8,128)S(1)}, f32[8,128]{1,0:T(8,128)}, u32[]{:S(2)}) copy-start(f32[8,128]{1,0:T(8,128)} %refs_11_.2) | copy-start | bytes 12292
  2.6 6.3 %copy-start.11 = (s32[8,128]{1,0:T(8,128)S(1)}, s32[8,128]{1,0:T(8,128)}, u32[]{:S(2)}) copy-start(s32[8,128]{1,0:T(8,128)} %refs_12_.2) | copy-start | bytes 12292
  2.6 6.3 %copy-start.12 = (s32[8,128]{1,0:T(8,128)S(1)}, s32[8,128]{1,0:T(8,128)}, u32[]{:S(2)}) copy-start(s32[8,128]{1,0:T(8,128)} %refs_13_.2) | copy-start | bytes 12292
  2.7 3.3 %collective-permute-start = (f32[6,32,128]{2,1,0:T(8,128)S(1)}, f32[6,32,128]{2,1,0:T(8,128)S(1)}, u32[]{:S(2)}, u32[]{:S(2)}) collective-permute-start(f32[6,32,128]{2,1,0:T(8,128)S(1)} %get-tuple-element.48), channel_id=1, source_target_pairs={{0,1},{1,0},{2,3},{3,2},{4,5},{5,4},{6,7},{7,6},{8,9},{9,8},{10,11... | collective-permute-start | bytes 294920 | tf_op jit(solution)/shard_map/ppermute | solution.py:742
  3.2 5.7 %collective-permute-start.1 = (f32[5,32,128]{2,1,0:T(8,128)S(1)}, f32[5,32,128]{2,1,0:T(8,128)S(1)}, u32[]{:S(2)}, u32[]{:S(2)}) collective-permute-start(f32[5,32,128]{2,1,0:T(8,128)S(1)} %get-tuple-element.50), channel_id=1, source_target_pairs={{0,4},{1,5},{4,0},{5,1},{8,12},{9,13},{12,8},{13,9},{2,6},{3,7},{6... | collective-permute-start | bytes 245768 | tf_op jit(solution)/shard_map/ppermute | solution.py:742
  5.8 3.0 %collective-permute-start.2 = (f32[5,32,128]{2,1,0:T(8,128)S(1)}, f32[5,32,128]{2,1,0:T(8,128)S(1)}, u32[]{:S(2)}, u32[]{:S(2)}) collective-permute-start(f32[5,32,128]{2,1,0:T(8,128)S(1)} %get-tuple-element.51), channel_id=1, source_target_pairs={{0,1},{1,0},{4,8},{5,9},{8,4},{9,5},{12,13},{13,12},{2,3},{3,2},{6... | collective-permute-start | bytes 245768 | tf_op jit(solution)/shard_map/ppermute | solution.py:742
  8.9 11.1 %copy-start.6 = (f32[3,4]{1,0:T(4,128)S(1)}, f32[3,4]{1,0:T(4,128)}, u32[]{:S(2)}) copy-start(f32[3,4]{1,0:T(4,128)} %refs_12_.3) | copy-start | bytes 148
  8.9 11.1 %copy-start.8 = (s32[2]{0:T(128)S(1)}, s32[2]{0:T(128)}, u32[]{:S(2)}) copy-start(s32[2]{0:T(128)} %refs_13_.3) | copy-start | bytes 28
  8.9 11.9 %copy-start.1 = (f32[6,16,32,128]{3,2,1,0:T(8,128)S(1)}, f32[6,16,32,128]{3,2,1,0:T(8,128)}, u32[]{:S(2)}) copy-start(f32[6,16,32,128]{3,2,1,0:T(8,128)} %refs_1_.5) | copy-start | bytes 4718596
  8.9 11.9 %copy-start.3 = (f32[6,16,32,128]{3,2,1,0:T(8,128)S(1)}, f32[6,16,32,128]{3,2,1,0:T(8,128)}, u32[]{:S(2)}) copy-start(f32[6,16,32,128]{3,2,1,0:T(8,128)} %refs_2_.5) | copy-start | bytes 4718596
  10.0 9.9 %collective-permute-start.5 = (f32[7,32,128]{2,1,0:T(8,128)S(1)}, f32[7,32,128]{2,1,0:T(8,128)S(1)}, u32[]{:S(2)}, u32[]{:S(2)}) collective-permute-start(f32[7,32,128]{2,1,0:T(8,128)S(1)} %get-tuple-element.55), channel_id=1, source_target_pairs={{0,1},{1,0},{2,3},{3,2},{4,5},{5,4},{6,7},{7,6},{8,9},{9,8},{10,11... | collective-permute-start | bytes 344072 | tf_op jit(solution)/shard_map/ppermute | solution.py:742
  10.1 12.8 %collective-permute-start.6 = (f32[6,32,128]{2,1,0:T(8,128)S(1)}, f32[6,32,128]{2,1,0:T(8,128)S(1)}, u32[]{:S(2)}, u32[]{:S(2)}) collective-permute-start(f32[6,32,128]{2,1,0:T(8,128)S(1)} %get-tuple-element.60), channel_id=1, source_target_pairs={{0,4},{1,5},{4,0},{5,1},{8,12},{9,13},{12,8},{13,9},{2,6},{3,7},{6... | collective-permute-start | bytes 294920 | tf_op jit(solution)/shard_map/ppermute | solution.py:742
  13.0 9.9 %collective-permute-start.7 = (f32[6,32,128]{2,1,0:T(8,128)S(1)}, f32[6,32,128]{2,1,0:T(8,128)S(1)}, u32[]{:S(2)}, u32[]{:S(2)}) collective-permute-start(f32[6,32,128]{2,1,0:T(8,128)S(1)} %get-tuple-element.61), channel_id=1, source_target_pairs={{0,1},{1,0},{4,8},{5,9},{8,4},{9,5},{12,13},{13,12},{2,3},{3,2},{6... | collective-permute-start | bytes 294920 | tf_op jit(solution)/shard_map/ppermute | solution.py:742
  13.2 3.5 %collective-permute-start.4 = (f32[96,128]{1,0:T(8,128)S(1)}, f32[96,128]{1,0:T(8,128)S(1)}, u32[]{:S(2)}, u32[]{:S(2)}) collective-permute-start(f32[96,128]{1,0:T(8,128)S(1)} %get-tuple-element.54.refs_0_), channel_id=1, source_target_pairs={{0,3},{1,2},{2,1},{3,0},{4,7},{5,6},{6,5},{7,4},{8,11},{9,10},{10,... | collective-permute-start | bytes 147464 | tf_op jit(solution)/shard_map/ppermute | solution.py:742
  14.6 5.3 %collective-permute-start.3 = (f32[96,128]{1,0:T(8,128)S(1)}, f32[96,128]{1,0:T(8,128)S(1)}, u32[]{:S(2)}, u32[]{:S(2)}) collective-permute-start(f32[96,128]{1,0:T(8,128)S(1)} %get-tuple-element.54.refs_0_), channel_id=1, source_target_pairs={{0,2},{1,3},{2,0},{3,1},{4,6},{5,7},{6,4},{7,5},{8,10},{9,11},{10,... | collective-permute-start | bytes 147464 | tf_op jit(solution)/shard_map/ppermute | solution.py:742
  16.7 6.2 %collective-permute-start.8 = (f32[32,128]{1,0:T(8,128)S(1)}, f32[32,128]{1,0:T(8,128)S(1)}, u32[]{:S(2)}, u32[]{:S(2)}) collective-permute-start(f32[32,128]{1,0:T(8,128)S(1)} %get-tuple-element.62), channel_id=1, source_target_pairs={{0,6},{1,7},{2,4},{3,5},{4,2},{5,3},{6,0},{7,1},{8,14},{9,15},{10,... | collective-permute-start | bytes 49160 | tf_op jit(solution)/shard_map/ppermute | solution.py:742
  20.0 2.9 %collective-permute-start.9 = (f32[32,128]{1,0:T(8,128)S(1)}, f32[32,128]{1,0:T(8,128)S(1)}, u32[]{:S(2)}, u32[]{:S(2)}) collective-permute-start(f32[32,128]{1,0:T(8,128)S(1)} %get-tuple-element.63), channel_id=1, source_target_pairs={{0,1},{1,0},{2,3},{3,2},{4,10},{5,11},{6,8},{7,9},{8,6},{9,7},{10,... | collective-permute-start | bytes 49160 | tf_op jit(solution)/shard_map/ppermute | solution.py:742
  24.2 2.3 %collective-permute-start.10 = (f32[6,32,128]{2,1,0:T(8,128)S(1)}, f32[6,32,128]{2,1,0:T(8,128)S(1)}, u32[]{:S(2)}, u32[]{:S(2)}) collective-permute-start(f32[6,32,128]{2,1,0:T(8,128)S(1)} %get-tuple-element.66), channel_id=1, source_target_pairs={{0,1},{1,0},{2,3},{3,2},{4,5},{5,4},{6,7},{7,6},{8,9},{9,8},{10,11... | collective-permute-start | bytes 294920 | tf_op jit(solution)/shard_map/ppermute | solution.py:742
  24.7 4.6 %collective-permute-start.11 = (f32[5,32,128]{2,1,0:T(8,128)S(1)}, f32[5,32,128]{2,1,0:T(8,128)S(1)}, u32[]{:S(2)}, u32[]{:S(2)}) collective-permute-start(f32[5,32,128]{2,1,0:T(8,128)S(1)} %get-tuple-element.68), channel_id=1, source_target_pairs={{0,4},{1,5},{4,0},{5,1},{8,12},{9,13},{12,8},{13,9},{2,6},{3,7},{6... | collective-permute-start | bytes 245768 | tf_op jit(solution)/shard_map/ppermute | solution.py:742
  26.3 3.0 %collective-permute-start.12 = (f32[5,32,128]{2,1,0:T(8,128)S(1)}, f32[5,32,128]{2,1,0:T(8,128)S(1)}, u32[]{:S(2)}, u32[]{:S(2)}) collective-permute-start(f32[5,32,128]{2,1,0:T(8,128)S(1)} %get-tuple-element.69), channel_id=1, source_target_pairs={{0,1},{1,0},{4,8},{5,9},{8,4},{9,5},{12,13},{13,12},{2,3},{3,2},{6... | collective-permute-start | bytes 245768 | tf_op jit(solution)/shard_map/ppermute | solution.py:742
  30.4 7.3 %collective-permute-start.15 = (f32[7,32,128]{2,1,0:T(8,128)S(1)}, f32[7,32,128]{2,1,0:T(8,128)S(1)}, u32[]{:S(2)}, u32[]{:S(2)}) collective-permute-start(f32[7,32,128]{2,1,0:T(8,128)S(1)} %get-tuple-element.75), channel_id=1, source_target_pairs={{0,1},{1,0},{2,3},{3,2},{4,5},{5,4},{6,7},{7,6},{8,9},{9,8},{10,11... | collective-permute-start | bytes 344072 | tf_op jit(solution)/shard_map/ppermute | solution.py:742
  30.5 11.5 %collective-permute-start.16 = (f32[6,32,128]{2,1,0:T(8,128)S(1)}, f32[6,32,128]{2,1,0:T(8,128)S(1)}, u32[]{:S(2)}, u32[]{:S(2)}) collective-permute-start(f32[6,32,128]{2,1,0:T(8,128)S(1)} %get-tuple-element.83), channel_id=1, source_target_pairs={{0,4},{1,5},{4,0},{5,1},{8,12},{9,13},{12,8},{13,9},{2,6},{3,7},{6... | collective-permute-start | bytes 294920 | tf_op jit(solution)/shard_map/ppermute | solution.py:742
  32.4 9.6 %collective-permute-start.17 = (f32[6,32,128]{2,1,0:T(8,128)S(1)}, f32[6,32,128]{2,1,0:T(8,128)S(1)}, u32[]{:S(2)}, u32[]{:S(2)}) collective-permute-start(f32[6,32,128]{2,1,0:T(8,128)S(1)} %get-tuple-element.84), channel_id=1, source_target_pairs={{0,1},{1,0},{4,8},{5,9},{8,4},{9,5},{12,13},{13,12},{2,3},{3,2},{6... | collective-permute-start | bytes 294920 | tf_op jit(solution)/shard_map/ppermute | solution.py:742
  32.6 3.3 %collective-permute-start.14 = (f32[64,128]{1,0:T(8,128)S(1)}, f32[64,128]{1,0:T(8,128)S(1)}, u32[]{:S(2)}, u32[]{:S(2)}) collective-permute-start(f32[64,128]{1,0:T(8,128)S(1)} %get-tuple-element.74.refs_0_), channel_id=1, source_target_pairs={{0,3},{1,2},{2,1},{3,0},{4,7},{5,6},{6,5},{7,4},{8,11},{9,10},{10,... | collective-permute-start | bytes 98312 | tf_op jit(solution)/shard_map/ppermute | solution.py:742
  33.8 3.9 %collective-permute-start.13 = (f32[64,128]{1,0:T(8,128)S(1)}, f32[64,128]{1,0:T(8,128)S(1)}, u32[]{:S(2)}, u32[]{:S(2)}) collective-permute-start(f32[64,128]{1,0:T(8,128)S(1)} %get-tuple-element.74.refs_0_), channel_id=1, source_target_pairs={{0,2},{1,3},{2,0},{3,1},{4,6},{5,7},{6,4},{7,5},{8,10},{9,11},{10,... | collective-permute-start | bytes 98312 | tf_op jit(solution)/shard_map/ppermute | solution.py:742
  35.9 6.1 %collective-permute-start.18 = (f32[32,128]{1,0:T(8,128)S(1)}, f32[32,128]{1,0:T(8,128)S(1)}, u32[]{:S(2)}, u32[]{:S(2)}) collective-permute-start(f32[32,128]{1,0:T(8,128)S(1)} %get-tuple-element.85), channel_id=1, source_target_pairs={{0,6},{1,7},{2,4},{3,5},{4,2},{5,3},{6,0},{7,1},{8,14},{9,15},{10,... | collective-permute-start | bytes 49160 | tf_op jit(solution)/shard_map/ppermute | solution.py:742
  37.7 4.3 %collective-permute-start.19 = (f32[32,128]{1,0:T(8,128)S(1)}, f32[32,128]{1,0:T(8,128)S(1)}, u32[]{:S(2)}, u32[]{:S(2)}) collective-permute-start(f32[32,128]{1,0:T(8,128)S(1)} %get-tuple-element.86), channel_id=1, source_target_pairs={{0,1},{1,0},{2,3},{3,2},{4,10},{5,11},{6,8},{7,9},{8,6},{9,7},{10,... | collective-permute-start | bytes 49160 | tf_op jit(solution)/shard_map/ppermute | solution.py:742
  (1 other events, 1.4 us)

commit v9 on v8

--- a/solution.py
+++ b/solution.py
@@ -187,20 +187,20 @@
     def right(self, i):
         return jnp.where(self.even, self.first[i], self.second[i])
 
-    def changed(self, plane, comp, node):
+    def changed(self, plane, comp, end, node):
         if self.change is None or comp == 1:
             return plane
-        line = self.change[comp // 2, pl.ds(node, 1), :]
+        line = self.change[end, pl.ds(comp + node, 1), :]
         return plane + jnp.where(self.on_fault, line, 0.0)
 
     def __call__(self, comp, place):
         if place < 0:
             plane = self.left(self.tail.index((comp, place)))
-            return jnp.where(self.any_left, self.changed(plane, comp, place + 2), 0.0)
+            return jnp.where(self.any_left, self.changed(plane, comp, 0, place + 2), 0.0)
         if place >= self.count:
             beyond = place - self.count
             plane = self.right(self.head.index((comp, beyond)))
-            return jnp.where(self.any_right, self.changed(plane, comp, beyond + 2), 0.0)
+            return jnp.where(self.any_right, self.changed(plane, comp, 1, beyond), 0.0)
         return self.field(comp, place)
 
     def rows(self, comp, x):
@@ -361,16 +361,12 @@
     labels = [r.material[x, row, :] for x in range(count)]
     push = [looked_up(label, r.table, 2, CLASSES) for label in labels]
     lines = dict(enumerate(push, 2 * count))
-    halves = hasattr(r, "prestress")
-    if halves:
+    if hasattr(r, "prestress"):
         own = r.normal.shape[0]
         still = [[r.prestress[i, pl.ds(c, 1), :] for i in range(own)] for c in (0, 1)]
         for field in (r.normal, r.slip, r.zone, r.mask):
             still.append([field[pl.ds(i, 1), :].astype(jnp.float32) for i in range(own)])
         lines.update(enumerate(sum(still, []), 3 * count))
-    else:
-        still = [[r.still[i, pl.ds(x, 1), :] for x in range(count)] for i in range(6)]
-        still[3] = [r.slip[pl.ds(x, 1), :] for x in range(count)]
 
     def write(x, new):
         for c in range(3):
@@ -389,20 +385,6 @@
         r.face_out[pl.ds(i, 1), :] = line
     set_strip(r, strip, r.face_out)
     edge_planes(new, VEL_TAIL, VEL_HEAD, r.one_out, r.two_out)
-
-    even = even_strike()
-    fields = [*faces, push, *still]
-    for i, field in enumerate(fields):
-        for j in (0, 1):
-            tail, head = field[len(field) - 2 + j], field[j]
-            at = pl.ds(2 * i + j, 1)
-            one, two = jnp.where(even, tail, head), jnp.where(even, head, tail)
-            for line, plane, alone in (
-                (one, r.one_out, r.line_one_out),
-                (two, r.two_out, r.line_two_out),
-            ):
-                plane[plane.shape[0] - 1, at, :] = line
-                alone[at, :] = line
 
 
 def stress_of(r):
@@ -491,6 +473,14 @@
     r.change_out[0] = change_x
     r.change_out[1] = change_z
 
+    even = even_strike()
+    for c, field in enumerate((change_x, change_z)):
+        tail, head = field[count - 2 : count], field[:2]
+        r.fix_one_out[pl.ds(2 * c, 2), :] = jnp.where(even, tail, head)
+        r.fix_two_out[pl.ds(2 * c, 2), :] = jnp.where(even, head, tail)
+    for out in (r.fix_one_out, r.fix_two_out):
+        out[pl.ds(4, 4), :] = jnp.zeros((4, depths), jnp.float32)
+
     on_fault = lax.broadcasted_iota(jnp.int32, (rows, depths), 0) == fault_row(rows)
     ends = jnp.zeros((count, depths), jnp.float32)
     pair = lax.broadcasted_iota(jnp.int32, (count, depths), 1) // 2
@@ -501,37 +491,6 @@
         ends = jnp.where(pair == first + k, turned, ends)
     line = jnp.sum(ends, axis=0, keepdims=True)
     r.strip_out[0] = r.strip[0] + jnp.where(on_fault, line, 0.0)
-
-
-def end_changes(count, r):
-    depths = r.line_one.shape[1]
-    middle = lax.axis_size(GY) // 2
-    side = lax.axis_index(GY)
-    even = even_strike()
-    last = r.one.shape[0] - 1
-    pieces = []
-    for i in range(9):
-        at = pl.ds(2 * i, 2)
-        one, two = r.one[last, at, :], r.two[last, at, :]
-        far_one, far_two = r.line_one[at, :], r.line_two[at, :]
-        left, right = jnp.where(even, two, one), jnp.where(even, one, two)
-        far_left, far_right = jnp.where(even, far_two, far_one), jnp.where(even, far_one, far_two)
-        if i < 3:
-            pieces += [(i, left, right), (3 + i, far_left, far_right)]
-        else:
-            left = jnp.where(side == middle, left, far_left)
-            right = jnp.where(side == middle, far_right, right)
-            pieces.append((3 + i, left, right))
-    for i, left, right in pieces:
-        r.nodes[i, pl.ds(0, 2), :] = left
-        r.nodes[i, pl.ds(2, 2), :] = right
-    held = [r.nodes[i, pl.ds(0, 4), :] for i in range(12)]
-    row = lax.broadcasted_iota(jnp.int32, (4, depths), 0)
-    lane = lax.broadcasted_iota(jnp.int32, (4, depths), 1) + lax.axis_index(GZ) * depths
-    place = jnp.where(row < 2, row - 2, count + row - 2) + lax.axis_index(GX) * count
-    change = slipped(r, held[:3], held[3:6], held[6:], held[9], place, lane)
-    for i in range(2):
-        r.nodes[i, pl.ds(0, 4), :] = change[i]
 
 
 def stress_planes(r, xs, edges, planes, write):
@@ -621,7 +580,9 @@
 def stress_edge(last, r):
     count, rows, depths = r.material.shape
     edges = Edges(rows, depths, by_loads=True)
-    end_changes(count, r)
+    even = even_strike()
+    r.nodes[0] = jnp.where(even, r.fix_two[...], r.fix_one[...])
+    r.nodes[1] = jnp.where(even, r.fix_one[...], r.fix_two[...])
     on_fault = edges.row == fault_row(rows)
     field = Field(count, r.velocity)
     planes = Planes(field, VEL_TAIL, VEL_HEAD, r.one, r.two, r.nodes, on_fault)
@@ -723,19 +684,6 @@
             across.append((place, over))
             cross.append((place, over ^ 1 if side in pair else over))
     return ((GY, GZ), across), ((GY, GZ), cross)
-
-
-def far_swap(route, pair, sides):
-    pairs = []
-    for place, partner in route[1]:
-        for side in range(sides):
-            here = ((place // 2) * sides + side) * 2 + place % 2
-            if place // 2 == partner // 2 or side not in pair:
-                there = here ^ 1
-            else:
-                there = ((partner // 2) * sides + sum(pair) - side) * 2 + partner % 2
-            pairs.append((here, there))
-    return (GX, GY, GZ), sorted(pairs)
 
 
 def sent(block, route):
@@ -777,7 +725,6 @@
     deep = (GZ, [(0, 1), (1, 0)])
     pair = (middle - 1, middle)
     across, cross = fault_swaps(pair, sides)
-    far = [far_swap(route, pair, sides) for route in swaps]
 
     plane = (rows, depths)
     edge_planes = max(len(STRESS_TAIL), len(STRESS_HEAD))
@@ -787,7 +734,7 @@
 
     inner, edge = (count - 4, *plane), (4, *plane)
     inner_ends = {"ends": pltpu.VMEM((count - 4, 3, *plane), jnp.float32)}
-    nodes = pltpu.VMEM((12, TILE, depths), jnp.float32)
+    nodes = pltpu.VMEM((2, TILE, depths), jnp.float32)
     edge_ends = {"ends": pltpu.VMEM((4, 3, *plane), jnp.float32)}
 
     def travelled(packed):
@@ -847,33 +794,27 @@
         )
         face_rows = 3 * count
         ins = {**ins, **halos, **free}
-        if still:
-            ins.update(slip=slip, **still)
-        else:
+        if not still:
             ins.update(prestress=prestress, normal=normal_stress, slip=slip_path)
             ins.update(zone=zone_label, mask=fault_mask)
             face_rows += 6 * normal_stress.shape[0]
         face_rows = -(-face_rows // rows) * rows
-        outs = {"edge": (3, *edge), "face": (face_rows, depths), "line_one": plane, "line_two": plane}
         packed = call(
             velocity_edge,
             "velocity_edge",
             ins,
-            {**outs, **travelling(edge_planes + 1)},
+            {"edge": (3, *edge), "face": (face_rows, depths), **travelling(edge_planes)},
             scratch=edge_ends,
         )
         free = {"inner": free["inner"], "edge": packed["edge"]}
         strip, halos = travelled(packed)
         face = packed["face"]
-        rules = {"friction": friction_table, "anchor": patch_anchor}
         ins = {"face": face, "other": sent(face, across), "cross": sent(face, cross), **strip}
-        ins.update(rules)
-        halos["line_one"] = sent(packed["line_one"], far[0])
-        halos["line_two"] = sent(packed["line_two"], far[1])
-        halos.update(rules)
+        ins.update(friction=friction_table, anchor=patch_anchor)
         if still:
             ins.update(slip=slip, **still)
         outs = {"change": (2, 2 * count, depths), "slip": (2 * count, depths), "strip": (1, *plane)}
+        outs.update(fix_one=(TILE, depths), fix_two=(TILE, depths))
         if last and not banded:
             outs["new_slip"] = (count // sides, depths)
         if not still:
@@ -883,6 +824,8 @@
         if not still:
             still = {"still": packed["still"]}
         strip = {"strip": packed["strip"]}
+        halos["fix_one"] = sent(packed["fix_one"], swaps[0])
+        halos["fix_two"] = sent(packed["fix_two"], swaps[1])
         ins = {**free, "change": packed["change"], **parts, **props, **strip}
         if banded:
             joined = jnp.concatenate(

time: 44.3 us -> 45.5 us (1.027)
  waiting for transfers between devices: 5.72 us -> 9.27 us
  starting transfers between devices: 19.7 us -> 17.6 us
    ppermute x20, waiting for transfers between devices: 5.72 us -> 9.27 us  [sent(): return lax.ppermute(block, *route)]
    ppermute x20, starting transfers between devices: 19.7 us -> 17.6 us  [sent(): return lax.ppermute(block, *route)]
  transfers between devices with their start and end apart: 20 -> 20, of which waited for: 5 -> 6; matrix products, arithmetic and copies ran while one was open for 0% -> 0% of each run, Pallas kernels for 23% -> 22%
where the time goes in v9:
time: 45.5 us; the launch traced here: 45.3 us
  starting transfers between devices  17.6 us (39%)
  Pallas kernels  16.1 us (35%)
  waiting for transfers between devices  9.27 us (20%)
  local copies, waits for them, and re-layouts  1.47 us (3%)
  between operations  0.89 us (2%)
    ppermute x20, starting transfers between devices, sent(): return lax.ppermute(block, *route)  17.6 us
    pallas_call x11, Pallas kernels, call(): pl.pallas_call(body, out_shape=shapes, in_specs=[place(key) for key in in...  16.1 us
    ppermute x20, waiting for transfers between devices, sent(): return lax.ppermute(block, *route)  9.27 us
    unnamed x26, local copies, waits for them, and re-layouts  1.47 us
  transfers between devices with their start and end apart: 20, of which 6 were waited for; matrix products, arithmetic and copies ran while one was open for 0% of the time, Pallas kernels for 22%

profile of v9, /device:TPU:0, one launch (start us, length us, event | category | flops | bytes accessed | tf_op | source)
XLA Modules:
  0.0 45.3 jit_solution(13053527778947399024)
XLA Ops:
  0.6 1.4 %copy-done = f32[6,16,32,128]{3,2,1,0:T(8,128)S(1)} copy-done((f32[6,16,32,128]{3,2,1,0:T(8,128)S(1)}, f32[6,16,32,128]{3,2,1,0:T(8,128)}, u32[]{:S(2)}) %copy-start) | copy-done | bytes 1572888
  2.0 0.5 %pack.1 = (f32[5,32,128]{2,1,0:T(8,128)S(1)}, f32[5,32,128]{2,1,0:T(8,128)S(1)}, f32[6,32,128]{2,1,0:T(8,128)S(1)}) custom-call(f32[6,16,32,128]{3,2,1,0:T(8,128)S(1)} %copy-done), custom_call_target="tpu_custom_call" | custom-call | bytes 3690000 | tf_op jit(solution)/shard_map/pack/pallas_call | solution.py:639
  2.7 0.5 %collective-permute-start = (f32[6,32,128]{2,1,0:T(8,128)S(1)}, f32[6,32,128]{2,1,0:T(8,128)S(1)}, u32[]{:S(2)}, u32[]{:S(2)}) collective-permute-start(f32[6,32,128]{2,1,0:T(8,128)S(1)} %get-tuple-element.48), channel_id=1, source_target_pairs={{0,1},{1,0},{2,3},{3,2},{4,5},{5,4},{6,7},{7,6},{8,9},{9,8},{10,11... | collective-permute-start | bytes 294920 | tf_op jit(solution)/shard_map/ppermute | solution.py:690
  3.2 2.6 %collective-permute-start.1 = (f32[5,32,128]{2,1,0:T(8,128)S(1)}, f32[5,32,128]{2,1,0:T(8,128)S(1)}, u32[]{:S(2)}, u32[]{:S(2)}) collective-permute-start(f32[5,32,128]{2,1,0:T(8,128)S(1)} %get-tuple-element.50), channel_id=1, source_target_pairs={{0,4},{1,5},{4,0},{5,1},{8,12},{9,13},{12,8},{13,9},{2,6},{3,7},{6... | collective-permute-start | bytes 245768 | tf_op jit(solution)/shard_map/ppermute | solution.py:690
  5.8 0.2 collective-permute-start.2
  6.0 1.6 %velocity_inner.2 = (f32[3,12,32,128]{3,2,1,0:T(8,128)S(1)}, f32[32,128]{1,0:T(8,128)S(1)}) custom-call(f32[3,16,32,128]{3,2,1,0:T(8,128)S(1)} %copy-done.4, f32[6,16,32,128]{3,2,1,0:T(8,128)S(1)} %copy-done, s32[16,32,128]{2,1,0:T(8,128)S(1)} %copy-done.2, f32[5,8]{1,0:T(8,128)S(1)} %copy-done.5, f32[6,32,128]{2,1,0:T(8,128)S(1)} %collective-permute-done.refs_4_), custom_call_target="tpu_custom_call" | custom-call | bytes 11070000 | tf_op jit(solution)/shard_map/velocity_inner/pallas_call | solution.py:639
  7.6 1.3 %collective-permute-done.1.refs_5_ = f32[5,32,128]{2,1,0:T(8,128)S(1)} collective-permute-done((f32[5,32,128]{2,1,0:T(8,128)S(1)}, f32[5,32,128]{2,1,0:T(8,128)S(1)}, u32[]{:S(2)}, u32[]{:S(2)}) %collective-permute-start.1) | collective-permute-done | bytes 81952 | tf_op jit(solution)/shard_map/ppermute | solution.py:690
  9.0 1.1 %velocity_edge.2 = (f32[3,4,32,128]{3,2,1,0:T(8,128)S(1)}, f32[96,128]{1,0:T(8,128)S(1)}, f32[5,32,128]{2,1,0:T(8,128)S(1)}, f32[5,32,128]{2,1,0:T(8,128)S(1)}, f32[6,32,128]{2,1,0:T(8,128)S(1)}) custom-call(f32[3,16,32,128]{3,2,1,0:T(8,128)S(1)} %copy-done.4, f32[6,16,32,128]{3,2,1,0:T(8,128)S(1)} %copy-done, s32[16,32,128]{2,1,0:T(8,128)S(1)} %copy-done.2, ...), custom_call_target="tpu_custom_call" | custom-call | bytes 3690000 | tf_op jit(solution)/shard_map/velocity_edge/pallas_call | solution.py:639
  10.1 2.9 %collective-permute-start.6 = (f32[5,32,128]{2,1,0:T(8,128)S(1)}, f32[5,32,128]{2,1,0:T(8,128)S(1)}, u32[]{:S(2)}, u32[]{:S(2)}) collective-permute-start(f32[5,32,128]{2,1,0:T(8,128)S(1)} %get-tuple-element.60), channel_id=1, source_target_pairs={{0,4},{1,5},{4,0},{5,1},{8,12},{9,13},{12,8},{13,9},{2,6},{3,7},{6... | collective-permute-start | bytes 245768 | tf_op jit(solution)/shard_map/ppermute | solution.py:690
  13.2 1.4 %collective-permute-start.4 = (f32[96,128]{1,0:T(8,128)S(1)}, f32[96,128]{1,0:T(8,128)S(1)}, u32[]{:S(2)}, u32[]{:S(2)}) collective-permute-start(f32[96,128]{1,0:T(8,128)S(1)} %get-tuple-element.54.refs_0_), channel_id=1, source_target_pairs={{0,3},{1,2},{2,1},{3,0},{4,7},{5,6},{6,5},{7,4},{8,11},{9,10},{10,... | collective-permute-start | bytes 147464 | tf_op jit(solution)/shard_map/ppermute | solution.py:690
  14.6 0.5 %collective-permute-start.3 = (f32[96,128]{1,0:T(8,128)S(1)}, f32[96,128]{1,0:T(8,128)S(1)}, u32[]{:S(2)}, u32[]{:S(2)}) collective-permute-start(f32[96,128]{1,0:T(8,128)S(1)} %get-tuple-element.54.refs_0_), channel_id=1, source_target_pairs={{0,2},{1,3},{2,0},{3,1},{4,6},{5,7},{6,4},{7,5},{8,10},{9,11},{10,... | collective-permute-start | bytes 147464 | tf_op jit(solution)/shard_map/ppermute | solution.py:690
  15.2 1.5 %collective-permute-done.4.refs_2_ = f32[96,128]{1,0:T(8,128)S(1)} collective-permute-done((f32[96,128]{1,0:T(8,128)S(1)}, f32[96,128]{1,0:T(8,128)S(1)}, u32[]{:S(2)}, u32[]{:S(2)}) %collective-permute-start.4) | collective-permute-done | bytes 49184 | tf_op jit(solution)/shard_map/ppermute | solution.py:690
  16.7 2.0 %collective-permute-done.3.refs_1_ = f32[96,128]{1,0:T(8,128)S(1)} collective-permute-done((f32[96,128]{1,0:T(8,128)S(1)}, f32[96,128]{1,0:T(8,128)S(1)}, u32[]{:S(2)}, u32[]{:S(2)}) %collective-permute-start.3) | collective-permute-done | bytes 49184 | tf_op jit(solution)/shard_map/ppermute | solution.py:690
  18.7 0.8 %fault.2 = (f32[2,32,128]{2,1,0:T(8,128)S(1)}, f32[32,128]{1,0:T(8,128)S(1)}, f32[1,32,128]{2,1,0:T(8,128)S(1)}, f32[8,128]{1,0:T(8,128)S(1)}, f32[8,128]{1,0:T(8,128)S(1)}, /*index=5*/f32[6,32,128]{2,1,0:T(8,128)S(1)}) custom-call(f32[96,128]{1,0:T(8,128)S(1)} %get-tuple-element.54.refs_0_, f32[96,128]{1,0:T(8,128)S(1)} %collective-permute-done.3.refs_1_, ...), custom_call_target="tpu_custom_call" | custom-call | bytes 3690000 | tf_op jit(solution)/shard_map/fault/pallas_call | solution.py:639
  19.5 1.7 %collective-permute-start.8 = (f32[8,128]{1,0:T(8,128)S(1)}, f32[8,128]{1,0:T(8,128)S(1)}, u32[]{:S(2)}, u32[]{:S(2)}) collective-permute-start(f32[8,128]{1,0:T(8,128)S(1)} %get-tuple-element.62), channel_id=1, source_target_pairs={{0,4},{1,5},{4,0},{5,1},{8,12},{9,13},{12,8},{13,9},{2,6},{3,7},{6... | collective-permute-start | bytes 12296 | tf_op jit(solution)/shard_map/ppermute | solution.py:690
  21.2 2.1 %stress_inner.2 = (f32[3,16,32,128]{3,2,1,0:T(8,128)S(1)}, f32[6,12,32,128]{3,2,1,0:T(8,128)S(1)}, f32[6,12,32,128]{3,2,1,0:T(8,128)S(1)}, f32[32,128]{1,0:T(8,128)S(1)}) custom-call(f32[3,12,32,128]{3,2,1,0:T(8,128)S(1)} %get-tuple-element.49.refs_7_.refs_0_, f32[3,4,32,128]{3,2,1,0:T(8,128)S(1)} %get-tuple-element.53.refs_1_, ...), custom_call_target="tpu_custom_call" | custom-call | bytes 11070000 | tf_op jit(solution)/shard_map/stress_inner/pallas_call | solution.py:639
  23.3 1.2 %stress_edge.2 = (f32[6,4,32,128]{3,2,1,0:T(8,128)S(1)}, f32[6,4,32,128]{3,2,1,0:T(8,128)S(1)}, f32[5,32,128]{2,1,0:T(8,128)S(1)}, f32[5,32,128]{2,1,0:T(8,128)S(1)}, f32[6,32,128]{2,1,0:T(8,128)S(1)}) custom-call(f32[3,16,32,128]{3,2,1,0:T(8,128)S(1)} %get-tuple-element.58.refs_0_, f32[6,16,32,128]{3,2,1,0:T(8,128)S(1)} %copy-done.1, ...), custom_call_target="tpu_custom_call" | custom-call | bytes 3690000 | tf_op jit(solution)/shard_map/stress_edge/pallas_call | solution.py:639
  24.5 0.6 %collective-permute-start.10 = (f32[6,32,128]{2,1,0:T(8,128)S(1)}, f32[6,32,128]{2,1,0:T(8,128)S(1)}, u32[]{:S(2)}, u32[]{:S(2)}) collective-permute-start(f32[6,32,128]{2,1,0:T(8,128)S(1)} %get-tuple-element.66), channel_id=1, source_target_pairs={{0,1},{1,0},{2,3},{3,2},{4,5},{5,4},{6,7},{7,6},{8,9},{9,8},{10,11... | collective-permute-start | bytes 294920 | tf_op jit(solution)/shard_map/ppermute | solution.py:690
  25.0 1.7 %collective-permute-start.11 = (f32[5,32,128]{2,1,0:T(8,128)S(1)}, f32[5,32,128]{2,1,0:T(8,128)S(1)}, u32[]{:S(2)}, u32[]{:S(2)}) collective-permute-start(f32[5,32,128]{2,1,0:T(8,128)S(1)} %get-tuple-element.68), channel_id=1, source_target_pairs={{0,4},{1,5},{4,0},{5,1},{8,12},{9,13},{12,8},{13,9},{2,6},{3,7},{6... | collective-permute-start | bytes 245768 | tf_op jit(solution)/shard_map/ppermute | solution.py:690
  26.8 0.2 collective-permute-start.12
  27.0 1.6 %velocity_inner.3 = (f32[3,12,32,128]{3,2,1,0:T(8,128)S(1)}, f32[32,128]{1,0:T(8,128)S(1)}) custom-call(f32[3,16,32,128]{3,2,1,0:T(8,128)S(1)} %get-tuple-element.58.refs_0_, f32[6,12,32,128]{3,2,1,0:T(8,128)S(1)} %get-tuple-element.59.refs_10_.refs_1_.refs_3_, f32[6,4,32,128]{3,2,1,0:T(8,128)S(1)} %get-tuple-element.65.refs_2_.refs_4_, ...), custom_call_target="tpu_custom_call" | custom-call | bytes 11070000 | tf_op jit(solution)/shard_map/velocity_inner/pallas_call | solution.py:639
  28.6 1.3 %collective-permute-done.11.refs_6_ = f32[5,32,128]{2,1,0:T(8,128)S(1)} collective-permute-done((f32[5,32,128]{2,1,0:T(8,128)S(1)}, f32[5,32,128]{2,1,0:T(8,128)S(1)}, u32[]{:S(2)}, u32[]{:S(2)}) %collective-permute-start.11) | collective-permute-done | bytes 81952 | tf_op jit(solution)/shard_map/ppermute | solution.py:690
  29.8 1.1 %velocity_edge.3 = (f32[3,4,32,128]{3,2,1,0:T(8,128)S(1)}, f32[64,128]{1,0:T(8,128)S(1)}, f32[5,32,128]{2,1,0:T(8,128)S(1)}, f32[5,32,128]{2,1,0:T(8,128)S(1)}, f32[6,32,128]{2,1,0:T(8,128)S(1)}) custom-call(f32[3,16,32,128]{3,2,1,0:T(8,128)S(1)} %get-tuple-element.58.refs_0_, f32[6,12,32,128]{3,2,1,0:T(8,128)S(1)} %get-tuple-element.59.refs_10_.refs_1_.refs_3_, ...), custom_call_target="tpu_custom_call" | custom-call | bytes 3690000 | tf_op jit(solution)/shard_map/velocity_edge/pallas_call | solution.py:639
  31.0 1.8 %collective-permute-start.16 = (f32[5,32,128]{2,1,0:T(8,128)S(1)}, f32[5,32,128]{2,1,0:T(8,128)S(1)}, u32[]{:S(2)}, u32[]{:S(2)}) collective-permute-start(f32[5,32,128]{2,1,0:T(8,128)S(1)} %get-tuple-element.83), channel_id=1, source_target_pairs={{0,4},{1,5},{4,0},{5,1},{8,12},{9,13},{12,8},{13,9},{2,6},{3,7},{6... | collective-permute-start | bytes 245768 | tf_op jit(solution)/shard_map/ppermute | solution.py:690
  33.0 1.2 %collective-permute-start.14 = (f32[64,128]{1,0:T(8,128)S(1)}, f32[64,128]{1,0:T(8,128)S(1)}, u32[]{:S(2)}, u32[]{:S(2)}) collective-permute-start(f32[64,128]{1,0:T(8,128)S(1)} %get-tuple-element.72.refs_0_), channel_id=1, source_target_pairs={{0,3},{1,2},{2,1},{3,0},{4,7},{5,6},{6,5},{7,4},{8,11},{9,10},{10,... | collective-permute-start | bytes 98312 | tf_op jit(solution)/shard_map/ppermute | solution.py:690
  34.2 0.8 %collective-permute-start.13 = (f32[64,128]{1,0:T(8,128)S(1)}, f32[64,128]{1,0:T(8,128)S(1)}, u32[]{:S(2)}, u32[]{:S(2)}) collective-permute-start(f32[64,128]{1,0:T(8,128)S(1)} %get-tuple-element.72.refs_0_), channel_id=1, source_target_pairs={{0,2},{1,3},{2,0},{3,1},{4,6},{5,7},{6,4},{7,5},{8,10},{9,11},{10,... | collective-permute-start | bytes 98312 | tf_op jit(solution)/shard_map/ppermute | solution.py:690
  34.9 1.4 %collective-permute-done.14.refs_2_ = f32[64,128]{1,0:T(8,128)S(1)} collective-permute-done((f32[64,128]{1,0:T(8,128)S(1)}, f32[64,128]{1,0:T(8,128)S(1)}, u32[]{:S(2)}, u32[]{:S(2)}) %collective-permute-start.14) | collective-permute-done | bytes 32800 | tf_op jit(solution)/shard_map/ppermute | solution.py:690
  36.3 1.8 %collective-permute-done.13.refs_1_ = f32[64,128]{1,0:T(8,128)S(1)} collective-permute-done((f32[64,128]{1,0:T(8,128)S(1)}, f32[64,128]{1,0:T(8,128)S(1)}, u32[]{:S(2)}, u32[]{:S(2)}) %collective-permute-start.13) | collective-permute-done | bytes 32800 | tf_op jit(solution)/shard_map/ppermute | solution.py:690
  38.1 1.3 %fault.3 = (f32[2,32,128]{2,1,0:T(8,128)S(1)}, f32[32,128]{1,0:T(8,128)}, f32[1,32,128]{2,1,0:T(8,128)S(1)}, f32[8,128]{1,0:T(8,128)S(1)}, f32[8,128]{1,0:T(8,128)S(1)}, /*index=5*/f32[8,128]{1,0:T(8,128)S(1)}) custom-call(f32[64,128]{1,0:T(8,128)S(1)} %get-tuple-element.72.refs_0_, f32[64,128]{1,0:T(8,128)S(1)} %collective-permute-done.13.refs_1_, ...), custom_call_target="tpu_custom_call" | custom-call | bytes 3690000 | tf_op jit(solution)/shard_map/fault/pallas_call | solution.py:639
  39.4 0.9 %collective-permute-start.18 = (f32[8,128]{1,0:T(8,128)S(1)}, f32[8,128]{1,0:T(8,128)S(1)}, u32[]{:S(2)}, u32[]{:S(2)}) collective-permute-start(f32[8,128]{1,0:T(8,128)S(1)} %get-tuple-element.85), channel_id=1, source_target_pairs={{0,4},{1,5},{4,0},{5,1},{8,12},{9,13},{12,8},{13,9},{2,6},{3,7},{6... | collective-permute-start | bytes 12296 | tf_op jit(solution)/shard_map/ppermute | solution.py:690
  40.3 2.9 %stress_inner.3 = (f32[3,16,32,128]{3,2,1,0:T(8,128)S(1)}, f32[3,16,32,128]{3,2,1,0:T(8,128)}, f32[6,16,32,128]{3,2,1,0:T(8,128)}, f32[6,16,32,128]{3,2,1,0:T(8,128)}, f32[8,128]{1,0:T(8,128)}) custom-call(f32[3,12,32,128]{3,2,1,0:T(8,128)S(1)} %get-tuple-element.67.refs_8_.refs_0_, f32[3,4,32,128]{3,2,1,0:T(8,128)S(1)} %get-tuple-element.71.refs_1_, ...), custom_call_target="tpu_custom_call" | custom-call | bytes 11070000 | tf_op jit(solution)/shard_map/stress_inner/pallas_call | solution.py:639
  43.2 2.0 %stress_edge.3 = (f32[6,16,32,128]{3,2,1,0:T(8,128)}, f32[6,16,32,128]{3,2,1,0:T(8,128)}) custom-call(f32[3,16,32,128]{3,2,1,0:T(8,128)S(1)} %get-tuple-element.82.refs_0_, f32[6,12,32,128]{3,2,1,0:T(8,128)S(1)} %get-tuple-element.59.refs_10_.refs_1_.refs_3_, ...), custom_call_target="tpu_custom_call", output_to_operand_aliasing={{0}: (12, {}), {1}: (13, {})} | custom-call | bytes 3690000 | tf_op jit(solution)/shard_map/stress_edge/pallas_call | solution.py:639
  (45 shorter events, 0.6 us)
Async XLA Ops:
  2.0 4.0 %copy-start.2 = (s32[16,32,128]{2,1,0:T(8,128)S(1)}, s32[16,32,128]{2,1,0:T(8,128)}, u32[]{:S(2)}) copy-start(s32[16,32,128]{2,1,0:T(8,128)} %refs_5_.7) | copy-start | bytes 786436
  2.0 4.0 %copy-start.4 = (f32[3,16,32,128]{3,2,1,0:T(8,128)S(1)}, f32[3,16,32,128]{3,2,1,0:T(8,128)}, u32[]{:S(2)}) copy-start(f32[3,16,32,128]{3,2,1,0:T(8,128)} %refs_0_.5) | copy-start | bytes 2359300
  2.0 4.0 %copy-start.5 = (f32[5,8]{1,0:T(8,128)S(1)}, f32[5,8]{1,0:T(8,128)}, u32[]{:S(2)}) copy-start(f32[5,8]{1,0:T(8,128)} %refs_6_.3) | copy-start | bytes 484
  2.6 6.3 %copy-start.6 = (f32[8,2,128]{2,1,0:T(2,128)S(1)}, f32[8,2,128]{2,1,0:T(2,128)}, u32[]{:S(2)}) copy-start(f32[8,2,128]{2,1,0:T(2,128)} %refs_9_.1) | copy-start | bytes 24580
  2.6 6.3 %copy-start.8 = (f32[8,128]{1,0:T(8,128)S(1)}, f32[8,128]{1,0:T(8,128)}, u32[]{:S(2)}) copy-start(f32[8,128]{1,0:T(8,128)} %refs_10_.1) | copy-start | bytes 12292
  2.6 6.3 %copy-start.9 = (f32[8,128]{1,0:T(8,128)S(1)}, f32[8,128]{1,0:T(8,128)}, u32[]{:S(2)}) copy-start(f32[8,128]{1,0:T(8,128)} %refs_11_.1) | copy-start | bytes 12292
  2.6 6.3 %copy-start.10 = (s32[8,128]{1,0:T(8,128)S(1)}, s32[8,128]{1,0:T(8,128)}, u32[]{:S(2)}) copy-start(s32[8,128]{1,0:T(8,128)} %refs_12_.1) | copy-start | bytes 12292
  2.6 6.3 %copy-start.11 = (s32[8,128]{1,0:T(8,128)S(1)}, s32[8,128]{1,0:T(8,128)}, u32[]{:S(2)}) copy-start(s32[8,128]{1,0:T(8,128)} %refs_13_.1) | copy-start | bytes 12292
  2.7 3.3 %collective-permute-start = (f32[6,32,128]{2,1,0:T(8,128)S(1)}, f32[6,32,128]{2,1,0:T(8,128)S(1)}, u32[]{:S(2)}, u32[]{:S(2)}) collective-permute-start(f32[6,32,128]{2,1,0:T(8,128)S(1)} %get-tuple-element.48), channel_id=1, source_target_pairs={{0,1},{1,0},{2,3},{3,2},{4,5},{5,4},{6,7},{7,6},{8,9},{9,8},{10,11... | collective-permute-start | bytes 294920 | tf_op jit(solution)/shard_map/ppermute | solution.py:690
  3.2 5.7 %collective-permute-start.1 = (f32[5,32,128]{2,1,0:T(8,128)S(1)}, f32[5,32,128]{2,1,0:T(8,128)S(1)}, u32[]{:S(2)}, u32[]{:S(2)}) collective-permute-start(f32[5,32,128]{2,1,0:T(8,128)S(1)} %get-tuple-element.50), channel_id=1, source_target_pairs={{0,4},{1,5},{4,0},{5,1},{8,12},{9,13},{12,8},{13,9},{2,6},{3,7},{6... | collective-permute-start | bytes 245768 | tf_op jit(solution)/shard_map/ppermute | solution.py:690
  5.8 3.0 %collective-permute-start.2 = (f32[5,32,128]{2,1,0:T(8,128)S(1)}, f32[5,32,128]{2,1,0:T(8,128)S(1)}, u32[]{:S(2)}, u32[]{:S(2)}) collective-permute-start(f32[5,32,128]{2,1,0:T(8,128)S(1)} %get-tuple-element.51), channel_id=1, source_target_pairs={{0,1},{1,0},{4,8},{5,9},{8,4},{9,5},{12,13},{13,12},{2,3},{3,2},{6... | collective-permute-start | bytes 245768 | tf_op jit(solution)/shard_map/ppermute | solution.py:690
  8.9 9.8 %copy-start.7 = (f32[3,4]{1,0:T(4,128)S(1)}, f32[3,4]{1,0:T(4,128)}, u32[]{:S(2)}) copy-start(f32[3,4]{1,0:T(4,128)} %refs_4_.11) | copy-start | bytes 148
  8.9 9.8 %copy-start.12 = (s32[2]{0:T(128)S(1)}, s32[2]{0:T(128)}, u32[]{:S(2)}) copy-start(s32[2]{0:T(128)} %refs_5_.6) | copy-start | bytes 28
  8.9 12.2 %copy-start.1 = (f32[6,16,32,128]{3,2,1,0:T(8,128)S(1)}, f32[6,16,32,128]{3,2,1,0:T(8,128)}, u32[]{:S(2)}) copy-start(f32[6,16,32,128]{3,2,1,0:T(8,128)} %refs_1_.5) | copy-start | bytes 4718596
  8.9 12.2 %copy-start.3 = (f32[6,16,32,128]{3,2,1,0:T(8,128)S(1)}, f32[6,16,32,128]{3,2,1,0:T(8,128)}, u32[]{:S(2)}) copy-start(f32[6,16,32,128]{3,2,1,0:T(8,128)} %refs_2_.5) | copy-start | bytes 4718596
  10.0 8.7 %collective-permute-start.5 = (f32[6,32,128]{2,1,0:T(8,128)S(1)}, f32[6,32,128]{2,1,0:T(8,128)S(1)}, u32[]{:S(2)}, u32[]{:S(2)}) collective-permute-start(f32[6,32,128]{2,1,0:T(8,128)S(1)} %get-tuple-element.55), channel_id=1, source_target_pairs={{0,1},{1,0},{2,3},{3,2},{4,5},{5,4},{6,7},{7,6},{8,9},{9,8},{10,11... | collective-permute-start | bytes 294920 | tf_op jit(solution)/shard_map/ppermute | solution.py:690
  10.1 13.2 %collective-permute-start.6 = (f32[5,32,128]{2,1,0:T(8,128)S(1)}, f32[5,32,128]{2,1,0:T(8,128)S(1)}, u32[]{:S(2)}, u32[]{:S(2)}) collective-permute-start(f32[5,32,128]{2,1,0:T(8,128)S(1)} %get-tuple-element.60), channel_id=1, source_target_pairs={{0,4},{1,5},{4,0},{5,1},{8,12},{9,13},{12,8},{13,9},{2,6},{3,7},{6... | collective-permute-start | bytes 245768 | tf_op jit(solution)/shard_map/ppermute | solution.py:690
  13.0 10.2 %collective-permute-start.7 = (f32[5,32,128]{2,1,0:T(8,128)S(1)}, f32[5,32,128]{2,1,0:T(8,128)S(1)}, u32[]{:S(2)}, u32[]{:S(2)}) collective-permute-start(f32[5,32,128]{2,1,0:T(8,128)S(1)} %get-tuple-element.61), channel_id=1, source_target_pairs={{0,1},{1,0},{4,8},{5,9},{8,4},{9,5},{12,13},{13,12},{2,3},{3,2},{6... | collective-permute-start | bytes 245768 | tf_op jit(solution)/shard_map/ppermute | solution.py:690
  13.2 3.5 %collective-permute-start.4 = (f32[96,128]{1,0:T(8,128)S(1)}, f32[96,128]{1,0:T(8,128)S(1)}, u32[]{:S(2)}, u32[]{:S(2)}) collective-permute-start(f32[96,128]{1,0:T(8,128)S(1)} %get-tuple-element.54.refs_0_), channel_id=1, source_target_pairs={{0,3},{1,2},{2,1},{3,0},{4,7},{5,6},{6,5},{7,4},{8,11},{9,10},{10,... | collective-permute-start | bytes 147464 | tf_op jit(solution)/shard_map/ppermute | solution.py:690
  14.6 4.1 %collective-permute-start.3 = (f32[96,128]{1,0:T(8,128)S(1)}, f32[96,128]{1,0:T(8,128)S(1)}, u32[]{:S(2)}, u32[]{:S(2)}) collective-permute-start(f32[96,128]{1,0:T(8,128)S(1)} %get-tuple-element.54.refs_0_), channel_id=1, source_target_pairs={{0,2},{1,3},{2,0},{3,1},{4,6},{5,7},{6,4},{7,5},{8,10},{9,11},{10,... | collective-permute-start | bytes 147464 | tf_op jit(solution)/shard_map/ppermute | solution.py:690
  19.5 3.8 %collective-permute-start.8 = (f32[8,128]{1,0:T(8,128)S(1)}, f32[8,128]{1,0:T(8,128)S(1)}, u32[]{:S(2)}, u32[]{:S(2)}) collective-permute-start(f32[8,128]{1,0:T(8,128)S(1)} %get-tuple-element.62), channel_id=1, source_target_pairs={{0,4},{1,5},{4,0},{5,1},{8,12},{9,13},{12,8},{13,9},{2,6},{3,7},{6... | collective-permute-start | bytes 12296 | tf_op jit(solution)/shard_map/ppermute | solution.py:690
  21.2 2.1 %collective-permute-start.9 = (f32[8,128]{1,0:T(8,128)S(1)}, f32[8,128]{1,0:T(8,128)S(1)}, u32[]{:S(2)}, u32[]{:S(2)}) collective-permute-start(f32[8,128]{1,0:T(8,128)S(1)} %get-tuple-element.63), channel_id=1, source_target_pairs={{0,1},{1,0},{4,8},{5,9},{8,4},{9,5},{12,13},{13,12},{2,3},{3,2},{6... | collective-permute-start | bytes 12296 | tf_op jit(solution)/shard_map/ppermute | solution.py:690
  24.5 2.5 %collective-permute-start.10 = (f32[6,32,128]{2,1,0:T(8,128)S(1)}, f32[6,32,128]{2,1,0:T(8,128)S(1)}, u32[]{:S(2)}, u32[]{:S(2)}) collective-permute-start(f32[6,32,128]{2,1,0:T(8,128)S(1)} %get-tuple-element.66), channel_id=1, source_target_pairs={{0,1},{1,0},{2,3},{3,2},{4,5},{5,4},{6,7},{7,6},{8,9},{9,8},{10,11... | collective-permute-start | bytes 294920 | tf_op jit(solution)/shard_map/ppermute | solution.py:690
  25.0 4.8 %collective-permute-start.11 = (f32[5,32,128]{2,1,0:T(8,128)S(1)}, f32[5,32,128]{2,1,0:T(8,128)S(1)}, u32[]{:S(2)}, u32[]{:S(2)}) collective-permute-start(f32[5,32,128]{2,1,0:T(8,128)S(1)} %get-tuple-element.68), channel_id=1, source_target_pairs={{0,4},{1,5},{4,0},{5,1},{8,12},{9,13},{12,8},{13,9},{2,6},{3,7},{6... | collective-permute-start | bytes 245768 | tf_op jit(solution)/shard_map/ppermute | solution.py:690
  26.8 3.0 %collective-permute-start.12 = (f32[5,32,128]{2,1,0:T(8,128)S(1)}, f32[5,32,128]{2,1,0:T(8,128)S(1)}, u32[]{:S(2)}, u32[]{:S(2)}) collective-permute-start(f32[5,32,128]{2,1,0:T(8,128)S(1)} %get-tuple-element.69), channel_id=1, source_target_pairs={{0,1},{1,0},{4,8},{5,9},{8,4},{9,5},{12,13},{13,12},{2,3},{3,2},{6... | collective-permute-start | bytes 245768 | tf_op jit(solution)/shard_map/ppermute | solution.py:690
  30.9 7.2 %collective-permute-start.15 = (f32[6,32,128]{2,1,0:T(8,128)S(1)}, f32[6,32,128]{2,1,0:T(8,128)S(1)}, u32[]{:S(2)}, u32[]{:S(2)}) collective-permute-start(f32[6,32,128]{2,1,0:T(8,128)S(1)} %get-tuple-element.73), channel_id=1, source_target_pairs={{0,1},{1,0},{2,3},{3,2},{4,5},{5,4},{6,7},{7,6},{8,9},{9,8},{10,11... | collective-permute-start | bytes 294920 | tf_op jit(solution)/shard_map/ppermute | solution.py:690
  31.0 12.2 %collective-permute-start.16 = (f32[5,32,128]{2,1,0:T(8,128)S(1)}, f32[5,32,128]{2,1,0:T(8,128)S(1)}, u32[]{:S(2)}, u32[]{:S(2)}) collective-permute-start(f32[5,32,128]{2,1,0:T(8,128)S(1)} %get-tuple-element.83), channel_id=1, source_target_pairs={{0,4},{1,5},{4,0},{5,1},{8,12},{9,13},{12,8},{13,9},{2,6},{3,7},{6... | collective-permute-start | bytes 245768 | tf_op jit(solution)/shard_map/ppermute | solution.py:690
  32.8 10.4 %collective-permute-start.17 = (f32[5,32,128]{2,1,0:T(8,128)S(1)}, f32[5,32,128]{2,1,0:T(8,128)S(1)}, u32[]{:S(2)}, u32[]{:S(2)}) collective-permute-start(f32[5,32,128]{2,1,0:T(8,128)S(1)} %get-tuple-element.84), channel_id=1, source_target_pairs={{0,1},{1,0},{4,8},{5,9},{8,4},{9,5},{12,13},{13,12},{2,3},{3,2},{6... | collective-permute-start | bytes 245768 | tf_op jit(solution)/shard_map/ppermute | solution.py:690
  33.0 3.3 %collective-permute-start.14 = (f32[64,128]{1,0:T(8,128)S(1)}, f32[64,128]{1,0:T(8,128)S(1)}, u32[]{:S(2)}, u32[]{:S(2)}) collective-permute-start(f32[64,128]{1,0:T(8,128)S(1)} %get-tuple-element.72.refs_0_), channel_id=1, source_target_pairs={{0,3},{1,2},{2,1},{3,0},{4,7},{5,6},{6,5},{7,4},{8,11},{9,10},{10,... | collective-permute-start | bytes 98312 | tf_op jit(solution)/shard_map/ppermute | solution.py:690
  34.2 3.9 %collective-permute-start.13 = (f32[64,128]{1,0:T(8,128)S(1)}, f32[64,128]{1,0:T(8,128)S(1)}, u32[]{:S(2)}, u32[]{:S(2)}) collective-permute-start(f32[64,128]{1,0:T(8,128)S(1)} %get-tuple-element.72.refs_0_), channel_id=1, source_target_pairs={{0,2},{1,3},{2,0},{3,1},{4,6},{5,7},{6,4},{7,5},{8,10},{9,11},{10,... | collective-permute-start | bytes 98312 | tf_op jit(solution)/shard_map/ppermute | solution.py:690
  39.4 3.8 %collective-permute-start.18 = (f32[8,128]{1,0:T(8,128)S(1)}, f32[8,128]{1,0:T(8,128)S(1)}, u32[]{:S(2)}, u32[]{:S(2)}) collective-permute-start(f32[8,128]{1,0:T(8,128)S(1)} %get-tuple-element.85), channel_id=1, source_target_pairs={{0,4},{1,5},{4,0},{5,1},{8,12},{9,13},{12,8},{13,9},{2,6},{3,7},{6... | collective-permute-start | bytes 12296 | tf_op jit(solution)/shard_map/ppermute | solution.py:690
  40.3 2.9 %collective-permute-start.19 = (f32[8,128]{1,0:T(8,128)S(1)}, f32[8,128]{1,0:T(8,128)S(1)}, u32[]{:S(2)}, u32[]{:S(2)}) collective-permute-start(f32[8,128]{1,0:T(8,128)S(1)} %get-tuple-element.86), channel_id=1, source_target_pairs={{0,1},{1,0},{4,8},{5,9},{8,4},{9,5},{12,13},{13,12},{2,3},{3,2},{6... | collective-permute-start | bytes 12296 | tf_op jit(solution)/shard_map/ppermute | solution.py:690
  (1 other events, 1.4 us)

commit v10 on v7

--- a/solution.py
+++ b/solution.py
@@ -17,6 +17,7 @@
 FAR = -1.0 / 24.0
 DT = 0.15
 TILE = 8
+ENS, GX, GY, GZ = "ens", "gx", "gy", "gz"
 STRIP_PLANES = 6
 
 XX, YY, ZZ, XY, XZ, YZ = range(6)
@@ -49,7 +50,7 @@
         row = lax.broadcasted_iota(jnp.int32, (TILE, depths), 0)
         self.row = lax.broadcasted_iota(jnp.int32, (rows, depths), 0)
         self.tile_row = row
-        self.deep = lax.axis_index("gz")
+        self.deep = lax.axis_index(GZ)
         near = (self.deep == 0) & (lane < 2) | (self.deep == 1) & (lane >= depths - 2)
         self.near = jnp.where(near, 1.0, 0.0)
         self.zero = jnp.minimum(self.deep, 0)
@@ -177,8 +178,8 @@
         self.first, self.second = first, second
         self.tail, self.head = tail, head
         self.even = even_strike()
-        self.any_left = lax.axis_index("gx") > 0
-        self.any_right = lax.axis_index("gx") < lax.axis_size("gx") - 1
+        self.any_left = lax.axis_index(GX) > 0
+        self.any_right = lax.axis_index(GX) < lax.axis_size(GX) - 1
 
     def left(self, i):
         plane = jnp.where(self.even, self.second[i], self.first[i])
@@ -228,7 +229,7 @@
 
 
 def even_strike():
-    return lax.axis_index("gx") % 2 == 0
+    return lax.axis_index(GX) % 2 == 0
 
 
 def edge_planes(field, tail, head, first_out, second_out):
@@ -246,7 +247,7 @@
 
 
 def fault_row(rows):
-    return jnp.where(lax.axis_index("gy") == lax.axis_size("gy") // 2, 0, rows - 1)
+    return jnp.where(lax.axis_index(GY) == lax.axis_size(GY) // 2, 0, rows - 1)
 
 
 def pack_kernel(r):
@@ -283,107 +284,106 @@
         r.strip_out[i] = jnp.zeros_like(strip)
 
 
-def unpack(r, xs, edges):
+def unpack(count, r, edges):
     strip = r.strip[0]
-    for i, x in enumerate(xs):
+    for x in range(count):
         for k in range(3):
-            r.ends[i, k] = edges.ends(strip, x, k)
-
-
-def velocity_planes(r, xs, edges, planes, write):
-    band = Bands(getattr(r, "lower", None), getattr(r, "upper", None), STRESS_TAIL_Y, STRESS_HEAD_Y)
-    unpack(r, xs, edges)
-
-    def new(x):
-        push = DT * looked_up(r.material[x], r.table, 2, CLASSES)
-        ends = [r.ends[xs.index(x), k] for k in range(3)]
-        along_x = (
-            planes.forward_x(XX, x)
-            + edges.backward_y(planes, XY, x, band(XY, x))
-            + edges.backward_z(planes(XZ, x), ends[0])
-        )
-        along_y = (
-            planes.backward_x(XY, x)
-            + edges.forward_y(planes, YY, x, band(YY, x))
-            + edges.backward_z(planes(YZ, x), ends[1])
-        )
-        along_z = (
-            planes.backward_x(XZ, x)
-            + edges.backward_y(planes, YZ, x, band(YZ, x))
-            + edges.forward_z(planes(ZZ, x), ends[2])
-        )
-        rates = (along_x, along_y, along_z)
-        return [r.velocity[c, x] + push * rate for c, rate in enumerate(rates)]
-
-    for group in grouped(xs, 3 if len(xs) % 3 == 0 else 2):
-        for x, values in [(x, new(x)) for x in group]:
-            write(x, values)
-
-
-def velocity_inner(r):
+            r.ends[x, k] = edges.ends(strip, x, k)
+
+
+def velocity_across(planes, x):
+    return planes.forward_x(XX, x), planes.backward_x(XY, x), planes.backward_x(XZ, x)
+
+
+def velocity_inner(first, r):
     count, rows, depths = r.material.shape
     edges = Edges(rows, depths)
-    planes = Planes(stress_of(r), STRESS_TAIL, STRESS_HEAD)
-
-    def write(x, new):
-        for c in range(3):
-            r.inner_out[c, x - 2] = new[c]
-
-    velocity_planes(r, inside(count), edges, planes, write)
+    planes = Planes(stress_of(count, r), STRESS_TAIL, STRESS_HEAD)
+    band = Bands(getattr(r, "lower", None), getattr(r, "upper", None), STRESS_TAIL_Y, STRESS_HEAD_Y)
+    unpack(count, r, edges)
+
+    def beside(x):
+        ends = [r.ends[x, k] for k in range(3)]
+        return (
+            edges.backward_y(planes, XY, x, band(XY, x)) + edges.backward_z(planes(XZ, x), ends[0]),
+            edges.forward_y(planes, YY, x, band(YY, x)) + edges.backward_z(planes(YZ, x), ends[1]),
+            edges.backward_y(planes, YZ, x, band(YZ, x)) + edges.forward_z(planes(ZZ, x), ends[2]),
+        )
+
+    def push(x):
+        return DT * looked_up(r.material[x], r.table, 2, CLASSES)
+
+    def new(x):
+        rates = zip(velocity_across(planes, x), beside(x))
+        return [r.velocity[c, x] + push(x) * (a + b) for c, (a, b) in enumerate(rates)]
+
+    for group in grouped(inside(count), 3 if (count - 4) % 3 == 0 else 2):
+        for x, values in [(x, new(x)) for x in group]:
+            for c in range(3):
+                r.inner_out[c, x - 2] = values[c]
+    for group in grouped(ends_of(count), 2):
+        for x, values in [(x, (*beside(x), push(x))) for x in group]:
+            for c in range(4):
+                r.part_out[c, ends_of(count).index(x)] = values[c]
     strip = jnp.zeros((rows, depths), jnp.float32)
     for x in inside(count):
         strip = edges.packed(strip, x, [r.inner_out[c, x - 2] for c in VEL_SLOTS])
     r.strip_inner_out[...] = strip
 
-
-def velocity_edge(first, r):
-    count, rows, depths = r.material.shape
-    edges = Edges(rows, depths)
-    planes = Planes(stress_of(r), STRESS_TAIL, STRESS_HEAD, r.one, r.two)
-    fault = fault_row(rows)
-    places = ends_of(count)
-    row = pl.ds(fault, 1)
+    row = pl.ds(fault_row(rows), 1)
+    lines = {}
+    for x in inside(count):
+        for i, c in enumerate((0, 2)):
+            lines[i * count + x] = r.inner_out[c, x - 2, row, :]
     if first:
-        labels = [r.material[x, row, :] for x in range(count)]
-        lines = [looked_up(label, r.table, 2, CLASSES) for label in labels]
-        for x, line in enumerate(lines):
-            r.face_out[pl.ds(2 * count + x, 1), :] = line
+        for x in range(count):
+            labels = r.material[x, row, :]
+            lines[2 * count + x] = looked_up(labels, r.table, 2, CLASSES)
     if hasattr(r, "prestress"):
         own = r.normal.shape[0]
         place = 3 * count
-        lines = [r.prestress[i, pl.ds(c, 1), :] for c in (0, 1) for i in range(own)]
-        fields = [field[...] for field in (r.normal, r.slip, r.zone, r.mask)]
-        for i, line in enumerate(lines):
-            r.face_out[pl.ds(place + i, 1), :] = line
-        for i, field in enumerate(fields):
-            r.face_out[pl.ds(place + (2 + i) * own, own), :] = field.astype(jnp.float32)
-
-
-    def write(x, new):
-        for c in range(3):
-            r.edge_out[c, places.index(x)] = new[c]
-
-    velocity_planes(r, places, edges, planes, write)
+        for c in (0, 1):
+            for i in range(own):
+                lines[place + c * own + i] = r.prestress[i, pl.ds(c, 1), :]
+        for j, field in enumerate((r.normal, r.slip, r.zone, r.mask), 2):
+            for i in range(own):
+                lines[place + j * own + i] = field[pl.ds(i, 1), :].astype(jnp.float32)
+    for i, line in lines.items():
+        r.face_inner_out[pl.ds(i, 1), :] = line
+
+
+def velocity_edge(count, r):
+    rows, depths = r.one.shape[1:]
+    edges = Edges(rows, depths)
+    planes = Planes(stress_of(count, r), STRESS_TAIL, STRESS_HEAD, r.one, r.two)
+    places = ends_of(count)
+    new = []
+    for i, x in enumerate(places):
+        rates = [a + r.part[c, i] for c, a in enumerate(velocity_across(planes, x))]
+        new.append([r.velocity[c, x] + r.part[3, i] * rate for c, rate in enumerate(rates)])
+    faces = r.face_inner[...]
     strip = r.strip_inner[...]
     for i, x in enumerate(places):
-        strip = edges.packed(strip, x, [r.edge_out[c, i] for c in VEL_SLOTS])
+        strip = edges.packed(strip, x, [new[i][c] for c in VEL_SLOTS])
+        for c in range(3):
+            r.edge_out[c, i] = new[i][c]
+    r.face_out[...] = faces
     set_strip(r, strip)
-    new = Field(count, r.inner, r.edge_out)
-    lines = [new.rows(c, x)(fault, 1) for c in (0, 2) for x in range(count)]
-    for i, line in enumerate(lines):
+    fault = fault_row(rows)
+    edge = Field(count, None, r.edge_out)
+    lines = {i * count + x: edge.rows(c, x)(fault, 1) for x in places for i, c in enumerate((0, 2))}
+    for i, line in lines.items():
         r.face_out[pl.ds(i, 1), :] = line
-    edge_planes(new, VEL_TAIL, VEL_HEAD, r.one_out, r.two_out)
-
-
-def stress_of(r):
-    count = r.material.shape[0]
+    edge_planes(edge, VEL_TAIL, VEL_HEAD, r.one_out, r.two_out)
+
+
+def stress_of(count, r):
     if hasattr(r, "stress"):
         return Field(count, r.stress)
     return Field(count, r.stress_inner, r.stress_edge)
 
 
-def memory_of(r):
-    count = r.material.shape[0]
+def memory_of(count, r):
     if hasattr(r, "memory"):
         return Field(count, r.memory)
     return Field(count, r.memory_inner, r.memory_edge)
@@ -394,8 +394,8 @@
     own_first, other_first = (own_face, other_face) if first else (r.face_first, r.other_first)
     rows, depths = r.strip.shape[1:]
     count = r.change_out.shape[1]
-    middle = lax.axis_size("gy") // 2
-    side = lax.axis_index("gy")
+    middle = lax.axis_size(GY) // 2
+    side = lax.axis_index(GY)
     plus = side == middle
     minus = side == middle - 1
 
@@ -417,8 +417,8 @@
     slip = still[3] if first else r.slip[...]
     zone, mask = still[4], still[5]
 
-    row = lax.broadcasted_iota(jnp.int32, (count, depths), 0) + lax.axis_index("gx") * count
-    deep = lax.broadcasted_iota(jnp.int32, (count, depths), 1) + lax.axis_index("gz") * depths
+    row = lax.broadcasted_iota(jnp.int32, (count, depths), 0) + lax.axis_index(GX) * count
+    deep = lax.broadcasted_iota(jnp.int32, (count, depths), 1) + lax.axis_index(GZ) * depths
     inside = (row >= r.anchor[0]) & (row < r.anchor[0] + 2 * PATCH)
     inside = inside & (deep >= r.anchor[1]) & (deep < r.anchor[1] + 2 * PATCH)
     dynamic = 0.4 * looked_up(zone, r.friction, 0, ZONES)
@@ -468,7 +468,7 @@
     ends = jnp.zeros((count, depths), jnp.float32)
     pair = lax.broadcasted_iota(jnp.int32, (count, depths), 1) // 2
     place = 4 * lax.broadcasted_iota(jnp.int32, (count, depths), 0)
-    upper = lax.axis_index("gz") == 0
+    upper = lax.axis_index(GZ) == 0
     for k, field in ((0, change_x), (2, change_z)):
         turned = jnp.where(upper, pltpu.roll(field, 2, 1), field)
         turned = pltpu.roll(turned, 2 * k, 1, stride=8, stride_axis=0)
@@ -477,42 +477,26 @@
     set_strip(r, r.strip[0] + jnp.where(on_fault, line, 0.0))
 
 
-def stress_planes(r, xs, edges, planes, write):
-    band = Bands(getattr(r, "lower", None), getattr(r, "upper", None), VEL_TAIL_Y, VEL_HEAD_Y)
-    stress, memory = stress_of(r), memory_of(r)
-    unpack(r, xs, edges)
-
-    def rates(x):
-        in_x, in_y, in_z = [r.ends[xs.index(x), k] for k in range(3)]
-        exx = planes.backward_x(0, x)
-        eyy = edges.backward_y(planes, 1, x, band(1, x))
-        ezz = edges.backward_z(planes(2, x), in_z)
-        exy = edges.forward_y(planes, 0, x, band(0, x)) + planes.forward_x(1, x)
-        exz = edges.forward_z(planes(0, x), in_x) + planes.forward_x(2, x)
-        eyz = edges.forward_z(planes(1, x), in_y) + edges.forward_y(planes, 2, x, band(2, x))
-        labels = r.material[x]
-        bulk = looked_up(labels, r.table, 0, CLASSES) * (exx + eyy + ezz)
-        shear = looked_up(labels, r.table, 1, CLASSES)
-        double = 2.0 * shear
-        return (
-            bulk + double * exx,
-            bulk + double * eyy,
-            bulk + double * ezz,
-            shear * exy,
-            shear * exz,
-            shear * eyz,
-        )
-
-    def new(x, elastic):
-        labels = r.material[x]
-        decay = jnp.exp(-DT / looked_up(labels, r.table, 3, CLASSES))
-        gain = (1.0 - decay) * (0.3 * looked_up(labels, r.table, 4, CLASSES))
-        kept = [decay * memory(c, x) - gain * elastic[c] for c in range(6)]
-        return [stress(c, x) + DT * (elastic[c] + kept[c]) for c in range(6)], kept
-
-    for group in grouped(xs, 2):
-        for x, elastic in [(x, rates(x)) for x in group]:
-            write(x, *new(x, elastic))
+def elastic_rates(planes, x, beside, lame, shear):
+    eyy, ezz, eyz, along_y, along_z = beside
+    exx = planes.backward_x(0, x)
+    exy = along_y + planes.forward_x(1, x)
+    exz = along_z + planes.forward_x(2, x)
+    bulk = lame * (exx + eyy + ezz)
+    double = 2.0 * shear
+    return (
+        bulk + double * exx,
+        bulk + double * eyy,
+        bulk + double * ezz,
+        shear * exy,
+        shear * exz,
+        shear * eyz,
+    )
+
+
+def stress_new(x, elastic, decay, gain, stress, memory):
+    kept = [decay * memory(c, x) - gain * elastic[c] for c in range(6)]
+    return [stress(c, x) + DT * (elastic[c] + kept[c]) for c in range(6)], kept
 
 
 def stress_inner(last, r):
@@ -550,7 +534,35 @@
             copy_out(stress_out.at[:, held], r.stress_out.at[:, out])
             copy_out(memory_out.at[:, held], r.memory_out.at[:, out])
 
-    stress_planes(r, inside(count), edges, planes, write)
+    band = Bands(getattr(r, "lower", None), getattr(r, "upper", None), VEL_TAIL_Y, VEL_HEAD_Y)
+    stress, memory = stress_of(count, r), memory_of(count, r)
+    unpack(count, r, edges)
+
+    def beside(x):
+        in_x, in_y, in_z = [r.ends[x, k] for k in range(3)]
+        return (
+            edges.backward_y(planes, 1, x, band(1, x)),
+            edges.backward_z(planes(2, x), in_z),
+            edges.forward_z(planes(1, x), in_y) + edges.forward_y(planes, 2, x, band(2, x)),
+            edges.forward_y(planes, 0, x, band(0, x)),
+            edges.forward_z(planes(0, x), in_x),
+        )
+
+    def moduli(x):
+        return [looked_up(r.material[x], r.table, i, CLASSES) for i in (0, 1)]
+
+    def fading(x):
+        labels = r.material[x]
+        decay = jnp.exp(-DT / looked_up(labels, r.table, 3, CLASSES))
+        return decay, (1.0 - decay) * (0.3 * looked_up(labels, r.table, 4, CLASSES))
+
+    for group in grouped(inside(count), 2):
+        for x, elastic in [(x, elastic_rates(planes, x, beside(x), *moduli(x))) for x in group]:
+            write(x, *stress_new(x, elastic, *fading(x), stress, memory))
+    for group in grouped(ends_of(count), 2):
+        for x, values in [(x, (*beside(x), *moduli(x), *fading(x))) for x in group]:
+            for c in range(9):
+                r.part_out[c, ends_of(count).index(x)] = values[c]
     if last:
         for copy in copies:
             copy.wait()
@@ -561,11 +573,12 @@
         r.strip_inner_out[...] = strip
 
 
-def stress_edge(last, r):
-    count, rows, depths = r.material.shape
-    edges = Edges(rows, depths, by_loads=True)
+def stress_edge(count, last, r):
+    rows, depths = r.one.shape[1:]
+    edges = Edges(rows, depths)
     planes = Planes(Field(count, r.velocity), VEL_TAIL, VEL_HEAD, r.one, r.two)
     places = ends_of(count)
+    stress, memory = stress_of(count, r), memory_of(count, r)
     copies = []
 
     def copy_out(source, out, span):
@@ -578,16 +591,21 @@
     else:
         stress_out, memory_out = r.stress_edge_out, r.memory_edge_out
 
-    def write(x, new, kept):
-        for c in range(6):
-            stress_out[c, places.index(x)] = new[c]
-            memory_out[c, places.index(x)] = kept[c]
-
-    stress_planes(r, places, edges, planes, write)
+    def elastic(i, x):
+        part = [r.part[c, i] for c in range(7)]
+        return elastic_rates(planes, x, part[:5], *part[5:])
+
+    for group in grouped(list(enumerate(places)), 2):
+        for (i, x), rates in [(at, elastic(*at)) for at in group]:
+            new, kept = stress_new(x, rates, r.part[7, i], r.part[8, i], stress, memory)
+            for c in range(6):
+                stress_out[c, i] = new[c]
+                memory_out[c, i] = kept[c]
+        if last:
+            held, span = pl.ds(group[0][0], 2), pl.ds(group[0][1], 2)
+            copy_out(stress_out.at[:, held], r.stress_out, span)
+            copy_out(memory_out.at[:, held], r.memory_out, span)
     if last:
-        for held, out in ((stress_out, r.stress_out), (memory_out, r.memory_out)):
-            copy_out(held.at[:, pl.ds(0, 2)], out, pl.ds(0, 2))
-            copy_out(held.at[:, pl.ds(2, 2)], out, pl.ds(count - 2, 2))
         for copy in copies:
             copy.wait()
     else:
@@ -595,8 +613,8 @@
         for i, x in enumerate(places):
             strip = edges.packed(strip, x, [stress_out[c, i] for c in STRESS_SLOTS])
         set_strip(r, strip)
-        new = Field(count, r.new_stress_inner, stress_out)
-        edge_planes(new, STRESS_TAIL, STRESS_HEAD, r.one_out, r.two_out)
+        edge = Field(count, None, stress_out)
+        edge_planes(edge, STRESS_TAIL, STRESS_HEAD, r.one_out, r.two_out)
 
 
 SCALARS = ("table", "friction", "anchor")
@@ -639,7 +657,7 @@
 
 
 def strike_swaps(count):
-    halves = lax.axis_size("gz")
+    halves = lax.axis_size(GZ)
     routes = []
     for start in (0, 1):
         partner = {}
@@ -649,7 +667,7 @@
                 partner[one], partner[other] = other, one
         for i in range(count * halves):
             partner.setdefault(i, i ^ 1)
-        routes.append((("gx", "gz"), sorted(partner.items())))
+        routes.append(((GX, GZ), sorted(partner.items())))
     return routes
 
 
@@ -684,20 +702,19 @@
     slip_path,
 ):
     _, count, rows, depths = velocity.shape
-    sides = lax.axis_size("gy")
+    sides = lax.axis_size(GY)
     middle = sides // 2
     banded = sides > 2
-    swaps = strike_swaps(lax.axis_size("gx"))
-    up_y, down_y = along("gy", sides, (middle - 1,))
-    across = ("gy", [(middle - 1, middle), (middle, middle - 1)])
-    deep = ("gz", [(0, 1), (1, 0)])
+    swaps = strike_swaps(lax.axis_size(GX))
+    up_y, down_y = along(GY, sides, (middle - 1,))
+    across = (GY, [(middle - 1, middle), (middle, middle - 1)])
+    deep = (GZ, [(0, 1), (1, 0)])
 
     plane = (rows, depths)
     edge_shape = (max(len(STRESS_TAIL), len(STRESS_HEAD)), *plane)
     travelling = {"one": edge_shape, "two": edge_shape, "strip": (STRIP_PLANES, *plane)}
     inner, edge = (count - 4, *plane), (4, *plane)
-    inner_ends = {"ends": pltpu.VMEM((count - 4, 3, *plane), jnp.float32)}
-    edge_ends = {"ends": pltpu.VMEM((4, 3, *plane), jnp.float32)}
+    ends = {"ends": pltpu.VMEM((count, 3, *plane), jnp.float32)}
 
     def travelled(packed):
         two = sent(packed["two"], swaps[1])
@@ -722,7 +739,7 @@
                 fault_mask.astype(jnp.float32),
             ]
         )
-        still = {"still": lax.all_gather(still, "gy", axis=1, tiled=True)}
+        still = {"still": lax.all_gather(still, GY, axis=1, tiled=True)}
     else:
         still = {}
 
@@ -744,28 +761,30 @@
         ins = {"velocity": velocity, **held_stress, **props, **strip}
         if banded:
             ins.update(bands(whole(parts, "stress"), STRESS_TAIL_Y, STRESS_HEAD_Y))
-        free = call(
-            velocity_inner,
-            "velocity_inner",
-            ins,
-            {"inner": (3, *inner), "strip_inner": plane},
-            scratch=inner_ends,
-            micros=3,
-        )
         face_rows = 2 * count
-        ins = {**ins, **halos, **free}
         if first:
             face_rows += count
             if not banded:
                 ins.update(prestress=prestress, normal=normal_stress, slip=slip_path)
                 ins.update(zone=zone_label, mask=fault_mask)
                 face_rows += 6 * normal_stress.shape[0]
+        outs = {"inner": (3, *inner), "part": (4, *edge), "strip_inner": plane}
+        outs["face_inner"] = (face_rows, depths)
+        free = call(
+            functools.partial(velocity_inner, first),
+            "velocity_inner",
+            ins,
+            outs,
+            scratch=ends,
+            micros=3,
+        )
+        ins = {"velocity": velocity, **held_stress, **halos}
+        ins.update({key: free[key] for key in outs if key != "inner"})
         packed = call(
-            functools.partial(velocity_edge, first),
+            functools.partial(velocity_edge, count),
             "velocity_edge",
             ins,
             {"edge": (3, *edge), "face": (face_rows, depths), **travelling},
-            scratch=edge_ends,
         )
         free = {"inner": free["inner"], "edge": packed["edge"]}
         face = packed["face"]
@@ -794,8 +813,8 @@
             band = bands(joined, VEL_TAIL_Y, VEL_HEAD_Y)
         else:
             band = {}
-        outs = {"velocity": velocity.shape}
-        extra = {"scratch": inner_ends}
+        outs = {"velocity": velocity.shape, "part": (9, *edge)}
+        extra = {"scratch": ends}
         if last:
             outs.update(new_velocity=velocity.shape, stress=stress.shape, memory=memory.shape)
             extra["apart"] = ["new_velocity_out", "stress_out", "memory_out"]
@@ -805,7 +824,7 @@
                 extra["apart"].append("new_slip_out")
             held = pltpu.VMEM((6, *inner), jnp.float32)
             sems = pltpu.SemaphoreType.DMA((count,))
-            extra["scratch"] = {"stress_held": held, "memory_held": held, "sems": sems, **inner_ends}
+            extra["scratch"] = {"stress_held": held, "memory_held": held, "sems": sems, **ends}
         else:
             outs.update(stress_inner=(6, *inner), memory_inner=(6, *inner), strip_inner=plane)
         done = call(
@@ -818,12 +837,12 @@
             **extra,
         )
         velocity = done["velocity"]
-        ins = {"velocity": velocity, **parts, **props, **strip, **halos, **band}
+        ins = {"velocity": velocity, "part": done["part"], **parts, **halos}
         if last:
             ins.update(stress_done=done["stress"], memory_done=done["memory"])
             held = pltpu.VMEM((6, *edge), jnp.float32)
             packed = call(
-                functools.partial(stress_edge, last),
+                functools.partial(stress_edge, count, last),
                 "stress_edge",
                 ins,
                 {"stress": stress.shape, "memory": memory.shape},
@@ -831,7 +850,6 @@
                     "stress_held": held,
                     "memory_held": held,
                     "sems": pltpu.SemaphoreType.DMA((4,)),
-                    **edge_ends,
                 },
                 apart=("stress_done", "memory_done", "stress_out", "memory_out"),
                 onto={"stress_done": "stress", "memory_done": "memory"},
@@ -841,13 +859,12 @@
             stress, memory = packed["stress"], packed["memory"]
             slip = done.get("new_slip", slip)
         else:
-            ins.update(new_stress_inner=done["stress_inner"], strip_inner=done["strip_inner"])
+            ins["strip_inner"] = done["strip_inner"]
             packed = call(
-                functools.partial(stress_edge, last),
+                functools.partial(stress_edge, count, last),
                 "stress_edge",
                 ins,
                 {"stress_edge": (6, *edge), "memory_edge": (6, *edge), **travelling},
-                scratch=edge_ends,
                 vmem=10,
             )
             parts = {
@@ -857,30 +874,30 @@
                 "memory_edge": packed["memory_edge"],
             }
     if banded:
-        held = jnp.where(lax.axis_index("gy") == middle, slip, 0.0)
-        slip = lax.psum_scatter(held, "gy", scatter_dimension=0, tiled=True)
+        held = jnp.where(lax.axis_index(GY) == middle, slip, 0.0)
+        slip = lax.psum_scatter(held, GY, scatter_dimension=0, tiled=True)
     return (velocity, stress, memory, slip)
 
 
 def solution(mesh):
     in_specs = (
-        P(None, ("ens", "gx"), "gy", "gz"),
-        P(None, ("ens", "gx"), "gy", "gz"),
-        P(None, ("ens", "gx"), "gy", "gz"),
-        P(("ens", "gx"), "gy", "gz"),
-        P(None, "ens"),
-        P(("ens", "gx", "gy"), "gz"),
-        P(("ens", "gx", "gy"), "gz"),
-        P("ens"),
-        P(None, "ens"),
-        P(("ens", "gx", "gy"), None, "gz"),
-        P(("ens", "gx", "gy"), "gz"),
-        P(("ens", "gx", "gy"), "gz"),
+        P(None, (ENS, GX), GY, GZ),
+        P(None, (ENS, GX), GY, GZ),
+        P(None, (ENS, GX), GY, GZ),
+        P((ENS, GX), GY, GZ),
+        P(None, ENS),
+        P((ENS, GX, GY), GZ),
+        P((ENS, GX, GY), GZ),
+        P(ENS),
+        P(None, ENS),
+        P((ENS, GX, GY), None, GZ),
+        P((ENS, GX, GY), GZ),
+        P((ENS, GX, GY), GZ),
     )
     out_specs = (
-        P(None, ("ens", "gx"), "gy", "gz"),
-        P(None, ("ens", "gx"), "gy", "gz"),
-        P(None, ("ens", "gx"), "gy", "gz"),
-        P(("ens", "gx", "gy"), "gz"),
+        P(None, (ENS, GX), GY, GZ),
+        P(None, (ENS, GX), GY, GZ),
+        P(None, (ENS, GX), GY, GZ),
+        P((ENS, GX, GY), GZ),
     )
     return jax.shard_map(shards, mesh=mesh, in_specs=in_specs, out_specs=out_specs, check_vma=False)

time: 39.8 us -> 36.2 us (0.910)
  Pallas kernels: 15.4 us -> 12.8 us
  waiting for transfers between devices: 8.05 us -> 7.07 us
    pallas_call x11, Pallas kernels: 15.4 us -> 12.8 us  [call(): pl.pallas_call(body, out_shape=shapes, in_specs=[place(key) for key in in...]
    ppermute x14, waiting for transfers between devices: 8.05 us -> 7.07 us  [sent(): return lax.ppermute(block, *route)]
  transfers between devices with their start and end apart: 14 -> 14, of which waited for: 5 -> 5; matrix products, arithmetic and copies ran while one was open for 0% -> 0% of each run, Pallas kernels for 20% -> 25%
where the time goes in v10:
time: 36.2 us; the launch traced here: 36 us
  starting transfers between devices  13.9 us (38%)
  Pallas kernels  12.8 us (35%)
  waiting for transfers between devices  7.07 us (20%)
  local copies, waits for them, and re-layouts  1.45 us (4%)
  between operations  0.84 us (2%)
    ppermute x14, starting transfers between devices, sent(): return lax.ppermute(block, *route)  13.9 us
    pallas_call x11, Pallas kernels, call(): pl.pallas_call(body, out_shape=shapes, in_specs=[place(key) for key in in...  12.8 us
    ppermute x14, waiting for transfers between devices, sent(): return lax.ppermute(block, *route)  7.07 us
    unnamed x26, local copies, waits for them, and re-layouts  1.45 us
  transfers between devices with their start and end apart: 14, of which 5 were waited for; matrix products, arithmetic and copies ran while one was open for 0% of the time, Pallas kernels for 25%

profile of v10, /device:TPU:0, one launch (start us, length us, event | category | flops | bytes accessed | tf_op | source)
XLA Modules:
  0.0 36.0 jit_solution(13567179132015231713)
XLA Ops:
  0.6 0.0 copy-start
  0.6 1.4 %copy-done = f32[6,16,32,128]{3,2,1,0:T(8,128)S(1)} copy-done((f32[6,16,32,128]{3,2,1,0:T(8,128)S(1)}, f32[6,16,32,128]{3,2,1,0:T(8,128)}, u32[]{:S(2)}) %copy-start) | copy-done | bytes 1572888
  2.1 0.6 %pack.1 = (f32[5,32,128]{2,1,0:T(8,128)S(1)}, f32[5,32,128]{2,1,0:T(8,128)S(1)}, f32[6,32,128]{2,1,0:T(8,128)S(1)}) custom-call(f32[6,16,32,128]{3,2,1,0:T(8,128)S(1)} %copy-done), custom_call_target="tpu_custom_call" | custom-call | bytes 3690000 | tf_op jit(solution)/shard_map/pack/pallas_call | solution.py:636
  2.7 0.5 %collective-permute-start = (f32[6,32,128]{2,1,0:T(8,128)S(1)}, f32[6,32,128]{2,1,0:T(8,128)S(1)}, u32[]{:S(2)}, u32[]{:S(2)}) collective-permute-start(f32[6,32,128]{2,1,0:T(8,128)S(1)} %get-tuple-element.54), channel_id=1, source_target_pairs={{0,1},{1,0},{2,3},{3,2},{4,5},{5,4},{6,7},{7,6},{8,9},{9,8},{10,11... | collective-permute-start | bytes 294920 | tf_op jit(solution)/shard_map/ppermute | solution.py:675
  3.2 2.6 %collective-permute-start.1 = (f32[5,32,128]{2,1,0:T(8,128)S(1)}, f32[5,32,128]{2,1,0:T(8,128)S(1)}, u32[]{:S(2)}, u32[]{:S(2)}) collective-permute-start(f32[5,32,128]{2,1,0:T(8,128)S(1)} %get-tuple-element.56), channel_id=1, source_target_pairs={{0,4},{1,5},{4,0},{5,1},{8,12},{9,13},{12,8},{13,9},{2,6},{3,7},{6... | collective-permute-start | bytes 245768 | tf_op jit(solution)/shard_map/ppermute | solution.py:675
  5.8 0.2 collective-permute-start.2
  6.1 1.9 %velocity_inner.2 = (f32[3,12,32,128]{3,2,1,0:T(8,128)S(1)}, f32[4,4,32,128]{3,2,1,0:T(8,128)S(1)}, f32[32,128]{1,0:T(8,128)S(1)}, f32[96,128]{1,0:T(8,128)S(1)}) custom-call(f32[3,16,32,128]{3,2,1,0:T(8,128)S(1)} %copy-done.4, f32[6,16,32,128]{3,2,1,0:T(8,128)S(1)} %copy-done, s32[16,32,128]{2,1,0:T(8,128)S(1)} %copy-done.3, f32[5,8]{1,0:T(8,128)S(1)} %copy-done.5, ...), custom_call_target="tpu_custom_call" | custom-call | bytes 11070000 | tf_op jit(solution)/shard_map/velocity_inner/pallas_call | solution.py:636
  7.9 0.9 %collective-permute-done.1.refs_2_ = f32[5,32,128]{2,1,0:T(8,128)S(1)} collective-permute-done((f32[5,32,128]{2,1,0:T(8,128)S(1)}, f32[5,32,128]{2,1,0:T(8,128)S(1)}, u32[]{:S(2)}, u32[]{:S(2)}) %collective-permute-start.1) | collective-permute-done | bytes 81952 | tf_op jit(solution)/shard_map/ppermute | solution.py:675
  8.9 0.2 velocity_edge.2
  9.0 1.7 %collective-permute-start.3 = (f32[96,128]{1,0:T(8,128)S(1)}, f32[96,128]{1,0:T(8,128)S(1)}, u32[]{:S(2)}, u32[]{:S(2)}) collective-permute-start(f32[96,128]{1,0:T(8,128)S(1)} %get-tuple-element.65.refs_3_.refs_9_), channel_id=1, source_target_pairs={{0,2},{2,0},{1,3},{3,1},{4,6},{6,4},{5,7},{7,5},{8,10},{10,8},{9,1... | collective-permute-start | bytes 147464 | tf_op jit(solution)/shard_map/ppermute | solution.py:675
  10.8 2.4 %collective-permute-done.3.refs_4_.refs_10_ = f32[96,128]{1,0:T(8,128)S(1)} collective-permute-done((f32[96,128]{1,0:T(8,128)S(1)}, f32[96,128]{1,0:T(8,128)S(1)}, u32[]{:S(2)}, u32[]{:S(2)}) %collective-permute-start.3) | collective-permute-done | bytes 49184 | tf_op jit(solution)/shard_map/ppermute | solution.py:675
  13.2 0.8 %fault.2 = (f32[2,16,128]{2,1,0:T(8,128)S(1)}, f32[16,128]{1,0:T(8,128)S(1)}, f32[5,32,128]{2,1,0:T(8,128)S(1)}, f32[5,32,128]{2,1,0:T(8,128)S(1)}, f32[6,32,128...) custom-call(f32[5,32,128]{2,1,0:T(8,128)S(1)} %get-tuple-element.62.refs_0_, f32[5,32,128]{2,1,0:T(8,128)S(1)} %get-tuple-element.63.refs_1_, ...), custom_call_target="tpu_custom_call" | custom-call | bytes 3690000 | tf_op jit(solution)/shard_map/fault/pallas_call | solution.py:636
  14.0 0.1 collective-permute-start.4
  14.0 2.9 %collective-permute-start.5 = (f32[5,32,128]{2,1,0:T(8,128)S(1)}, f32[5,32,128]{2,1,0:T(8,128)S(1)}, u32[]{:S(2)}, u32[]{:S(2)}) collective-permute-start(f32[5,32,128]{2,1,0:T(8,128)S(1)} %get-tuple-element.71), channel_id=1, source_target_pairs={{0,4},{1,5},{4,0},{5,1},{8,12},{9,13},{12,8},{13,9},{2,6},{3,7},{6... | collective-permute-start | bytes 245768 | tf_op jit(solution)/shard_map/ppermute | solution.py:675
  17.0 0.2 collective-permute-start.6
  17.2 2.4 %stress_inner.2 = (f32[3,16,32,128]{3,2,1,0:T(8,128)S(1)}, f32[9,4,32,128]{3,2,1,0:T(8,128)S(1)}, f32[6,12,32,128]{3,2,1,0:T(8,128)S(1)}, f32[6,12,32,128]{3,2,1,0:T(8,128)S(1)}, f32[32,128]{1,0:T(8,128)S(1)}) custom-call(f32[3,12,32,128]{3,2,1,0:T(8,128)S(1)} %get-tuple-element.55.refs_0_, f32[3,4,32,128]{3,2,1,0:T(8,128)S(1)} %get-tuple-element.61.refs_1_, ...), custom_call_target="tpu_custom_call" | custom-call | bytes 11070000 | tf_op jit(solution)/shard_map/stress_inner/pallas_call | solution.py:636
  19.6 0.4 %collective-permute-done.5.refs_4_ = f32[5,32,128]{2,1,0:T(8,128)S(1)} collective-permute-done((f32[5,32,128]{2,1,0:T(8,128)S(1)}, f32[5,32,128]{2,1,0:T(8,128)S(1)}, u32[]{:S(2)}, u32[]{:S(2)}) %collective-permute-start.5) | collective-permute-done | bytes 81952 | tf_op jit(solution)/shard_map/ppermute | solution.py:675
  20.0 0.2 stress_edge.2
  20.3 0.1 collective-permute-start.7
  20.3 1.8 %collective-permute-start.8 = (f32[5,32,128]{2,1,0:T(8,128)S(1)}, f32[5,32,128]{2,1,0:T(8,128)S(1)}, u32[]{:S(2)}, u32[]{:S(2)}) collective-permute-start(f32[5,32,128]{2,1,0:T(8,128)S(1)} %get-tuple-element.77), channel_id=1, source_target_pairs={{0,4},{1,5},{4,0},{5,1},{8,12},{9,13},{12,8},{13,9},{2,6},{3,7},{6... | collective-permute-start | bytes 245768 | tf_op jit(solution)/shard_map/ppermute | solution.py:675
  22.2 0.2 collective-permute-start.9
  22.3 1.8 %velocity_inner.3 = (f32[3,12,32,128]{3,2,1,0:T(8,128)S(1)}, f32[4,4,32,128]{3,2,1,0:T(8,128)S(1)}, f32[32,128]{1,0:T(8,128)S(1)}, f32[32,128]{1,0:T(8,128)S(1)}) custom-call(f32[3,16,32,128]{3,2,1,0:T(8,128)S(1)} %get-tuple-element.68.refs_0_, f32[6,12,32,128]{3,2,1,0:T(8,128)S(1)} %get-tuple-element.69.refs_1_.refs_3_.refs_2_, ...), custom_call_target="tpu_custom_call" | custom-call | bytes 11070000 | tf_op jit(solution)/shard_map/velocity_inner/pallas_call | solution.py:636
  24.2 1.0 %collective-permute-done.8.refs_3_ = f32[5,32,128]{2,1,0:T(8,128)S(1)} collective-permute-done((f32[5,32,128]{2,1,0:T(8,128)S(1)}, f32[5,32,128]{2,1,0:T(8,128)S(1)}, u32[]{:S(2)}, u32[]{:S(2)}) %collective-permute-start.8) | collective-permute-done | bytes 81952 | tf_op jit(solution)/shard_map/ppermute | solution.py:675
  25.2 0.2 velocity_edge.3
  25.4 1.6 %collective-permute-start.10 = (f32[32,128]{1,0:T(8,128)S(1)}, f32[32,128]{1,0:T(8,128)S(1)}, u32[]{:S(2)}, u32[]{:S(2)}) collective-permute-start(f32[32,128]{1,0:T(8,128)S(1)} %get-tuple-element.86.refs_3_), channel_id=1, source_target_pairs={{0,2},{2,0},{1,3},{3,1},{4,6},{6,4},{5,7},{7,5},{8,10},{10,8},{9,1... | collective-permute-start | bytes 49160 | tf_op jit(solution)/shard_map/ppermute | solution.py:675
  26.9 2.2 %collective-permute-done.10.refs_4_ = f32[32,128]{1,0:T(8,128)S(1)} collective-permute-done((f32[32,128]{1,0:T(8,128)S(1)}, f32[32,128]{1,0:T(8,128)S(1)}, u32[]{:S(2)}, u32[]{:S(2)}) %collective-permute-start.10) | collective-permute-done | bytes 16416 | tf_op jit(solution)/shard_map/ppermute | solution.py:675
  29.2 0.8 %fault.3 = (f32[2,16,128]{2,1,0:T(8,128)S(1)}, f32[8,128]{1,0:T(8,128)S(1)}, f32[5,32,128]{2,1,0:T(8,128)S(1)}, f32[5,32,128]{2,1,0:T(8,128)S(1)}, f32[6,32,128]{2,1,0:T(8,128)S(1)}) custom-call(f32[5,32,128]{2,1,0:T(8,128)S(1)} %get-tuple-element.83.refs_0_, f32[5,32,128]{2,1,0:T(8,128)S(1)} %get-tuple-element.84.refs_1_, ...), custom_call_target="tpu_custom_call" | custom-call | bytes 3690000 | tf_op jit(solution)/shard_map/fault/pallas_call | solution.py:636
  29.9 0.1 collective-permute-start.11
  30.0 1.8 %collective-permute-start.12 = (f32[5,32,128]{2,1,0:T(8,128)S(1)}, f32[5,32,128]{2,1,0:T(8,128)S(1)}, u32[]{:S(2)}, u32[]{:S(2)}) collective-permute-start(f32[5,32,128]{2,1,0:T(8,128)S(1)} %get-tuple-element.97), channel_id=1, source_target_pairs={{0,4},{1,5},{4,0},{5,1},{8,12},{9,13},{12,8},{13,9},{2,6},{3,7},{6... | collective-permute-start | bytes 245768 | tf_op jit(solution)/shard_map/ppermute | solution.py:675
  31.8 0.2 collective-permute-start.13
  32.0 3.0 %stress_inner.3 = (f32[3,16,32,128]{3,2,1,0:T(8,128)S(1)}, f32[9,4,32,128]{3,2,1,0:T(8,128)S(1)}, f32[3,16,32,128]{3,2,1,0:T(8,128)}, f32[6,16,32,128]{3,2,1,0:T...) custom-call(f32[3,12,32,128]{3,2,1,0:T(8,128)S(1)} %get-tuple-element.76.refs_0_, ...), custom_call_target="tpu_custom_call" | custom-call | bytes 11070000 | tf_op jit(solution)/shard_map/stress_inner/pallas_call | solution.py:636
  35.0 1.0 %stress_edge.3 = (f32[6,16,32,128]{3,2,1,0:T(8,128)}, f32[6,16,32,128]{3,2,1,0:T(8,128)}) custom-call(f32[3,16,32,128]{3,2,1,0:T(8,128)S(1)} %get-tuple-element.95.refs_0_, f32[9,4,32,128]{3,2,1,0:T(8,128)S(1)} %get-tuple-element.96.refs_1_, ...), custom_call_target="tpu_custom_call", output_to_operand_aliasing={{0}: (8, {}), {1}: (9, {})} | custom-call | bytes 3690000 | tf_op jit(solution)/shard_map/stress_edge/pallas_call | solution.py:636
  (33 shorter events, 0.1 us)
Async XLA Ops:
  0.6 1.4 %copy-start = (f32[6,16,32,128]{3,2,1,0:T(8,128)S(1)}, f32[6,16,32,128]{3,2,1,0:T(8,128)}, u32[]{:S(2)}) copy-start(f32[6,16,32,128]{3,2,1,0:T(8,128)} %refs_2_.3) | copy-start | bytes 4718596
  2.0 3.9 %copy-start.3 = (s32[16,32,128]{2,1,0:T(8,128)S(1)}, s32[16,32,128]{2,1,0:T(8,128)}, u32[]{:S(2)}) copy-start(s32[16,32,128]{2,1,0:T(8,128)} %refs_7_.3) | copy-start | bytes 786436
  2.0 3.9 %copy-start.4 = (f32[3,16,32,128]{3,2,1,0:T(8,128)S(1)}, f32[3,16,32,128]{3,2,1,0:T(8,128)}, u32[]{:S(2)}) copy-start(f32[3,16,32,128]{3,2,1,0:T(8,128)} %refs_0_.5) | copy-start | bytes 2359300
  2.0 4.0 %copy-start.5 = (f32[5,8]{1,0:T(8,128)S(1)}, f32[5,8]{1,0:T(8,128)}, u32[]{:S(2)}) copy-start(f32[5,8]{1,0:T(8,128)} %refs_8_.3) | copy-start | bytes 484
  2.1 4.0 %copy-start.6 = (f32[8,2,128]{2,1,0:T(2,128)S(1)}, f32[8,2,128]{2,1,0:T(2,128)}, u32[]{:S(2)}) copy-start(f32[8,2,128]{2,1,0:T(2,128)} %refs_5_.4) | copy-start | bytes 24580
  2.1 4.0 %copy-start.8 = (f32[8,128]{1,0:T(8,128)S(1)}, f32[8,128]{1,0:T(8,128)}, u32[]{:S(2)}) copy-start(f32[8,128]{1,0:T(8,128)} %refs_6_.4) | copy-start | bytes 12292
  2.1 4.0 %copy-start.9 = (f32[8,128]{1,0:T(8,128)S(1)}, f32[8,128]{1,0:T(8,128)}, u32[]{:S(2)}) copy-start(f32[8,128]{1,0:T(8,128)} %refs_7_.2) | copy-start | bytes 12292
  2.1 4.0 %copy-start.10 = (s32[8,128]{1,0:T(8,128)S(1)}, s32[8,128]{1,0:T(8,128)}, u32[]{:S(2)}) copy-start(s32[8,128]{1,0:T(8,128)} %refs_8_.2) | copy-start | bytes 12292
  2.1 4.0 %copy-start.11 = (s32[8,128]{1,0:T(8,128)S(1)}, s32[8,128]{1,0:T(8,128)}, u32[]{:S(2)}) copy-start(s32[8,128]{1,0:T(8,128)} %refs_9_.1) | copy-start | bytes 12292
  2.7 3.3 %collective-permute-start = (f32[6,32,128]{2,1,0:T(8,128)S(1)}, f32[6,32,128]{2,1,0:T(8,128)S(1)}, u32[]{:S(2)}, u32[]{:S(2)}) collective-permute-start(f32[6,32,128]{2,1,0:T(8,128)S(1)} %get-tuple-element.54), channel_id=1, source_target_pairs={{0,1},{1,0},{2,3},{3,2},{4,5},{5,4},{6,7},{7,6},{8,9},{9,8},{10,11... | collective-permute-start | bytes 294920 | tf_op jit(solution)/shard_map/ppermute | solution.py:675
  3.2 5.7 %collective-permute-start.1 = (f32[5,32,128]{2,1,0:T(8,128)S(1)}, f32[5,32,128]{2,1,0:T(8,128)S(1)}, u32[]{:S(2)}, u32[]{:S(2)}) collective-permute-start(f32[5,32,128]{2,1,0:T(8,128)S(1)} %get-tuple-element.56), channel_id=1, source_target_pairs={{0,4},{1,5},{4,0},{5,1},{8,12},{9,13},{12,8},{13,9},{2,6},{3,7},{6... | collective-permute-start | bytes 245768 | tf_op jit(solution)/shard_map/ppermute | solution.py:675
  5.8 3.0 %collective-permute-start.2 = (f32[5,32,128]{2,1,0:T(8,128)S(1)}, f32[5,32,128]{2,1,0:T(8,128)S(1)}, u32[]{:S(2)}, u32[]{:S(2)}) collective-permute-start(f32[5,32,128]{2,1,0:T(8,128)S(1)} %get-tuple-element.57), channel_id=1, source_target_pairs={{0,1},{1,0},{4,8},{5,9},{8,4},{9,5},{12,13},{13,12},{2,3},{3,2},{6... | collective-permute-start | bytes 245768 | tf_op jit(solution)/shard_map/ppermute | solution.py:675
  7.9 5.3 %copy-start.7 = (f32[3,4]{1,0:T(4,128)S(1)}, f32[3,4]{1,0:T(4,128)}, u32[]{:S(2)}) copy-start(f32[3,4]{1,0:T(4,128)} %refs_5_.7) | copy-start | bytes 148
  7.9 5.3 %copy-start.12 = (s32[2]{0:T(128)S(1)}, s32[2]{0:T(128)}, u32[]{:S(2)}) copy-start(s32[2]{0:T(128)} %refs_6_.7) | copy-start | bytes 28
  8.9 8.3 %copy-start.1 = (f32[6,16,32,128]{3,2,1,0:T(8,128)S(1)}, f32[6,16,32,128]{3,2,1,0:T(8,128)}, u32[]{:S(2)}) copy-start(f32[6,16,32,128]{3,2,1,0:T(8,128)} %refs_2_.3) | copy-start | bytes 4718596
  8.9 8.3 %copy-start.2 = (f32[6,16,32,128]{3,2,1,0:T(8,128)S(1)}, f32[6,16,32,128]{3,2,1,0:T(8,128)}, u32[]{:S(2)}) copy-start(f32[6,16,32,128]{3,2,1,0:T(8,128)} %refs_3_.6) | copy-start | bytes 4718596
  9.0 4.2 %collective-permute-start.3 = (f32[96,128]{1,0:T(8,128)S(1)}, f32[96,128]{1,0:T(8,128)S(1)}, u32[]{:S(2)}, u32[]{:S(2)}) collective-permute-start(f32[96,128]{1,0:T(8,128)S(1)} %get-tuple-element.65.refs_3_.refs_9_), channel_id=1, source_target_pairs={{0,2},{2,0},{1,3},{3,1},{4,6},{6,4},{5,7},{7,5},{8,10},{10,8},{9,1... | collective-permute-start | bytes 147464 | tf_op jit(solution)/shard_map/ppermute | solution.py:675
  14.0 3.2 %collective-permute-start.4 = (f32[6,32,128]{2,1,0:T(8,128)S(1)}, f32[6,32,128]{2,1,0:T(8,128)S(1)}, u32[]{:S(2)}, u32[]{:S(2)}) collective-permute-start(f32[6,32,128]{2,1,0:T(8,128)S(1)} %get-tuple-element.67), channel_id=1, source_target_pairs={{0,1},{1,0},{2,3},{3,2},{4,5},{5,4},{6,7},{7,6},{8,9},{9,8},{10,11... | collective-permute-start | bytes 294920 | tf_op jit(solution)/shard_map/ppermute | solution.py:675
  14.0 6.0 %collective-permute-start.5 = (f32[5,32,128]{2,1,0:T(8,128)S(1)}, f32[5,32,128]{2,1,0:T(8,128)S(1)}, u32[]{:S(2)}, u32[]{:S(2)}) collective-permute-start(f32[5,32,128]{2,1,0:T(8,128)S(1)} %get-tuple-element.71), channel_id=1, source_target_pairs={{0,4},{1,5},{4,0},{5,1},{8,12},{9,13},{12,8},{13,9},{2,6},{3,7},{6... | collective-permute-start | bytes 245768 | tf_op jit(solution)/shard_map/ppermute | solution.py:675
  17.0 3.0 %collective-permute-start.6 = (f32[5,32,128]{2,1,0:T(8,128)S(1)}, f32[5,32,128]{2,1,0:T(8,128)S(1)}, u32[]{:S(2)}, u32[]{:S(2)}) collective-permute-start(f32[5,32,128]{2,1,0:T(8,128)S(1)} %get-tuple-element.72), channel_id=1, source_target_pairs={{0,1},{1,0},{4,8},{5,9},{8,4},{9,5},{12,13},{13,12},{2,3},{3,2},{6... | collective-permute-start | bytes 245768 | tf_op jit(solution)/shard_map/ppermute | solution.py:675
  20.3 2.1 %collective-permute-start.7 = (f32[6,32,128]{2,1,0:T(8,128)S(1)}, f32[6,32,128]{2,1,0:T(8,128)S(1)}, u32[]{:S(2)}, u32[]{:S(2)}) collective-permute-start(f32[6,32,128]{2,1,0:T(8,128)S(1)} %get-tuple-element.75), channel_id=1, source_target_pairs={{0,1},{1,0},{2,3},{3,2},{4,5},{5,4},{6,7},{7,6},{8,9},{9,8},{10,11... | collective-permute-start | bytes 294920 | tf_op jit(solution)/shard_map/ppermute | solution.py:675
  20.3 4.9 %collective-permute-start.8 = (f32[5,32,128]{2,1,0:T(8,128)S(1)}, f32[5,32,128]{2,1,0:T(8,128)S(1)}, u32[]{:S(2)}, u32[]{:S(2)}) collective-permute-start(f32[5,32,128]{2,1,0:T(8,128)S(1)} %get-tuple-element.77), channel_id=1, source_target_pairs={{0,4},{1,5},{4,0},{5,1},{8,12},{9,13},{12,8},{13,9},{2,6},{3,7},{6... | collective-permute-start | bytes 245768 | tf_op jit(solution)/shard_map/ppermute | solution.py:675
  22.2 3.0 %collective-permute-start.9 = (f32[5,32,128]{2,1,0:T(8,128)S(1)}, f32[5,32,128]{2,1,0:T(8,128)S(1)}, u32[]{:S(2)}, u32[]{:S(2)}) collective-permute-start(f32[5,32,128]{2,1,0:T(8,128)S(1)} %get-tuple-element.78), channel_id=1, source_target_pairs={{0,1},{1,0},{4,8},{5,9},{8,4},{9,5},{12,13},{13,12},{2,3},{3,2},{6... | collective-permute-start | bytes 245768 | tf_op jit(solution)/shard_map/ppermute | solution.py:675
  25.4 3.8 %collective-permute-start.10 = (f32[32,128]{1,0:T(8,128)S(1)}, f32[32,128]{1,0:T(8,128)S(1)}, u32[]{:S(2)}, u32[]{:S(2)}) collective-permute-start(f32[32,128]{1,0:T(8,128)S(1)} %get-tuple-element.86.refs_3_), channel_id=1, source_target_pairs={{0,2},{2,0},{1,3},{3,1},{4,6},{6,4},{5,7},{7,5},{8,10},{10,8},{9,1... | collective-permute-start | bytes 49160 | tf_op jit(solution)/shard_map/ppermute | solution.py:675
  29.9 2.1 %collective-permute-start.11 = (f32[6,32,128]{2,1,0:T(8,128)S(1)}, f32[6,32,128]{2,1,0:T(8,128)S(1)}, u32[]{:S(2)}, u32[]{:S(2)}) collective-permute-start(f32[6,32,128]{2,1,0:T(8,128)S(1)} %get-tuple-element.92), channel_id=1, source_target_pairs={{0,1},{1,0},{2,3},{3,2},{4,5},{5,4},{6,7},{7,6},{8,9},{9,8},{10,11... | collective-permute-start | bytes 294920 | tf_op jit(solution)/shard_map/ppermute | solution.py:675
  30.0 5.0 %collective-permute-start.12 = (f32[5,32,128]{2,1,0:T(8,128)S(1)}, f32[5,32,128]{2,1,0:T(8,128)S(1)}, u32[]{:S(2)}, u32[]{:S(2)}) collective-permute-start(f32[5,32,128]{2,1,0:T(8,128)S(1)} %get-tuple-element.97), channel_id=1, source_target_pairs={{0,4},{1,5},{4,0},{5,1},{8,12},{9,13},{12,8},{13,9},{2,6},{3,7},{6... | collective-permute-start | bytes 245768 | tf_op jit(solution)/shard_map/ppermute | solution.py:675
  31.8 3.2 %collective-permute-start.13 = (f32[5,32,128]{2,1,0:T(8,128)S(1)}, f32[5,32,128]{2,1,0:T(8,128)S(1)}, u32[]{:S(2)}, u32[]{:S(2)}) collective-permute-start(f32[5,32,128]{2,1,0:T(8,128)S(1)} %get-tuple-element.98), channel_id=1, source_target_pairs={{0,1},{1,0},{4,8},{5,9},{8,4},{9,5},{12,13},{13,12},{2,3},{3,2},{6... | collective-permute-start | bytes 245768 | tf_op jit(solution)/shard_map/ppermute | solution.py:675

commit v11 on v10

--- a/solution.py
+++ b/solution.py
@@ -250,28 +250,26 @@
     return jnp.where(lax.axis_index(GY) == lax.axis_size(GY) // 2, 0, rows - 1)
 
 
-def pack_kernel(r):
+def pack_kernel(names, r):
     count, rows, depths = r.stress.shape[1:]
-    whole = [(comp, 0, count) for comp in STRESS_SLOTS]
-    some = {}
-    for comp, place in STRESS_TAIL + STRESS_HEAD:
-        if comp not in STRESS_SLOTS:
-            some.setdefault((comp, place < 0), []).append(place % count)
-    some = [(comp, min(at), max(at) + 1) for (comp, _), at in some.items()]
+    order = (XZ, YZ, ZZ, XX, XY, YY)
+    pairs = [(r.stress.at[c], r.stress_out.at[c]) for c in order]
+    pairs += [(getattr(r, key), getattr(r, f"{key}_out")) for key in names]
     copies = []
-    for i, (comp, start, stop) in enumerate(some + whole):
-        span = pl.ds(start, stop - start)
-        copy = pltpu.make_async_copy(r.stress.at[comp, span], r.held.at[comp, span], r.sems.at[i])
+    for i, (source, out) in enumerate(pairs):
+        copy = pltpu.make_async_copy(source, out, r.sems.at[i])
         copy.start()
         copies.append(copy)
     edges = Edges(rows, depths)
-    for copy in copies:
+    for copy in copies[:5]:
         copy.wait()
-    edge_planes(Field(count, r.held), STRESS_TAIL, STRESS_HEAD, r.one_out, r.two_out)
+    edge_planes(Field(count, r.stress_out), STRESS_TAIL, STRESS_HEAD, r.one_out, r.two_out)
     strip = jnp.zeros((rows, depths), jnp.float32)
     for x in range(count):
-        strip = edges.packed(strip, x, [r.held[c, x] for c in STRESS_SLOTS])
+        strip = edges.packed(strip, x, [r.stress_out[c, x] for c in STRESS_SLOTS])
     set_strip(r, strip)
+    for copy in copies[5:]:
+        copy.wait()
 
 
 def grouped(xs, size):
@@ -632,7 +630,10 @@
             return pl.BlockSpec(memory_space=pltpu.HBM)
         return pl.BlockSpec(memory_space=pltpu.SMEM if key in SCALARS else pltpu.VMEM)
 
-    shapes = [jax.ShapeDtypeStruct(shape, jnp.float32) for shape in outs.values()]
+    shapes = [
+        shape if hasattr(shape, "dtype") else jax.ShapeDtypeStruct(shape, jnp.float32)
+        for shape in outs.values()
+    ]
     result = pl.pallas_call(
         body,
         out_shape=shapes,
@@ -743,17 +744,23 @@
     else:
         still = {}
 
-    parts = {"stress": stress, "memory": memory}
-    props = {"material": material, "table": material_table}
+    held = {"velocity": velocity, "material": material}
+    if not banded:
+        held.update(prestress=prestress, normal=normal_stress, slip=slip_path)
+        held.update(zone=zone_label, mask=fault_mask)
+    ins = {"stress": stress, **held}
     packed = call(
-        pack_kernel,
+        functools.partial(pack_kernel, list(held)),
         "pack",
-        {"stress": stress},
-        travelling,
-        scratch={"held": pltpu.VMEM(stress.shape, jnp.float32), "sems": pltpu.SemaphoreType.DMA((8,))},
-        apart=("stress",),
-        vmem=6,
+        {key: pltpu.with_memory_space_constraint(a, pltpu.HBM) for key, a in ins.items()},
+        {**travelling, **{key: jax.ShapeDtypeStruct(a.shape, a.dtype) for key, a in ins.items()}},
+        scratch={"sems": pltpu.SemaphoreType.DMA((6 + len(held),))},
+        apart=list(ins),
     )
+    velocity = packed["velocity"]
+    parts = {"stress": packed["stress"], "memory": memory}
+    props = {"material": packed["material"], "table": material_table}
+    friction_ins = {key: packed[key] for key in held if key not in ("velocity", "material")}
     for step in range(STEPS):
         first, last = step == 0, step == STEPS - 1
         held_stress = {key: parts[key] for key in parts if key.startswith("stress")}
@@ -765,8 +772,7 @@
         if first:
             face_rows += count
             if not banded:
-                ins.update(prestress=prestress, normal=normal_stress, slip=slip_path)
-                ins.update(zone=zone_label, mask=fault_mask)
+                ins.update(friction_ins)
                 face_rows += 6 * normal_stress.shape[0]
         outs = {"inner": (3, *inner), "part": (4, *edge), "strip_inner": plane}
         outs["face_inner"] = (face_rows, depths)

time: 36.2 us -> 36 us (level)
  local copies, waits for them, and re-layouts: 1.45 us -> 0.02 us
  Pallas kernels: 12.8 us -> 14 us
    unnamed x26 -> x8, local copies, waits for them, and re-layouts: 1.45 us -> 0.02 us
    pallas_call x11, Pallas kernels: 12.8 us -> 14 us  [call(): pl.pallas_call(body, out_shape=shapes, in_specs=[place(key) for key in in...]
where the time goes in v11:
time: 36 us; the launch traced here: 35.8 us
  Pallas kernels  14 us (39%)
  starting transfers between devices  13.9 us (39%)
  waiting for transfers between devices  7.12 us (20%)
  between operations  0.75 us (2%)
    pallas_call x11, Pallas kernels, call(): pl.pallas_call(body, out_shape=shapes, in_specs=[place(key) for key in in...  14 us
    ppermute x14, starting transfers between devices, sent(): return lax.ppermute(block, *route)  13.9 us
    ppermute x14, waiting for transfers between devices, sent(): return lax.ppermute(block, *route)  7.12 us
  transfers between devices with their start and end apart: 14, of which 5 were waited for; matrix products, arithmetic and copies ran while one was open for 0% of the time, Pallas kernels for 25%

profile of v11, /device:TPU:0, one launch (start us, length us, event | category | flops | bytes accessed | tf_op | source)
XLA Modules:
  0.0 35.8 jit_solution(4216398930649960566)
XLA Ops:
  0.6 1.8 %pack.1 = (f32[5,32,128]{2,1,0:T(8,128)S(1)}, f32[5,32,128]{2,1,0:T(8,128)S(1)}, f32[6,32,128]{2,1,0:T(8,128)S(1)}, f32[6,16,32,128]{3,2,1,0:T(8,128)S(1)}, f32[...) custom-call(f32[6,16,32,128]{3,2,1,0:T(8,128)} %refs_0_.1, ...), custom_call_target="tpu_custom_call" | custom-call | bytes 3690000 | tf_op jit(solution)/shard_map/pack/pallas_call | solution.py:637
  2.4 0.5 %collective-permute-start = (f32[6,32,128]{2,1,0:T(8,128)S(1)}, f32[6,32,128]{2,1,0:T(8,128)S(1)}, u32[]{:S(2)}, u32[]{:S(2)}) collective-permute-start(f32[6,32,128]{2,1,0:T(8,128)S(1)} %get-tuple-element.65), channel_id=1, source_target_pairs={{0,1},{1,0},{2,3},{3,2},{4,5},{5,4},{6,7},{7,6},{8,9},{9,8},{10,11... | collective-permute-start | bytes 294920 | tf_op jit(solution)/shard_map/ppermute | solution.py:676
  3.0 2.6 %collective-permute-start.1 = (f32[5,32,128]{2,1,0:T(8,128)S(1)}, f32[5,32,128]{2,1,0:T(8,128)S(1)}, u32[]{:S(2)}, u32[]{:S(2)}) collective-permute-start(f32[5,32,128]{2,1,0:T(8,128)S(1)} %get-tuple-element.72), channel_id=1, source_target_pairs={{0,4},{1,5},{4,0},{5,1},{8,12},{9,13},{12,8},{13,9},{2,6},{3,7},{6... | collective-permute-start | bytes 245768 | tf_op jit(solution)/shard_map/ppermute | solution.py:676
  5.6 0.2 collective-permute-start.2
  5.8 1.9 %velocity_inner.2 = (f32[3,12,32,128]{3,2,1,0:T(8,128)S(1)}, f32[4,4,32,128]{3,2,1,0:T(8,128)S(1)}, f32[32,128]{1,0:T(8,128)S(1)}, f32[96,128]{1,0:T(8,128)S(1)}) custom-call(f32[3,16,32,128]{3,2,1,0:T(8,128)S(1)} %get-tuple-element.62.refs_0_, f32[6,16,32,128]{3,2,1,0:T(8,128)S(1)} %get-tuple-element.63.refs_1_.refs_3_.refs_2_, ...), custom_call_target="tpu_custom_call" | custom-call | bytes 11070000 | tf_op jit(solution)/shard_map/velocity_inner/pallas_call | solution.py:637
  7.7 0.0 copy-start.2
  7.7 0.0 copy-start.3
  7.7 1.0 %collective-permute-done.1.refs_2_ = f32[5,32,128]{2,1,0:T(8,128)S(1)} collective-permute-done((f32[5,32,128]{2,1,0:T(8,128)S(1)}, f32[5,32,128]{2,1,0:T(8,128)S(1)}, u32[]{:S(2)}, u32[]{:S(2)}) %collective-permute-start.1) | collective-permute-done | bytes 81952 | tf_op jit(solution)/shard_map/ppermute | solution.py:676
  8.7 0.2 velocity_edge.2
  8.8 1.7 %collective-permute-start.3 = (f32[96,128]{1,0:T(8,128)S(1)}, f32[96,128]{1,0:T(8,128)S(1)}, u32[]{:S(2)}, u32[]{:S(2)}) collective-permute-start(f32[96,128]{1,0:T(8,128)S(1)} %get-tuple-element.81.refs_3_.refs_9_), channel_id=1, source_target_pairs={{0,2},{2,0},{1,3},{3,1},{4,6},{6,4},{5,7},{7,5},{8,10},{10,8},{9,1... | collective-permute-start | bytes 147464 | tf_op jit(solution)/shard_map/ppermute | solution.py:676
  10.6 2.4 %collective-permute-done.3.refs_4_.refs_10_ = f32[96,128]{1,0:T(8,128)S(1)} collective-permute-done((f32[96,128]{1,0:T(8,128)S(1)}, f32[96,128]{1,0:T(8,128)S(1)}, u32[]{:S(2)}, u32[]{:S(2)}) %collective-permute-start.3) | collective-permute-done | bytes 49184 | tf_op jit(solution)/shard_map/ppermute | solution.py:676
  13.0 0.8 %fault.2 = (f32[2,16,128]{2,1,0:T(8,128)S(1)}, f32[16,128]{1,0:T(8,128)S(1)}, f32[5,32,128]{2,1,0:T(8,128)S(1)}, f32[5,32,128]{2,1,0:T(8,128)S(1)}, f32[6,32,128...) custom-call(f32[5,32,128]{2,1,0:T(8,128)S(1)} %get-tuple-element.78.refs_0_, f32[5,32,128]{2,1,0:T(8,128)S(1)} %get-tuple-element.79.refs_1_, ...), custom_call_target="tpu_custom_call" | custom-call | bytes 3690000 | tf_op jit(solution)/shard_map/fault/pallas_call | solution.py:637
  13.7 0.1 collective-permute-start.4
  13.8 2.9 %collective-permute-start.5 = (f32[5,32,128]{2,1,0:T(8,128)S(1)}, f32[5,32,128]{2,1,0:T(8,128)S(1)}, u32[]{:S(2)}, u32[]{:S(2)}) collective-permute-start(f32[5,32,128]{2,1,0:T(8,128)S(1)} %get-tuple-element.87), channel_id=1, source_target_pairs={{0,4},{1,5},{4,0},{5,1},{8,12},{9,13},{12,8},{13,9},{2,6},{3,7},{6... | collective-permute-start | bytes 245768 | tf_op jit(solution)/shard_map/ppermute | solution.py:676
  16.8 0.2 collective-permute-start.6
  16.9 2.4 %stress_inner.2 = (f32[3,16,32,128]{3,2,1,0:T(8,128)S(1)}, f32[9,4,32,128]{3,2,1,0:T(8,128)S(1)}, f32[6,12,32,128]{3,2,1,0:T(8,128)S(1)}, f32[6,12,32,128]{3,2,1,0:T(8,128)S(1)}, f32[32,128]{1,0:T(8,128)S(1)}) custom-call(f32[3,12,32,128]{3,2,1,0:T(8,128)S(1)} %get-tuple-element.71.refs_0_, f32[3,4,32,128]{3,2,1,0:T(8,128)S(1)} %get-tuple-element.77.refs_1_, ...), custom_call_target="tpu_custom_call" | custom-call | bytes 11070000 | tf_op jit(solution)/shard_map/stress_inner/pallas_call | solution.py:637
  19.4 0.5 %collective-permute-done.5.refs_4_ = f32[5,32,128]{2,1,0:T(8,128)S(1)} collective-permute-done((f32[5,32,128]{2,1,0:T(8,128)S(1)}, f32[5,32,128]{2,1,0:T(8,128)S(1)}, u32[]{:S(2)}, u32[]{:S(2)}) %collective-permute-start.5) | collective-permute-done | bytes 81952 | tf_op jit(solution)/shard_map/ppermute | solution.py:676
  19.8 0.2 stress_edge.2
  20.1 0.1 collective-permute-start.7
  20.1 1.8 %collective-permute-start.8 = (f32[5,32,128]{2,1,0:T(8,128)S(1)}, f32[5,32,128]{2,1,0:T(8,128)S(1)}, u32[]{:S(2)}, u32[]{:S(2)}) collective-permute-start(f32[5,32,128]{2,1,0:T(8,128)S(1)} %get-tuple-element.93), channel_id=1, source_target_pairs={{0,4},{1,5},{4,0},{5,1},{8,12},{9,13},{12,8},{13,9},{2,6},{3,7},{6... | collective-permute-start | bytes 245768 | tf_op jit(solution)/shard_map/ppermute | solution.py:676
  21.9 0.2 collective-permute-start.9
  22.1 1.8 %velocity_inner.3 = (f32[3,12,32,128]{3,2,1,0:T(8,128)S(1)}, f32[4,4,32,128]{3,2,1,0:T(8,128)S(1)}, f32[32,128]{1,0:T(8,128)S(1)}, f32[32,128]{1,0:T(8,128)S(1)}) custom-call(f32[3,16,32,128]{3,2,1,0:T(8,128)S(1)} %get-tuple-element.84.refs_0_, f32[6,12,32,128]{3,2,1,0:T(8,128)S(1)} %get-tuple-element.85.refs_1_.refs_3_.refs_2_, ...), custom_call_target="tpu_custom_call" | custom-call | bytes 11070000 | tf_op jit(solution)/shard_map/velocity_inner/pallas_call | solution.py:637
  24.0 1.0 %collective-permute-done.8.refs_3_ = f32[5,32,128]{2,1,0:T(8,128)S(1)} collective-permute-done((f32[5,32,128]{2,1,0:T(8,128)S(1)}, f32[5,32,128]{2,1,0:T(8,128)S(1)}, u32[]{:S(2)}, u32[]{:S(2)}) %collective-permute-start.8) | collective-permute-done | bytes 81952 | tf_op jit(solution)/shard_map/ppermute | solution.py:676
  25.0 0.2 velocity_edge.3
  25.2 1.6 %collective-permute-start.10 = (f32[32,128]{1,0:T(8,128)S(1)}, f32[32,128]{1,0:T(8,128)S(1)}, u32[]{:S(2)}, u32[]{:S(2)}) collective-permute-start(f32[32,128]{1,0:T(8,128)S(1)} %get-tuple-element.102.refs_3_), channel_id=1, source_target_pairs={{0,2},{2,0},{1,3},{3,1},{4,6},{6,4},{5,7},{7,5},{8,10},{10,8},{9,1... | collective-permute-start | bytes 49160 | tf_op jit(solution)/shard_map/ppermute | solution.py:676
  26.7 2.2 %collective-permute-done.10.refs_4_ = f32[32,128]{1,0:T(8,128)S(1)} collective-permute-done((f32[32,128]{1,0:T(8,128)S(1)}, f32[32,128]{1,0:T(8,128)S(1)}, u32[]{:S(2)}, u32[]{:S(2)}) %collective-permute-start.10) | collective-permute-done | bytes 16416 | tf_op jit(solution)/shard_map/ppermute | solution.py:676
  29.0 0.8 %fault.3 = (f32[2,16,128]{2,1,0:T(8,128)S(1)}, f32[8,128]{1,0:T(8,128)S(1)}, f32[5,32,128]{2,1,0:T(8,128)S(1)}, f32[5,32,128]{2,1,0:T(8,128)S(1)}, f32[6,32,128]{2,1,0:T(8,128)S(1)}) custom-call(f32[5,32,128]{2,1,0:T(8,128)S(1)} %get-tuple-element.99.refs_0_, f32[5,32,128]{2,1,0:T(8,128)S(1)} %get-tuple-element.100.refs_1_, ...), custom_call_target="tpu_custom_call" | custom-call | bytes 3690000 | tf_op jit(solution)/shard_map/fault/pallas_call | solution.py:637
  29.7 0.1 collective-permute-start.11
  29.8 1.8 %collective-permute-start.12 = (f32[5,32,128]{2,1,0:T(8,128)S(1)}, f32[5,32,128]{2,1,0:T(8,128)S(1)}, u32[]{:S(2)}, u32[]{:S(2)}) collective-permute-start(f32[5,32,128]{2,1,0:T(8,128)S(1)} %get-tuple-element.113), channel_id=1, source_target_pairs={{0,4},{1,5},{4,0},{5,1},{8,12},{9,13},{12,8},{13,9},{2,6},{3,7},{6... | collective-permute-start | bytes 245768 | tf_op jit(solution)/shard_map/ppermute | solution.py:676
  31.6 0.2 collective-permute-start.13
  31.8 3.0 %stress_inner.3 = (f32[3,16,32,128]{3,2,1,0:T(8,128)S(1)}, f32[9,4,32,128]{3,2,1,0:T(8,128)S(1)}, f32[3,16,32,128]{3,2,1,0:T(8,128)}, f32[6,16,32,128]{3,2,1,0:T...) custom-call(f32[3,12,32,128]{3,2,1,0:T(8,128)S(1)} %get-tuple-element.92.refs_0_, ...), custom_call_target="tpu_custom_call" | custom-call | bytes 11070000 | tf_op jit(solution)/shard_map/stress_inner/pallas_call | solution.py:637
  34.8 1.0 %stress_edge.3 = (f32[6,16,32,128]{3,2,1,0:T(8,128)}, f32[6,16,32,128]{3,2,1,0:T(8,128)}) custom-call(f32[3,16,32,128]{3,2,1,0:T(8,128)S(1)} %get-tuple-element.111.refs_0_, f32[9,4,32,128]{3,2,1,0:T(8,128)S(1)} %get-tuple-element.112.refs_1_, ...), custom_call_target="tpu_custom_call", output_to_operand_aliasing={{0}: (8, {}), {1}: (9, {})} | custom-call | bytes 3690000 | tf_op jit(solution)/shard_map/stress_edge/pallas_call | solution.py:637
  (15 shorter events, 0.0 us)
Async XLA Ops:
  0.6 5.1 %copy-start.1 = (f32[5,8]{1,0:T(8,128)S(1)}, f32[5,8]{1,0:T(8,128)}, u32[]{:S(2)}) copy-start(f32[5,8]{1,0:T(8,128)} %refs_8_.1) | copy-start | bytes 484
  2.4 3.3 %collective-permute-start = (f32[6,32,128]{2,1,0:T(8,128)S(1)}, f32[6,32,128]{2,1,0:T(8,128)S(1)}, u32[]{:S(2)}, u32[]{:S(2)}) collective-permute-start(f32[6,32,128]{2,1,0:T(8,128)S(1)} %get-tuple-element.65), channel_id=1, source_target_pairs={{0,1},{1,0},{2,3},{3,2},{4,5},{5,4},{6,7},{7,6},{8,9},{9,8},{10,11... | collective-permute-start | bytes 294920 | tf_op jit(solution)/shard_map/ppermute | solution.py:676
  3.0 5.7 %collective-permute-start.1 = (f32[5,32,128]{2,1,0:T(8,128)S(1)}, f32[5,32,128]{2,1,0:T(8,128)S(1)}, u32[]{:S(2)}, u32[]{:S(2)}) collective-permute-start(f32[5,32,128]{2,1,0:T(8,128)S(1)} %get-tuple-element.72), channel_id=1, source_target_pairs={{0,4},{1,5},{4,0},{5,1},{8,12},{9,13},{12,8},{13,9},{2,6},{3,7},{6... | collective-permute-start | bytes 245768 | tf_op jit(solution)/shard_map/ppermute | solution.py:676
  5.6 3.0 %collective-permute-start.2 = (f32[5,32,128]{2,1,0:T(8,128)S(1)}, f32[5,32,128]{2,1,0:T(8,128)S(1)}, u32[]{:S(2)}, u32[]{:S(2)}) collective-permute-start(f32[5,32,128]{2,1,0:T(8,128)S(1)} %get-tuple-element.73), channel_id=1, source_target_pairs={{0,1},{1,0},{4,8},{5,9},{8,4},{9,5},{12,13},{13,12},{2,3},{3,2},{6... | collective-permute-start | bytes 245768 | tf_op jit(solution)/shard_map/ppermute | solution.py:676
  7.7 5.3 %copy-start.2 = (f32[3,4]{1,0:T(4,128)S(1)}, f32[3,4]{1,0:T(4,128)}, u32[]{:S(2)}) copy-start(f32[3,4]{1,0:T(4,128)} %refs_5_.5) | copy-start | bytes 148
  7.7 5.3 %copy-start.3 = (s32[2]{0:T(128)S(1)}, s32[2]{0:T(128)}, u32[]{:S(2)}) copy-start(s32[2]{0:T(128)} %refs_6_.7) | copy-start | bytes 28
  8.7 8.3 %copy-start = (f32[6,16,32,128]{3,2,1,0:T(8,128)S(1)}, f32[6,16,32,128]{3,2,1,0:T(8,128)}, u32[]{:S(2)}) copy-start(f32[6,16,32,128]{3,2,1,0:T(8,128)} %refs_3_.5) | copy-start | bytes 4718596
  8.8 4.2 %collective-permute-start.3 = (f32[96,128]{1,0:T(8,128)S(1)}, f32[96,128]{1,0:T(8,128)S(1)}, u32[]{:S(2)}, u32[]{:S(2)}) collective-permute-start(f32[96,128]{1,0:T(8,128)S(1)} %get-tuple-element.81.refs_3_.refs_9_), channel_id=1, source_target_pairs={{0,2},{2,0},{1,3},{3,1},{4,6},{6,4},{5,7},{7,5},{8,10},{10,8},{9,1... | collective-permute-start | bytes 147464 | tf_op jit(solution)/shard_map/ppermute | solution.py:676
  13.7 3.2 %collective-permute-start.4 = (f32[6,32,128]{2,1,0:T(8,128)S(1)}, f32[6,32,128]{2,1,0:T(8,128)S(1)}, u32[]{:S(2)}, u32[]{:S(2)}) collective-permute-start(f32[6,32,128]{2,1,0:T(8,128)S(1)} %get-tuple-element.83), channel_id=1, source_target_pairs={{0,1},{1,0},{2,3},{3,2},{4,5},{5,4},{6,7},{7,6},{8,9},{9,8},{10,11... | collective-permute-start | bytes 294920 | tf_op jit(solution)/shard_map/ppermute | solution.py:676
  13.8 6.0 %collective-permute-start.5 = (f32[5,32,128]{2,1,0:T(8,128)S(1)}, f32[5,32,128]{2,1,0:T(8,128)S(1)}, u32[]{:S(2)}, u32[]{:S(2)}) collective-permute-start(f32[5,32,128]{2,1,0:T(8,128)S(1)} %get-tuple-element.87), channel_id=1, source_target_pairs={{0,4},{1,5},{4,0},{5,1},{8,12},{9,13},{12,8},{13,9},{2,6},{3,7},{6... | collective-permute-start | bytes 245768 | tf_op jit(solution)/shard_map/ppermute | solution.py:676
  16.8 3.0 %collective-permute-start.6 = (f32[5,32,128]{2,1,0:T(8,128)S(1)}, f32[5,32,128]{2,1,0:T(8,128)S(1)}, u32[]{:S(2)}, u32[]{:S(2)}) collective-permute-start(f32[5,32,128]{2,1,0:T(8,128)S(1)} %get-tuple-element.88), channel_id=1, source_target_pairs={{0,1},{1,0},{4,8},{5,9},{8,4},{9,5},{12,13},{13,12},{2,3},{3,2},{6... | collective-permute-start | bytes 245768 | tf_op jit(solution)/shard_map/ppermute | solution.py:676
  20.1 2.1 %collective-permute-start.7 = (f32[6,32,128]{2,1,0:T(8,128)S(1)}, f32[6,32,128]{2,1,0:T(8,128)S(1)}, u32[]{:S(2)}, u32[]{:S(2)}) collective-permute-start(f32[6,32,128]{2,1,0:T(8,128)S(1)} %get-tuple-element.91), channel_id=1, source_target_pairs={{0,1},{1,0},{2,3},{3,2},{4,5},{5,4},{6,7},{7,6},{8,9},{9,8},{10,11... | collective-permute-start | bytes 294920 | tf_op jit(solution)/shard_map/ppermute | solution.py:676
  20.1 4.9 %collective-permute-start.8 = (f32[5,32,128]{2,1,0:T(8,128)S(1)}, f32[5,32,128]{2,1,0:T(8,128)S(1)}, u32[]{:S(2)}, u32[]{:S(2)}) collective-permute-start(f32[5,32,128]{2,1,0:T(8,128)S(1)} %get-tuple-element.93), channel_id=1, source_target_pairs={{0,4},{1,5},{4,0},{5,1},{8,12},{9,13},{12,8},{13,9},{2,6},{3,7},{6... | collective-permute-start | bytes 245768 | tf_op jit(solution)/shard_map/ppermute | solution.py:676
  21.9 3.0 %collective-permute-start.9 = (f32[5,32,128]{2,1,0:T(8,128)S(1)}, f32[5,32,128]{2,1,0:T(8,128)S(1)}, u32[]{:S(2)}, u32[]{:S(2)}) collective-permute-start(f32[5,32,128]{2,1,0:T(8,128)S(1)} %get-tuple-element.94), channel_id=1, source_target_pairs={{0,1},{1,0},{4,8},{5,9},{8,4},{9,5},{12,13},{13,12},{2,3},{3,2},{6... | collective-permute-start | bytes 245768 | tf_op jit(solution)/shard_map/ppermute | solution.py:676
  25.2 3.8 %collective-permute-start.10 = (f32[32,128]{1,0:T(8,128)S(1)}, f32[32,128]{1,0:T(8,128)S(1)}, u32[]{:S(2)}, u32[]{:S(2)}) collective-permute-start(f32[32,128]{1,0:T(8,128)S(1)} %get-tuple-element.102.refs_3_), channel_id=1, source_target_pairs={{0,2},{2,0},{1,3},{3,1},{4,6},{6,4},{5,7},{7,5},{8,10},{10,8},{9,1... | collective-permute-start | bytes 49160 | tf_op jit(solution)/shard_map/ppermute | solution.py:676
  29.7 2.1 %collective-permute-start.11 = (f32[6,32,128]{2,1,0:T(8,128)S(1)}, f32[6,32,128]{2,1,0:T(8,128)S(1)}, u32[]{:S(2)}, u32[]{:S(2)}) collective-permute-start(f32[6,32,128]{2,1,0:T(8,128)S(1)} %get-tuple-element.108), channel_id=1, source_target_pairs={{0,1},{1,0},{2,3},{3,2},{4,5},{5,4},{6,7},{7,6},{8,9},{9,8},{10,11... | collective-permute-start | bytes 294920 | tf_op jit(solution)/shard_map/ppermute | solution.py:676
  29.8 5.0 %collective-permute-start.12 = (f32[5,32,128]{2,1,0:T(8,128)S(1)}, f32[5,32,128]{2,1,0:T(8,128)S(1)}, u32[]{:S(2)}, u32[]{:S(2)}) collective-permute-start(f32[5,32,128]{2,1,0:T(8,128)S(1)} %get-tuple-element.113), channel_id=1, source_target_pairs={{0,4},{1,5},{4,0},{5,1},{8,12},{9,13},{12,8},{13,9},{2,6},{3,7},{6... | collective-permute-start | bytes 245768 | tf_op jit(solution)/shard_map/ppermute | solution.py:676
  31.6 3.2 %collective-permute-start.13 = (f32[5,32,128]{2,1,0:T(8,128)S(1)}, f32[5,32,128]{2,1,0:T(8,128)S(1)}, u32[]{:S(2)}, u32[]{:S(2)}) collective-permute-start(f32[5,32,128]{2,1,0:T(8,128)S(1)} %get-tuple-element.114), channel_id=1, source_target_pairs={{0,1},{1,0},{4,8},{5,9},{8,4},{9,5},{12,13},{13,12},{2,3},{3,2},{6... | collective-permute-start | bytes 245768 | tf_op jit(solution)/shard_map/ppermute | solution.py:676

commit v12 on v10

--- a/solution.py
+++ b/solution.py
@@ -252,14 +252,14 @@
 
 def pack_kernel(r):
     count, rows, depths = r.stress.shape[1:]
-    whole = [(comp, 0, count) for comp in STRESS_SLOTS]
+    pieces = [(comp, 0, count) for comp in STRESS_SLOTS]
     some = {}
     for comp, place in STRESS_TAIL + STRESS_HEAD:
         if comp not in STRESS_SLOTS:
             some.setdefault((comp, place < 0), []).append(place % count)
-    some = [(comp, min(at), max(at) + 1) for (comp, _), at in some.items()]
+    pieces += [(comp, min(at), max(at) + 1) for (comp, _), at in some.items()]
     copies = []
-    for i, (comp, start, stop) in enumerate(some + whole):
+    for i, (comp, start, stop) in enumerate(pieces):
         span = pl.ds(start, stop - start)
         copy = pltpu.make_async_copy(r.stress.at[comp, span], r.held.at[comp, span], r.sems.at[i])
         copy.start()
@@ -272,6 +272,17 @@
     for x in range(count):
         strip = edges.packed(strip, x, [r.held[c, x] for c in STRESS_SLOTS])
     set_strip(r, strip)
+
+
+def bring_kernel(names, r):
+    copies = []
+    for i, key in enumerate(names):
+        source, out = getattr(r, key), getattr(r, f"{key}_out")
+        copies.append(pltpu.make_async_copy(source, out, r.sems.at[i]))
+    for copy in copies:
+        copy.start()
+    for copy in copies:
+        copy.wait()
 
 
 def grouped(xs, size):
@@ -632,7 +643,10 @@
             return pl.BlockSpec(memory_space=pltpu.HBM)
         return pl.BlockSpec(memory_space=pltpu.SMEM if key in SCALARS else pltpu.VMEM)
 
-    shapes = [jax.ShapeDtypeStruct(shape, jnp.float32) for shape in outs.values()]
+    shapes = [
+        shape if hasattr(shape, "dtype") else jax.ShapeDtypeStruct(shape, jnp.float32)
+        for shape in outs.values()
+    ]
     result = pl.pallas_call(
         body,
         out_shape=shapes,
@@ -743,17 +757,33 @@
     else:
         still = {}
 
-    parts = {"stress": stress, "memory": memory}
-    props = {"material": material, "table": material_table}
+    held = {"velocity": velocity, "material": material}
+    if not banded:
+        held.update(prestress=prestress, normal=normal_stress, slip=slip_path)
+        held.update(zone=zone_label, mask=fault_mask)
+    ins = {"stress": stress, **held}
+    ins = {key: pltpu.with_memory_space_constraint(a, pltpu.HBM) for key, a in ins.items()}
+    sems = {"sems": pltpu.SemaphoreType.DMA((8,))}
     packed = call(
         pack_kernel,
         "pack",
-        {"stress": stress},
+        {"stress": ins["stress"]},
         travelling,
-        scratch={"held": pltpu.VMEM(stress.shape, jnp.float32), "sems": pltpu.SemaphoreType.DMA((8,))},
+        scratch={"held": pltpu.VMEM(stress.shape, jnp.float32), **sems},
         apart=("stress",),
-        vmem=6,
     )
+    brought = call(
+        functools.partial(bring_kernel, list(ins)),
+        "bring",
+        ins,
+        {key: jax.ShapeDtypeStruct(a.shape, a.dtype) for key, a in ins.items()},
+        scratch=sems,
+        apart=list(ins),
+    )
+    velocity = brought["velocity"]
+    parts = {"stress": brought["stress"], "memory": memory}
+    props = {"material": brought["material"], "table": material_table}
+    friction_ins = {key: brought[key] for key in held if key not in ("velocity", "material")}
     for step in range(STEPS):
         first, last = step == 0, step == STEPS - 1
         held_stress = {key: parts[key] for key in parts if key.startswith("stress")}
@@ -765,8 +795,7 @@
         if first:
             face_rows += count
             if not banded:
-                ins.update(prestress=prestress, normal=normal_stress, slip=slip_path)
-                ins.update(zone=zone_label, mask=fault_mask)
+                ins.update(friction_ins)
                 face_rows += 6 * normal_stress.shape[0]
         outs = {"inner": (3, *inner), "part": (4, *edge), "strip_inner": plane}
         outs["face_inner"] = (face_rows, depths)

time: 36.2 us -> 36.6 us (1.011)
  Pallas kernels: 12.8 us -> 15.4 us
  local copies, waits for them, and re-layouts: 1.45 us -> 0.03 us
  waiting for transfers between devices: 7.07 us -> 6.39 us
    pallas_call x11 -> x12, Pallas kernels: 12.8 us -> 15.4 us  [call(): pl.pallas_call(body, out_shape=shapes, in_specs=[place(key) for key in in...]
    unnamed x26 -> x8, local copies, waits for them, and re-layouts: 1.45 us -> 0.03 us
    ppermute x14, waiting for transfers between devices: 7.07 us -> 6.39 us  [sent(): return lax.ppermute(block, *route)]
  transfers between devices with their start and end apart: 14 -> 14, of which waited for: 5 -> 4; matrix products, arithmetic and copies ran while one was open for 0% -> 0% of each run, Pallas kernels for 25% -> 30%
where the time goes in v12:
time: 36.6 us; the launch traced here: 36.4 us
  Pallas kernels  15.4 us (42%)
  starting transfers between devices  13.8 us (38%)
  waiting for transfers between devices  6.39 us (17%)
  between operations  0.79 us (2%)
    pallas_call x12, Pallas kernels, call(): pl.pallas_call(body, out_shape=shapes, in_specs=[place(key) for key in in...  15.4 us
    ppermute x14, starting transfers between devices, sent(): return lax.ppermute(block, *route)  13.8 us
    ppermute x14, waiting for transfers between devices, sent(): return lax.ppermute(block, *route)  6.39 us
  transfers between devices with their start and end apart: 14, of which 4 were waited for; matrix products, arithmetic and copies ran while one was open for 0% of the time, Pallas kernels for 30%

profile of v12, /device:TPU:0, one launch (start us, length us, event | category | flops | bytes accessed | tf_op | source)
XLA Modules:
  0.0 36.4 jit_solution(9227339311802661898)
XLA Ops:
  0.6 1.5 %pack.1 = (f32[5,32,128]{2,1,0:T(8,128)S(1)}, f32[5,32,128]{2,1,0:T(8,128)S(1)}, f32[6,32,128]{2,1,0:T(8,128)S(1)}) custom-call(f32[6,16,32,128]{3,2,1,0:T(8,128)} %refs_0_.3), custom_call_target="tpu_custom_call" | custom-call | bytes 3690000 | tf_op jit(solution)/shard_map/pack/pallas_call | solution.py:650
  2.1 0.0 copy-start.1
  2.1 0.5 %collective-permute-start = (f32[6,32,128]{2,1,0:T(8,128)S(1)}, f32[6,32,128]{2,1,0:T(8,128)S(1)}, u32[]{:S(2)}, u32[]{:S(2)}) collective-permute-start(f32[6,32,128]{2,1,0:T(8,128)S(1)} %get-tuple-element.65), channel_id=1, source_target_pairs={{0,1},{1,0},{2,3},{3,2},{4,5},{5,4},{6,7},{7,6},{8,9},{9,8},{10,11... | collective-permute-start | bytes 294920 | tf_op jit(solution)/shard_map/ppermute | solution.py:689
  2.6 2.6 %collective-permute-start.1 = (f32[5,32,128]{2,1,0:T(8,128)S(1)}, f32[5,32,128]{2,1,0:T(8,128)S(1)}, u32[]{:S(2)}, u32[]{:S(2)}) collective-permute-start(f32[5,32,128]{2,1,0:T(8,128)S(1)} %get-tuple-element.72), channel_id=1, source_target_pairs={{0,4},{1,5},{4,0},{5,1},{8,12},{9,13},{12,8},{13,9},{2,6},{3,7},{6... | collective-permute-start | bytes 245768 | tf_op jit(solution)/shard_map/ppermute | solution.py:689
  5.3 0.2 collective-permute-start.2
  5.4 1.7 %bring.1 = (f32[6,16,32,128]{3,2,1,0:T(8,128)S(1)}, f32[3,16,32,128]{3,2,1,0:T(8,128)S(1)}, s32[16,32,128]{2,1,0:T(8,128)S(1)}, f32[8,2,128]{2,1,0:T(2,128)S(1)}...) custom-call(f32[6,16,32,128]{3,2,1,0:T(8,128)} %refs_0_.3, ...), custom_call_target="tpu_custom_call" | custom-call | bytes 3690000 | tf_op jit(solution)/shard_map/bring/pallas_call | solution.py:650
  7.2 1.9 %velocity_inner.2 = (f32[3,12,32,128]{3,2,1,0:T(8,128)S(1)}, f32[4,4,32,128]{3,2,1,0:T(8,128)S(1)}, f32[32,128]{1,0:T(8,128)S(1)}, f32[96,128]{1,0:T(8,128)S(1)}) custom-call(f32[3,16,32,128]{3,2,1,0:T(8,128)S(1)} %get-tuple-element.62.refs_0_, f32[6,16,32,128]{3,2,1,0:T(8,128)S(1)} %get-tuple-element.63.refs_1_.refs_3_.refs_2_, ...), custom_call_target="tpu_custom_call" | custom-call | bytes 11070000 | tf_op jit(solution)/shard_map/velocity_inner/pallas_call | solution.py:650
  9.1 0.0 copy-start.2
  9.2 0.2 velocity_edge.2
  9.3 1.5 %collective-permute-start.3 = (f32[96,128]{1,0:T(8,128)S(1)}, f32[96,128]{1,0:T(8,128)S(1)}, u32[]{:S(2)}, u32[]{:S(2)}) collective-permute-start(f32[96,128]{1,0:T(8,128)S(1)} %get-tuple-element.81.refs_3_.refs_9_), channel_id=1, source_target_pairs={{0,2},{2,0},{1,3},{3,1},{4,6},{6,4},{5,7},{7,5},{8,10},{10,8},{9,1... | collective-permute-start | bytes 147464 | tf_op jit(solution)/shard_map/ppermute | solution.py:689
  10.9 2.6 %collective-permute-done.3.refs_4_.refs_10_ = f32[96,128]{1,0:T(8,128)S(1)} collective-permute-done((f32[96,128]{1,0:T(8,128)S(1)}, f32[96,128]{1,0:T(8,128)S(1)}, u32[]{:S(2)}, u32[]{:S(2)}) %collective-permute-start.3) | collective-permute-done | bytes 49184 | tf_op jit(solution)/shard_map/ppermute | solution.py:689
  13.5 0.8 %fault.2 = (f32[2,16,128]{2,1,0:T(8,128)S(1)}, f32[16,128]{1,0:T(8,128)S(1)}, f32[5,32,128]{2,1,0:T(8,128)S(1)}, f32[5,32,128]{2,1,0:T(8,128)S(1)}, f32[6,32,128...) custom-call(f32[5,32,128]{2,1,0:T(8,128)S(1)} %get-tuple-element.78.refs_0_, f32[5,32,128]{2,1,0:T(8,128)S(1)} %get-tuple-element.79.refs_1_, ...), custom_call_target="tpu_custom_call" | custom-call | bytes 3690000 | tf_op jit(solution)/shard_map/fault/pallas_call | solution.py:650
  14.3 0.1 collective-permute-start.4
  14.3 3.1 %collective-permute-start.5 = (f32[5,32,128]{2,1,0:T(8,128)S(1)}, f32[5,32,128]{2,1,0:T(8,128)S(1)}, u32[]{:S(2)}, u32[]{:S(2)}) collective-permute-start(f32[5,32,128]{2,1,0:T(8,128)S(1)} %get-tuple-element.87), channel_id=1, source_target_pairs={{0,4},{1,5},{4,0},{5,1},{8,12},{9,13},{12,8},{13,9},{2,6},{3,7},{6... | collective-permute-start | bytes 245768 | tf_op jit(solution)/shard_map/ppermute | solution.py:689
  17.4 0.2 collective-permute-start.6
  17.6 2.4 %stress_inner.2 = (f32[3,16,32,128]{3,2,1,0:T(8,128)S(1)}, f32[9,4,32,128]{3,2,1,0:T(8,128)S(1)}, f32[6,12,32,128]{3,2,1,0:T(8,128)S(1)}, f32[6,12,32,128]{3,2,1,0:T(8,128)S(1)}, f32[32,128]{1,0:T(8,128)S(1)}) custom-call(f32[3,12,32,128]{3,2,1,0:T(8,128)S(1)} %get-tuple-element.71.refs_0_, f32[3,4,32,128]{3,2,1,0:T(8,128)S(1)} %get-tuple-element.77.refs_1_, ...), custom_call_target="tpu_custom_call" | custom-call | bytes 11070000 | tf_op jit(solution)/shard_map/stress_inner/pallas_call | solution.py:650
  20.0 0.5 %collective-permute-done.5.refs_4_ = f32[5,32,128]{2,1,0:T(8,128)S(1)} collective-permute-done((f32[5,32,128]{2,1,0:T(8,128)S(1)}, f32[5,32,128]{2,1,0:T(8,128)S(1)}, u32[]{:S(2)}, u32[]{:S(2)}) %collective-permute-start.5) | collective-permute-done | bytes 81952 | tf_op jit(solution)/shard_map/ppermute | solution.py:689
  20.4 0.2 stress_edge.2
  20.7 0.1 collective-permute-start.7
  20.7 1.8 %collective-permute-start.8 = (f32[5,32,128]{2,1,0:T(8,128)S(1)}, f32[5,32,128]{2,1,0:T(8,128)S(1)}, u32[]{:S(2)}, u32[]{:S(2)}) collective-permute-start(f32[5,32,128]{2,1,0:T(8,128)S(1)} %get-tuple-element.93), channel_id=1, source_target_pairs={{0,4},{1,5},{4,0},{5,1},{8,12},{9,13},{12,8},{13,9},{2,6},{3,7},{6... | collective-permute-start | bytes 245768 | tf_op jit(solution)/shard_map/ppermute | solution.py:689
  22.6 0.2 collective-permute-start.9
  22.7 1.8 %velocity_inner.3 = (f32[3,12,32,128]{3,2,1,0:T(8,128)S(1)}, f32[4,4,32,128]{3,2,1,0:T(8,128)S(1)}, f32[32,128]{1,0:T(8,128)S(1)}, f32[32,128]{1,0:T(8,128)S(1)}) custom-call(f32[3,16,32,128]{3,2,1,0:T(8,128)S(1)} %get-tuple-element.84.refs_0_, f32[6,12,32,128]{3,2,1,0:T(8,128)S(1)} %get-tuple-element.85.refs_1_.refs_3_.refs_2_, ...), custom_call_target="tpu_custom_call" | custom-call | bytes 11070000 | tf_op jit(solution)/shard_map/velocity_inner/pallas_call | solution.py:650
  24.6 1.0 %collective-permute-done.8.refs_3_ = f32[5,32,128]{2,1,0:T(8,128)S(1)} collective-permute-done((f32[5,32,128]{2,1,0:T(8,128)S(1)}, f32[5,32,128]{2,1,0:T(8,128)S(1)}, u32[]{:S(2)}, u32[]{:S(2)}) %collective-permute-start.8) | collective-permute-done | bytes 81952 | tf_op jit(solution)/shard_map/ppermute | solution.py:689
  25.6 0.2 velocity_edge.3
  25.8 1.5 %collective-permute-start.10 = (f32[32,128]{1,0:T(8,128)S(1)}, f32[32,128]{1,0:T(8,128)S(1)}, u32[]{:S(2)}, u32[]{:S(2)}) collective-permute-start(f32[32,128]{1,0:T(8,128)S(1)} %get-tuple-element.102.refs_3_), channel_id=1, source_target_pairs={{0,2},{2,0},{1,3},{3,1},{4,6},{6,4},{5,7},{7,5},{8,10},{10,8},{9,1... | collective-permute-start | bytes 49160 | tf_op jit(solution)/shard_map/ppermute | solution.py:689
  27.3 2.3 %collective-permute-done.10.refs_4_ = f32[32,128]{1,0:T(8,128)S(1)} collective-permute-done((f32[32,128]{1,0:T(8,128)S(1)}, f32[32,128]{1,0:T(8,128)S(1)}, u32[]{:S(2)}, u32[]{:S(2)}) %collective-permute-start.10) | collective-permute-done | bytes 16416 | tf_op jit(solution)/shard_map/ppermute | solution.py:689
  29.6 0.8 %fault.3 = (f32[2,16,128]{2,1,0:T(8,128)S(1)}, f32[8,128]{1,0:T(8,128)S(1)}, f32[5,32,128]{2,1,0:T(8,128)S(1)}, f32[5,32,128]{2,1,0:T(8,128)S(1)}, f32[6,32,128]{2,1,0:T(8,128)S(1)}) custom-call(f32[5,32,128]{2,1,0:T(8,128)S(1)} %get-tuple-element.99.refs_0_, f32[5,32,128]{2,1,0:T(8,128)S(1)} %get-tuple-element.100.refs_1_, ...), custom_call_target="tpu_custom_call" | custom-call | bytes 3690000 | tf_op jit(solution)/shard_map/fault/pallas_call | solution.py:650
  30.3 0.1 collective-permute-start.11
  30.4 1.8 %collective-permute-start.12 = (f32[5,32,128]{2,1,0:T(8,128)S(1)}, f32[5,32,128]{2,1,0:T(8,128)S(1)}, u32[]{:S(2)}, u32[]{:S(2)}) collective-permute-start(f32[5,32,128]{2,1,0:T(8,128)S(1)} %get-tuple-element.113), channel_id=1, source_target_pairs={{0,4},{1,5},{4,0},{5,1},{8,12},{9,13},{12,8},{13,9},{2,6},{3,7},{6... | collective-permute-start | bytes 245768 | tf_op jit(solution)/shard_map/ppermute | solution.py:689
  32.2 0.2 collective-permute-start.13
  32.4 3.0 %stress_inner.3 = (f32[3,16,32,128]{3,2,1,0:T(8,128)S(1)}, f32[9,4,32,128]{3,2,1,0:T(8,128)S(1)}, f32[3,16,32,128]{3,2,1,0:T(8,128)}, f32[6,16,32,128]{3,2,1,0:T...) custom-call(f32[3,12,32,128]{3,2,1,0:T(8,128)S(1)} %get-tuple-element.92.refs_0_, ...), custom_call_target="tpu_custom_call" | custom-call | bytes 11070000 | tf_op jit(solution)/shard_map/stress_inner/pallas_call | solution.py:650
  35.4 1.0 %stress_edge.3 = (f32[6,16,32,128]{3,2,1,0:T(8,128)}, f32[6,16,32,128]{3,2,1,0:T(8,128)}) custom-call(f32[3,16,32,128]{3,2,1,0:T(8,128)S(1)} %get-tuple-element.111.refs_0_, f32[9,4,32,128]{3,2,1,0:T(8,128)S(1)} %get-tuple-element.112.refs_1_, ...), custom_call_target="tpu_custom_call", output_to_operand_aliasing={{0}: (8, {}), {1}: (9, {})} | custom-call | bytes 3690000 | tf_op jit(solution)/shard_map/stress_edge/pallas_call | solution.py:650
  (16 shorter events, 0.0 us)
Async XLA Ops:
  2.1 5.1 %copy-start.1 = (f32[5,8]{1,0:T(8,128)S(1)}, f32[5,8]{1,0:T(8,128)}, u32[]{:S(2)}) copy-start(f32[5,8]{1,0:T(8,128)} %refs_8_.1) | copy-start | bytes 484
  2.1 5.1 %collective-permute-start = (f32[6,32,128]{2,1,0:T(8,128)S(1)}, f32[6,32,128]{2,1,0:T(8,128)S(1)}, u32[]{:S(2)}, u32[]{:S(2)}) collective-permute-start(f32[6,32,128]{2,1,0:T(8,128)S(1)} %get-tuple-element.65), channel_id=1, source_target_pairs={{0,1},{1,0},{2,3},{3,2},{4,5},{5,4},{6,7},{7,6},{8,9},{9,8},{10,11... | collective-permute-start | bytes 294920 | tf_op jit(solution)/shard_map/ppermute | solution.py:689
  2.6 6.5 %collective-permute-start.1 = (f32[5,32,128]{2,1,0:T(8,128)S(1)}, f32[5,32,128]{2,1,0:T(8,128)S(1)}, u32[]{:S(2)}, u32[]{:S(2)}) collective-permute-start(f32[5,32,128]{2,1,0:T(8,128)S(1)} %get-tuple-element.72), channel_id=1, source_target_pairs={{0,4},{1,5},{4,0},{5,1},{8,12},{9,13},{12,8},{13,9},{2,6},{3,7},{6... | collective-permute-start | bytes 245768 | tf_op jit(solution)/shard_map/ppermute | solution.py:689
  5.3 3.9 %collective-permute-start.2 = (f32[5,32,128]{2,1,0:T(8,128)S(1)}, f32[5,32,128]{2,1,0:T(8,128)S(1)}, u32[]{:S(2)}, u32[]{:S(2)}) collective-permute-start(f32[5,32,128]{2,1,0:T(8,128)S(1)} %get-tuple-element.73), channel_id=1, source_target_pairs={{0,1},{1,0},{4,8},{5,9},{8,4},{9,5},{12,13},{13,12},{2,3},{3,2},{6... | collective-permute-start | bytes 245768 | tf_op jit(solution)/shard_map/ppermute | solution.py:689
  9.1 4.4 %copy-start.2 = (f32[3,4]{1,0:T(4,128)S(1)}, f32[3,4]{1,0:T(4,128)}, u32[]{:S(2)}) copy-start(f32[3,4]{1,0:T(4,128)} %refs_5_.5) | copy-start | bytes 148
  9.1 4.4 %copy-start.3 = (s32[2]{0:T(128)S(1)}, s32[2]{0:T(128)}, u32[]{:S(2)}) copy-start(s32[2]{0:T(128)} %refs_6_.7) | copy-start | bytes 28
  9.1 8.4 %copy-start = (f32[6,16,32,128]{3,2,1,0:T(8,128)S(1)}, f32[6,16,32,128]{3,2,1,0:T(8,128)}, u32[]{:S(2)}) copy-start(f32[6,16,32,128]{3,2,1,0:T(8,128)} %refs_3_.5) | copy-start | bytes 4718596
  9.3 4.2 %collective-permute-start.3 = (f32[96,128]{1,0:T(8,128)S(1)}, f32[96,128]{1,0:T(8,128)S(1)}, u32[]{:S(2)}, u32[]{:S(2)}) collective-permute-start(f32[96,128]{1,0:T(8,128)S(1)} %get-tuple-element.81.refs_3_.refs_9_), channel_id=1, source_target_pairs={{0,2},{2,0},{1,3},{3,1},{4,6},{6,4},{5,7},{7,5},{8,10},{10,8},{9,1... | collective-permute-start | bytes 147464 | tf_op jit(solution)/shard_map/ppermute | solution.py:689
  14.3 3.3 %collective-permute-start.4 = (f32[6,32,128]{2,1,0:T(8,128)S(1)}, f32[6,32,128]{2,1,0:T(8,128)S(1)}, u32[]{:S(2)}, u32[]{:S(2)}) collective-permute-start(f32[6,32,128]{2,1,0:T(8,128)S(1)} %get-tuple-element.83), channel_id=1, source_target_pairs={{0,1},{1,0},{2,3},{3,2},{4,5},{5,4},{6,7},{7,6},{8,9},{9,8},{10,11... | collective-permute-start | bytes 294920 | tf_op jit(solution)/shard_map/ppermute | solution.py:689
  14.3 6.1 %collective-permute-start.5 = (f32[5,32,128]{2,1,0:T(8,128)S(1)}, f32[5,32,128]{2,1,0:T(8,128)S(1)}, u32[]{:S(2)}, u32[]{:S(2)}) collective-permute-start(f32[5,32,128]{2,1,0:T(8,128)S(1)} %get-tuple-element.87), channel_id=1, source_target_pairs={{0,4},{1,5},{4,0},{5,1},{8,12},{9,13},{12,8},{13,9},{2,6},{3,7},{6... | collective-permute-start | bytes 245768 | tf_op jit(solution)/shard_map/ppermute | solution.py:689
  17.4 3.0 %collective-permute-start.6 = (f32[5,32,128]{2,1,0:T(8,128)S(1)}, f32[5,32,128]{2,1,0:T(8,128)S(1)}, u32[]{:S(2)}, u32[]{:S(2)}) collective-permute-start(f32[5,32,128]{2,1,0:T(8,128)S(1)} %get-tuple-element.88), channel_id=1, source_target_pairs={{0,1},{1,0},{4,8},{5,9},{8,4},{9,5},{12,13},{13,12},{2,3},{3,2},{6... | collective-permute-start | bytes 245768 | tf_op jit(solution)/shard_map/ppermute | solution.py:689
  20.7 2.1 %collective-permute-start.7 = (f32[6,32,128]{2,1,0:T(8,128)S(1)}, f32[6,32,128]{2,1,0:T(8,128)S(1)}, u32[]{:S(2)}, u32[]{:S(2)}) collective-permute-start(f32[6,32,128]{2,1,0:T(8,128)S(1)} %get-tuple-element.91), channel_id=1, source_target_pairs={{0,1},{1,0},{2,3},{3,2},{4,5},{5,4},{6,7},{7,6},{8,9},{9,8},{10,11... | collective-permute-start | bytes 294920 | tf_op jit(solution)/shard_map/ppermute | solution.py:689
  20.7 4.9 %collective-permute-start.8 = (f32[5,32,128]{2,1,0:T(8,128)S(1)}, f32[5,32,128]{2,1,0:T(8,128)S(1)}, u32[]{:S(2)}, u32[]{:S(2)}) collective-permute-start(f32[5,32,128]{2,1,0:T(8,128)S(1)} %get-tuple-element.93), channel_id=1, source_target_pairs={{0,4},{1,5},{4,0},{5,1},{8,12},{9,13},{12,8},{13,9},{2,6},{3,7},{6... | collective-permute-start | bytes 245768 | tf_op jit(solution)/shard_map/ppermute | solution.py:689
  22.6 3.0 %collective-permute-start.9 = (f32[5,32,128]{2,1,0:T(8,128)S(1)}, f32[5,32,128]{2,1,0:T(8,128)S(1)}, u32[]{:S(2)}, u32[]{:S(2)}) collective-permute-start(f32[5,32,128]{2,1,0:T(8,128)S(1)} %get-tuple-element.94), channel_id=1, source_target_pairs={{0,1},{1,0},{4,8},{5,9},{8,4},{9,5},{12,13},{13,12},{2,3},{3,2},{6... | collective-permute-start | bytes 245768 | tf_op jit(solution)/shard_map/ppermute | solution.py:689
  25.8 3.8 %collective-permute-start.10 = (f32[32,128]{1,0:T(8,128)S(1)}, f32[32,128]{1,0:T(8,128)S(1)}, u32[]{:S(2)}, u32[]{:S(2)}) collective-permute-start(f32[32,128]{1,0:T(8,128)S(1)} %get-tuple-element.102.refs_3_), channel_id=1, source_target_pairs={{0,2},{2,0},{1,3},{3,1},{4,6},{6,4},{5,7},{7,5},{8,10},{10,8},{9,1... | collective-permute-start | bytes 49160 | tf_op jit(solution)/shard_map/ppermute | solution.py:689
  30.3 2.1 %collective-permute-start.11 = (f32[6,32,128]{2,1,0:T(8,128)S(1)}, f32[6,32,128]{2,1,0:T(8,128)S(1)}, u32[]{:S(2)}, u32[]{:S(2)}) collective-permute-start(f32[6,32,128]{2,1,0:T(8,128)S(1)} %get-tuple-element.108), channel_id=1, source_target_pairs={{0,1},{1,0},{2,3},{3,2},{4,5},{5,4},{6,7},{7,6},{8,9},{9,8},{10,11... | collective-permute-start | bytes 294920 | tf_op jit(solution)/shard_map/ppermute | solution.py:689
  30.4 5.0 %collective-permute-start.12 = (f32[5,32,128]{2,1,0:T(8,128)S(1)}, f32[5,32,128]{2,1,0:T(8,128)S(1)}, u32[]{:S(2)}, u32[]{:S(2)}) collective-permute-start(f32[5,32,128]{2,1,0:T(8,128)S(1)} %get-tuple-element.113), channel_id=1, source_target_pairs={{0,4},{1,5},{4,0},{5,1},{8,12},{9,13},{12,8},{13,9},{2,6},{3,7},{6... | collective-permute-start | bytes 245768 | tf_op jit(solution)/shard_map/ppermute | solution.py:689
  32.2 3.2 %collective-permute-start.13 = (f32[5,32,128]{2,1,0:T(8,128)S(1)}, f32[5,32,128]{2,1,0:T(8,128)S(1)}, u32[]{:S(2)}, u32[]{:S(2)}) collective-permute-start(f32[5,32,128]{2,1,0:T(8,128)S(1)} %get-tuple-element.114), channel_id=1, source_target_pairs={{0,1},{1,0},{4,8},{5,9},{8,4},{9,5},{12,13},{13,12},{2,3},{3,2},{6... | collective-permute-start | bytes 245768 | tf_op jit(solution)/shard_map/ppermute | solution.py:689

commit v13 on v11

--- a/solution.py
+++ b/solution.py
@@ -261,13 +261,15 @@
         copy.start()
         copies.append(copy)
     edges = Edges(rows, depths)
-    for copy in copies[:5]:
+    for copy in copies[:3]:
         copy.wait()
-    edge_planes(Field(count, r.stress_out), STRESS_TAIL, STRESS_HEAD, r.one_out, r.two_out)
     strip = jnp.zeros((rows, depths), jnp.float32)
     for x in range(count):
         strip = edges.packed(strip, x, [r.stress_out[c, x] for c in STRESS_SLOTS])
     set_strip(r, strip)
+    for copy in copies[3:5]:
+        copy.wait()
+    edge_planes(Field(count, r.stress_out), STRESS_TAIL, STRESS_HEAD, r.one_out, r.two_out)
     for copy in copies[5:]:
         copy.wait()
 
@@ -452,7 +454,8 @@
 
     def line(planes, i):
         comp, place = planes[min(i, len(planes) - 1)]
-        return still_line if comp == 1 else r.change_out[comp // 2, pl.ds(place % count, 1), :]
+        at = place % count
+        return still_line if comp == 1 else (change_x, change_z)[comp // 2][at : at + 1]
 
     pairs = []
     for i in range(r.one_out.shape[0]):

time: 36 us -> 36 us (level)
  no operation moved by 1% of the time
where the time goes in v13:
time: 36 us; the launch traced here: 35.8 us
  Pallas kernels  14 us (39%)
  starting transfers between devices  13.9 us (39%)
  waiting for transfers between devices  7.12 us (20%)
  between operations  0.76 us (2%)
    pallas_call x11, Pallas kernels, call(): pl.pallas_call(body, out_shape=shapes, in_specs=[place(key) for key in in...  14 us
    ppermute x14, starting transfers between devices, sent(): return lax.ppermute(block, *route)  13.9 us
    ppermute x14, waiting for transfers between devices, sent(): return lax.ppermute(block, *route)  7.12 us
  transfers between devices with their start and end apart: 14, of which 5 were waited for; matrix products, arithmetic and copies ran while one was open for 0% of the time, Pallas kernels for 25%

profile of v13, /device:TPU:0, one launch (start us, length us, event | category | flops | bytes accessed | tf_op | source)
XLA Modules:
  0.0 35.8 jit_solution(7342166254515474662)
XLA Ops:
  0.6 1.8 %pack.1 = (f32[5,32,128]{2,1,0:T(8,128)S(1)}, f32[5,32,128]{2,1,0:T(8,128)S(1)}, f32[6,32,128]{2,1,0:T(8,128)S(1)}, f32[6,16,32,128]{3,2,1,0:T(8,128)S(1)}, f32[...) custom-call(f32[6,16,32,128]{3,2,1,0:T(8,128)} %refs_0_.1, ...), custom_call_target="tpu_custom_call" | custom-call | bytes 3690000 | tf_op jit(solution)/shard_map/pack/pallas_call | solution.py:640
  2.4 0.5 %collective-permute-start = (f32[6,32,128]{2,1,0:T(8,128)S(1)}, f32[6,32,128]{2,1,0:T(8,128)S(1)}, u32[]{:S(2)}, u32[]{:S(2)}) collective-permute-start(f32[6,32,128]{2,1,0:T(8,128)S(1)} %get-tuple-element.65), channel_id=1, source_target_pairs={{0,1},{1,0},{2,3},{3,2},{4,5},{5,4},{6,7},{7,6},{8,9},{9,8},{10,11... | collective-permute-start | bytes 294920 | tf_op jit(solution)/shard_map/ppermute | solution.py:679
  3.0 2.6 %collective-permute-start.1 = (f32[5,32,128]{2,1,0:T(8,128)S(1)}, f32[5,32,128]{2,1,0:T(8,128)S(1)}, u32[]{:S(2)}, u32[]{:S(2)}) collective-permute-start(f32[5,32,128]{2,1,0:T(8,128)S(1)} %get-tuple-element.72), channel_id=1, source_target_pairs={{0,4},{1,5},{4,0},{5,1},{8,12},{9,13},{12,8},{13,9},{2,6},{3,7},{6... | collective-permute-start | bytes 245768 | tf_op jit(solution)/shard_map/ppermute | solution.py:679
  5.6 0.2 collective-permute-start.2
  5.8 1.9 %velocity_inner.2 = (f32[3,12,32,128]{3,2,1,0:T(8,128)S(1)}, f32[4,4,32,128]{3,2,1,0:T(8,128)S(1)}, f32[32,128]{1,0:T(8,128)S(1)}, f32[96,128]{1,0:T(8,128)S(1)}) custom-call(f32[3,16,32,128]{3,2,1,0:T(8,128)S(1)} %get-tuple-element.62.refs_0_, f32[6,16,32,128]{3,2,1,0:T(8,128)S(1)} %get-tuple-element.63.refs_1_.refs_3_.refs_2_, ...), custom_call_target="tpu_custom_call" | custom-call | bytes 11070000 | tf_op jit(solution)/shard_map/velocity_inner/pallas_call | solution.py:640
  7.7 0.0 copy-start.2
  7.7 0.0 copy-start.3
  7.7 1.0 %collective-permute-done.1.refs_2_ = f32[5,32,128]{2,1,0:T(8,128)S(1)} collective-permute-done((f32[5,32,128]{2,1,0:T(8,128)S(1)}, f32[5,32,128]{2,1,0:T(8,128)S(1)}, u32[]{:S(2)}, u32[]{:S(2)}) %collective-permute-start.1) | collective-permute-done | bytes 81952 | tf_op jit(solution)/shard_map/ppermute | solution.py:679
  8.7 0.2 velocity_edge.2
  8.8 1.7 %collective-permute-start.3 = (f32[96,128]{1,0:T(8,128)S(1)}, f32[96,128]{1,0:T(8,128)S(1)}, u32[]{:S(2)}, u32[]{:S(2)}) collective-permute-start(f32[96,128]{1,0:T(8,128)S(1)} %get-tuple-element.81.refs_3_.refs_9_), channel_id=1, source_target_pairs={{0,2},{2,0},{1,3},{3,1},{4,6},{6,4},{5,7},{7,5},{8,10},{10,8},{9,1... | collective-permute-start | bytes 147464 | tf_op jit(solution)/shard_map/ppermute | solution.py:679
  10.6 2.4 %collective-permute-done.3.refs_4_.refs_10_ = f32[96,128]{1,0:T(8,128)S(1)} collective-permute-done((f32[96,128]{1,0:T(8,128)S(1)}, f32[96,128]{1,0:T(8,128)S(1)}, u32[]{:S(2)}, u32[]{:S(2)}) %collective-permute-start.3) | collective-permute-done | bytes 49184 | tf_op jit(solution)/shard_map/ppermute | solution.py:679
  13.0 0.8 %fault.2 = (f32[2,16,128]{2,1,0:T(8,128)S(1)}, f32[16,128]{1,0:T(8,128)S(1)}, f32[5,32,128]{2,1,0:T(8,128)S(1)}, f32[5,32,128]{2,1,0:T(8,128)S(1)}, f32[6,32,128...) custom-call(f32[5,32,128]{2,1,0:T(8,128)S(1)} %get-tuple-element.78.refs_0_, f32[5,32,128]{2,1,0:T(8,128)S(1)} %get-tuple-element.79.refs_1_, ...), custom_call_target="tpu_custom_call" | custom-call | bytes 3690000 | tf_op jit(solution)/shard_map/fault/pallas_call | solution.py:640
  13.7 0.1 collective-permute-start.4
  13.8 2.9 %collective-permute-start.5 = (f32[5,32,128]{2,1,0:T(8,128)S(1)}, f32[5,32,128]{2,1,0:T(8,128)S(1)}, u32[]{:S(2)}, u32[]{:S(2)}) collective-permute-start(f32[5,32,128]{2,1,0:T(8,128)S(1)} %get-tuple-element.87), channel_id=1, source_target_pairs={{0,4},{1,5},{4,0},{5,1},{8,12},{9,13},{12,8},{13,9},{2,6},{3,7},{6... | collective-permute-start | bytes 245768 | tf_op jit(solution)/shard_map/ppermute | solution.py:679
  16.8 0.2 collective-permute-start.6
  16.9 2.4 %stress_inner.2 = (f32[3,16,32,128]{3,2,1,0:T(8,128)S(1)}, f32[9,4,32,128]{3,2,1,0:T(8,128)S(1)}, f32[6,12,32,128]{3,2,1,0:T(8,128)S(1)}, f32[6,12,32,128]{3,2,1,0:T(8,128)S(1)}, f32[32,128]{1,0:T(8,128)S(1)}) custom-call(f32[3,12,32,128]{3,2,1,0:T(8,128)S(1)} %get-tuple-element.71.refs_0_, f32[3,4,32,128]{3,2,1,0:T(8,128)S(1)} %get-tuple-element.77.refs_1_, ...), custom_call_target="tpu_custom_call" | custom-call | bytes 11070000 | tf_op jit(solution)/shard_map/stress_inner/pallas_call | solution.py:640
  19.4 0.5 %collective-permute-done.5.refs_4_ = f32[5,32,128]{2,1,0:T(8,128)S(1)} collective-permute-done((f32[5,32,128]{2,1,0:T(8,128)S(1)}, f32[5,32,128]{2,1,0:T(8,128)S(1)}, u32[]{:S(2)}, u32[]{:S(2)}) %collective-permute-start.5) | collective-permute-done | bytes 81952 | tf_op jit(solution)/shard_map/ppermute | solution.py:679
  19.8 0.2 stress_edge.2
  20.1 0.1 collective-permute-start.7
  20.1 1.8 %collective-permute-start.8 = (f32[5,32,128]{2,1,0:T(8,128)S(1)}, f32[5,32,128]{2,1,0:T(8,128)S(1)}, u32[]{:S(2)}, u32[]{:S(2)}) collective-permute-start(f32[5,32,128]{2,1,0:T(8,128)S(1)} %get-tuple-element.93), channel_id=1, source_target_pairs={{0,4},{1,5},{4,0},{5,1},{8,12},{9,13},{12,8},{13,9},{2,6},{3,7},{6... | collective-permute-start | bytes 245768 | tf_op jit(solution)/shard_map/ppermute | solution.py:679
  21.9 0.2 collective-permute-start.9
  22.1 1.8 %velocity_inner.3 = (f32[3,12,32,128]{3,2,1,0:T(8,128)S(1)}, f32[4,4,32,128]{3,2,1,0:T(8,128)S(1)}, f32[32,128]{1,0:T(8,128)S(1)}, f32[32,128]{1,0:T(8,128)S(1)}) custom-call(f32[3,16,32,128]{3,2,1,0:T(8,128)S(1)} %get-tuple-element.84.refs_0_, f32[6,12,32,128]{3,2,1,0:T(8,128)S(1)} %get-tuple-element.85.refs_1_.refs_3_.refs_2_, ...), custom_call_target="tpu_custom_call" | custom-call | bytes 11070000 | tf_op jit(solution)/shard_map/velocity_inner/pallas_call | solution.py:640
  24.0 1.0 %collective-permute-done.8.refs_3_ = f32[5,32,128]{2,1,0:T(8,128)S(1)} collective-permute-done((f32[5,32,128]{2,1,0:T(8,128)S(1)}, f32[5,32,128]{2,1,0:T(8,128)S(1)}, u32[]{:S(2)}, u32[]{:S(2)}) %collective-permute-start.8) | collective-permute-done | bytes 81952 | tf_op jit(solution)/shard_map/ppermute | solution.py:679
  25.0 0.2 velocity_edge.3
  25.2 1.6 %collective-permute-start.10 = (f32[32,128]{1,0:T(8,128)S(1)}, f32[32,128]{1,0:T(8,128)S(1)}, u32[]{:S(2)}, u32[]{:S(2)}) collective-permute-start(f32[32,128]{1,0:T(8,128)S(1)} %get-tuple-element.102.refs_3_), channel_id=1, source_target_pairs={{0,2},{2,0},{1,3},{3,1},{4,6},{6,4},{5,7},{7,5},{8,10},{10,8},{9,1... | collective-permute-start | bytes 49160 | tf_op jit(solution)/shard_map/ppermute | solution.py:679
  26.7 2.2 %collective-permute-done.10.refs_4_ = f32[32,128]{1,0:T(8,128)S(1)} collective-permute-done((f32[32,128]{1,0:T(8,128)S(1)}, f32[32,128]{1,0:T(8,128)S(1)}, u32[]{:S(2)}, u32[]{:S(2)}) %collective-permute-start.10) | collective-permute-done | bytes 16416 | tf_op jit(solution)/shard_map/ppermute | solution.py:679
  29.0 0.8 %fault.3 = (f32[2,16,128]{2,1,0:T(8,128)S(1)}, f32[8,128]{1,0:T(8,128)S(1)}, f32[5,32,128]{2,1,0:T(8,128)S(1)}, f32[5,32,128]{2,1,0:T(8,128)S(1)}, f32[6,32,128]{2,1,0:T(8,128)S(1)}) custom-call(f32[5,32,128]{2,1,0:T(8,128)S(1)} %get-tuple-element.99.refs_0_, f32[5,32,128]{2,1,0:T(8,128)S(1)} %get-tuple-element.100.refs_1_, ...), custom_call_target="tpu_custom_call" | custom-call | bytes 3690000 | tf_op jit(solution)/shard_map/fault/pallas_call | solution.py:640
  29.7 0.1 collective-permute-start.11
  29.8 1.8 %collective-permute-start.12 = (f32[5,32,128]{2,1,0:T(8,128)S(1)}, f32[5,32,128]{2,1,0:T(8,128)S(1)}, u32[]{:S(2)}, u32[]{:S(2)}) collective-permute-start(f32[5,32,128]{2,1,0:T(8,128)S(1)} %get-tuple-element.113), channel_id=1, source_target_pairs={{0,4},{1,5},{4,0},{5,1},{8,12},{9,13},{12,8},{13,9},{2,6},{3,7},{6... | collective-permute-start | bytes 245768 | tf_op jit(solution)/shard_map/ppermute | solution.py:679
  31.6 0.2 collective-permute-start.13
  31.8 3.0 %stress_inner.3 = (f32[3,16,32,128]{3,2,1,0:T(8,128)S(1)}, f32[9,4,32,128]{3,2,1,0:T(8,128)S(1)}, f32[3,16,32,128]{3,2,1,0:T(8,128)}, f32[6,16,32,128]{3,2,1,0:T...) custom-call(f32[3,12,32,128]{3,2,1,0:T(8,128)S(1)} %get-tuple-element.92.refs_0_, ...), custom_call_target="tpu_custom_call" | custom-call | bytes 11070000 | tf_op jit(solution)/shard_map/stress_inner/pallas_call | solution.py:640
  34.8 1.0 %stress_edge.3 = (f32[6,16,32,128]{3,2,1,0:T(8,128)}, f32[6,16,32,128]{3,2,1,0:T(8,128)}) custom-call(f32[3,16,32,128]{3,2,1,0:T(8,128)S(1)} %get-tuple-element.111.refs_0_, f32[9,4,32,128]{3,2,1,0:T(8,128)S(1)} %get-tuple-element.112.refs_1_, ...), custom_call_target="tpu_custom_call", output_to_operand_aliasing={{0}: (8, {}), {1}: (9, {})} | custom-call | bytes 3690000 | tf_op jit(solution)/shard_map/stress_edge/pallas_call | solution.py:640
  (15 shorter events, 0.0 us)
Async XLA Ops:
  0.6 5.1 %copy-start.1 = (f32[5,8]{1,0:T(8,128)S(1)}, f32[5,8]{1,0:T(8,128)}, u32[]{:S(2)}) copy-start(f32[5,8]{1,0:T(8,128)} %refs_8_.1) | copy-start | bytes 484
  2.4 3.3 %collective-permute-start = (f32[6,32,128]{2,1,0:T(8,128)S(1)}, f32[6,32,128]{2,1,0:T(8,128)S(1)}, u32[]{:S(2)}, u32[]{:S(2)}) collective-permute-start(f32[6,32,128]{2,1,0:T(8,128)S(1)} %get-tuple-element.65), channel_id=1, source_target_pairs={{0,1},{1,0},{2,3},{3,2},{4,5},{5,4},{6,7},{7,6},{8,9},{9,8},{10,11... | collective-permute-start | bytes 294920 | tf_op jit(solution)/shard_map/ppermute | solution.py:679
  3.0 5.7 %collective-permute-start.1 = (f32[5,32,128]{2,1,0:T(8,128)S(1)}, f32[5,32,128]{2,1,0:T(8,128)S(1)}, u32[]{:S(2)}, u32[]{:S(2)}) collective-permute-start(f32[5,32,128]{2,1,0:T(8,128)S(1)} %get-tuple-element.72), channel_id=1, source_target_pairs={{0,4},{1,5},{4,0},{5,1},{8,12},{9,13},{12,8},{13,9},{2,6},{3,7},{6... | collective-permute-start | bytes 245768 | tf_op jit(solution)/shard_map/ppermute | solution.py:679
  5.6 3.0 %collective-permute-start.2 = (f32[5,32,128]{2,1,0:T(8,128)S(1)}, f32[5,32,128]{2,1,0:T(8,128)S(1)}, u32[]{:S(2)}, u32[]{:S(2)}) collective-permute-start(f32[5,32,128]{2,1,0:T(8,128)S(1)} %get-tuple-element.73), channel_id=1, source_target_pairs={{0,1},{1,0},{4,8},{5,9},{8,4},{9,5},{12,13},{13,12},{2,3},{3,2},{6... | collective-permute-start | bytes 245768 | tf_op jit(solution)/shard_map/ppermute | solution.py:679
  7.7 5.3 %copy-start.2 = (f32[3,4]{1,0:T(4,128)S(1)}, f32[3,4]{1,0:T(4,128)}, u32[]{:S(2)}) copy-start(f32[3,4]{1,0:T(4,128)} %refs_5_.5) | copy-start | bytes 148
  7.7 5.3 %copy-start.3 = (s32[2]{0:T(128)S(1)}, s32[2]{0:T(128)}, u32[]{:S(2)}) copy-start(s32[2]{0:T(128)} %refs_6_.7) | copy-start | bytes 28
  8.7 8.3 %copy-start = (f32[6,16,32,128]{3,2,1,0:T(8,128)S(1)}, f32[6,16,32,128]{3,2,1,0:T(8,128)}, u32[]{:S(2)}) copy-start(f32[6,16,32,128]{3,2,1,0:T(8,128)} %refs_3_.5) | copy-start | bytes 4718596
  8.8 4.2 %collective-permute-start.3 = (f32[96,128]{1,0:T(8,128)S(1)}, f32[96,128]{1,0:T(8,128)S(1)}, u32[]{:S(2)}, u32[]{:S(2)}) collective-permute-start(f32[96,128]{1,0:T(8,128)S(1)} %get-tuple-element.81.refs_3_.refs_9_), channel_id=1, source_target_pairs={{0,2},{2,0},{1,3},{3,1},{4,6},{6,4},{5,7},{7,5},{8,10},{10,8},{9,1... | collective-permute-start | bytes 147464 | tf_op jit(solution)/shard_map/ppermute | solution.py:679
  13.7 3.2 %collective-permute-start.4 = (f32[6,32,128]{2,1,0:T(8,128)S(1)}, f32[6,32,128]{2,1,0:T(8,128)S(1)}, u32[]{:S(2)}, u32[]{:S(2)}) collective-permute-start(f32[6,32,128]{2,1,0:T(8,128)S(1)} %get-tuple-element.83), channel_id=1, source_target_pairs={{0,1},{1,0},{2,3},{3,2},{4,5},{5,4},{6,7},{7,6},{8,9},{9,8},{10,11... | collective-permute-start | bytes 294920 | tf_op jit(solution)/shard_map/ppermute | solution.py:679
  13.8 6.0 %collective-permute-start.5 = (f32[5,32,128]{2,1,0:T(8,128)S(1)}, f32[5,32,128]{2,1,0:T(8,128)S(1)}, u32[]{:S(2)}, u32[]{:S(2)}) collective-permute-start(f32[5,32,128]{2,1,0:T(8,128)S(1)} %get-tuple-element.87), channel_id=1, source_target_pairs={{0,4},{1,5},{4,0},{5,1},{8,12},{9,13},{12,8},{13,9},{2,6},{3,7},{6... | collective-permute-start | bytes 245768 | tf_op jit(solution)/shard_map/ppermute | solution.py:679
  16.8 3.0 %collective-permute-start.6 = (f32[5,32,128]{2,1,0:T(8,128)S(1)}, f32[5,32,128]{2,1,0:T(8,128)S(1)}, u32[]{:S(2)}, u32[]{:S(2)}) collective-permute-start(f32[5,32,128]{2,1,0:T(8,128)S(1)} %get-tuple-element.88), channel_id=1, source_target_pairs={{0,1},{1,0},{4,8},{5,9},{8,4},{9,5},{12,13},{13,12},{2,3},{3,2},{6... | collective-permute-start | bytes 245768 | tf_op jit(solution)/shard_map/ppermute | solution.py:679
  20.1 2.1 %collective-permute-start.7 = (f32[6,32,128]{2,1,0:T(8,128)S(1)}, f32[6,32,128]{2,1,0:T(8,128)S(1)}, u32[]{:S(2)}, u32[]{:S(2)}) collective-permute-start(f32[6,32,128]{2,1,0:T(8,128)S(1)} %get-tuple-element.91), channel_id=1, source_target_pairs={{0,1},{1,0},{2,3},{3,2},{4,5},{5,4},{6,7},{7,6},{8,9},{9,8},{10,11... | collective-permute-start | bytes 294920 | tf_op jit(solution)/shard_map/ppermute | solution.py:679
  20.1 4.9 %collective-permute-start.8 = (f32[5,32,128]{2,1,0:T(8,128)S(1)}, f32[5,32,128]{2,1,0:T(8,128)S(1)}, u32[]{:S(2)}, u32[]{:S(2)}) collective-permute-start(f32[5,32,128]{2,1,0:T(8,128)S(1)} %get-tuple-element.93), channel_id=1, source_target_pairs={{0,4},{1,5},{4,0},{5,1},{8,12},{9,13},{12,8},{13,9},{2,6},{3,7},{6... | collective-permute-start | bytes 245768 | tf_op jit(solution)/shard_map/ppermute | solution.py:679
  21.9 3.0 %collective-permute-start.9 = (f32[5,32,128]{2,1,0:T(8,128)S(1)}, f32[5,32,128]{2,1,0:T(8,128)S(1)}, u32[]{:S(2)}, u32[]{:S(2)}) collective-permute-start(f32[5,32,128]{2,1,0:T(8,128)S(1)} %get-tuple-element.94), channel_id=1, source_target_pairs={{0,1},{1,0},{4,8},{5,9},{8,4},{9,5},{12,13},{13,12},{2,3},{3,2},{6... | collective-permute-start | bytes 245768 | tf_op jit(solution)/shard_map/ppermute | solution.py:679
  25.2 3.8 %collective-permute-start.10 = (f32[32,128]{1,0:T(8,128)S(1)}, f32[32,128]{1,0:T(8,128)S(1)}, u32[]{:S(2)}, u32[]{:S(2)}) collective-permute-start(f32[32,128]{1,0:T(8,128)S(1)} %get-tuple-element.102.refs_3_), channel_id=1, source_target_pairs={{0,2},{2,0},{1,3},{3,1},{4,6},{6,4},{5,7},{7,5},{8,10},{10,8},{9,1... | collective-permute-start | bytes 49160 | tf_op jit(solution)/shard_map/ppermute | solution.py:679
  29.7 2.1 %collective-permute-start.11 = (f32[6,32,128]{2,1,0:T(8,128)S(1)}, f32[6,32,128]{2,1,0:T(8,128)S(1)}, u32[]{:S(2)}, u32[]{:S(2)}) collective-permute-start(f32[6,32,128]{2,1,0:T(8,128)S(1)} %get-tuple-element.108), channel_id=1, source_target_pairs={{0,1},{1,0},{2,3},{3,2},{4,5},{5,4},{6,7},{7,6},{8,9},{9,8},{10,11... | collective-permute-start | bytes 294920 | tf_op jit(solution)/shard_map/ppermute | solution.py:679
  29.8 5.0 %collective-permute-start.12 = (f32[5,32,128]{2,1,0:T(8,128)S(1)}, f32[5,32,128]{2,1,0:T(8,128)S(1)}, u32[]{:S(2)}, u32[]{:S(2)}) collective-permute-start(f32[5,32,128]{2,1,0:T(8,128)S(1)} %get-tuple-element.113), channel_id=1, source_target_pairs={{0,4},{1,5},{4,0},{5,1},{8,12},{9,13},{12,8},{13,9},{2,6},{3,7},{6... | collective-permute-start | bytes 245768 | tf_op jit(solution)/shard_map/ppermute | solution.py:679
  31.6 3.2 %collective-permute-start.13 = (f32[5,32,128]{2,1,0:T(8,128)S(1)}, f32[5,32,128]{2,1,0:T(8,128)S(1)}, u32[]{:S(2)}, u32[]{:S(2)}) collective-permute-start(f32[5,32,128]{2,1,0:T(8,128)S(1)} %get-tuple-element.114), channel_id=1, source_target_pairs={{0,1},{1,0},{4,8},{5,9},{8,4},{9,5},{12,13},{13,12},{2,3},{3,2},{6... | collective-permute-start | bytes 245768 | tf_op jit(solution)/shard_map/ppermute | solution.py:679

commit v14 on v13

--- a/solution.py
+++ b/solution.py
@@ -440,12 +440,9 @@
     half = r.slip_out.shape[0]
     if half < count:
         new_slip = jnp.where(plus, new_slip[half:], new_slip[:half])
-    r.slip_out[...] = new_slip
     sign = jnp.where(minus, DT, 0.0) * minus_b - jnp.where(plus, DT, 0.0) * plus_b
     change_x = (trial_x * factor - pre_x) * sign
     change_z = (trial_z * factor - pre_z) * sign
-    r.change_out[0] = change_x
-    r.change_out[1] = change_z
 
     fault = fault_row(rows)
     on_fault = lax.broadcasted_iota(jnp.int32, (rows, depths), 0) == fault
@@ -463,9 +460,6 @@
         one, two = jnp.where(even, right, left), jnp.where(even, left, right)
         one = r.one[i] + jnp.where(on_fault, one, 0.0)
         pairs.append((one, r.two[i] + jnp.where(on_fault, two, 0.0)))
-    for i, (one, two) in enumerate(pairs):
-        r.one_out[i] = one
-        r.two_out[i] = two
     ends = jnp.zeros((count, depths), jnp.float32)
     pair = lax.broadcasted_iota(jnp.int32, (count, depths), 1) // 2
     place = 4 * lax.broadcasted_iota(jnp.int32, (count, depths), 0)
@@ -475,7 +469,15 @@
         turned = pltpu.roll(turned, 2 * k, 1, stride=8, stride_axis=0)
         ends = jnp.where(pair == place + k, turned, ends)
     line = jnp.sum(ends, axis=0, keepdims=True)
-    set_strip(r, r.strip[0] + jnp.where(on_fault, line, 0.0))
+    strip = r.strip[0] + jnp.where(on_fault, line, 0.0)
+
+    for i, (one, two) in enumerate(pairs):
+        r.one_out[i] = one
+        r.two_out[i] = two
+    set_strip(r, strip)
+    r.slip_out[...] = new_slip
+    r.change_out[0] = change_x
+    r.change_out[1] = change_z
 
 
 def elastic_rates(planes, x, beside, lame, shear):

time: 36 us -> 36 us (level)
  no operation moved by 1% of the time
where the time goes in v14:
time: 36 us; the launch traced here: 35.8 us
  Pallas kernels  14 us (39%)
  starting transfers between devices  13.9 us (39%)
  waiting for transfers between devices  7.12 us (20%)
  between operations  0.76 us (2%)
    pallas_call x11, Pallas kernels, call(): pl.pallas_call(body, out_shape=shapes, in_specs=[place(key) for key in in...  14 us
    ppermute x14, starting transfers between devices, sent(): return lax.ppermute(block, *route)  13.9 us
    ppermute x14, waiting for transfers between devices, sent(): return lax.ppermute(block, *route)  7.12 us
  transfers between devices with their start and end apart: 14, of which 5 were waited for; matrix products, arithmetic and copies ran while one was open for 0% of the time, Pallas kernels for 25%

profile of v14, /device:TPU:0, one launch (start us, length us, event | category | flops | bytes accessed | tf_op | source)
XLA Modules:
  0.0 35.8 jit_solution(2111846992372064543)
XLA Ops:
  0.6 1.8 %pack.1 = (f32[5,32,128]{2,1,0:T(8,128)S(1)}, f32[5,32,128]{2,1,0:T(8,128)S(1)}, f32[6,32,128]{2,1,0:T(8,128)S(1)}, f32[6,16,32,128]{3,2,1,0:T(8,128)S(1)}, f32[...) custom-call(f32[6,16,32,128]{3,2,1,0:T(8,128)} %refs_0_.1, ...), custom_call_target="tpu_custom_call" | custom-call | bytes 3690000 | tf_op jit(solution)/shard_map/pack/pallas_call | solution.py:642
  2.4 0.5 %collective-permute-start = (f32[6,32,128]{2,1,0:T(8,128)S(1)}, f32[6,32,128]{2,1,0:T(8,128)S(1)}, u32[]{:S(2)}, u32[]{:S(2)}) collective-permute-start(f32[6,32,128]{2,1,0:T(8,128)S(1)} %get-tuple-element.65), channel_id=1, source_target_pairs={{0,1},{1,0},{2,3},{3,2},{4,5},{5,4},{6,7},{7,6},{8,9},{9,8},{10,11... | collective-permute-start | bytes 294920 | tf_op jit(solution)/shard_map/ppermute | solution.py:681
  3.0 2.6 %collective-permute-start.1 = (f32[5,32,128]{2,1,0:T(8,128)S(1)}, f32[5,32,128]{2,1,0:T(8,128)S(1)}, u32[]{:S(2)}, u32[]{:S(2)}) collective-permute-start(f32[5,32,128]{2,1,0:T(8,128)S(1)} %get-tuple-element.72), channel_id=1, source_target_pairs={{0,4},{1,5},{4,0},{5,1},{8,12},{9,13},{12,8},{13,9},{2,6},{3,7},{6... | collective-permute-start | bytes 245768 | tf_op jit(solution)/shard_map/ppermute | solution.py:681
  5.6 0.2 collective-permute-start.2
  5.8 1.9 %velocity_inner.2 = (f32[3,12,32,128]{3,2,1,0:T(8,128)S(1)}, f32[4,4,32,128]{3,2,1,0:T(8,128)S(1)}, f32[32,128]{1,0:T(8,128)S(1)}, f32[96,128]{1,0:T(8,128)S(1)}) custom-call(f32[3,16,32,128]{3,2,1,0:T(8,128)S(1)} %get-tuple-element.62.refs_0_, f32[6,16,32,128]{3,2,1,0:T(8,128)S(1)} %get-tuple-element.63.refs_1_.refs_3_.refs_2_, ...), custom_call_target="tpu_custom_call" | custom-call | bytes 11070000 | tf_op jit(solution)/shard_map/velocity_inner/pallas_call | solution.py:642
  7.7 0.0 copy-start.2
  7.7 0.0 copy-start.3
  7.7 1.0 %collective-permute-done.1.refs_2_ = f32[5,32,128]{2,1,0:T(8,128)S(1)} collective-permute-done((f32[5,32,128]{2,1,0:T(8,128)S(1)}, f32[5,32,128]{2,1,0:T(8,128)S(1)}, u32[]{:S(2)}, u32[]{:S(2)}) %collective-permute-start.1) | collective-permute-done | bytes 81952 | tf_op jit(solution)/shard_map/ppermute | solution.py:681
  8.7 0.2 velocity_edge.2
  8.8 1.7 %collective-permute-start.3 = (f32[96,128]{1,0:T(8,128)S(1)}, f32[96,128]{1,0:T(8,128)S(1)}, u32[]{:S(2)}, u32[]{:S(2)}) collective-permute-start(f32[96,128]{1,0:T(8,128)S(1)} %get-tuple-element.81.refs_3_.refs_9_), channel_id=1, source_target_pairs={{0,2},{2,0},{1,3},{3,1},{4,6},{6,4},{5,7},{7,5},{8,10},{10,8},{9,1... | collective-permute-start | bytes 147464 | tf_op jit(solution)/shard_map/ppermute | solution.py:681
  10.6 2.4 %collective-permute-done.3.refs_4_.refs_10_ = f32[96,128]{1,0:T(8,128)S(1)} collective-permute-done((f32[96,128]{1,0:T(8,128)S(1)}, f32[96,128]{1,0:T(8,128)S(1)}, u32[]{:S(2)}, u32[]{:S(2)}) %collective-permute-start.3) | collective-permute-done | bytes 49184 | tf_op jit(solution)/shard_map/ppermute | solution.py:681
  13.0 0.8 %fault.2 = (f32[2,16,128]{2,1,0:T(8,128)S(1)}, f32[16,128]{1,0:T(8,128)S(1)}, f32[5,32,128]{2,1,0:T(8,128)S(1)}, f32[5,32,128]{2,1,0:T(8,128)S(1)}, f32[6,32,128...) custom-call(f32[5,32,128]{2,1,0:T(8,128)S(1)} %get-tuple-element.78.refs_0_, f32[5,32,128]{2,1,0:T(8,128)S(1)} %get-tuple-element.79.refs_1_, ...), custom_call_target="tpu_custom_call" | custom-call | bytes 3690000 | tf_op jit(solution)/shard_map/fault/pallas_call | solution.py:642
  13.7 0.1 collective-permute-start.4
  13.8 2.9 %collective-permute-start.5 = (f32[5,32,128]{2,1,0:T(8,128)S(1)}, f32[5,32,128]{2,1,0:T(8,128)S(1)}, u32[]{:S(2)}, u32[]{:S(2)}) collective-permute-start(f32[5,32,128]{2,1,0:T(8,128)S(1)} %get-tuple-element.87), channel_id=1, source_target_pairs={{0,4},{1,5},{4,0},{5,1},{8,12},{9,13},{12,8},{13,9},{2,6},{3,7},{6... | collective-permute-start | bytes 245768 | tf_op jit(solution)/shard_map/ppermute | solution.py:681
  16.8 0.2 collective-permute-start.6
  16.9 2.4 %stress_inner.2 = (f32[3,16,32,128]{3,2,1,0:T(8,128)S(1)}, f32[9,4,32,128]{3,2,1,0:T(8,128)S(1)}, f32[6,12,32,128]{3,2,1,0:T(8,128)S(1)}, f32[6,12,32,128]{3,2,1,0:T(8,128)S(1)}, f32[32,128]{1,0:T(8,128)S(1)}) custom-call(f32[3,12,32,128]{3,2,1,0:T(8,128)S(1)} %get-tuple-element.71.refs_0_, f32[3,4,32,128]{3,2,1,0:T(8,128)S(1)} %get-tuple-element.77.refs_1_, ...), custom_call_target="tpu_custom_call" | custom-call | bytes 11070000 | tf_op jit(solution)/shard_map/stress_inner/pallas_call | solution.py:642
  19.4 0.5 %collective-permute-done.5.refs_4_ = f32[5,32,128]{2,1,0:T(8,128)S(1)} collective-permute-done((f32[5,32,128]{2,1,0:T(8,128)S(1)}, f32[5,32,128]{2,1,0:T(8,128)S(1)}, u32[]{:S(2)}, u32[]{:S(2)}) %collective-permute-start.5) | collective-permute-done | bytes 81952 | tf_op jit(solution)/shard_map/ppermute | solution.py:681
  19.8 0.2 stress_edge.2
  20.1 0.1 collective-permute-start.7
  20.1 1.8 %collective-permute-start.8 = (f32[5,32,128]{2,1,0:T(8,128)S(1)}, f32[5,32,128]{2,1,0:T(8,128)S(1)}, u32[]{:S(2)}, u32[]{:S(2)}) collective-permute-start(f32[5,32,128]{2,1,0:T(8,128)S(1)} %get-tuple-element.93), channel_id=1, source_target_pairs={{0,4},{1,5},{4,0},{5,1},{8,12},{9,13},{12,8},{13,9},{2,6},{3,7},{6... | collective-permute-start | bytes 245768 | tf_op jit(solution)/shard_map/ppermute | solution.py:681
  21.9 0.2 collective-permute-start.9
  22.1 1.8 %velocity_inner.3 = (f32[3,12,32,128]{3,2,1,0:T(8,128)S(1)}, f32[4,4,32,128]{3,2,1,0:T(8,128)S(1)}, f32[32,128]{1,0:T(8,128)S(1)}, f32[32,128]{1,0:T(8,128)S(1)}) custom-call(f32[3,16,32,128]{3,2,1,0:T(8,128)S(1)} %get-tuple-element.84.refs_0_, f32[6,12,32,128]{3,2,1,0:T(8,128)S(1)} %get-tuple-element.85.refs_1_.refs_3_.refs_2_, ...), custom_call_target="tpu_custom_call" | custom-call | bytes 11070000 | tf_op jit(solution)/shard_map/velocity_inner/pallas_call | solution.py:642
  24.0 1.0 %collective-permute-done.8.refs_3_ = f32[5,32,128]{2,1,0:T(8,128)S(1)} collective-permute-done((f32[5,32,128]{2,1,0:T(8,128)S(1)}, f32[5,32,128]{2,1,0:T(8,128)S(1)}, u32[]{:S(2)}, u32[]{:S(2)}) %collective-permute-start.8) | collective-permute-done | bytes 81952 | tf_op jit(solution)/shard_map/ppermute | solution.py:681
  25.0 0.2 velocity_edge.3
  25.2 1.6 %collective-permute-start.10 = (f32[32,128]{1,0:T(8,128)S(1)}, f32[32,128]{1,0:T(8,128)S(1)}, u32[]{:S(2)}, u32[]{:S(2)}) collective-permute-start(f32[32,128]{1,0:T(8,128)S(1)} %get-tuple-element.102.refs_3_), channel_id=1, source_target_pairs={{0,2},{2,0},{1,3},{3,1},{4,6},{6,4},{5,7},{7,5},{8,10},{10,8},{9,1... | collective-permute-start | bytes 49160 | tf_op jit(solution)/shard_map/ppermute | solution.py:681
  26.7 2.2 %collective-permute-done.10.refs_4_ = f32[32,128]{1,0:T(8,128)S(1)} collective-permute-done((f32[32,128]{1,0:T(8,128)S(1)}, f32[32,128]{1,0:T(8,128)S(1)}, u32[]{:S(2)}, u32[]{:S(2)}) %collective-permute-start.10) | collective-permute-done | bytes 16416 | tf_op jit(solution)/shard_map/ppermute | solution.py:681
  29.0 0.8 %fault.3 = (f32[2,16,128]{2,1,0:T(8,128)S(1)}, f32[8,128]{1,0:T(8,128)S(1)}, f32[5,32,128]{2,1,0:T(8,128)S(1)}, f32[5,32,128]{2,1,0:T(8,128)S(1)}, f32[6,32,128]{2,1,0:T(8,128)S(1)}) custom-call(f32[5,32,128]{2,1,0:T(8,128)S(1)} %get-tuple-element.99.refs_0_, f32[5,32,128]{2,1,0:T(8,128)S(1)} %get-tuple-element.100.refs_1_, ...), custom_call_target="tpu_custom_call" | custom-call | bytes 3690000 | tf_op jit(solution)/shard_map/fault/pallas_call | solution.py:642
  29.7 0.1 collective-permute-start.11
  29.8 1.8 %collective-permute-start.12 = (f32[5,32,128]{2,1,0:T(8,128)S(1)}, f32[5,32,128]{2,1,0:T(8,128)S(1)}, u32[]{:S(2)}, u32[]{:S(2)}) collective-permute-start(f32[5,32,128]{2,1,0:T(8,128)S(1)} %get-tuple-element.113), channel_id=1, source_target_pairs={{0,4},{1,5},{4,0},{5,1},{8,12},{9,13},{12,8},{13,9},{2,6},{3,7},{6... | collective-permute-start | bytes 245768 | tf_op jit(solution)/shard_map/ppermute | solution.py:681
  31.6 0.2 collective-permute-start.13
  31.8 3.0 %stress_inner.3 = (f32[3,16,32,128]{3,2,1,0:T(8,128)S(1)}, f32[9,4,32,128]{3,2,1,0:T(8,128)S(1)}, f32[3,16,32,128]{3,2,1,0:T(8,128)}, f32[6,16,32,128]{3,2,1,0:T...) custom-call(f32[3,12,32,128]{3,2,1,0:T(8,128)S(1)} %get-tuple-element.92.refs_0_, ...), custom_call_target="tpu_custom_call" | custom-call | bytes 11070000 | tf_op jit(solution)/shard_map/stress_inner/pallas_call | solution.py:642
  34.8 1.0 %stress_edge.3 = (f32[6,16,32,128]{3,2,1,0:T(8,128)}, f32[6,16,32,128]{3,2,1,0:T(8,128)}) custom-call(f32[3,16,32,128]{3,2,1,0:T(8,128)S(1)} %get-tuple-element.111.refs_0_, f32[9,4,32,128]{3,2,1,0:T(8,128)S(1)} %get-tuple-element.112.refs_1_, ...), custom_call_target="tpu_custom_call", output_to_operand_aliasing={{0}: (8, {}), {1}: (9, {})} | custom-call | bytes 3690000 | tf_op jit(solution)/shard_map/stress_edge/pallas_call | solution.py:642
  (15 shorter events, 0.0 us)
Async XLA Ops:
  0.6 5.1 %copy-start.1 = (f32[5,8]{1,0:T(8,128)S(1)}, f32[5,8]{1,0:T(8,128)}, u32[]{:S(2)}) copy-start(f32[5,8]{1,0:T(8,128)} %refs_8_.1) | copy-start | bytes 484
  2.4 3.3 %collective-permute-start = (f32[6,32,128]{2,1,0:T(8,128)S(1)}, f32[6,32,128]{2,1,0:T(8,128)S(1)}, u32[]{:S(2)}, u32[]{:S(2)}) collective-permute-start(f32[6,32,128]{2,1,0:T(8,128)S(1)} %get-tuple-element.65), channel_id=1, source_target_pairs={{0,1},{1,0},{2,3},{3,2},{4,5},{5,4},{6,7},{7,6},{8,9},{9,8},{10,11... | collective-permute-start | bytes 294920 | tf_op jit(solution)/shard_map/ppermute | solution.py:681
  3.0 5.7 %collective-permute-start.1 = (f32[5,32,128]{2,1,0:T(8,128)S(1)}, f32[5,32,128]{2,1,0:T(8,128)S(1)}, u32[]{:S(2)}, u32[]{:S(2)}) collective-permute-start(f32[5,32,128]{2,1,0:T(8,128)S(1)} %get-tuple-element.72), channel_id=1, source_target_pairs={{0,4},{1,5},{4,0},{5,1},{8,12},{9,13},{12,8},{13,9},{2,6},{3,7},{6... | collective-permute-start | bytes 245768 | tf_op jit(solution)/shard_map/ppermute | solution.py:681
  5.6 3.0 %collective-permute-start.2 = (f32[5,32,128]{2,1,0:T(8,128)S(1)}, f32[5,32,128]{2,1,0:T(8,128)S(1)}, u32[]{:S(2)}, u32[]{:S(2)}) collective-permute-start(f32[5,32,128]{2,1,0:T(8,128)S(1)} %get-tuple-element.73), channel_id=1, source_target_pairs={{0,1},{1,0},{4,8},{5,9},{8,4},{9,5},{12,13},{13,12},{2,3},{3,2},{6... | collective-permute-start | bytes 245768 | tf_op jit(solution)/shard_map/ppermute | solution.py:681
  7.7 5.3 %copy-start.2 = (f32[3,4]{1,0:T(4,128)S(1)}, f32[3,4]{1,0:T(4,128)}, u32[]{:S(2)}) copy-start(f32[3,4]{1,0:T(4,128)} %refs_5_.5) | copy-start | bytes 148
  7.7 5.3 %copy-start.3 = (s32[2]{0:T(128)S(1)}, s32[2]{0:T(128)}, u32[]{:S(2)}) copy-start(s32[2]{0:T(128)} %refs_6_.7) | copy-start | bytes 28
  8.7 8.3 %copy-start = (f32[6,16,32,128]{3,2,1,0:T(8,128)S(1)}, f32[6,16,32,128]{3,2,1,0:T(8,128)}, u32[]{:S(2)}) copy-start(f32[6,16,32,128]{3,2,1,0:T(8,128)} %refs_3_.5) | copy-start | bytes 4718596
  8.8 4.2 %collective-permute-start.3 = (f32[96,128]{1,0:T(8,128)S(1)}, f32[96,128]{1,0:T(8,128)S(1)}, u32[]{:S(2)}, u32[]{:S(2)}) collective-permute-start(f32[96,128]{1,0:T(8,128)S(1)} %get-tuple-element.81.refs_3_.refs_9_), channel_id=1, source_target_pairs={{0,2},{2,0},{1,3},{3,1},{4,6},{6,4},{5,7},{7,5},{8,10},{10,8},{9,1... | collective-permute-start | bytes 147464 | tf_op jit(solution)/shard_map/ppermute | solution.py:681
  13.7 3.2 %collective-permute-start.4 = (f32[6,32,128]{2,1,0:T(8,128)S(1)}, f32[6,32,128]{2,1,0:T(8,128)S(1)}, u32[]{:S(2)}, u32[]{:S(2)}) collective-permute-start(f32[6,32,128]{2,1,0:T(8,128)S(1)} %get-tuple-element.83), channel_id=1, source_target_pairs={{0,1},{1,0},{2,3},{3,2},{4,5},{5,4},{6,7},{7,6},{8,9},{9,8},{10,11... | collective-permute-start | bytes 294920 | tf_op jit(solution)/shard_map/ppermute | solution.py:681
  13.8 6.0 %collective-permute-start.5 = (f32[5,32,128]{2,1,0:T(8,128)S(1)}, f32[5,32,128]{2,1,0:T(8,128)S(1)}, u32[]{:S(2)}, u32[]{:S(2)}) collective-permute-start(f32[5,32,128]{2,1,0:T(8,128)S(1)} %get-tuple-element.87), channel_id=1, source_target_pairs={{0,4},{1,5},{4,0},{5,1},{8,12},{9,13},{12,8},{13,9},{2,6},{3,7},{6... | collective-permute-start | bytes 245768 | tf_op jit(solution)/shard_map/ppermute | solution.py:681
  16.8 3.0 %collective-permute-start.6 = (f32[5,32,128]{2,1,0:T(8,128)S(1)}, f32[5,32,128]{2,1,0:T(8,128)S(1)}, u32[]{:S(2)}, u32[]{:S(2)}) collective-permute-start(f32[5,32,128]{2,1,0:T(8,128)S(1)} %get-tuple-element.88), channel_id=1, source_target_pairs={{0,1},{1,0},{4,8},{5,9},{8,4},{9,5},{12,13},{13,12},{2,3},{3,2},{6... | collective-permute-start | bytes 245768 | tf_op jit(solution)/shard_map/ppermute | solution.py:681
  20.1 2.1 %collective-permute-start.7 = (f32[6,32,128]{2,1,0:T(8,128)S(1)}, f32[6,32,128]{2,1,0:T(8,128)S(1)}, u32[]{:S(2)}, u32[]{:S(2)}) collective-permute-start(f32[6,32,128]{2,1,0:T(8,128)S(1)} %get-tuple-element.91), channel_id=1, source_target_pairs={{0,1},{1,0},{2,3},{3,2},{4,5},{5,4},{6,7},{7,6},{8,9},{9,8},{10,11... | collective-permute-start | bytes 294920 | tf_op jit(solution)/shard_map/ppermute | solution.py:681
  20.1 4.9 %collective-permute-start.8 = (f32[5,32,128]{2,1,0:T(8,128)S(1)}, f32[5,32,128]{2,1,0:T(8,128)S(1)}, u32[]{:S(2)}, u32[]{:S(2)}) collective-permute-start(f32[5,32,128]{2,1,0:T(8,128)S(1)} %get-tuple-element.93), channel_id=1, source_target_pairs={{0,4},{1,5},{4,0},{5,1},{8,12},{9,13},{12,8},{13,9},{2,6},{3,7},{6... | collective-permute-start | bytes 245768 | tf_op jit(solution)/shard_map/ppermute | solution.py:681
  21.9 3.0 %collective-permute-start.9 = (f32[5,32,128]{2,1,0:T(8,128)S(1)}, f32[5,32,128]{2,1,0:T(8,128)S(1)}, u32[]{:S(2)}, u32[]{:S(2)}) collective-permute-start(f32[5,32,128]{2,1,0:T(8,128)S(1)} %get-tuple-element.94), channel_id=1, source_target_pairs={{0,1},{1,0},{4,8},{5,9},{8,4},{9,5},{12,13},{13,12},{2,3},{3,2},{6... | collective-permute-start | bytes 245768 | tf_op jit(solution)/shard_map/ppermute | solution.py:681
  25.2 3.8 %collective-permute-start.10 = (f32[32,128]{1,0:T(8,128)S(1)}, f32[32,128]{1,0:T(8,128)S(1)}, u32[]{:S(2)}, u32[]{:S(2)}) collective-permute-start(f32[32,128]{1,0:T(8,128)S(1)} %get-tuple-element.102.refs_3_), channel_id=1, source_target_pairs={{0,2},{2,0},{1,3},{3,1},{4,6},{6,4},{5,7},{7,5},{8,10},{10,8},{9,1... | collective-permute-start | bytes 49160 | tf_op jit(solution)/shard_map/ppermute | solution.py:681
  29.7 2.1 %collective-permute-start.11 = (f32[6,32,128]{2,1,0:T(8,128)S(1)}, f32[6,32,128]{2,1,0:T(8,128)S(1)}, u32[]{:S(2)}, u32[]{:S(2)}) collective-permute-start(f32[6,32,128]{2,1,0:T(8,128)S(1)} %get-tuple-element.108), channel_id=1, source_target_pairs={{0,1},{1,0},{2,3},{3,2},{4,5},{5,4},{6,7},{7,6},{8,9},{9,8},{10,11... | collective-permute-start | bytes 294920 | tf_op jit(solution)/shard_map/ppermute | solution.py:681
  29.8 5.0 %collective-permute-start.12 = (f32[5,32,128]{2,1,0:T(8,128)S(1)}, f32[5,32,128]{2,1,0:T(8,128)S(1)}, u32[]{:S(2)}, u32[]{:S(2)}) collective-permute-start(f32[5,32,128]{2,1,0:T(8,128)S(1)} %get-tuple-element.113), channel_id=1, source_target_pairs={{0,4},{1,5},{4,0},{5,1},{8,12},{9,13},{12,8},{13,9},{2,6},{3,7},{6... | collective-permute-start | bytes 245768 | tf_op jit(solution)/shard_map/ppermute | solution.py:681
  31.6 3.2 %collective-permute-start.13 = (f32[5,32,128]{2,1,0:T(8,128)S(1)}, f32[5,32,128]{2,1,0:T(8,128)S(1)}, u32[]{:S(2)}, u32[]{:S(2)}) collective-permute-start(f32[5,32,128]{2,1,0:T(8,128)S(1)} %get-tuple-element.114), channel_id=1, source_target_pairs={{0,1},{1,0},{4,8},{5,9},{8,4},{9,5},{12,13},{13,12},{2,3},{3,2},{6... | collective-permute-start | bytes 245768 | tf_op jit(solution)/shard_map/ppermute | solution.py:681
